TPU v7x, 32 devices: a whole 2x2x4 slice. The times are simulated.
32 devices in a mesh: gx: 4 (over z), gy: 8 (over y, x, core).
Axes of the slice: x: 2, y: 2, z: 4, core: 2. Of those that a mesh axis runs over, the one named last changes fastest.
Arguments:
- temps: float32 [2, 128, 96, 128], P(None, 'gx', 'gy'), may hold values from 0.5 to 2
- right_side: float32 [2, 128, 96, 128], P(None, 'gx', 'gy'), may hold values from -5 to 5
- exchange: float32 [128, 96, 128], P('gx', 'gy'), may hold values from 0.1 to 1
- coupling: float32 [128, 96, 128], P('gx', 'gy'), may hold values from 0.05 to 0.5
Outputs:
- fields: float32 [2, 128, 96, 128], P(None, 'gx', 'gy')
All inputs are finite; a program needn't handle non-finite values.
Results may differ from a plain program's by a relative error of at most 0.000027.
Values sent between devices are 32-bit elements; how exact they have to be, the bound alone decides.
No kernel may reach another device: no remote copies, remote signals or barrier semaphores. Data moves between devices by JAX's collectives and lax.ppermute only.
A program may use at most 64 MiB of HBM per device.

v0:
```python
import jax
import jax.numpy as jnp
from jax import lax
from jax.sharding import PartitionSpec as P

SWEEPS = 2


solid_cap = 0.5
gas_cap = 0.02
flow_rate = 40.0
gas_conduct = 0.05
axis_weights = (1.0, 1.0, 1.0, 1.0, 0.25, 0.25)
relaxation = 0.8
lump_factor = 0.25


def padded_2(x, sides, width):
    for axis, dim in sides:
        count, length = (lax.axis_size(axis), x.shape[dim])
        up = [(i, (i + 1) % count) for i in range(count - 1)]
        down = [(j, i) for i, j in up]
        last = lax.slice_in_dim(x, length - width, length, axis=dim)
        leading = lax.slice_in_dim(x, 0, width, axis=dim)
        before = lax.ppermute(last, axis, up)
        after = lax.ppermute(leading, axis, down)
        x = jnp.concatenate([before, x, after], axis=dim)
    return x


def entering(part, axis, combine, identity):
    place = lax.axis_index(axis)
    gathered = jax.tree.map(lambda a: lax.all_gather(a, axis), part)
    state = jax.tree.map(lambda a, e: jnp.zeros_like(a) + jnp.asarray(e, a.dtype), part, identity)

    def one(lap, state):
        return combine(
            state, jax.tree.map(lambda a: lax.dynamic_index_in_dim(a, lap, 0, False), gathered)
        )

    return lax.fori_loop(0, place, one, state)


def neighbours(padded):
    center = padded[1:-1, 1:-1]
    z_padded = jnp.pad(center, ((0, 0), (0, 0), (1, 1)))
    return (
        center,
        (
            padded[2:, 1:-1],
            padded[:-2, 1:-1],
            padded[1:-1, 2:],
            padded[1:-1, :-2],
            z_padded[:, :, 2:],
            z_padded[:, :, :-2],
        ),
    )


def face_weights(cond_padded):
    conductivity, beside_all = neighbours(cond_padded)
    return tuple(
        (weight * 0.5 * (conductivity + other) for weight, other in zip(axis_weights, beside_all))
    )


def apply_operator(fields_padded, face_list, coupling):
    solid, solid_around = neighbours(fields_padded[0])
    gas, gas_around = neighbours(fields_padded[1])
    exchange_term = coupling * (solid - gas)
    solid_out = solid_cap * solid + exchange_term
    gas_out = gas_cap * gas - exchange_term + flow_rate * (gas - gas_around[3])
    for face, weight, other_solid, other_gas in zip(
        face_list, axis_weights, solid_around, gas_around
    ):
        solid_out = solid_out + face * (solid - other_solid)
        gas_out = gas_out + gas_conduct * weight * (gas - other_gas)
    return jnp.stack([solid_out, gas_out])


def relax_step(fields, residual, solid_diag, coupling):
    gas_diag = gas_cap + coupling + flow_rate + gas_conduct * 2.0 * 2.25
    determinant = solid_diag * gas_diag - coupling * coupling
    delta_solid = (gas_diag * residual[0] + coupling * residual[1]) / determinant
    delta_gas = (coupling * residual[0] + solid_diag * residual[1]) / determinant
    return fields + relaxation * jnp.stack([delta_solid, delta_gas])


def coarse_sum(array):
    shape = array.shape
    lead = shape[:-3]
    return array.reshape(lead + (shape[-3] // 2, 2, shape[-2] // 2, 2, shape[-1])).sum(
        axis=(-4, -2)
    )


def spread(coarse):
    shape = coarse.shape
    wide = jnp.broadcast_to(
        coarse[:, :, None, :, None, :], (shape[0], shape[1], 2, shape[2], 2, shape[3])
    )
    return wide.reshape((shape[0], shape[1] * 2, shape[2] * 2, shape[3]))


def line_combine(earlier, later):
    return (later[0] * earlier[0], later[0] * earlier[1] + later[1])


def shards(temps, right_side, exchange, coupling):
    conductivity = 1.0 + 4.0 * exchange * temps[0] ** 3
    cond_padded = padded_2(conductivity, (("gx", 0), ("gy", 1)), 1)
    face_list = face_weights(cond_padded)
    solid_diag = solid_cap + coupling + sum(face_list)

    def residual_of(fields):
        padded = padded_2(fields, (("gx", 1), ("gy", 2)), 1)
        return right_side - apply_operator(padded, face_list, coupling)

    def smooth(fields):
        for sweep_index in range(SWEEPS):
            fields = relax_step(fields, residual_of(fields), solid_diag, coupling)
        return fields

    fields = smooth(temps)
    coarse_res = coarse_sum(residual_of(fields))
    coupling_sum = coarse_sum(coupling)
    solid_coarse = 4.0 * solid_cap + coupling_sum + lump_factor * coarse_sum(conductivity)
    gas_coarse = 4.0 * gas_cap + coupling_sum + 2.0 * flow_rate
    denominator = gas_coarse - coupling_sum * coupling_sum / solid_coarse
    slope = 2.0 * flow_rate / denominator
    offset = (coarse_res[1] + coupling_sum * coarse_res[0] / solid_coarse) / denominator
    slope_cum, offset_cum = lax.associative_scan(line_combine, (slope, offset), axis=1)
    block_slope = slope_cum[:, -1, :]
    block_offset = offset_cum[:, -1, :]
    identity = (jnp.ones_like(block_slope), jnp.zeros_like(block_offset))
    prefix_slope, incoming = entering((block_slope, block_offset), "gy", line_combine, identity)
    gas_error = slope_cum * incoming[:, None, :] + offset_cum
    solid_error = (coarse_res[0] + coupling_sum * gas_error) / solid_coarse
    fields = fields + spread(jnp.stack([solid_error, gas_error]))
    return smooth(fields)


def solution(mesh):
    return jax.shard_map(
        shards,
        mesh=mesh,
        in_specs=(
            P(None, "gx", "gy", None),
            P(None, "gx", "gy", None),
            P("gx", "gy", None),
            P("gx", "gy", None),
        ),
        out_specs=P(None, "gx", "gy", None),
        check_vma=False,
    )
```

profile of v0, /device:TPU:3, one launch (start us, length us, event | category | flops | bytes accessed | tf_op | source)
XLA Modules:
  0.0 120.5 jit_solution(17700376192265020490)
XLA Ops:
  1.0 3.2 %collective-permute-start = (f32[2,1,12,128]{3,1,2,0:T(1,128)S(1)}, f32[2,1,12,128]{3,1,2,0:T(1,128)S(1)}, u32[]{:S(2)}, u32[]{:S(2)}) collective-permute-start(f32[2,1,12,128]{3,1,2,0:T(1,128)S(1)} %get-tuple-element.105), channel_id=1, source_target_pairs={{0,8},{8,16},{16,24},{1,9},{9,17},{17,25},{2,10},{10,18},{18,26},{... | collective-permute-start | bytes 36872 | tf_op jit(solution)/shard_map/ppermute | solution.py:25
  7.9 4.6 %collective-permute-start.5 = (f32[1,12,128]{2,0,1:T(1,128)S(1)}, f32[1,12,128]{2,0,1:T(1,128)S(1)}, u32[]{:S(2)}, u32[]{:S(2)}) collective-permute-start(f32[1,12,128]{2,0,1:T(1,128)S(1)} %get-tuple-element.119), channel_id=1, source_target_pairs={{0,8},{8,16},{16,24},{1,9},{9,17},{17,25},{2,10},{10,18},{18,26},{... | collective-permute-start | bytes 18440 | tf_op jit(solution)/shard_map/ppermute | solution.py:25
  12.6 4.5 %collective-permute-start.2 = (f32[2,34,1,128]{3,1,2,0:T(8,128)S(1)}, f32[2,34,1,128]{3,1,2,0:T(8,128)S(1)}, u32[]{:S(2)}, u32[]{:S(2)}) collective-permute-start(f32[2,34,1,128]{3,1,2,0:T(8,128)S(1)} %get-tuple-element.95), channel_id=1, source_target_pairs={{0,1},{1,2},{2,3},{3,4},{4,5},{5,6},{6,7},{8,9},{9,10},{10,11},{11... | collective-permute-start | bytes 104456 | tf_op jit(solution)/shard_map/ppermute | solution.py:25
  17.1 1.9 %collective-permute-start.3 = (f32[2,34,1,128]{3,1,2,0:T(8,128)S(1)}, f32[2,34,1,128]{3,1,2,0:T(8,128)S(1)}, u32[]{:S(2)}, u32[]{:S(2)}) collective-permute-start(f32[2,34,1,128]{3,1,2,0:T(8,128)S(1)} %get-tuple-element.96), channel_id=1, source_target_pairs={{1,0},{2,1},{3,2},{4,3},{5,4},{6,5},{7,6},{9,8},{10,9},{11,10},{12... | collective-permute-start | bytes 104456 | tf_op jit(solution)/shard_map/ppermute | solution.py:26
  19.1 2.5 %collective-permute-start.6 = (f32[34,1,128]{2,0,1:T(8,128)S(1)}, f32[34,1,128]{2,0,1:T(8,128)S(1)}, u32[]{:S(2)}, u32[]{:S(2)}) collective-permute-start(f32[34,1,128]{2,0,1:T(8,128)S(1)} %get-tuple-element.118), channel_id=1, source_target_pairs={{1,0},{2,1},{3,2},{4,3},{5,4},{6,5},{7,6},{9,8},{10,9},{11,10},{12... | collective-permute-start | bytes 52232 | tf_op jit(solution)/shard_map/ppermute | solution.py:26
  21.6 3.9 %collective-permute-start.7 = (f32[34,1,128]{2,0,1:T(8,128)S(1)}, f32[34,1,128]{2,0,1:T(8,128)S(1)}, u32[]{:S(2)}, u32[]{:S(2)}) collective-permute-start(f32[34,1,128]{2,0,1:T(8,128)S(1)} %get-tuple-element.117), channel_id=1, source_target_pairs={{0,1},{1,2},{2,3},{3,4},{4,5},{5,6},{6,7},{8,9},{9,10},{10,11},{11... | collective-permute-start | bytes 52232 | tf_op jit(solution)/shard_map/ppermute | solution.py:25
  28.4 3.6 %collective-permute-start.8 = (f32[2,1,12,128]{3,1,2,0:T(1,128)S(1)}, f32[2,1,12,128]{3,1,2,0:T(1,128)S(1)}, u32[]{:S(2)}, u32[]{:S(2)}) collective-permute-start(f32[2,1,12,128]{3,1,2,0:T(1,128)S(1)} %get-tuple-element.103), channel_id=1, source_target_pairs={{0,8},{8,16},{16,24},{1,9},{9,17},{17,25},{2,10},{10,18},{18,26},{... | collective-permute-start | bytes 36872 | tf_op jit(solution)/shard_map/ppermute | solution.py:25
  33.3 3.1 %collective-permute-done.9 = f32[2,1,12,128]{3,1,2,0:T(1,128)S(1)} collective-permute-done((f32[2,1,12,128]{3,1,2,0:T(1,128)S(1)}, f32[2,1,12,128]{3,1,2,0:T(1,128)S(1)}, u32[]{:S(2)}, u32[]{:S(2)}) %collective-permute-start.9) | collective-permute-done | bytes 12320 | tf_op jit(solution)/shard_map/ppermute | solution.py:26
  36.5 6.1 %collective-permute-start.10 = (f32[2,34,1,128]{3,1,2,0:T(8,128)S(1)}, f32[2,34,1,128]{3,1,2,0:T(8,128)S(1)}, u32[]{:S(2)}, u32[]{:S(2)}) collective-permute-start(f32[2,34,1,128]{3,1,2,0:T(8,128)S(1)} %get-tuple-element.93), channel_id=1, source_target_pairs={{0,1},{1,2},{2,3},{3,4},{4,5},{5,6},{6,7},{8,9},{9,10},{10,11},{11... | collective-permute-start | bytes 104456 | tf_op jit(solution)/shard_map/ppermute | solution.py:25
  42.6 1.9 %collective-permute-start.11 = (f32[2,34,1,128]{3,1,2,0:T(8,128)S(1)}, f32[2,34,1,128]{3,1,2,0:T(8,128)S(1)}, u32[]{:S(2)}, u32[]{:S(2)}) collective-permute-start(f32[2,34,1,128]{3,1,2,0:T(8,128)S(1)} %get-tuple-element.94), channel_id=1, source_target_pairs={{1,0},{2,1},{3,2},{4,3},{5,4},{6,5},{7,6},{9,8},{10,9},{11,10},{12... | collective-permute-start | bytes 104456 | tf_op jit(solution)/shard_map/ppermute | solution.py:26
  44.5 4.3 %collective-permute-done.11 = f32[2,34,1,128]{3,1,2,0:T(8,128)S(1)} collective-permute-done((f32[2,34,1,128]{3,1,2,0:T(8,128)S(1)}, f32[2,34,1,128]{3,1,2,0:T(8,128)S(1)}, u32[]{:S(2)}, u32[]{:S(2)}) %collective-permute-start.11) | collective-permute-done | bytes 34848 | tf_op jit(solution)/shard_map/ppermute | solution.py:26
  49.8 3.2 %collective-permute-start.12 = (f32[2,1,12,128]{3,1,2,0:T(1,128)S(1)}, f32[2,1,12,128]{3,1,2,0:T(1,128)S(1)}, u32[]{:S(2)}, u32[]{:S(2)}) collective-permute-start(f32[2,1,12,128]{3,1,2,0:T(1,128)S(1)} %get-tuple-element.101), channel_id=1, source_target_pairs={{0,8},{8,16},{16,24},{1,9},{9,17},{17,25},{2,10},{10,18},{18,26},{... | collective-permute-start | bytes 36872 | tf_op jit(solution)/shard_map/ppermute | solution.py:25
  54.3 3.1 %collective-permute-done.13 = f32[2,1,12,128]{3,1,2,0:T(1,128)S(1)} collective-permute-done((f32[2,1,12,128]{3,1,2,0:T(1,128)S(1)}, f32[2,1,12,128]{3,1,2,0:T(1,128)S(1)}, u32[]{:S(2)}, u32[]{:S(2)}) %collective-permute-start.13) | collective-permute-done | bytes 12320 | tf_op jit(solution)/shard_map/ppermute | solution.py:26
  57.5 3.3 %collective-permute-start.14 = (f32[2,34,1,128]{3,1,2,0:T(8,128)S(1)}, f32[2,34,1,128]{3,1,2,0:T(8,128)S(1)}, u32[]{:S(2)}, u32[]{:S(2)}) collective-permute-start(f32[2,34,1,128]{3,1,2,0:T(8,128)S(1)} %get-tuple-element.91), channel_id=1, source_target_pairs={{0,1},{1,2},{2,3},{3,4},{4,5},{5,6},{6,7},{8,9},{9,10},{10,11},{11... | collective-permute-start | bytes 104456 | tf_op jit(solution)/shard_map/ppermute | solution.py:25
  63.0 4.0 %collective-permute-done.15 = f32[2,34,1,128]{3,1,2,0:T(8,128)S(1)} collective-permute-done((f32[2,34,1,128]{3,1,2,0:T(8,128)S(1)}, f32[2,34,1,128]{3,1,2,0:T(8,128)S(1)}, u32[]{:S(2)}, u32[]{:S(2)}) %collective-permute-start.15) | collective-permute-done | bytes 34848 | tf_op jit(solution)/shard_map/ppermute | solution.py:26
  68.4 8.0 %all-gather.1 = f32[128,1,128]{2,0,1:T(8,128)S(1)} all-gather(f32[16,1,128]{2,0,1:T(8,128)S(1)} %slice_add_fusion.1), channel_id=3, replica_groups=mesh['gx'=4,'gy'=8] {'gy'}, dimensions={0}, use_global_device_ids=true | all-gather | bytes 73728 | tf_op jit(solution)/shard_map/all_gather | solution.py:33
  76.5 8.2 %all-gather = f32[128,1,128]{2,0,1:T(8,128)S(1)} all-gather(f32[16,1,128]{2,0,1:T(8,128)S(1)} %slice_add_fusion.4), channel_id=2, replica_groups=mesh['gx'=4,'gy'=8] {'gy'}, dimensions={0}, use_global_device_ids=true | all-gather | bytes 73728 | tf_op jit(solution)/shard_map/all_gather | solution.py:33
  88.2 3.1 %collective-permute-done.17 = f32[2,1,12,128]{3,1,2,0:T(1,128)S(1)} collective-permute-done((f32[2,1,12,128]{3,1,2,0:T(1,128)S(1)}, f32[2,1,12,128]{3,1,2,0:T(1,128)S(1)}, u32[]{:S(2)}, u32[]{:S(2)}) %collective-permute-start.17) | collective-permute-done | bytes 12320 | tf_op jit(solution)/shard_map/ppermute | solution.py:26
  91.4 4.6 %collective-permute-start.18 = (f32[2,34,1,128]{3,1,2,0:T(8,128)S(1)}, f32[2,34,1,128]{3,1,2,0:T(8,128)S(1)}, u32[]{:S(2)}, u32[]{:S(2)}) collective-permute-start(f32[2,34,1,128]{3,1,2,0:T(8,128)S(1)} %get-tuple-element.89), channel_id=1, source_target_pairs={{0,1},{1,2},{2,3},{3,4},{4,5},{5,6},{6,7},{8,9},{9,10},{10,11},{11... | collective-permute-start | bytes 104456 | tf_op jit(solution)/shard_map/ppermute | solution.py:25
  97.9 4.3 %collective-permute-done.19 = f32[2,34,1,128]{3,1,2,0:T(8,128)S(1)} collective-permute-done((f32[2,34,1,128]{3,1,2,0:T(8,128)S(1)}, f32[2,34,1,128]{3,1,2,0:T(8,128)S(1)}, u32[]{:S(2)}, u32[]{:S(2)}) %collective-permute-start.19) | collective-permute-done | bytes 34848 | tf_op jit(solution)/shard_map/ppermute | solution.py:26
  106.1 3.1 %collective-permute-done.21 = f32[2,1,12,128]{3,1,2,0:T(1,128)S(1)} collective-permute-done((f32[2,1,12,128]{3,1,2,0:T(1,128)S(1)}, f32[2,1,12,128]{3,1,2,0:T(1,128)S(1)}, u32[]{:S(2)}, u32[]{:S(2)}) %collective-permute-start.21) | collective-permute-done | bytes 12320 | tf_op jit(solution)/shard_map/ppermute | solution.py:26
  109.2 3.3 %collective-permute-start.22 = (f32[2,34,1,128]{3,1,2,0:T(8,128)S(1)}, f32[2,34,1,128]{3,1,2,0:T(8,128)S(1)}, u32[]{:S(2)}, u32[]{:S(2)}) collective-permute-start(f32[2,34,1,128]{3,1,2,0:T(8,128)S(1)} %get-tuple-element.87), channel_id=1, source_target_pairs={{0,1},{1,2},{2,3},{3,4},{4,5},{5,6},{6,7},{8,9},{9,10},{10,11},{11... | collective-permute-start | bytes 104456 | tf_op jit(solution)/shard_map/ppermute | solution.py:25
  112.6 1.9 %collective-permute-start.23 = (f32[2,34,1,128]{3,1,2,0:T(8,128)S(1)}, f32[2,34,1,128]{3,1,2,0:T(8,128)S(1)}, u32[]{:S(2)}, u32[]{:S(2)}) collective-permute-start(f32[2,34,1,128]{3,1,2,0:T(8,128)S(1)} %get-tuple-element.88), channel_id=1, source_target_pairs={{1,0},{2,1},{3,2},{4,3},{5,4},{6,5},{7,6},{9,8},{10,9},{11,10},{12... | collective-permute-start | bytes 104456 | tf_op jit(solution)/shard_map/ppermute | solution.py:26
  114.5 4.3 %collective-permute-done.23 = f32[2,34,1,128]{3,1,2,0:T(8,128)S(1)} collective-permute-done((f32[2,34,1,128]{3,1,2,0:T(8,128)S(1)}, f32[2,34,1,128]{3,1,2,0:T(8,128)S(1)}, u32[]{:S(2)}, u32[]{:S(2)}) %collective-permute-start.23) | collective-permute-done | bytes 34848 | tf_op jit(solution)/shard_map/ppermute | solution.py:26
  (115 shorter events, 25.5 us)
Async XLA Ops:
  1.0 11.5 %collective-permute-start = (f32[2,1,12,128]{3,1,2,0:T(1,128)S(1)}, f32[2,1,12,128]{3,1,2,0:T(1,128)S(1)}, u32[]{:S(2)}, u32[]{:S(2)}) collective-permute-start(f32[2,1,12,128]{3,1,2,0:T(1,128)S(1)} %get-tuple-element.105), channel_id=1, source_target_pairs={{0,8},{8,16},{16,24},{1,9},{9,17},{17,25},{2,10},{10,18},{18,26},{... | collective-permute-start | bytes 36872 | tf_op jit(solution)/shard_map/ppermute | solution.py:25
  4.2 8.3 %collective-permute-start.1 = (f32[2,1,12,128]{3,1,2,0:T(1,128)S(1)}, f32[2,1,12,128]{3,1,2,0:T(1,128)S(1)}, u32[]{:S(2)}, u32[]{:S(2)}) collective-permute-start(f32[2,1,12,128]{3,1,2,0:T(1,128)S(1)} %get-tuple-element.106), channel_id=1, source_target_pairs={{8,0},{16,8},{24,16},{9,1},{17,9},{25,17},{10,2},{18,10},{26,18},{... | collective-permute-start | bytes 36872 | tf_op jit(solution)/shard_map/ppermute | solution.py:26
  6.6 12.4 %collective-permute-start.4 = (f32[1,12,128]{2,0,1:T(1,128)S(1)}, f32[1,12,128]{2,0,1:T(1,128)S(1)}, u32[]{:S(2)}, u32[]{:S(2)}) collective-permute-start(f32[1,12,128]{2,0,1:T(1,128)S(1)} %get-tuple-element.120), channel_id=1, source_target_pairs={{8,0},{16,8},{24,16},{9,1},{17,9},{25,17},{10,2},{18,10},{26,18},{... | collective-permute-start | bytes 18440 | tf_op jit(solution)/shard_map/ppermute | solution.py:26
  7.9 11.1 %collective-permute-start.5 = (f32[1,12,128]{2,0,1:T(1,128)S(1)}, f32[1,12,128]{2,0,1:T(1,128)S(1)}, u32[]{:S(2)}, u32[]{:S(2)}) collective-permute-start(f32[1,12,128]{2,0,1:T(1,128)S(1)} %get-tuple-element.119), channel_id=1, source_target_pairs={{0,8},{8,16},{16,24},{1,9},{9,17},{17,25},{2,10},{10,18},{18,26},{... | collective-permute-start | bytes 18440 | tf_op jit(solution)/shard_map/ppermute | solution.py:25
  12.6 13.0 %collective-permute-start.2 = (f32[2,34,1,128]{3,1,2,0:T(8,128)S(1)}, f32[2,34,1,128]{3,1,2,0:T(8,128)S(1)}, u32[]{:S(2)}, u32[]{:S(2)}) collective-permute-start(f32[2,34,1,128]{3,1,2,0:T(8,128)S(1)} %get-tuple-element.95), channel_id=1, source_target_pairs={{0,1},{1,2},{2,3},{3,4},{4,5},{5,6},{6,7},{8,9},{9,10},{10,11},{11... | collective-permute-start | bytes 104456 | tf_op jit(solution)/shard_map/ppermute | solution.py:25
  17.1 8.5 %collective-permute-start.3 = (f32[2,34,1,128]{3,1,2,0:T(8,128)S(1)}, f32[2,34,1,128]{3,1,2,0:T(8,128)S(1)}, u32[]{:S(2)}, u32[]{:S(2)}) collective-permute-start(f32[2,34,1,128]{3,1,2,0:T(8,128)S(1)} %get-tuple-element.96), channel_id=1, source_target_pairs={{1,0},{2,1},{3,2},{4,3},{5,4},{6,5},{7,6},{9,8},{10,9},{11,10},{12... | collective-permute-start | bytes 104456 | tf_op jit(solution)/shard_map/ppermute | solution.py:26
  19.1 7.8 %collective-permute-start.6 = (f32[34,1,128]{2,0,1:T(8,128)S(1)}, f32[34,1,128]{2,0,1:T(8,128)S(1)}, u32[]{:S(2)}, u32[]{:S(2)}) collective-permute-start(f32[34,1,128]{2,0,1:T(8,128)S(1)} %get-tuple-element.118), channel_id=1, source_target_pairs={{1,0},{2,1},{3,2},{4,3},{5,4},{6,5},{7,6},{9,8},{10,9},{11,10},{12... | collective-permute-start | bytes 52232 | tf_op jit(solution)/shard_map/ppermute | solution.py:26
  21.6 5.3 %collective-permute-start.7 = (f32[34,1,128]{2,0,1:T(8,128)S(1)}, f32[34,1,128]{2,0,1:T(8,128)S(1)}, u32[]{:S(2)}, u32[]{:S(2)}) collective-permute-start(f32[34,1,128]{2,0,1:T(8,128)S(1)} %get-tuple-element.117), channel_id=1, source_target_pairs={{0,1},{1,2},{2,3},{3,4},{4,5},{5,6},{6,7},{8,9},{9,10},{10,11},{11... | collective-permute-start | bytes 52232 | tf_op jit(solution)/shard_map/ppermute | solution.py:25
  28.4 5.0 %collective-permute-start.8 = (f32[2,1,12,128]{3,1,2,0:T(1,128)S(1)}, f32[2,1,12,128]{3,1,2,0:T(1,128)S(1)}, u32[]{:S(2)}, u32[]{:S(2)}) collective-permute-start(f32[2,1,12,128]{3,1,2,0:T(1,128)S(1)} %get-tuple-element.103), channel_id=1, source_target_pairs={{0,8},{8,16},{16,24},{1,9},{9,17},{17,25},{2,10},{10,18},{18,26},{... | collective-permute-start | bytes 36872 | tf_op jit(solution)/shard_map/ppermute | solution.py:25
  32.0 4.4 %collective-permute-start.9 = (f32[2,1,12,128]{3,1,2,0:T(1,128)S(1)}, f32[2,1,12,128]{3,1,2,0:T(1,128)S(1)}, u32[]{:S(2)}, u32[]{:S(2)}) collective-permute-start(f32[2,1,12,128]{3,1,2,0:T(1,128)S(1)} %get-tuple-element.104), channel_id=1, source_target_pairs={{8,0},{16,8},{24,16},{9,1},{17,9},{25,17},{10,2},{18,10},{26,18},{... | collective-permute-start | bytes 36872 | tf_op jit(solution)/shard_map/ppermute | solution.py:26
  36.5 8.0 %collective-permute-start.10 = (f32[2,34,1,128]{3,1,2,0:T(8,128)S(1)}, f32[2,34,1,128]{3,1,2,0:T(8,128)S(1)}, u32[]{:S(2)}, u32[]{:S(2)}) collective-permute-start(f32[2,34,1,128]{3,1,2,0:T(8,128)S(1)} %get-tuple-element.93), channel_id=1, source_target_pairs={{0,1},{1,2},{2,3},{3,4},{4,5},{5,6},{6,7},{8,9},{9,10},{10,11},{11... | collective-permute-start | bytes 104456 | tf_op jit(solution)/shard_map/ppermute | solution.py:25
  42.6 6.2 %collective-permute-start.11 = (f32[2,34,1,128]{3,1,2,0:T(8,128)S(1)}, f32[2,34,1,128]{3,1,2,0:T(8,128)S(1)}, u32[]{:S(2)}, u32[]{:S(2)}) collective-permute-start(f32[2,34,1,128]{3,1,2,0:T(8,128)S(1)} %get-tuple-element.94), channel_id=1, source_target_pairs={{1,0},{2,1},{3,2},{4,3},{5,4},{6,5},{7,6},{9,8},{10,9},{11,10},{12... | collective-permute-start | bytes 104456 | tf_op jit(solution)/shard_map/ppermute | solution.py:26
  49.8 4.5 %collective-permute-start.12 = (f32[2,1,12,128]{3,1,2,0:T(1,128)S(1)}, f32[2,1,12,128]{3,1,2,0:T(1,128)S(1)}, u32[]{:S(2)}, u32[]{:S(2)}) collective-permute-start(f32[2,1,12,128]{3,1,2,0:T(1,128)S(1)} %get-tuple-element.101), channel_id=1, source_target_pairs={{0,8},{8,16},{16,24},{1,9},{9,17},{17,25},{2,10},{10,18},{18,26},{... | collective-permute-start | bytes 36872 | tf_op jit(solution)/shard_map/ppermute | solution.py:25
  53.0 4.4 %collective-permute-start.13 = (f32[2,1,12,128]{3,1,2,0:T(1,128)S(1)}, f32[2,1,12,128]{3,1,2,0:T(1,128)S(1)}, u32[]{:S(2)}, u32[]{:S(2)}) collective-permute-start(f32[2,1,12,128]{3,1,2,0:T(1,128)S(1)} %get-tuple-element.102), channel_id=1, source_target_pairs={{8,0},{16,8},{24,16},{9,1},{17,9},{25,17},{10,2},{18,10},{26,18},{... | collective-permute-start | bytes 36872 | tf_op jit(solution)/shard_map/ppermute | solution.py:26
  57.5 5.6 %collective-permute-start.14 = (f32[2,34,1,128]{3,1,2,0:T(8,128)S(1)}, f32[2,34,1,128]{3,1,2,0:T(8,128)S(1)}, u32[]{:S(2)}, u32[]{:S(2)}) collective-permute-start(f32[2,34,1,128]{3,1,2,0:T(8,128)S(1)} %get-tuple-element.91), channel_id=1, source_target_pairs={{0,1},{1,2},{2,3},{3,4},{4,5},{5,6},{6,7},{8,9},{9,10},{10,11},{11... | collective-permute-start | bytes 104456 | tf_op jit(solution)/shard_map/ppermute | solution.py:25
  60.8 6.2 %collective-permute-start.15 = (f32[2,34,1,128]{3,1,2,0:T(8,128)S(1)}, f32[2,34,1,128]{3,1,2,0:T(8,128)S(1)}, u32[]{:S(2)}, u32[]{:S(2)}) collective-permute-start(f32[2,34,1,128]{3,1,2,0:T(8,128)S(1)} %get-tuple-element.92), channel_id=1, source_target_pairs={{1,0},{2,1},{3,2},{4,3},{5,4},{6,5},{7,6},{9,8},{10,9},{11,10},{12... | collective-permute-start | bytes 104456 | tf_op jit(solution)/shard_map/ppermute | solution.py:26
  85.2 3.0 %collective-permute-start.16 = (f32[2,1,12,128]{3,1,2,0:T(1,128)S(1)}, f32[2,1,12,128]{3,1,2,0:T(1,128)S(1)}, u32[]{:S(2)}, u32[]{:S(2)}) collective-permute-start(f32[2,1,12,128]{3,1,2,0:T(1,128)S(1)} %get-tuple-element.99), channel_id=1, source_target_pairs={{0,8},{8,16},{16,24},{1,9},{9,17},{17,25},{2,10},{10,18},{18,26},{... | collective-permute-start | bytes 36872 | tf_op jit(solution)/shard_map/ppermute | solution.py:25
  86.9 4.4 %collective-permute-start.17 = (f32[2,1,12,128]{3,1,2,0:T(1,128)S(1)}, f32[2,1,12,128]{3,1,2,0:T(1,128)S(1)}, u32[]{:S(2)}, u32[]{:S(2)}) collective-permute-start(f32[2,1,12,128]{3,1,2,0:T(1,128)S(1)} %get-tuple-element.100), channel_id=1, source_target_pairs={{8,0},{16,8},{24,16},{9,1},{17,9},{25,17},{10,2},{18,10},{26,18},{... | collective-permute-start | bytes 36872 | tf_op jit(solution)/shard_map/ppermute | solution.py:26
  91.4 6.5 %collective-permute-start.18 = (f32[2,34,1,128]{3,1,2,0:T(8,128)S(1)}, f32[2,34,1,128]{3,1,2,0:T(8,128)S(1)}, u32[]{:S(2)}, u32[]{:S(2)}) collective-permute-start(f32[2,34,1,128]{3,1,2,0:T(8,128)S(1)} %get-tuple-element.89), channel_id=1, source_target_pairs={{0,1},{1,2},{2,3},{3,4},{4,5},{5,6},{6,7},{8,9},{9,10},{10,11},{11... | collective-permute-start | bytes 104456 | tf_op jit(solution)/shard_map/ppermute | solution.py:25
  95.9 6.2 %collective-permute-start.19 = (f32[2,34,1,128]{3,1,2,0:T(8,128)S(1)}, f32[2,34,1,128]{3,1,2,0:T(8,128)S(1)}, u32[]{:S(2)}, u32[]{:S(2)}) collective-permute-start(f32[2,34,1,128]{3,1,2,0:T(8,128)S(1)} %get-tuple-element.90), channel_id=1, source_target_pairs={{1,0},{2,1},{3,2},{4,3},{5,4},{6,5},{7,6},{9,8},{10,9},{11,10},{12... | collective-permute-start | bytes 104456 | tf_op jit(solution)/shard_map/ppermute | solution.py:26
  103.1 3.0 %collective-permute-start.20 = (f32[2,1,12,128]{3,1,2,0:T(1,128)S(1)}, f32[2,1,12,128]{3,1,2,0:T(1,128)S(1)}, u32[]{:S(2)}, u32[]{:S(2)}) collective-permute-start(f32[2,1,12,128]{3,1,2,0:T(1,128)S(1)} %get-tuple-element.97), channel_id=1, source_target_pairs={{0,8},{8,16},{16,24},{1,9},{9,17},{17,25},{2,10},{10,18},{18,26},{... | collective-permute-start | bytes 36872 | tf_op jit(solution)/shard_map/ppermute | solution.py:25
  104.8 4.4 %collective-permute-start.21 = (f32[2,1,12,128]{3,1,2,0:T(1,128)S(1)}, f32[2,1,12,128]{3,1,2,0:T(1,128)S(1)}, u32[]{:S(2)}, u32[]{:S(2)}) collective-permute-start(f32[2,1,12,128]{3,1,2,0:T(1,128)S(1)} %get-tuple-element.98), channel_id=1, source_target_pairs={{8,0},{16,8},{24,16},{9,1},{17,9},{25,17},{10,2},{18,10},{26,18},{... | collective-permute-start | bytes 36872 | tf_op jit(solution)/shard_map/ppermute | solution.py:26
  109.2 5.3 %collective-permute-start.22 = (f32[2,34,1,128]{3,1,2,0:T(8,128)S(1)}, f32[2,34,1,128]{3,1,2,0:T(8,128)S(1)}, u32[]{:S(2)}, u32[]{:S(2)}) collective-permute-start(f32[2,34,1,128]{3,1,2,0:T(8,128)S(1)} %get-tuple-element.87), channel_id=1, source_target_pairs={{0,1},{1,2},{2,3},{3,4},{4,5},{5,6},{6,7},{8,9},{9,10},{10,11},{11... | collective-permute-start | bytes 104456 | tf_op jit(solution)/shard_map/ppermute | solution.py:25
  112.6 6.2 %collective-permute-start.23 = (f32[2,34,1,128]{3,1,2,0:T(8,128)S(1)}, f32[2,34,1,128]{3,1,2,0:T(8,128)S(1)}, u32[]{:S(2)}, u32[]{:S(2)}) collective-permute-start(f32[2,34,1,128]{3,1,2,0:T(8,128)S(1)} %get-tuple-element.88), channel_id=1, source_target_pairs={{1,0},{2,1},{3,2},{4,3},{5,4},{6,5},{7,6},{9,8},{10,9},{11,10},{12... | collective-permute-start | bytes 104456 | tf_op jit(solution)/shard_map/ppermute | solution.py:26
  (3 other events, 14.5 us)
where the time goes:
time: 121 us
  starting transfers between devices  63.6 us (53%)
  waiting for transfers between devices  29.4 us (24%)
  blocking collectives  16.2 us (13%)
  other arithmetic  7.21 us (6%)
  local copies, waits for them, and re-layouts  3.23 us (3%)
    ppermute x12, starting transfers between devices, padded_2(): before = lax.ppermute(last, axis, up)  43.7 us
    ppermute x12, waiting for transfers between devices, padded_2(): after = lax.ppermute(leading, axis, down)  29.4 us
    ppermute x12, starting transfers between devices, padded_2(): after = lax.ppermute(leading, axis, down)  19.9 us
    all_gather x2, blocking collectives, entering(): gathered = jax.tree.map(lambda a: lax.all_gather(a, axis), part)  16.2 us
  transfers between devices with their start and end apart: 24, of which 8 were waited for; matrix products, arithmetic and copies ran while one was open for 1% of the time, Pallas kernels for 0%

commit v1 on v0

v1 whole, which is shorter than its diff:
```python
import jax
import jax.numpy as jnp
from jax import lax
from jax.sharding import PartitionSpec as P

solid_cap = 0.5
gas_cap = 0.02
flow_rate = 40.0
gas_conduct = 0.05
relaxation = 0.8
lump_factor = 0.25

WX, WY = 5, 4


def swap_pairs(count, first):
    pairs = []
    for i in range(first, count - 1, 2):
        pairs += [(i, i + 1), (i + 1, i)]
    return pairs


def edges_of(x, axis, dim, width):
    count, length = lax.axis_size(axis), x.shape[dim]
    even = lax.axis_index(axis) % 2 == 0
    first = lax.slice_in_dim(x, 0, width, axis=dim)
    last = lax.slice_in_dim(x, length - width, length, axis=dim)
    one = lax.ppermute(jnp.where(even, last, first), axis, swap_pairs(count, 0))
    two = lax.ppermute(jnp.where(even, first, last), axis, swap_pairs(count, 1))
    return jnp.where(even, two, one), jnp.where(even, one, two)


def widened(x, axis, dim, width):
    before, after = edges_of(x, axis, dim, width)
    return jnp.concatenate([before, x, after], axis=dim)


def inside(axis, length, width):
    at = lax.axis_index(axis) * length + jnp.arange(-width, length + width)
    return ((at >= 0) & (at < lax.axis_size(axis) * length)).astype(jnp.float32)


def z_next(x):
    return jnp.pad(x[..., 1:], ((0, 0), (0, 0), (0, 1)))


def z_prev(x):
    return jnp.pad(x[..., :-1], ((0, 0), (0, 0), (1, 0)))


def crop(x, dx, dy):
    return x[dx : x.shape[0] - dx, dy : x.shape[1] - dy]


def residual(s, g, rs, rg, c, fx, fy, fz, diag):
    sc, gc = s[1:-1, 1:-1], g[1:-1, 1:-1]
    around_s = (
        fx[1:] * s[2:, 1:-1]
        + fx[:-1] * s[:-2, 1:-1]
        + fy[:, 1:] * s[1:-1, 2:]
        + fy[:, :-1] * s[1:-1, :-2]
        + fz * z_next(sc)
        + z_prev(fz * sc)
    )
    gas_diag = gas_cap + c + flow_rate + gas_conduct * 2.0 * 2.25
    around_g = gas_conduct * (
        g[2:, 1:-1] + g[:-2, 1:-1] + g[1:-1, 2:] + g[1:-1, :-2] + 0.25 * (z_next(gc) + z_prev(gc))
    ) + flow_rate * g[1:-1, :-2]
    res_s = rs - diag * sc + c * gc + around_s
    res_g = rg - gas_diag * gc + c * sc + around_g
    return res_s, res_g


def coarse_sum(a):
    return a.reshape(a.shape[0] // 2, 2, a.shape[1] // 2, 2, a.shape[2]).sum(axis=(1, 3))


def spread(a):
    x, y, z = a.shape
    return jnp.broadcast_to(a[:, None, :, None, :], (x, 2, y, 2, z)).reshape(2 * x, 2 * y, z)


def shards(temps, right_side, exchange, coupling):
    nx, ny, nz = exchange.shape
    fields = jnp.concatenate([temps, right_side, exchange[None], coupling[None]])
    fields = widened(fields, "gx", 1, WX)
    fields = widened(fields, "gy", 2, WY)
    s, g, rs, rg, e, c = (fields[k] for k in range(6))
    mask = (inside("gx", nx, WX)[:, None] * inside("gy", ny, WY)[None, :])[:, :, None]

    cond = (1.0 + 4.0 * e * s * s * s) * mask
    fx = 0.5 * (cond[1:] + cond[:-1])
    fy = 0.5 * (cond[:, 1:] + cond[:, :-1])
    fz_up = 0.125 * (cond + z_next(cond))
    fz_down = 0.125 * (cond + z_prev(cond))
    rs, rg, c, m = (crop(a, 1, 1) for a in (rs, rg, c, mask))
    fx, fy = fx[:, 1:-1], fy[1:-1]
    fz = crop(fz_up, 1, 1)
    diag = solid_cap + c + fx[1:] + fx[:-1] + fy[:, 1:] + fy[:, :-1] + fz + crop(fz_down, 1, 1)
    gas_diag = gas_cap + c + flow_rate + gas_conduct * 2.0 * 2.25
    inv = m * relaxation / (diag * gas_diag - c * c)
    a_ss, a_sg, a_gg = inv * gas_diag, inv * c, inv * diag

    def parts(dx, dy):
        fxk = fx[dx : fx.shape[0] - dx, dy : fx.shape[1] - dy]
        fyk = fy[dx : fy.shape[0] - dx, dy : fy.shape[1] - dy]
        return [crop(rs, dx, dy), crop(rg, dx, dy), crop(c, dx, dy), fxk, fyk, crop(fz, dx, dy), crop(diag, dx, dy)]

    def sweep(s, g, dx, dy):
        res_s, res_g = residual(s, g, *parts(dx, dy))
        ss, sg, gg = (crop(a, dx, dy) for a in (a_ss, a_sg, a_gg))
        return s[1:-1, 1:-1] + ss * res_s + sg * res_g, g[1:-1, 1:-1] + sg * res_s + gg * res_g

    s, g = sweep(s, g, 0, 0)
    s, g = sweep(s, g, 1, 1)
    hx, hy = WX - 3, WY - 3
    res_s, res_g = residual(s, g, *parts(2, 2))
    res_s, res_g = (crop(a, 0, hy) for a in (res_s, res_g))
    mk = crop(mask, WX - 2, WY)
    res_s, res_g = coarse_sum(res_s * mk), coarse_sum(res_g * mk)
    c_sum = coarse_sum(crop(c, WX - 3, WY - 1))
    k_sum = coarse_sum(crop(cond, WX - 2, WY))
    solid_coarse = 4.0 * solid_cap + c_sum + lump_factor * k_sum
    gas_coarse = 4.0 * gas_cap + c_sum + 2.0 * flow_rate
    lead, ratio = res_s / solid_coarse, c_sum / solid_coarse
    denominator = gas_coarse - c_sum * ratio
    slope = 2.0 * flow_rate / denominator
    offset = (res_g + c_sum * lead) / denominator

    rows = ny // 2
    slopes, offsets = [slope[:, 0]], [offset[:, 0]]
    for j in range(1, rows):
        slopes.append(slope[:, j] * slopes[-1])
        offsets.append(slope[:, j] * offsets[-1] + offset[:, j])

    count, me = lax.axis_size("gy"), lax.axis_index("gy")
    onward = jnp.stack([slopes[-1], offsets[-1], lead[:, -1], ratio[:, -1]])
    back = jnp.stack([slope[:, 0], offset[:, 0], lead[:, 0], ratio[:, 0]])
    to = jnp.arange(count)[:, None, None, None]
    sent = jnp.where(to > me, onward[None], back[None])
    got = lax.all_to_all(sent, "gy", 0, 0)
    gas_in = jnp.zeros_like(slopes[0])
    for d in range(count - 1):
        gas_in = jnp.where(d < me, got[d, 0] * gas_in + got[d, 1], gas_in)
    before = lax.dynamic_index_in_dim(got, jnp.maximum(me - 1, 0), 0, False)
    after = lax.dynamic_index_in_dim(got, jnp.minimum(me + 1, count - 1), 0, False)
    gas_err = [gas_in] + [slopes[j] * gas_in + offsets[j] for j in range(rows)]
    gas_err.append(after[0] * gas_err[-1] + after[1])
    gas_err = jnp.stack(gas_err, axis=1)
    lead = jnp.concatenate([before[2][:, None], lead, after[2][:, None]], axis=1)
    ratio = jnp.concatenate([before[3][:, None], ratio, after[3][:, None]], axis=1)
    solid_err = lead + ratio * gas_err
    mk = crop(mask, WX - 2, WY - 2)
    s = crop(s, 1, 0) + mk * spread(solid_err)
    g = crop(g, 1, 0) + mk * spread(gas_err)
    s, g = sweep(s, g, WX - 2, WY - 2)
    s, g = sweep(s, g, WX - 1, WY - 1)
    return jnp.stack([s, g])


def solution(mesh):
    return jax.shard_map(
        shards,
        mesh=mesh,
        in_specs=(
            P(None, "gx", "gy", None),
            P(None, "gx", "gy", None),
            P("gx", "gy", None),
            P("gx", "gy", None),
        ),
        out_specs=P(None, "gx", "gy", None),
        check_vma=False,
    )
```

time: 121 us -> 86.7 us (0.72)
  the two profiles are of different devices: /device:TPU:3 before, /device:TPU:16 now
where the time goes in v1:
time: 86.7 us; the launch traced here: 85.4 us
  other arithmetic  27 us (31%)
  starting transfers between devices  21.8 us (25%)
  local copies, waits for them, and re-layouts  20.2 us (23%)
  waiting for transfers between devices  15.8 us (18%)
    all_to_all x1, starting transfers between devices, shards(): got = lax.all_to_all(sent, 'gy', 0, 0)  17.5 us
    all_to_all x1, waiting for transfers between devices, shards(): got = lax.all_to_all(sent, 'gy', 0, 0)  7.61 us
    unnamed x7, other arithmetic  5.24 us
    reshape x4, local copies, waits for them, and re-layouts, coarse_sum(): a.reshape(a.shape[0] // 2, 2, a.shape[1] // 2, 2, a.shape[2])  5.04 us
    ppermute x2, waiting for transfers between devices, edges_of(): one = lax.ppermute(jnp.where(even, last, first), axis, swap_pairs(count, 0))  5.03 us
    slice x11, local copies, waits for them, and re-layouts, crop(): return x[dx:x.shape[0] - dx, dy:x.shape[1] - dy]  4.7 us
    mul x2, other arithmetic, shards(): res_s, res_g = (coarse_sum(res_s * mk), coarse_sum(res_g * mk))  4.29 us
    unnamed x34, local copies, waits for them, and re-layouts  3.66 us
  transfers between devices with their start and end apart: 5, of which 4 were waited for; matrix products, arithmetic and copies ran while one was open for 1% of the time, Pallas kernels for 0%

profile of v1, /device:TPU:16, one launch (start us, length us, event | category | flops | bytes accessed | tf_op | source)
XLA Modules:
  0.0 85.4 jit_solution(13022312049526683978)
XLA Ops:
  0.0 1.2 %copy.25 = f32[2,32,12,128]{3,2,1,0:T(8,128)S(1)} copy(f32[2,32,12,128]{3,1,2,0:T(8,128)} %param.4) | data formatting | bytes 786432 | tf_op args[0]
  1.2 1.2 %copy.26 = f32[2,32,12,128]{3,2,1,0:T(8,128)S(1)} copy(f32[2,32,12,128]{3,1,2,0:T(8,128)} %param.5) | data formatting | bytes 786432 | tf_op args[1]
  2.5 1.3 %copy_bitcast_fusion = (f32[1,32,12,128]{3,2,1,0:T(8,128)S(1)}, f32[1,32,12,128]{3,2,1,0:T(8,128)S(1)}) fusion(f32[32,12,128]{2,0,1:T(8,128)} %param.7, f32[32,12,128]{2,0,1:T(8,128)} %param.6), kind=kLoop, calls=%fused_computation.169 | loop fusion | bytes 786432 | tf_op jit(solution)/shard_map/broadcast_in_dim | solution.py:85
  3.8 1.6 %collective-permute-start.1 = (f32[6,5,12,128]{3,2,1,0:T(8,128)S(1)}, f32[6,5,12,128]{3,2,1,0:T(8,128)S(1)}, u32[]{:S(2)}, u32[]{:S(2)}) collective-permute-start(f32[6,5,12,128]{3,2,1,0:T(8,128)S(1)} %broadcast_select_fusion.7), channel_id=1, source_target_pairs={{0,8},{8,0},{16,24},{24,16},{1,9},{9,1},{17,25},{25,17},{2,10},{10... | collective-permute-start | bytes 552968 | tf_op jit(solution)/shard_map/ppermute | solution.py:28
  5.5 1.9 %collective-permute-start = (f32[6,5,12,128]{3,2,1,0:T(8,128)S(1)}, f32[6,5,12,128]{3,2,1,0:T(8,128)S(1)}, u32[]{:S(2)}, u32[]{:S(2)}) collective-permute-start(f32[6,5,12,128]{3,2,1,0:T(8,128)S(1)} %get-tuple-element.36), channel_id=1, source_target_pairs={{8,16},{16,8},{9,17},{17,9},{10,18},{18,10},{11,19},{19,11},{12,20... | collective-permute-start | bytes 552968 | tf_op jit(solution)/shard_map/ppermute | solution.py:29
  7.6 4.0 %collective-permute-done.1 = f32[6,5,12,128]{3,2,1,0:T(8,128)S(1)} collective-permute-done((f32[6,5,12,128]{3,2,1,0:T(8,128)S(1)}, f32[6,5,12,128]{3,2,1,0:T(8,128)S(1)}, u32[]{:S(2)}, u32[]{:S(2)}) %collective-permute-start.1) | collective-permute-done | bytes 184352 | tf_op jit(solution)/shard_map/ppermute | solution.py:28
  11.6 3.2 %collective-permute-done = f32[6,5,12,128]{3,2,1,0:T(8,128)S(1)} collective-permute-done((f32[6,5,12,128]{3,2,1,0:T(8,128)S(1)}, f32[6,5,12,128]{3,2,1,0:T(8,128)S(1)}, u32[]{:S(2)}, u32[]{:S(2)}) %collective-permute-start) | collective-permute-done | bytes 184352 | tf_op jit(solution)/shard_map/ppermute | solution.py:29
  16.0 1.0 %collective-permute-done.3 = f32[6,42,4,128]{3,2,1,0:T(4,128)S(1)} collective-permute-done((f32[6,42,4,128]{3,2,1,0:T(4,128)S(1)}, f32[6,42,4,128]{3,2,1,0:T(4,128)S(1)}, u32[]{:S(2)}, u32[]{:S(2)}) %collective-permute-start.3) | collective-permute-done | bytes 516128 | tf_op jit(solution)/shard_map/ppermute | solution.py:28
  17.1 1.6 %pad_maximum_fusion = f32[6,42,20,128]{3,2,1,0:T(8,128)S(1)} fusion(f32[6,42,4,128]{3,2,1,0:T(4,128)S(1)} %bitcast.290, f32[6,5,12,128]{3,2,1,0:T(8,128)S(1)} %get-tuple-element.57, f32[1,32,12,128]{3,2,1,0:T(8,128)S(1)} %get-tuple-element.87, f32[1,32,12,128]{3,2,1,0:T(8,128)S(1)} %get-tuple-element.88, f32[2,32,12,128]{3,2,1,0:T(8,128)S(1)} %copy.26, ...), kind=kLoop, calls=%fused_computation | loop fusion | flops 4515840 | bytes 5160960 | tf_op jit(solution)/shard_map/concatenate | solution.py:35
  20.3 2.0 %multiply_add_fusion.1 = (f32[40,18,128]{2,1,0:T(8,128)S(1)}, f32[40,18,128]{2,1,0:T(8,128)S(1)}, f32[40,18,128]{2,1,0:T(8,128)S(1)}, f32[40,18,128]{2,1,0:T(8,1...) fusion(f32[42,20,128]{2,1,0:T(8,128)S(1)} %get-tuple-element.43, ...), kind=kLoop, calls=%fused_computation.49 | loop fusion | flops 4515840 | bytes 11108640 | tf_op jit(solution)/shard_map/add | solution.py:112
  25.2 1.1 %slice_multiply_fusion.20 = (f32[36,14,128]{2,1,0:T(8,128)}, f32[36,14,128]{2,1,0:T(8,128)}, f32[36,14,128]{2,1,0:T(8,128)}, f32[36,14,128]{2,1,0:T(8,128)}, f32[36,14,128]{2,1,0:T(8,128)S(1)}) fusion(f32[38,16,128]{2,1,0:T(8,128)S(1)} %get-tuple-element.22, f32[41,20,128]{2,1,0:T(8,128)S(1)} %fusion.4), kind=kLoop, calls=%fused_computation.97 | loop fusion | flops 129024 | bytes 3096576 | tf_op jit(solution)/shard_map/mul | solution.py:58
  31.0 1.1 %fusion.45 = f32[36,12,128]{2,1,0:T(8,128)} fusion(f32[36,14,128]{2,1,0:T(8,128)S(1)} %slice.913, f32[36,14,127]{2,1,0:T(8,128)S(1)} %get-tuple-element.70, f32[36,14,127]{2,1,0:T(8,128)S(1)} %get-tuple-element.69, f32[36,14,128]{2,1,0:T(8,128)S(1)} %get-tuple-element.67, f32[36,14,128]{2,1,0:T(8,128)S(1)} %get-tuple-element.68, ...), kind=kLoop, calls=%fused_computation.101 | loop fusion | flops 829440 | bytes 2283264 | tf_op jit(solution)/shard_map/mul | solution.py:120
  32.1 1.8 %reshape.677 = f32[18,2,6,2,128]{4,3,2,1,0:T(2,128)} reshape(f32[36,12,128]{2,1,0:T(8,128)} %fusion.45) | data formatting | bytes 442368 | tf_op jit(solution)/shard_map/reshape | solution.py:75
  33.9 1.0 %slice_multiply_fusion.18 = f32[36,14,127]{2,1,0:T(8,128)S(1)} fusion(f32[36,14,128]{2,1,0:T(8,128)S(1)} %get-tuple-element.64, f32[36,14,128]{2,1,0:T(8,128)} %slice.942), kind=kLoop, calls=%fused_computation.95 | loop fusion | flops 64008 | bytes 768096 | tf_op jit(solution)/shard_map/mul | solution.py:63
  34.9 3.2 %fusion.38 = f32[36,12,128]{2,1,0:T(8,128)} fusion(f32[36,14,127]{2,1,0:T(8,128)S(1)} %slice_multiply_fusion.18, f32[36,14,128]{2,1,0:T(8,128)} %slice.932, f32[36,14,127]{2,1,0:T(8,128)} %slice.943, f32[36,14,128]{2,1,0:T(8,128)} %slice.942, f32[36,14,128]{2,1,0:T(8,128)} %slice.933, f32[36,14,128]{2,1,0:T(8,128)} %get-tuple-element.62, ...), kind=kLoop, calls=%fused_computation.84 | loop fusion | flops 774144 | bytes 3389184 | tf_op jit(solution)/shard_map/mul | solution.py:120
  38.1 1.1 %reshape.678 = f32[18,2,6,2,128]{4,3,2,1,0:T(2,128)S(1)} reshape(f32[36,12,128]{2,1,0:T(8,128)} %fusion.38) | data formatting | bytes 442368 | tf_op jit(solution)/shard_map/reshape | solution.py:75
  39.2 1.1 %reduce_sum.38 = f32[18,6,128]{2,1,0:T(8,128)S(1)} reduce(f32[18,2,6,2,128]{4,3,2,1,0:T(2,128)} %reshape.677, f32[]{:T(128)} %constant.47.clone.1), dimensions={1,3}, to_apply=%region_2.3 | reduce | flops 41472 | bytes 276484 | tf_op jit(solution)/shard_map/reduce_sum | solution.py:75
  41.1 1.1 %reshape.675 = f32[18,2,6,2,128]{4,3,2,1,0:T(2,128)S(1)} reshape(f32[36,12,128]{2,1,0:T(8,128)} %slice.905) | data formatting | bytes 442368 | tf_op jit(solution)/shard_map/reshape | solution.py:75
  42.9 1.1 %reshape.676 = f32[18,2,6,2,128]{4,3,2,1,0:T(2,128)S(1)} reshape(f32[36,12,128]{2,1,0:T(8,128)} %slice.906) | data formatting | bytes 442368 | tf_op jit(solution)/shard_map/reshape | solution.py:75
  44.8 1.0 %fusion.89 = (f32[18,6,128]{2,0,1:T(8,128)S(1)}, f32[18,6,128]{2,0,1:T(8,128)S(1)}, f32[18,6,128]{2,0,1:T(8,128)S(1)}, f32[18,6,128]{2,0,1:T(8,128)S(1)}) fusion(f32[18,6,128]{2,1,0:T(8,128)} %reduce_sum.36, f32[18,6,128]{2,1,0:T(8,128)} %reduce_sum.37, f32[18,6,128]{2,1,0:T(8,128)} %reduce_sum.39, f32[18,6,128]{2,1,0:T(8,128)S(1)} %reduce_sum.38), kind=kLoop, calls=%fused_computation.192 | loop fusion | flops 165888 | bytes 442368 | tf_op jit(solution)/shard_map/div | solution.py:127
  47.4 17.5 %all-to-all-start = ((f32[8,4,18,128]{3,2,1,0:T(8,128)}), f32[8,4,18,128]{3,2,1,0:T(8,128)}, u32[]{:S(2)}, u32[]{:S(2)}) async-start(f32[8,4,18,128]{3,2,1,0:T(8,128)} %broadcast_select_fusion.4), calls=%async_computation | async-start | bytes 786432 | tf_op jit(solution)/shard_map/all_to_all | solution.py:141
  65.7 7.6 %all-to-all-done = f32[8,4,18,128]{3,2,1,0:T(8,128)} async-done(((f32[8,4,18,128]{3,2,1,0:T(8,128)}), f32[8,4,18,128]{3,2,1,0:T(8,128)}, u32[]{:S(2)}, u32[]{:S(2)}) %all-to-all-start) | async-done | bytes 294944 | tf_op jit(solution)/shard_map/all_to_all | solution.py:141
  73.3 0.9 %constant_dynamic-update-slice_fusion.7 = (f32[18,8,128]{2,0,1:T(8,128)S(1)}, f32[18,1,128]{2,0,1:T(8,128)S(1)}) fusion(f32[8,4,18,128]{3,2,1,0:T(8,128)} %all-to-all-done, pred[]{:T(512)S(6)} %gt.40, pred[]{:T(512)S(6)} %gt.39, pred[]{:T(512)S(6)} %gt.38, pred[]{:T(512)S(6)} %gt.37, pred[]{:T(512)S(6)} %gt.36, pred[]{:T(512)S(6)} %gt.35, pred[]{:T(512)S(6)} %gt.34), kind=kLoop, calls=%fused_computation.207 | loop fusion | flops 48383 | bytes 153607
  80.1 1.1 %maximum_add_fusion = f32[18,8,128]{2,0,1:T(8,128)S(1)} fusion(f32[18,1,128]{2,0,1:T(8,128)S(1)} %get-tuple-element.61, f32[18,6,128]{2,0,1:T(8,128)} %copy-done.15, f32[18,1,128]{2,0,1:T(8,128)S(1)} %get-tuple-element.60, f32[18,8,128]{2,0,1:T(8,128)S(1)} %constant_dynamic-update-slice_fusion, f32[18,1,128]{2,0,1:T(8,128)S(1)} %get-tuple-element.59, ...), kind=kLoop, calls=%fused_computation.184 | loop fusion | flops 110592 | bytes 294912 | tf_op jit(solution)/shard_map/add | solution.py:152
  (119 shorter events, 25.2 us)
Async XLA Ops:
  3.8 7.8 %collective-permute-start.1 = (f32[6,5,12,128]{3,2,1,0:T(8,128)S(1)}, f32[6,5,12,128]{3,2,1,0:T(8,128)S(1)}, u32[]{:S(2)}, u32[]{:S(2)}) collective-permute-start(f32[6,5,12,128]{3,2,1,0:T(8,128)S(1)} %broadcast_select_fusion.7), channel_id=1, source_target_pairs={{0,8},{8,0},{16,24},{24,16},{1,9},{9,1},{17,25},{25,17},{2,10},{10... | collective-permute-start | bytes 552968 | tf_op jit(solution)/shard_map/ppermute | solution.py:28
  5.5 9.3 %collective-permute-start = (f32[6,5,12,128]{3,2,1,0:T(8,128)S(1)}, f32[6,5,12,128]{3,2,1,0:T(8,128)S(1)}, u32[]{:S(2)}, u32[]{:S(2)}) collective-permute-start(f32[6,5,12,128]{3,2,1,0:T(8,128)S(1)} %get-tuple-element.36), channel_id=1, source_target_pairs={{8,16},{16,8},{9,17},{17,9},{10,18},{18,10},{11,19},{19,11},{12,20... | collective-permute-start | bytes 552968 | tf_op jit(solution)/shard_map/ppermute | solution.py:29
  15.1 2.0 %collective-permute-start.3 = (f32[6,42,4,128]{3,2,1,0:T(4,128)S(1)}, f32[6,42,4,128]{3,2,1,0:T(4,128)S(1)}, u32[]{:S(2)}, u32[]{:S(2)}) collective-permute-start(f32[6,42,4,128]{3,2,1,0:T(4,128)S(1)} %bitcast.297), channel_id=1, source_target_pairs={{0,1},{1,0},{2,3},{3,2},{4,5},{5,4},{6,7},{7,6},{8,9},{9,8},{10,11... | collective-permute-start | bytes 1548296 | tf_op jit(solution)/shard_map/ppermute | solution.py:28
  15.2 1.9 %collective-permute-start.2 = (f32[6,42,4,128]{3,2,1,0:T(4,128)S(1)}, f32[6,42,4,128]{3,2,1,0:T(4,128)S(1)}, u32[]{:S(2)}, u32[]{:S(2)}) collective-permute-start(f32[6,42,4,128]{3,2,1,0:T(4,128)S(1)} %get-tuple-element.33), channel_id=1, source_target_pairs={{1,2},{2,1},{3,4},{4,3},{5,6},{6,5},{9,10},{10,9},{11,12},{12,11},... | collective-permute-start | bytes 1548296 | tf_op jit(solution)/shard_map/ppermute | solution.py:29
  18.9 5.4 %copy-start.2 = (f32[42,20,128]{2,1,0:T(8,128)}, f32[42,20,128]{2,1,0:T(8,128)S(1)}, u32[]{:S(2)}) copy-start(f32[42,20,128]{2,1,0:T(8,128)S(1)} %get-tuple-element.39) | copy-start | bytes 1290244
  18.9 9.0 %copy-start.4 = (f32[42,20,128]{2,1,0:T(8,128)}, f32[42,20,128]{2,1,0:T(8,128)S(1)}, u32[]{:S(2)}) copy-start(f32[42,20,128]{2,1,0:T(8,128)S(1)} %get-tuple-element.41) | copy-start | bytes 1290244
  22.3 0.8 copy-start.8
  22.3 4.9 %copy-start = (f32[40,18,128]{2,1,0:T(8,128)}, f32[40,18,128]{2,1,0:T(8,128)S(1)}, u32[]{:S(2)}) copy-start(f32[40,18,128]{2,1,0:T(8,128)S(1)} %get-tuple-element.30) | copy-start | bytes 1105924
  22.8 1.0 %copy-start.6 = (f32[40,18,128]{2,1,0:T(8,128)}, f32[40,18,128]{2,1,0:T(8,128)S(1)}, u32[]{:S(2)}) copy-start(f32[40,18,128]{2,1,0:T(8,128)S(1)} %get-tuple-element.32) | copy-start | bytes 1105924
  24.1 6.9 %copy-start.11 = (f32[36,14,128]{2,1,0:T(8,128)}, f32[36,14,128]{2,1,0:T(8,128)S(1)}, u32[]{:S(2)}) copy-start(f32[36,14,128]{2,1,0:T(8,128)S(1)} %get-tuple-element.65) | copy-start | bytes 774148
  24.3 6.7 %copy-start.10 = (f32[36,14,128]{2,1,0:T(8,128)}, f32[36,14,128]{2,1,0:T(8,128)S(1)}, u32[]{:S(2)}) copy-start(f32[36,14,128]{2,1,0:T(8,128)S(1)} %slice.914) | copy-start | bytes 774148
  45.8 0.6 copy-start.13
  45.8 0.7 copy-start.14
  45.9 0.7 copy-start.15
  47.4 25.9 %all-to-all-start = ((f32[8,4,18,128]{3,2,1,0:T(8,128)}), f32[8,4,18,128]{3,2,1,0:T(8,128)}, u32[]{:S(2)}, u32[]{:S(2)}) async-start(f32[8,4,18,128]{3,2,1,0:T(8,128)} %broadcast_select_fusion.4), calls=%async_computation | async-start | bytes 786432 | tf_op jit(solution)/shard_map/all_to_all | solution.py:141
  80.1 1.8 %copy-start.1 = (f32[40,18,128]{2,1,0:T(8,128)S(1)}, f32[40,18,128]{2,1,0:T(8,128)}, u32[]{:S(2)}) copy-start(f32[40,18,128]{2,1,0:T(8,128)} %copy-done) | copy-start | bytes 1105924
  80.1 1.9 %copy-start.3 = (f32[42,20,128]{2,1,0:T(8,128)S(1)}, f32[42,20,128]{2,1,0:T(8,128)}, u32[]{:S(2)}) copy-start(f32[42,20,128]{2,1,0:T(8,128)} %copy-done.2) | copy-start | bytes 1290244
  80.1 1.9 %copy-start.5 = (f32[42,20,128]{2,1,0:T(8,128)S(1)}, f32[42,20,128]{2,1,0:T(8,128)}, u32[]{:S(2)}) copy-start(f32[42,20,128]{2,1,0:T(8,128)} %copy-done.4) | copy-start | bytes 1290244
  80.1 1.9 %copy-start.9 = (f32[40,18,128]{2,1,0:T(8,128)S(1)}, f32[40,18,128]{2,1,0:T(8,128)}, u32[]{:S(2)}) copy-start(f32[40,18,128]{2,1,0:T(8,128)} %copy-done.8) | copy-start | bytes 1105924
  82.0 1.0 %copy-start.7 = (f32[40,18,128]{2,1,0:T(8,128)S(1)}, f32[40,18,128]{2,1,0:T(8,128)}, u32[]{:S(2)}) copy-start(f32[40,18,128]{2,1,0:T(8,128)} %copy-done.6) | copy-start | bytes 1105924
  82.7 1.0 %copy-start.12 = (f32[32,12,128]{2,1,0:T(8,128)S(1)}, f32[32,12,128]{2,1,0:T(8,128)}, u32[]{:S(2)}) copy-start(f32[32,12,128]{2,1,0:T(8,128)} %slice.1024) | copy-start | bytes 589828

commit v2 on v0

v2 whole, which is shorter than its diff:
```python
import functools

import jax
import jax.numpy as jnp
from jax import lax
from jax.experimental import pallas as pl
from jax.experimental.pallas import tpu as pltpu
from jax.sharding import PartitionSpec as P

SOLID_CAP, GAS_CAP, FLOW, CONDUCT, RELAX, LUMP = 0.5, 0.02, 40.0, 0.05, 0.8, 0.25
GAS_SELF = GAS_CAP + 4.5 * CONDUCT

PAD = 8
WX = 5
CROP = 4
(SA, GA, SB, GB, K, C, RS, RG, FX, FZ, H, FY, ASS, ASG, AGG) = range(15)
PLANES = 15
(M_S, M_G, M_K, M_C, M_FY, M_C2, M_D2, M_1S, M_1G, M_2S, M_2G, M_3S, M_3G) = range(13)
MESSAGE = 13

VMEM = pl.BlockSpec(memory_space=pltpu.VMEM)
PARAMS = pltpu.CompilerParams(vmem_limit_bytes=40 * 1024 * 1024)


def up_x(v):
    return pltpu.roll(v, v.shape[0] - 1, 0)


def down_x(v):
    return pltpu.roll(v, 1, 0)


def up_z(v):
    return pltpu.roll(v, v.shape[1] - 1, 1)


def down_z(v):
    return pltpu.roll(v, 1, 1)


def lanes(shape):
    return lax.broadcasted_iota(jnp.int32, shape, 1)


def x_mask(shape, nx):
    row = lax.broadcasted_iota(jnp.int32, shape, 0)
    place, count = lax.axis_index("gx"), lax.axis_size("gx")
    low = jnp.where(place == 0, PAD, PAD - WX)
    high = jnp.where(place == count - 1, PAD + nx, PAD + nx + WX)
    return jnp.where((row >= low) & (row < high), 1.0, 0.0).astype(jnp.float32)


def pack_kernel(temps, right, exchange, coupling, one, two):
    even = lax.axis_index("gx") % 2 == 0
    top = exchange.shape[1]
    parts = [(temps, 0, WX), (temps, 1, WX), (exchange, None, WX)]
    parts += [(right, 0, WX - 1), (right, 1, WX - 1), (coupling, None, WX - 1)]

    def row(y, carry):
        at = 0
        for ref, plane, width in parts:
            lead = (y,) if plane is None else (plane, y)
            low = ref[lead + (slice(0, width),)]
            high = ref[lead + (slice(top - width, top),)]
            one[y, at : at + width] = jnp.where(even, high, low)
            two[y, at : at + width] = jnp.where(even, low, high)
            at += width
        return carry

    lax.fori_loop(0, one.shape[0], row, 0)


def inner(s, g, c, h, fx, fz, edge):
    t = c * (s - g)
    flux_x = fx * (up_x(s) - s)
    flux_z = fz * (up_z(s) - s)
    part_s = (flux_x - down_x(flux_x)) + (flux_z - down_z(flux_z)) - h * s - t
    part_g = (
        t
        - GAS_SELF * g
        + CONDUCT * (up_x(g) + down_x(g))
        + edge[0] * up_z(g)
        + edge[1] * down_z(g)
    )
    return part_s, part_g


def edge_weights(shape):
    lane = lanes(shape)
    weight = jnp.float32(0.25 * CONDUCT)
    return jnp.where(lane == shape[1] - 1, 0.0, weight), jnp.where(lane == 0, 0.0, weight)


def row_inner(st, i, s_at, edge):
    return inner(st[s_at, i], st[s_at + 1, i], st[C, i], st[H, i], st[FX, i], st[FZ, i], edge)


def row_residual(st, i, s_at, edge):
    part_s, part_g = row_inner(st, i, s_at, edge)
    s, g, before = st[s_at, i], st[s_at + 1, i], st[s_at + 1, i - 1]
    part_s += st[FY, i] * (st[s_at, i + 1] - s) + st[FY, i - 1] * (st[s_at, i - 1] - s)
    part_g += CONDUCT * (st[s_at + 1, i + 1] + before) - FLOW * (g - before)
    return st[RS, i] + part_s, st[RG, i] + part_g


def relaxed(st, i, s_at, res_s, res_g):
    s = st[s_at, i] + st[ASS, i] * res_s + st[ASG, i] * res_g
    g = st[s_at + 1, i] + st[ASG, i] * res_s + st[AGG, i] * res_g
    return s, g


def faces(st, i):
    k = st[K, i]
    lane = lanes(k.shape)
    end = k.shape[1] - 1
    fx = 0.5 * (k + up_x(k))
    fz = jnp.where(lane == end, 0.0, 0.125 * (k + up_z(k)))
    h = SOLID_CAP + jnp.where((lane == 0) | (lane == end), 0.125 * k, 0.0)
    st[FX, i] = fx
    st[FZ, i] = fz
    st[H, i] = h
    return h + (fx + down_x(fx)) + (fz + down_z(fz))


def inverse(diag, c, mask):
    gas_diag = (GAS_SELF + FLOW) + c
    inv = (RELAX * mask) / (diag * gas_diag - c * c)
    return inv * gas_diag, inv * c, inv * diag


def store_inverse(st, i, diag, mask):
    st[ASS, i], st[ASG, i], st[AGG, i] = inverse(diag, st[C, i], mask)


def first_kernel(temps, right, exchange, coupling, one, two, st, out_one, out_two):
    ny, nx, nz = exchange.shape
    ext = nx + 2 * PAD
    even = lax.axis_index("gx") % 2 == 0
    shape = (ext, nz)
    mask = x_mask(shape, nx)
    edge = edge_weights(shape)
    zeros = jnp.zeros((PAD, nz), jnp.float32)

    def build(y, carry):
        i = y + 1
        at = 0
        for plane, own, width in (
            (SA, temps[0, y], WX),
            (GA, temps[1, y], WX),
            (K, exchange[y], WX),
            (RS, right[0, y], WX - 1),
            (RG, right[1, y], WX - 1),
            (C, coupling[y], WX - 1),
        ):
            a, b = one[y, at : at + width], two[y, at : at + width]
            st[plane, i, :PAD] = zeros
            st[plane, i, PAD + nx :] = zeros
            st[plane, i, PAD - width : PAD] = jnp.where(even, b, a)
            st[plane, i, PAD + nx : PAD + nx + width] = jnp.where(even, a, b)
            st[plane, i, PAD : PAD + nx] = own
            at += width
        return carry

    lax.fori_loop(0, ny, build, 0)

    def conduct(y, carry):
        s = st[SA, y + 1]
        st[K, y + 1] = (1.0 + 4.0 * st[K, y + 1] * s * s * s) * mask
        return carry

    lax.fori_loop(0, ny, conduct, 0)

    def row_diag(i):
        diag = faces(st, i) + st[C, i]
        st[FY, i] = 0.5 * (st[K, i] + st[K, i + 1])
        return diag + st[FY, i] + st[FY, i - 1]

    faces(st, 1)
    faces(st, ny)
    st[FY, 1] = 0.5 * (st[K, 1] + st[K, 2])

    def sweep(i, carry):
        store_inverse(st, i, row_diag(i), mask)
        st[SB, i], st[GB, i] = relaxed(st, i, SA, *row_residual(st, i, SA, edge))
        return carry

    lax.fori_loop(2, ny, sweep, 0)

    def diag_of(i):
        fx, fz = st[FX, i], st[FZ, i]
        return st[H, i] + (fx + down_x(fx)) + (fz + down_z(fz)) + st[C, i] + st[FY, i] + st[FY, i - 1]

    e, d = ny, ny - 1
    s, g, fy = st[SA, e], st[GA, e], st[FY, d]
    part_s, part_g = row_inner(st, e, SA, edge)
    m1s = st[RS, e] + part_s + fy * (st[SA, d] - s)
    m1g = st[RG, e] + part_g + CONDUCT * st[GA, d] - FLOW * (g - st[GA, d])
    s1, g1 = st[SB, d], st[GB, d]
    m2s = st[RS, e] + fy * s1
    m2g = st[RG, e] + (CONDUCT + FLOW) * g1
    part_s, part_g = row_inner(st, d, SB, edge)
    m3s = st[RS, d] + part_s - fy * s1 + st[FY, d - 1] * (st[SB, d - 1] - s1)
    m3g = st[RG, d] + part_g + CONDUCT * st[GB, d - 1] - FLOW * (g1 - st[GB, d - 1])
    onward = [s, g, st[K, e], st[C, e], fy, st[C, d], diag_of(d), m1s, m1g, m2s, m2g, m3s, m3g]

    e, d = 1, 2
    s, g, fy = st[SA, e], st[GA, e], st[FY, e]
    part_s, part_g = row_inner(st, e, SA, edge)
    m1s = st[RS, e] + part_s + fy * (st[SA, d] - s)
    m1g = st[RG, e] + part_g + CONDUCT * st[GA, d] - FLOW * g
    s1, g1 = st[SB, d], st[GB, d]
    m2s = st[RS, e] + fy * s1
    m2g = st[RG, e] + CONDUCT * g1
    part_s, part_g = row_inner(st, d, SB, edge)
    m3s = st[RS, d] + part_s - fy * s1 + st[FY, d] * (st[SB, d + 1] - s1)
    m3g = st[RG, d] + part_g + CONDUCT * st[GB, d + 1] - FLOW * g1
    back = [s, g, st[K, e], st[C, e], fy, st[C, d], diag_of(d), m1s, m1g, m2s, m2g, m3s, m3g]

    even_y = lax.axis_index("gy") % 2 == 0
    for plane, (a, b) in enumerate(zip(onward, back)):
        a, b = a[CROP : ext - CROP], b[CROP : ext - CROP]
        out_one[plane] = jnp.where(even_y, a, b)
        out_two[plane] = jnp.where(even_y, b, a)


def outer_residual(st, i, s_at, rs, rg, fy_out, edge, after):
    part_s, part_g = row_inner(st, i, s_at, edge)
    s, g = st[s_at, i], st[s_at + 1, i]
    if after:
        part_s += st[FY, i - 1] * (st[s_at, i - 1] - s)
        part_g += (CONDUCT + FLOW) * st[s_at + 1, i - 1]
    else:
        part_s += st[FY, i] * (st[s_at, i + 1] - s)
        part_g += CONDUCT * st[s_at + 1, i + 1]
    return rs + part_s - fy_out * s, rg + part_g - FLOW * g


def pair_x(v):
    row = lax.broadcasted_iota(jnp.int32, v.shape, 0)
    return v + jnp.where(row % 2 == 0, up_x(v), down_x(v))


def second_kernel(st_in, one, two, st, extra, coarse, sides, message, before, after, squeeze):
    del st_in
    planes, rows, ext, nz = st.shape
    ny, nx = rows - 2, ext - 2 * PAD
    shape = (ext, nz)
    me, count = lax.axis_index("gy"), lax.axis_size("gy")
    even = me % 2 == 0
    mask = x_mask(shape, nx)
    low = jnp.where(me == 0, 0.0, mask)
    high = jnp.where(me == count - 1, 0.0, mask)
    edge = edge_weights(shape)
    zeros = jnp.zeros((PAD, nz), jnp.float32)

    def unpack(plane, carry):
        a, b = one[plane], two[plane]
        for ref, v in ((before, jnp.where(even, b, a)), (after, jnp.where(even, a, b))):
            ref[plane, :PAD] = zeros
            ref[plane, ext - PAD :] = zeros
            ref[plane, CROP : ext - CROP] = v
        return carry

    lax.fori_loop(0, MESSAGE, unpack, 0)

    last = ny + 1
    for i, ref in ((0, before), (last, after)):
        st[SA, i], st[GA, i], st[K, i], st[C, i] = ref[M_S], ref[M_G], ref[M_K], ref[M_C]
    st[FY, 0] = 0.5 * (st[K, 0] + st[K, 1])
    st[FY, ny] = 0.5 * (st[K, ny] + st[K, last])

    def diag_of(i):
        fx, fz = st[FX, i], st[FZ, i]
        return st[H, i] + (fx + down_x(fx)) + (fz + down_z(fz)) + st[C, i]

    store_inverse(st, 1, diag_of(1) + st[FY, 0] + st[FY, 1], mask)
    store_inverse(st, ny, diag_of(ny) + st[FY, ny - 1] + st[FY, ny], mask)
    store_inverse(st, 0, faces(st, 0) + st[C, 0] + before[M_FY] + st[FY, 0], low)
    store_inverse(st, last, faces(st, last) + st[C, last] + after[M_FY] + st[FY, ny], high)

    res_s = before[M_1S] + st[FY, 0] * (st[SA, 1] - st[SA, 0])
    res_g = before[M_1G] + CONDUCT * st[GA, 1]
    st[SB, 0], st[GB, 0] = relaxed(st, 0, SA, res_s, res_g)
    res_s = after[M_1S] + st[FY, ny] * (st[SA, ny] - st[SA, last])
    res_g = after[M_1G] + (CONDUCT + FLOW) * st[GA, ny]
    st[SB, last], st[GB, last] = relaxed(st, last, SA, res_s, res_g)
    for i in (1, ny):
        st[SB, i], st[GB, i] = relaxed(st, i, SA, *row_residual(st, i, SA, edge))

    for i, ref, is_after, inside in ((0, before, False, low), (last, after, True, high)):
        res = outer_residual(st, i, SB, ref[M_2S], ref[M_2G], ref[M_FY], edge, is_after)
        st[SA, i], st[GA, i] = relaxed(st, i, SB, *res)
        ss, sg, gg = inverse(jnp.maximum(ref[M_D2], SOLID_CAP), ref[M_C2], inside)
        to, back = (CONDUCT + FLOW, CONDUCT) if is_after else (CONDUCT, CONDUCT + FLOW)
        res_s = ref[M_3S] + ref[M_FY] * st[SB, i]
        res_g = ref[M_3G] + to * st[GB, i]
        side = 3 if is_after else 0
        extra[side] = ref[M_2S] + ref[M_FY] * (ss * res_s + sg * res_g)
        extra[side + 1] = ref[M_2G] + back * (sg * res_s + gg * res_g)
        extra[side + 2] = ref[M_FY]

    def sweep(i, carry):
        st[SA, i], st[GA, i] = relaxed(st, i, SB, *row_residual(st, i, SB, edge))
        return carry

    lax.fori_loop(1, ny + 1, sweep, 0)

    def coefficients(c_sum, k_sum):
        solid = 4.0 * SOLID_CAP + c_sum + LUMP * k_sum
        ratio = c_sum / solid
        denominator = (4.0 * GAS_CAP + 2.0 * FLOW) + c_sum - c_sum * ratio
        return solid, ratio, denominator

    def coarse_row(j, carry):
        slopes, offsets = carry
        i = 2 * j + 1
        res_s, res_g = row_residual(st, i, SA, edge)
        more_s, more_g = row_residual(st, i + 1, SA, edge)
        res_s, res_g = pair_x((res_s + more_s) * mask), pair_x((res_g + more_g) * mask)
        c_sum = pair_x(st[C, i] + st[C, i + 1])
        solid, ratio, denominator = coefficients(c_sum, pair_x(st[K, i] + st[K, i + 1]))
        lead = res_s / solid
        slope = (2.0 * FLOW) / denominator
        offset = (res_g + c_sum * lead) / denominator
        slopes, offsets = slope * slopes, slope * offsets + offset
        coarse[0, j], coarse[1, j], coarse[2, j], coarse[3, j] = lead, ratio, slopes, offsets
        return slopes, offsets

    blocks = ny // 2
    slopes, offsets = lax.fori_loop(0, blocks, coarse_row, (jnp.ones(shape, jnp.float32), jnp.zeros(shape, jnp.float32)))

    for side, (i, ref) in enumerate(((0, before), (last, after))):
        k2 = 2.0 * ref[M_FY] - ref[M_K]
        solid, ratio, denominator = coefficients(pair_x(ref[M_C] + ref[M_C2]), pair_x(ref[M_K] + k2))
        sides[side] = ratio
        if side:
            sides[2] = (2.0 * FLOW) / denominator

    squeeze[0], squeeze[1], squeeze[2] = slopes, offsets, coarse[0, blocks - 1]
    squeeze[3], squeeze[4] = coarse[0, 0], coarse[3, 0]
    span = nx // 2 + 2
    pick = pl.ds(PAD - 2, span, 2)
    thin = [squeeze[k, pick, :] for k in range(5)]
    blank = jnp.zeros_like(thin[0])

    def fill(d, carry):
        onward = d > me
        for k, (a, b) in enumerate(zip(thin[:3], thin[3:] + [blank])):
            message[d, k * span : (k + 1) * span] = jnp.where(onward, a, b)
        return carry

    lax.fori_loop(0, count, fill, 0)


def third_kernel(st, extra, coarse, sides, got, out, sc, wide):
    planes, rows, ext, nz = st.shape
    ny, nx = rows - 2, ext - 2 * PAD
    shape = (ext, nz)
    me, count = lax.axis_index("gy"), lax.axis_size("gy")
    edge = edge_weights(shape)
    span = nx // 2 + 2
    blocks = ny // 2

    def fold(d, gas):
        return got[d, :span] * gas + got[d, span : 2 * span]

    gas_in = lax.fori_loop(0, me, fold, jnp.zeros((span, nz), jnp.float32))
    inside_low, inside_high = me > 0, me < count - 1
    prev, following = jnp.maximum(me - 1, 0), jnp.minimum(me + 1, count - 1)
    lead_low = jnp.where(inside_low, got[prev, 2 * span : 3 * span], 0.0)
    lead_high = jnp.where(inside_high, got[following, :span], 0.0)
    offset_high = jnp.where(inside_high, got[following, span : 2 * span], 0.0)
    for k, v in enumerate((gas_in, lead_low, lead_high, offset_high)):
        wide[k, : PAD - 2] = jnp.zeros((PAD - 2, nz), jnp.float32)
        wide[k, ext - PAD + 2 :] = jnp.zeros((PAD - 2, nz), jnp.float32)
        wide[k, pl.ds(PAD - 2, span, 2), :] = v
        wide[k, pl.ds(PAD - 1, span, 2), :] = v

    gas_in = wide[0]
    last = ny + 1
    solid_low = wide[1] + sides[0] * gas_in
    sc[0, 0] = st[SA, 0] + solid_low
    sc[1, 0] = st[GA, 0] + gas_in

    def correct(j, carry):
        gas = coarse[2, j] * gas_in + coarse[3, j]
        solid = coarse[0, j] + coarse[1, j] * gas
        for i in (2 * j + 1, 2 * j + 2):
            sc[0, i] = st[SA, i] + solid
            sc[1, i] = st[GA, i] + gas
        return carry

    lax.fori_loop(0, blocks, correct, 0)
    gas = coarse[2, blocks - 1] * gas_in + coarse[3, blocks - 1]
    gas_high = jnp.where(inside_high, sides[2] * gas + wide[3], 0.0)
    solid_high = wide[2] + sides[1] * gas_high
    sc[0, last] = st[SA, last] + solid_high
    sc[1, last] = st[GA, last] + gas_high

    view = Fields(st, sc)
    for i, is_after, solid, gas in ((0, False, solid_low, gas_in), (last, True, solid_high, gas_high)):
        side = 3 if is_after else 0
        fy = extra[side + 2]
        rs = extra[side] + fy * solid
        rg = extra[side + 1] + (CONDUCT if is_after else CONDUCT + FLOW) * gas
        res = outer_residual(view, i, SA, rs, rg, fy, edge, is_after)
        sc[2, i], sc[3, i] = relaxed(view, i, SA, *res)

    def sweep(i, carry):
        sc[2, i], sc[3, i] = relaxed(view, i, SA, *row_residual(view, i, SA, edge))
        return carry

    lax.fori_loop(1, ny + 1, sweep, 0)

    def final(i, carry):
        s, g = relaxed(view, i, SB, *row_residual(view, i, SB, edge))
        out[0, i - 1] = s[PAD : PAD + nx]
        out[1, i - 1] = g[PAD : PAD + nx]
        return carry

    lax.fori_loop(1, ny + 1, final, 0)


class Fields:
    def __init__(self, st, sc):
        self.st, self.sc = st, sc

    def __getitem__(self, at):
        return (self.sc if at[0] <= GB else self.st)[at]


def swap(one, two, axis):
    def pairs(first):
        out = []
        for i in range(first, lax.axis_size(axis) - 1, 2):
            out += [(i, i + 1), (i + 1, i)]
        return out

    return lax.ppermute(one, axis, pairs(0)), lax.ppermute(two, axis, pairs(1))


def shards(temps, right_side, exchange, coupling):
    temps, right_side = (jnp.transpose(a, (0, 2, 1, 3)) for a in (temps, right_side))
    exchange, coupling = (jnp.transpose(a, (1, 0, 2)) for a in (exchange, coupling))
    ny, nx, nz = exchange.shape
    ext = nx + 2 * PAD
    f32 = functools.partial(jax.ShapeDtypeStruct, dtype=jnp.float32)

    strip = f32((ny, 32, nz))
    one, two = pl.pallas_call(
        pack_kernel,
        out_shape=(strip, strip),
        in_specs=[VMEM] * 4,
        out_specs=(VMEM, VMEM),
        compiler_params=PARAMS,
        name="pack_x",
    )(temps, right_side, exchange, coupling)
    one, two = swap(one, two, "gx")

    state = f32((PLANES, ny + 2, ext, nz))
    letter = f32((MESSAGE, ext - 2 * CROP, nz))
    st, one, two = pl.pallas_call(
        first_kernel,
        out_shape=(state, letter, letter),
        in_specs=[VMEM] * 6,
        out_specs=(VMEM,) * 3,
        compiler_params=PARAMS,
        name="first",
    )(temps, right_side, exchange, coupling, one, two)
    one, two = swap(one, two, "gy")

    count = lax.axis_size("gy")
    span = nx // 2 + 2
    height = (3 * span + 7) // 8 * 8
    st, extra, coarse, sides, message = pl.pallas_call(
        second_kernel,
        out_shape=(state, f32((6, ext, nz)), f32((4, ny // 2, ext, nz)), f32((3, ext, nz)), f32((count, height, nz))),
        in_specs=[VMEM] * 3,
        out_specs=(VMEM,) * 5,
        scratch_shapes=[pltpu.VMEM((MESSAGE, ext, nz), jnp.float32)] * 2 + [pltpu.VMEM((5, ext, nz), jnp.float32)],
        input_output_aliases={0: 0},
        compiler_params=PARAMS,
        name="second",
    )(st, one, two)
    got = lax.all_to_all(message, "gy", 0, 0)

    out = pl.pallas_call(
        third_kernel,
        out_shape=f32((2, ny, nx, nz)),
        in_specs=[VMEM] * 5,
        out_specs=VMEM,
        scratch_shapes=[pltpu.VMEM((4, ny + 2, ext, nz), jnp.float32), pltpu.VMEM((4, ext, nz), jnp.float32)],
        compiler_params=PARAMS,
        name="third",
    )(st, extra, coarse, sides, got)
    return jnp.transpose(out, (0, 2, 1, 3))


def solution(mesh):
    return jax.shard_map(
        shards,
        mesh=mesh,
        in_specs=(
            P(None, "gx", "gy", None),
            P(None, "gx", "gy", None),
            P("gx", "gy", None),
            P("gx", "gy", None),
        ),
        out_specs=P(None, "gx", "gy", None),
        check_vma=False,
    )
```

time: 121 us -> 45.8 us (0.38)
  the two profiles are of different devices: /device:TPU:3 before, /device:TPU:16 now
where the time goes in v2:
time: 45.8 us; the launch traced here: 45.5 us
  blocking collectives  18.8 us (41%)
  Pallas kernels  11.3 us (25%)
  waiting for transfers between devices  7.17 us (16%)
  starting transfers between devices  4.3 us (9%)
  local copies, waits for them, and re-layouts  3.84 us (8%)
    all_to_all x1, blocking collectives, shards(): got = lax.all_to_all(message, 'gy', 0, 0)  18.8 us
    pallas_call x1, Pallas kernels, shards(): pl.pallas_call(third_kernel, out_shape=f32((2, ny, nx, nz)), in_specs=[VM...  4.87 us
    ppermute x2, waiting for transfers between devices, swap(): lax.ppermute(one, axis, pairs(0))  3.99 us
    unnamed x8, local copies, waits for them, and re-layouts  3.84 us
    pallas_call x1, Pallas kernels, shards(): pl.pallas_call(second_kernel, out_shape=(state, f32((6, ext, nz)), f32((4...  3.7 us
    ppermute x2, waiting for transfers between devices, swap(): lax.ppermute(two, axis, pairs(1))  3.18 us
    pallas_call x1, Pallas kernels, shards(): pl.pallas_call(first_kernel, out_shape=(state, letter, letter), in_specs=...  2.65 us
    ppermute x2, starting transfers between devices, swap(): lax.ppermute(two, axis, pairs(1))  2.59 us
  transfers between devices with their start and end apart: 4, of which 3 were waited for; matrix products, arithmetic and copies ran while one was open for 0% of the time, Pallas kernels for 0%

profile of v2, /device:TPU:16, one launch (start us, length us, event | category | flops | bytes accessed | tf_op | source)
XLA Modules:
  0.0 45.5 jit_solution(11349985474567983621)
XLA Ops:
  0.0 0.0 copy-start
  0.0 1.0 %copy-done = f32[2,32,12,128]{3,1,2,0:T(8,128)S(1)} copy-done((f32[2,32,12,128]{3,1,2,0:T(8,128)S(1)}, f32[2,32,12,128]{3,1,2,0:T(8,128)}, u32[]{:S(2)}) %copy-start) | copy-done | bytes 393240
  1.0 0.0 copy-start.1
  1.0 1.0 %copy-done.1 = f32[2,32,12,128]{3,1,2,0:T(8,128)S(1)} copy-done((f32[2,32,12,128]{3,1,2,0:T(8,128)S(1)}, f32[2,32,12,128]{3,1,2,0:T(8,128)}, u32[]{:S(2)}) %copy-start.1) | copy-done | bytes 393240
  2.0 0.0 copy-start.2
  2.0 0.9 %copy-done.2 = f32[32,12,128]{2,0,1:T(8,128)S(1)} copy-done((f32[32,12,128]{2,0,1:T(8,128)S(1)}, f32[32,12,128]{2,0,1:T(8,128)}, u32[]{:S(2)}) %copy-start.2) | copy-done | bytes 196632
  2.9 0.0 copy-start.3
  2.9 0.9 %copy-done.3 = f32[32,12,128]{2,0,1:T(8,128)S(1)} copy-done((f32[32,12,128]{2,0,1:T(8,128)S(1)}, f32[32,12,128]{2,0,1:T(8,128)}, u32[]{:S(2)}) %copy-start.3) | copy-done | bytes 196632
  3.8 0.1 pack_x.1
  3.9 1.6 %collective-permute-start = (f32[12,32,128]{2,1,0:T(8,128)S(1)}, f32[12,32,128]{2,1,0:T(8,128)S(1)}, u32[]{:S(2)}, u32[]{:S(2)}) collective-permute-start(f32[12,32,128]{2,1,0:T(8,128)S(1)} %get-tuple-element.15), channel_id=1, source_target_pairs={{0,8},{8,0},{16,24},{24,16},{1,9},{9,1},{17,25},{25,17},{2,10},{10... | collective-permute-start | bytes 589832 | tf_op jit(solution)/shard_map/ppermute | solution.py:439
  5.6 1.9 %collective-permute-start.1 = (f32[12,32,128]{2,1,0:T(8,128)S(1)}, f32[12,32,128]{2,1,0:T(8,128)S(1)}, u32[]{:S(2)}, u32[]{:S(2)}) collective-permute-start(f32[12,32,128]{2,1,0:T(8,128)S(1)} %get-tuple-element.16), channel_id=1, source_target_pairs={{8,16},{16,8},{9,17},{17,9},{10,18},{18,10},{11,19},{19,11},{12,20... | collective-permute-start | bytes 589832 | tf_op jit(solution)/shard_map/ppermute | solution.py:439
  7.5 3.1 %collective-permute-done.one = f32[12,32,128]{2,1,0:T(8,128)S(1)} collective-permute-done((f32[12,32,128]{2,1,0:T(8,128)S(1)}, f32[12,32,128]{2,1,0:T(8,128)S(1)}, u32[]{:S(2)}, u32[]{:S(2)}) %collective-permute-start) | collective-permute-done | bytes 196640 | tf_op jit(solution)/shard_map/ppermute | solution.py:439
  10.7 3.2 %collective-permute-done.1.two = f32[12,32,128]{2,1,0:T(8,128)S(1)} collective-permute-done((f32[12,32,128]{2,1,0:T(8,128)S(1)}, f32[12,32,128]{2,1,0:T(8,128)S(1)}, u32[]{:S(2)}, u32[]{:S(2)}) %collective-permute-start.1) | collective-permute-done | bytes 196640 | tf_op jit(solution)/shard_map/ppermute | solution.py:439
  13.8 2.7 %first.1 = (f32[15,14,48,128]{3,2,1,0:T(8,128)S(1)}, f32[13,40,128]{2,1,0:T(8,128)S(1)}, f32[13,40,128]{2,1,0:T(8,128)S(1)}) custom-call(f32[2,12,32,128]{3,2,1,0:T(8,128)S(1)} %bitcast.6, f32[2,12,32,128]{3,2,1,0:T(8,128)S(1)} %bitcast.8, f32[12,32,128]{2,1,0:T(8,128)S(1)} %bitcast.10, f32[12,32,128]{2,1,0:T(8,128)S(1)} %bitcast.12, ...), custom_call_target="tpu_custom_call" | custom-call | tf_op jit(solution)/shard_map/first/pallas_call | solution.py:462
  16.5 0.1 collective-permute-start.2
  16.6 0.7 %collective-permute-start.3 = (f32[13,40,128]{2,1,0:T(8,128)S(1)}, f32[13,40,128]{2,1,0:T(8,128)S(1)}, u32[]{:S(2)}, u32[]{:S(2)}) collective-permute-start(f32[13,40,128]{2,1,0:T(8,128)S(1)} %get-tuple-element.19), channel_id=1, source_target_pairs={{1,2},{2,1},{3,4},{4,3},{5,6},{6,5},{9,10},{10,9},{11,12},{12,11},... | collective-permute-start | bytes 798728 | tf_op jit(solution)/shard_map/ppermute | solution.py:439
  17.3 0.8 %collective-permute-done.2.one = f32[13,40,128]{2,1,0:T(8,128)S(1)} collective-permute-done((f32[13,40,128]{2,1,0:T(8,128)S(1)}, f32[13,40,128]{2,1,0:T(8,128)S(1)}, u32[]{:S(2)}, u32[]{:S(2)}) %collective-permute-start.2) | collective-permute-done | bytes 266272 | tf_op jit(solution)/shard_map/ppermute | solution.py:439
  18.1 0.0 collective-permute-done.3.two
  18.1 3.7 %second.1 = (f32[15,14,48,128]{3,2,1,0:T(8,128)S(1)}, f32[6,48,128]{2,1,0:T(8,128)S(1)}, f32[4,6,48,128]{3,2,1,0:T(8,128)S(1)}, f32[3,48,128]{2,1,0:T(8,128)S(1)}, f32[8,56,128]{2,1,0:T(8,128)S(1)}) custom-call(f32[15,14,48,128]{3,2,1,0:T(8,128)S(1)} %get-tuple-element.17.st_in, ...), custom_call_target="tpu_custom_call", output_to_operand_aliasing={{0}: (0, {})} | custom-call | tf_op jit(solution)/shard_map/second/pallas_call | solution.py:475
  21.8 18.8 %all_to_all.5.got = f32[8,56,128]{2,1,0:T(8,128)S(1)} all-to-all(f32[8,56,128]{2,1,0:T(8,128)S(1)} %get-tuple-element.24), channel_id=1, replica_groups=mesh['gx'=4,'gy'=8] {'gy'}, dimensions={0} | all-to-all | bytes 458752 | tf_op jit(solution)/shard_map/all_to_all | solution.py:485
  40.6 4.9 %third.1 = f32[2,12,32,128]{3,2,1,0:T(8,128)} custom-call(f32[15,14,48,128]{3,2,1,0:T(8,128)S(1)} %get-tuple-element.20.st, f32[6,48,128]{2,1,0:T(8,128)S(1)} %get-tuple-element.21.extra, f32[4,6,48,128]{3,2,1,0:T(8,128)S(1)} %get-tuple-element.22.coarse, f32[3,48,128]{2,1,0:T(8,128)S(1)} %get-tuple-element.23.sides, f32[8,56,128]{2,1,0:T(8,128)S(1)} %all_to_all.5.got), custom_call_target="tpu_custom_call" | custom-call | tf_op jit(solution)/shard_map/third/pallas_call | solution.py:487
Async XLA Ops:
  0.0 1.0 %copy-start = (f32[2,32,12,128]{3,1,2,0:T(8,128)S(1)}, f32[2,32,12,128]{3,1,2,0:T(8,128)}, u32[]{:S(2)}) copy-start(f32[2,32,12,128]{3,1,2,0:T(8,128)} %param.4) | copy-start | bytes 1179652
  1.0 1.0 %copy-start.1 = (f32[2,32,12,128]{3,1,2,0:T(8,128)S(1)}, f32[2,32,12,128]{3,1,2,0:T(8,128)}, u32[]{:S(2)}) copy-start(f32[2,32,12,128]{3,1,2,0:T(8,128)} %param.5) | copy-start | bytes 1179652
  2.0 0.9 %copy-start.2 = (f32[32,12,128]{2,0,1:T(8,128)S(1)}, f32[32,12,128]{2,0,1:T(8,128)}, u32[]{:S(2)}) copy-start(f32[32,12,128]{2,0,1:T(8,128)} %param.6) | copy-start | bytes 589828
  2.9 0.9 %copy-start.3 = (f32[32,12,128]{2,0,1:T(8,128)S(1)}, f32[32,12,128]{2,0,1:T(8,128)}, u32[]{:S(2)}) copy-start(f32[32,12,128]{2,0,1:T(8,128)} %param.7) | copy-start | bytes 589828
  3.9 6.7 %collective-permute-start = (f32[12,32,128]{2,1,0:T(8,128)S(1)}, f32[12,32,128]{2,1,0:T(8,128)S(1)}, u32[]{:S(2)}, u32[]{:S(2)}) collective-permute-start(f32[12,32,128]{2,1,0:T(8,128)S(1)} %get-tuple-element.15), channel_id=1, source_target_pairs={{0,8},{8,0},{16,24},{24,16},{1,9},{9,1},{17,25},{25,17},{2,10},{10... | collective-permute-start | bytes 589832 | tf_op jit(solution)/shard_map/ppermute | solution.py:439
  5.6 8.2 %collective-permute-start.1 = (f32[12,32,128]{2,1,0:T(8,128)S(1)}, f32[12,32,128]{2,1,0:T(8,128)S(1)}, u32[]{:S(2)}, u32[]{:S(2)}) collective-permute-start(f32[12,32,128]{2,1,0:T(8,128)S(1)} %get-tuple-element.16), channel_id=1, source_target_pairs={{8,16},{16,8},{9,17},{17,9},{10,18},{18,10},{11,19},{19,11},{12,20... | collective-permute-start | bytes 589832 | tf_op jit(solution)/shard_map/ppermute | solution.py:439
  16.5 1.6 %collective-permute-start.2 = (f32[13,40,128]{2,1,0:T(8,128)S(1)}, f32[13,40,128]{2,1,0:T(8,128)S(1)}, u32[]{:S(2)}, u32[]{:S(2)}) collective-permute-start(f32[13,40,128]{2,1,0:T(8,128)S(1)} %get-tuple-element.18), channel_id=1, source_target_pairs={{0,1},{1,0},{2,3},{3,2},{4,5},{5,4},{6,7},{7,6},{8,9},{9,8},{10,11... | collective-permute-start | bytes 798728 | tf_op jit(solution)/shard_map/ppermute | solution.py:439
  16.6 1.5 %collective-permute-start.3 = (f32[13,40,128]{2,1,0:T(8,128)S(1)}, f32[13,40,128]{2,1,0:T(8,128)S(1)}, u32[]{:S(2)}, u32[]{:S(2)}) collective-permute-start(f32[13,40,128]{2,1,0:T(8,128)S(1)} %get-tuple-element.19), channel_id=1, source_target_pairs={{1,2},{2,1},{3,4},{4,3},{5,6},{6,5},{9,10},{10,9},{11,12},{12,11},... | collective-permute-start | bytes 798728 | tf_op jit(solution)/shard_map/ppermute | solution.py:439

commit v3 on v2

--- a/solution.py
+++ b/solution.py
@@ -18,7 +18,10 @@
 (M_S, M_G, M_K, M_C, M_FY, M_C2, M_D2, M_1S, M_1G, M_2S, M_2G, M_3S, M_3G) = range(13)
 MESSAGE = 13
 
+GROUP = 3
+
 VMEM = pl.BlockSpec(memory_space=pltpu.VMEM)
+HBM = pl.BlockSpec(memory_space=pltpu.HBM)
 PARAMS = pltpu.CompilerParams(vmem_limit_bytes=40 * 1024 * 1024)
 
 
@@ -50,24 +53,77 @@
     return jnp.where((row >= low) & (row < high), 1.0, 0.0).astype(jnp.float32)
 
 
-def pack_kernel(temps, right, exchange, coupling, one, two):
+STRIP = ((SA, WX), (GA, WX), (K, WX), (RS, WX - 1), (RG, WX - 1), (C, WX - 1))
+STRIP_ROWS = sum(width for plane, width in STRIP)
+
+
+def pack_kernel(temps, right, exchange, coupling, one, two, pair_low, pair_high, single_low, single_high, sems):
     even = lax.axis_index("gx") % 2 == 0
-    top = exchange.shape[1]
-    parts = [(temps, 0, WX), (temps, 1, WX), (exchange, None, WX)]
-    parts += [(right, 0, WX - 1), (right, 1, WX - 1), (coupling, None, WX - 1)]
-
-    def row(y, carry):
-        at = 0
-        for ref, plane, width in parts:
-            lead = (y,) if plane is None else (plane, y)
-            low = ref[lead + (slice(0, width),)]
-            high = ref[lead + (slice(top - width, top),)]
-            one[y, at : at + width] = jnp.where(even, high, low)
-            two[y, at : at + width] = jnp.where(even, low, high)
+    ny, nx, nz = exchange.shape
+    copies = []
+    for k, ref in enumerate((temps, right, exchange, coupling)):
+        low, high, at = (pair_low, pair_high, k) if k < 2 else (single_low, single_high, k - 2)
+        lead = (slice(None),) * (ref.ndim - 2)
+        copies.append(pltpu.make_async_copy(ref.at[lead + (slice(0, 8),)], low.at[at], sems.at[2 * k]))
+        copies.append(pltpu.make_async_copy(ref.at[lead + (slice(nx - 8, nx),)], high.at[at], sems.at[2 * k + 1]))
+    for copy in copies:
+        copy.start()
+    for copy in copies:
+        copy.wait()
+    parts = [(pair_low, pair_high, (0, 0)), (pair_low, pair_high, (0, 1)), (single_low, single_high, (0,))]
+    parts += [(pair_low, pair_high, (1, 0)), (pair_low, pair_high, (1, 1)), (single_low, single_high, (1,))]
+    at = 0
+    for y in range(ny):
+        for (first, last, where), (plane, width) in zip(parts, STRIP):
+            low = first[where + (y, slice(0, width))]
+            high = last[where + (y, slice(8 - width, 8))]
+            one[at : at + width] = jnp.where(even, high, low)
+            two[at : at + width] = jnp.where(even, low, high)
             at += width
+
+
+def load_kernel(temps, right, exchange, coupling, st, sems):
+    ny, nx, nz = exchange.shape
+    planes, rows, ext, nz = st.shape
+    copies = []
+    for k, (plane, ref) in enumerate(
+        ((SA, temps.at[0]), (K, exchange), (GA, temps.at[1]), (RS, right.at[0]), (RG, right.at[1]), (C, coupling))
+    ):
+        to = st.at[plane, pl.ds(1, ny), pl.ds(PAD, nx)]
+        copies.append(pltpu.make_async_copy(ref, to, sems.at[k]))
+    for copy in copies:
+        copy.start()
+    zeros = jnp.zeros((PAD, nz), jnp.float32)
+
+    def clear(i, carry):
+        for plane, width in STRIP:
+            st[plane, i, :PAD] = zeros
+            st[plane, i, PAD + nx :] = zeros
         return carry
 
-    lax.fori_loop(0, one.shape[0], row, 0)
+    lax.fori_loop(1, ny + 1, clear, 0)
+    for copy in copies:
+        copy.wait()
+
+    def conduct(i, carry):
+        s = st[SA, i, PAD : PAD + nx]
+        st[K, i, PAD : PAD + nx] = 1.0 + 4.0 * st[K, i, PAD : PAD + nx] * s * s * s
+        return carry
+
+    lax.fori_loop(1, ny + 1, conduct, 0)
+
+
+def place_halo(st, one, two, y, nx, mask):
+    even = lax.axis_index("gx") % 2 == 0
+    at, i = y * STRIP_ROWS, y + 1
+    for plane, width in STRIP:
+        a, b = one[at : at + width], two[at : at + width]
+        st[plane, i, PAD - width : PAD] = jnp.where(even, b, a)
+        st[plane, i, PAD + nx : PAD + nx + width] = jnp.where(even, a, b)
+        at += width
+    for part in (slice(0, PAD), slice(PAD + nx, 2 * PAD + nx)):
+        s = st[SA, i, part]
+        st[K, i, part] = (1.0 + 4.0 * st[K, i, part] * s * s * s) * mask[part]
 
 
 def inner(s, g, c, h, fx, fz, edge):
@@ -109,17 +165,13 @@
     return s, g
 
 
-def faces(st, i):
-    k = st[K, i]
+def faces(k):
     lane = lanes(k.shape)
     end = k.shape[1] - 1
     fx = 0.5 * (k + up_x(k))
     fz = jnp.where(lane == end, 0.0, 0.125 * (k + up_z(k)))
     h = SOLID_CAP + jnp.where((lane == 0) | (lane == end), 0.125 * k, 0.0)
-    st[FX, i] = fx
-    st[FZ, i] = fz
-    st[H, i] = h
-    return h + (fx + down_x(fx)) + (fz + down_z(fz))
+    return fx, fz, h, h + (fx + down_x(fx)) + (fz + down_z(fz))
 
 
 def inverse(diag, c, mask):
@@ -128,63 +180,47 @@
     return inv * gas_diag, inv * c, inv * diag
 
 
-def store_inverse(st, i, diag, mask):
-    st[ASS, i], st[ASG, i], st[AGG, i] = inverse(diag, st[C, i], mask)
-
-
-def first_kernel(temps, right, exchange, coupling, one, two, st, out_one, out_two):
-    ny, nx, nz = exchange.shape
-    ext = nx + 2 * PAD
-    even = lax.axis_index("gx") % 2 == 0
+def grouped(rows, work):
+    for start in range(0, len(rows), GROUP):
+        stores = []
+        for i in rows[start : start + GROUP]:
+            stores += work(i)
+        for ref, at, value in stores:
+            ref[at] = value
+
+
+def row_coefficients(st, i, mask):
+    fx, fz, h, diag = faces(st[K, i])
+    fy = 0.5 * (st[K, i] + st[K, i + 1])
+    before = 0.5 * (st[K, i] + st[K, i - 1])
+    ss, sg, gg = inverse(diag + st[C, i] + fy + before, st[C, i], mask)
+    values = ((FX, fx), (FZ, fz), (H, h), (FY, fy), (ASS, ss), (ASG, sg), (AGG, gg))
+    return [(st, (plane, i), v) for plane, v in values]
+
+
+def row_sweep(st, i, source, target, edge):
+    s, g = relaxed(st, i, source, *row_residual(st, i, source, edge))
+    return [(st, (target, i), s), (st, (target + 1, i), g)]
+
+
+def first_kernel(st_in, one, two, st, out_one, out_two):
+    del st_in
+    planes, rows, ext, nz = st.shape
+    ny, nx = rows - 2, ext - 2 * PAD
     shape = (ext, nz)
     mask = x_mask(shape, nx)
     edge = edge_weights(shape)
-    zeros = jnp.zeros((PAD, nz), jnp.float32)
-
-    def build(y, carry):
-        i = y + 1
-        at = 0
-        for plane, own, width in (
-            (SA, temps[0, y], WX),
-            (GA, temps[1, y], WX),
-            (K, exchange[y], WX),
-            (RS, right[0, y], WX - 1),
-            (RG, right[1, y], WX - 1),
-            (C, coupling[y], WX - 1),
-        ):
-            a, b = one[y, at : at + width], two[y, at : at + width]
-            st[plane, i, :PAD] = zeros
-            st[plane, i, PAD + nx :] = zeros
-            st[plane, i, PAD - width : PAD] = jnp.where(even, b, a)
-            st[plane, i, PAD + nx : PAD + nx + width] = jnp.where(even, a, b)
-            st[plane, i, PAD : PAD + nx] = own
-            at += width
-        return carry
-
-    lax.fori_loop(0, ny, build, 0)
-
-    def conduct(y, carry):
-        s = st[SA, y + 1]
-        st[K, y + 1] = (1.0 + 4.0 * st[K, y + 1] * s * s * s) * mask
-        return carry
-
-    lax.fori_loop(0, ny, conduct, 0)
-
-    def row_diag(i):
-        diag = faces(st, i) + st[C, i]
-        st[FY, i] = 0.5 * (st[K, i] + st[K, i + 1])
-        return diag + st[FY, i] + st[FY, i - 1]
-
-    faces(st, 1)
-    faces(st, ny)
+
+    for y in list(range(4)) + list(range(ny - 4, ny)):
+        place_halo(st, one, two, y, nx, mask)
+    for i in (1, ny):
+        fx, fz, h, diag = faces(st[K, i])
+        st[FX, i], st[FZ, i], st[H, i] = fx, fz, h
     st[FY, 1] = 0.5 * (st[K, 1] + st[K, 2])
-
-    def sweep(i, carry):
-        store_inverse(st, i, row_diag(i), mask)
-        st[SB, i], st[GB, i] = relaxed(st, i, SA, *row_residual(st, i, SA, edge))
-        return carry
-
-    lax.fori_loop(2, ny, sweep, 0)
+    st[FY, ny - 3] = 0.5 * (st[K, ny - 3] + st[K, ny - 2])
+    ends = [2, 3, ny - 2, ny - 1]
+    grouped(ends, lambda i: row_coefficients(st, i, mask))
+    grouped(ends, lambda i: row_sweep(st, i, SA, SB, edge))
 
     def diag_of(i):
         fx, fz = st[FX, i], st[FZ, i]
@@ -240,8 +276,44 @@
     return v + jnp.where(row % 2 == 0, up_x(v), down_x(v))
 
 
-def second_kernel(st_in, one, two, st, extra, coarse, sides, message, before, after, squeeze):
+def coarse_coefficients(c_sum, k_sum):
+    solid = 4.0 * SOLID_CAP + c_sum + LUMP * k_sum
+    ratio = c_sum / solid
+    denominator = (4.0 * GAS_CAP + 2.0 * FLOW) + c_sum - c_sum * ratio
+    return solid, ratio, denominator
+
+
+def coarse_row(st, coarse, j, mask, edge):
+    i = 2 * j + 1
+    res_s, res_g = row_residual(st, i, SA, edge)
+    more_s, more_g = row_residual(st, i + 1, SA, edge)
+    res_s, res_g = pair_x((res_s + more_s) * mask), pair_x((res_g + more_g) * mask)
+    c_sum = pair_x(st[C, i] + st[C, i + 1])
+    solid, ratio, denominator = coarse_coefficients(c_sum, pair_x(st[K, i] + st[K, i + 1]))
+    lead = res_s / solid
+    values = (lead, ratio, (2.0 * FLOW) / denominator, (res_g + c_sum * lead) / denominator)
+    return [(coarse, (k, j), v) for k, v in enumerate(values)]
+
+
+def inner_kernel(st_in, one, two, st, coarse):
     del st_in
+    planes, rows, ext, nz = st.shape
+    ny, nx = rows - 2, ext - 2 * PAD
+    shape = (ext, nz)
+    mask = x_mask(shape, nx)
+    edge = edge_weights(shape)
+    for y in range(4, ny - 4):
+        place_halo(st, one, two, y, nx, mask)
+    grouped(list(range(4, ny - 2)), lambda i: row_coefficients(st, i, mask))
+    grouped(list(range(4, ny - 2)), lambda i: row_sweep(st, i, SA, SB, edge))
+    grouped(list(range(3, ny - 1)), lambda i: row_sweep(st, i, SB, SA, edge))
+    for j in range(2, ny // 2 - 2):
+        for ref, at, value in coarse_row(st, coarse, j, mask, edge):
+            ref[at] = value
+
+
+def second_kernel(st_in, coarse_in, one, two, st, coarse, extra, sides, message, before, after, squeeze):
+    del st_in, coarse_in
     planes, rows, ext, nz = st.shape
     ny, nx = rows - 2, ext - 2 * PAD
     shape = (ext, nz)
@@ -253,41 +325,41 @@
     edge = edge_weights(shape)
     zeros = jnp.zeros((PAD, nz), jnp.float32)
 
-    def unpack(plane, carry):
+    for plane in range(MESSAGE):
         a, b = one[plane], two[plane]
         for ref, v in ((before, jnp.where(even, b, a)), (after, jnp.where(even, a, b))):
             ref[plane, :PAD] = zeros
             ref[plane, ext - PAD :] = zeros
             ref[plane, CROP : ext - CROP] = v
-        return carry
-
-    lax.fori_loop(0, MESSAGE, unpack, 0)
 
     last = ny + 1
-    for i, ref in ((0, before), (last, after)):
+    ends = ((0, before, low), (last, after, high))
+    for i, ref, inside in ends:
         st[SA, i], st[GA, i], st[K, i], st[C, i] = ref[M_S], ref[M_G], ref[M_K], ref[M_C]
     st[FY, 0] = 0.5 * (st[K, 0] + st[K, 1])
     st[FY, ny] = 0.5 * (st[K, ny] + st[K, last])
-
-    def diag_of(i):
+    for i in (1, ny):
         fx, fz = st[FX, i], st[FZ, i]
-        return st[H, i] + (fx + down_x(fx)) + (fz + down_z(fz)) + st[C, i]
-
-    store_inverse(st, 1, diag_of(1) + st[FY, 0] + st[FY, 1], mask)
-    store_inverse(st, ny, diag_of(ny) + st[FY, ny - 1] + st[FY, ny], mask)
-    store_inverse(st, 0, faces(st, 0) + st[C, 0] + before[M_FY] + st[FY, 0], low)
-    store_inverse(st, last, faces(st, last) + st[C, last] + after[M_FY] + st[FY, ny], high)
-
-    res_s = before[M_1S] + st[FY, 0] * (st[SA, 1] - st[SA, 0])
-    res_g = before[M_1G] + CONDUCT * st[GA, 1]
-    st[SB, 0], st[GB, 0] = relaxed(st, 0, SA, res_s, res_g)
-    res_s = after[M_1S] + st[FY, ny] * (st[SA, ny] - st[SA, last])
-    res_g = after[M_1G] + (CONDUCT + FLOW) * st[GA, ny]
-    st[SB, last], st[GB, last] = relaxed(st, last, SA, res_s, res_g)
-    for i in (1, ny):
-        st[SB, i], st[GB, i] = relaxed(st, i, SA, *row_residual(st, i, SA, edge))
-
-    for i, ref, is_after, inside in ((0, before, False, low), (last, after, True, high)):
+        diag = st[H, i] + (fx + down_x(fx)) + (fz + down_z(fz)) + st[C, i] + st[FY, i - 1] + st[FY, i]
+        st[ASS, i], st[ASG, i], st[AGG, i] = inverse(diag, st[C, i], mask)
+    for i, ref, inside in ends:
+        fx, fz, h, diag = faces(st[K, i])
+        st[FX, i], st[FZ, i], st[H, i] = fx, fz, h
+        diag += st[C, i] + ref[M_FY] + st[FY, min(i, ny)]
+        st[ASS, i], st[ASG, i], st[AGG, i] = inverse(diag, st[C, i], inside)
+
+    res = before[M_1S] + st[FY, 0] * (st[SA, 1] - st[SA, 0]), before[M_1G] + CONDUCT * st[GA, 1]
+    new_low = relaxed(st, 0, SA, *res)
+    res = after[M_1S] + st[FY, ny] * (st[SA, ny] - st[SA, last]), after[M_1G] + (CONDUCT + FLOW) * st[GA, ny]
+    new_high = relaxed(st, last, SA, *res)
+    stores = row_sweep(st, 1, SA, SB, edge) + row_sweep(st, ny, SA, SB, edge)
+    st[SB, 0], st[GB, 0] = new_low
+    st[SB, last], st[GB, last] = new_high
+    for ref, at, value in stores:
+        ref[at] = value
+
+    for i, ref, inside in ends:
+        is_after = i > 0
         res = outer_residual(st, i, SB, ref[M_2S], ref[M_2G], ref[M_FY], edge, is_after)
         st[SA, i], st[GA, i] = relaxed(st, i, SB, *res)
         ss, sg, gg = inverse(jnp.maximum(ref[M_D2], SOLID_CAP), ref[M_C2], inside)
@@ -298,46 +370,28 @@
         extra[side] = ref[M_2S] + ref[M_FY] * (ss * res_s + sg * res_g)
         extra[side + 1] = ref[M_2G] + back * (sg * res_s + gg * res_g)
         extra[side + 2] = ref[M_FY]
-
-    def sweep(i, carry):
-        st[SA, i], st[GA, i] = relaxed(st, i, SB, *row_residual(st, i, SB, edge))
-        return carry
-
-    lax.fori_loop(1, ny + 1, sweep, 0)
-
-    def coefficients(c_sum, k_sum):
-        solid = 4.0 * SOLID_CAP + c_sum + LUMP * k_sum
-        ratio = c_sum / solid
-        denominator = (4.0 * GAS_CAP + 2.0 * FLOW) + c_sum - c_sum * ratio
-        return solid, ratio, denominator
-
-    def coarse_row(j, carry):
-        slopes, offsets = carry
-        i = 2 * j + 1
-        res_s, res_g = row_residual(st, i, SA, edge)
-        more_s, more_g = row_residual(st, i + 1, SA, edge)
-        res_s, res_g = pair_x((res_s + more_s) * mask), pair_x((res_g + more_g) * mask)
-        c_sum = pair_x(st[C, i] + st[C, i + 1])
-        solid, ratio, denominator = coefficients(c_sum, pair_x(st[K, i] + st[K, i + 1]))
-        lead = res_s / solid
-        slope = (2.0 * FLOW) / denominator
-        offset = (res_g + c_sum * lead) / denominator
-        slopes, offsets = slope * slopes, slope * offsets + offset
-        coarse[0, j], coarse[1, j], coarse[2, j], coarse[3, j] = lead, ratio, slopes, offsets
-        return slopes, offsets
+    grouped([1, 2, ny - 1, ny], lambda i: row_sweep(st, i, SB, SA, edge))
 
     blocks = ny // 2
-    slopes, offsets = lax.fori_loop(0, blocks, coarse_row, (jnp.ones(shape, jnp.float32), jnp.zeros(shape, jnp.float32)))
-
-    for side, (i, ref) in enumerate(((0, before), (last, after))):
+    for j in (0, 1, blocks - 2, blocks - 1):
+        for ref, at, value in coarse_row(st, coarse, j, mask, edge):
+            ref[at] = value
+    first_offset = coarse[3, 0]
+    slopes, offsets = coarse[2, 0], first_offset
+    for j in range(1, blocks):
+        slope = coarse[2, j]
+        slopes, offsets = slope * slopes, slope * offsets + coarse[3, j]
+        coarse[2, j], coarse[3, j] = slopes, offsets
+
+    for side, (i, ref, inside) in enumerate(ends):
         k2 = 2.0 * ref[M_FY] - ref[M_K]
-        solid, ratio, denominator = coefficients(pair_x(ref[M_C] + ref[M_C2]), pair_x(ref[M_K] + k2))
+        solid, ratio, denominator = coarse_coefficients(pair_x(ref[M_C] + ref[M_C2]), pair_x(ref[M_K] + k2))
         sides[side] = ratio
         if side:
             sides[2] = (2.0 * FLOW) / denominator
 
     squeeze[0], squeeze[1], squeeze[2] = slopes, offsets, coarse[0, blocks - 1]
-    squeeze[3], squeeze[4] = coarse[0, 0], coarse[3, 0]
+    squeeze[3], squeeze[4] = coarse[0, 0], first_offset
     span = nx // 2 + 2
     pick = pl.ds(PAD - 2, span, 2)
     thin = [squeeze[k, pick, :] for k in range(5)]
@@ -352,7 +406,7 @@
     lax.fori_loop(0, count, fill, 0)
 
 
-def third_kernel(st, extra, coarse, sides, got, out, sc, wide):
+def third_kernel(st, extra, coarse, sides, got, out, sc, wide, done, sems):
     planes, rows, ext, nz = st.shape
     ny, nx = rows - 2, ext - 2 * PAD
     shape = (ext, nz)
@@ -406,19 +460,36 @@
         res = outer_residual(view, i, SA, rs, rg, fy, edge, is_after)
         sc[2, i], sc[3, i] = relaxed(view, i, SA, *res)
 
-    def sweep(i, carry):
-        sc[2, i], sc[3, i] = relaxed(view, i, SA, *row_residual(view, i, SA, edge))
+    def sweep(k, carry):
+        stores = []
+        for r in range(GROUP):
+            i = GROUP * k + 1 + r
+            new_s, new_g = relaxed(view, i, SA, *row_residual(view, i, SA, edge))
+            stores += [((2, i), new_s), ((3, i), new_g)]
+        for at, value in stores:
+            sc[at] = value
         return carry
 
-    lax.fori_loop(1, ny + 1, sweep, 0)
-
-    def final(i, carry):
-        s, g = relaxed(view, i, SB, *row_residual(view, i, SB, edge))
-        out[0, i - 1] = s[PAD : PAD + nx]
-        out[1, i - 1] = g[PAD : PAD + nx]
+    lax.fori_loop(0, ny // GROUP, sweep, 0)
+
+    def leaving(k):
+        part = pl.ds(GROUP * k, GROUP)
+        return pltpu.make_async_copy(done.at[:, part], out.at[:, part], sems.at[k])
+
+    def final(k, carry):
+        stores = []
+        for r in range(GROUP):
+            i = GROUP * k + 1 + r
+            new_s, new_g = relaxed(view, i, SB, *row_residual(view, i, SB, edge))
+            stores += [((0, i - 1), new_s), ((1, i - 1), new_g)]
+        for at, value in stores:
+            done[at] = value[PAD : PAD + nx]
+        leaving(k).start()
         return carry
 
-    lax.fori_loop(1, ny + 1, final, 0)
+    lax.fori_loop(0, ny // GROUP, final, 0)
+    for k in range(ny // GROUP):
+        leaving(k).wait()
 
 
 class Fields:
@@ -429,29 +500,37 @@
         return (self.sc if at[0] <= GB else self.st)[at]
 
 
-def swap(one, two, axis):
+def swap(one, two, axis, second_first=False):
     def pairs(first):
         out = []
         for i in range(first, lax.axis_size(axis) - 1, 2):
             out += [(i, i + 1), (i + 1, i)]
         return out
 
+    if second_first:
+        two = lax.ppermute(two, axis, pairs(1))
+        return lax.ppermute(one, axis, pairs(0)), two
     return lax.ppermute(one, axis, pairs(0)), lax.ppermute(two, axis, pairs(1))
 
 
 def shards(temps, right_side, exchange, coupling):
     temps, right_side = (jnp.transpose(a, (0, 2, 1, 3)) for a in (temps, right_side))
     exchange, coupling = (jnp.transpose(a, (1, 0, 2)) for a in (exchange, coupling))
+    temps, right_side, exchange, coupling = (
+        pltpu.with_memory_space_constraint(a, pltpu.HBM) for a in (temps, right_side, exchange, coupling)
+    )
     ny, nx, nz = exchange.shape
     ext = nx + 2 * PAD
     f32 = functools.partial(jax.ShapeDtypeStruct, dtype=jnp.float32)
 
-    strip = f32((ny, 32, nz))
+    strip = f32(((ny * STRIP_ROWS + 7) // 8 * 8, nz))
+    edges = [pltpu.VMEM((2, 2, ny, 8, nz), jnp.float32)] * 2 + [pltpu.VMEM((2, ny, 8, nz), jnp.float32)] * 2
     one, two = pl.pallas_call(
         pack_kernel,
         out_shape=(strip, strip),
-        in_specs=[VMEM] * 4,
+        in_specs=[HBM] * 4,
         out_specs=(VMEM, VMEM),
+        scratch_shapes=edges + [pltpu.SemaphoreType.DMA((8,))],
         compiler_params=PARAMS,
         name="pack_x",
     )(temps, right_side, exchange, coupling)
@@ -459,37 +538,63 @@
 
     state = f32((PLANES, ny + 2, ext, nz))
     letter = f32((MESSAGE, ext - 2 * CROP, nz))
-    st, one, two = pl.pallas_call(
+    st = pl.pallas_call(
+        load_kernel,
+        out_shape=state,
+        in_specs=[HBM] * 4,
+        out_specs=VMEM,
+        scratch_shapes=[pltpu.SemaphoreType.DMA((6,))],
+        compiler_params=PARAMS,
+        name="load",
+    )(temps, right_side, exchange, coupling)
+    st, out_one, out_two = pl.pallas_call(
         first_kernel,
         out_shape=(state, letter, letter),
-        in_specs=[VMEM] * 6,
+        in_specs=[VMEM] * 3,
         out_specs=(VMEM,) * 3,
+        input_output_aliases={0: 0},
         compiler_params=PARAMS,
         name="first",
-    )(temps, right_side, exchange, coupling, one, two)
-    one, two = swap(one, two, "gy")
+    )(st, one, two)
+    y_one, y_two = swap(out_one, out_two, "gy", True)
+
+    rows = f32((4, ny // 2, ext, nz))
+    st, coarse = pl.pallas_call(
+        inner_kernel,
+        out_shape=(state, rows),
+        in_specs=[VMEM] * 3,
+        out_specs=(VMEM,) * 2,
+        input_output_aliases={0: 0},
+        compiler_params=PARAMS,
+        name="inner",
+    )(st, one, two)
 
     count = lax.axis_size("gy")
     span = nx // 2 + 2
     height = (3 * span + 7) // 8 * 8
-    st, extra, coarse, sides, message = pl.pallas_call(
+    st, coarse, extra, sides, message = pl.pallas_call(
         second_kernel,
-        out_shape=(state, f32((6, ext, nz)), f32((4, ny // 2, ext, nz)), f32((3, ext, nz)), f32((count, height, nz))),
-        in_specs=[VMEM] * 3,
+        out_shape=(state, rows, f32((6, ext, nz)), f32((3, ext, nz)), f32((count, height, nz))),
+        in_specs=[VMEM] * 4,
         out_specs=(VMEM,) * 5,
         scratch_shapes=[pltpu.VMEM((MESSAGE, ext, nz), jnp.float32)] * 2 + [pltpu.VMEM((5, ext, nz), jnp.float32)],
-        input_output_aliases={0: 0},
+        input_output_aliases={0: 0, 1: 1},
         compiler_params=PARAMS,
         name="second",
-    )(st, one, two)
+    )(st, coarse, y_one, y_two)
     got = lax.all_to_all(message, "gy", 0, 0)
 
     out = pl.pallas_call(
         third_kernel,
         out_shape=f32((2, ny, nx, nz)),
         in_specs=[VMEM] * 5,
-        out_specs=VMEM,
-        scratch_shapes=[pltpu.VMEM((4, ny + 2, ext, nz), jnp.float32), pltpu.VMEM((4, ext, nz), jnp.float32)],
+        out_specs=HBM,
+        scratch_shapes=[
+            pltpu.VMEM((4, ny + 2, ext, nz), jnp.float32),
+            pltpu.VMEM((4, ext, nz), jnp.float32),
+            pltpu.VMEM((2, ny, nx, nz), jnp.float32),
+            pltpu.SemaphoreType.DMA((ny // GROUP,)),
+        ],
         compiler_params=PARAMS,
         name="third",
     )(st, extra, coarse, sides, got)

time: 45.8 us -> 35.6 us (0.78)
  local copies, waits for them, and re-layouts: 3.84 us -> 0 us
  waiting for transfers between devices: 7.17 us -> 4.22 us
  Pallas kernels: 11.3 us -> 8.86 us
  blocking collectives: 18.8 us -> 18 us
    unnamed x8 -> x0, local copies, waits for them, and re-layouts: 3.84 us -> none
    ppermute x2 -> x1, waiting for transfers between devices: 3.99 us -> 1.04 us  [swap(): lax.ppermute(one, axis, pairs(0))]
    pallas_call x1, Pallas kernels: 4.87 us -> 2.49 us  [shards(): pl.pallas_call(third_kernel, out_shape=f32((2, ny, nx, nz)), in_specs=[VM...]
    pallas_call x1, Pallas kernels: 2.65 us -> 0.7 us  [shards(): pl.pallas_call(first_kernel, out_shape=(state, letter, letter), in_specs=...]
    pallas_call x2 -> x4, Pallas kernels: 3.79 us -> 5.68 us  [the longest x1 1.7 us: shards(): pl.pallas_call(inner_kernel, out_shape=(state, rows), in_specs=[VMEM] * 3...]
    all_to_all x1, blocking collectives: 18.8 us -> 18 us  [shards(): got = lax.all_to_all(message, 'gy', 0, 0)]
    ppermute x0 -> x2, starting transfers between devices: none -> 0.75 us  [the longest x1 0.68 us: swap(): two = lax.ppermute(two, axis, pairs(1))]
    ppermute x2 -> x1, starting transfers between devices: 2.59 us -> 1.91 us  [swap(): lax.ppermute(two, axis, pairs(1))]
  transfers between devices with their start and end apart: 4 -> 4, of which waited for: 3 -> 2; matrix products, arithmetic and copies ran while one was open for 0% -> 0% of each run, Pallas kernels for 0% -> 9%
where the time goes in v3:
time: 35.6 us; the launch traced here: 35.4 us
  blocking collectives  18 us (51%)
  Pallas kernels  8.86 us (25%)
  starting transfers between devices  4.3 us (12%)
  waiting for transfers between devices  4.22 us (12%)
    all_to_all x1, blocking collectives, shards(): got = lax.all_to_all(message, 'gy', 0, 0)  18 us
    ppermute x1, waiting for transfers between devices, swap(): lax.ppermute(two, axis, pairs(1))  3.18 us
    pallas_call x1, Pallas kernels, shards(): pl.pallas_call(third_kernel, out_shape=f32((2, ny, nx, nz)), in_specs=[VM...  2.49 us
    ppermute x1, starting transfers between devices, swap(): lax.ppermute(two, axis, pairs(1))  1.91 us
    pallas_call x1, Pallas kernels, shards(): pl.pallas_call(inner_kernel, out_shape=(state, rows), in_specs=[VMEM] * 3...  1.7 us
    ppermute x1, starting transfers between devices, swap(): lax.ppermute(one, axis, pairs(0))  1.64 us
    pallas_call x1, Pallas kernels, shards(): pl.pallas_call(load_kernel, out_shape=state, in_specs=[HBM] * 4, out_spec...  1.49 us
    pallas_call x1, Pallas kernels, shards(): pl.pallas_call(second_kernel, out_shape=(state, rows, f32((6, ext, nz)),...  1.3 us
  transfers between devices with their start and end apart: 4, of which 2 were waited for; matrix products, arithmetic and copies ran while one was open for 0% of the time, Pallas kernels for 9%

profile of v3, /device:TPU:16, one launch (start us, length us, event | category | flops | bytes accessed | tf_op | source)
XLA Modules:
  0.0 35.4 jit_solution(17420592410583734749)
XLA Ops:
  0.0 1.2 %pack_x.1 = (f32[328,128]{1,0:T(8,128)S(1)}, f32[328,128]{1,0:T(8,128)S(1)}) custom-call(f32[2,12,32,128]{3,2,1,0:T(8,128)} %bitcast.5, f32[2,12,32,128]{3,2,1,0:T(8,128)} %bitcast.7, f32[12,32,128]{2,1,0:T(8,128)} %bitcast.9, f32[12,32,128]{2,1,0:T(8,128)} %bitcast.11), custom_call_target="tpu_custom_call" | custom-call | tf_op jit(solution)/shard_map/pack_x/pallas_call | solution.py:528
  1.2 1.6 %collective-permute-start = (f32[328,128]{1,0:T(8,128)S(1)}, f32[328,128]{1,0:T(8,128)S(1)}, u32[]{:S(2)}, u32[]{:S(2)}) collective-permute-start(f32[328,128]{1,0:T(8,128)S(1)} %get-tuple-element.17), channel_id=1, source_target_pairs={{0,8},{8,0},{16,24},{24,16},{1,9},{9,1},{17,25},{25,17},{2,10},{10... | collective-permute-start | bytes 503816 | tf_op jit(solution)/shard_map/ppermute | solution.py:513
  2.8 1.9 %collective-permute-start.1 = (f32[328,128]{1,0:T(8,128)S(1)}, f32[328,128]{1,0:T(8,128)S(1)}, u32[]{:S(2)}, u32[]{:S(2)}) collective-permute-start(f32[328,128]{1,0:T(8,128)S(1)} %get-tuple-element.18), channel_id=1, source_target_pairs={{8,16},{16,8},{9,17},{17,9},{10,18},{18,10},{11,19},{19,11},{12,20... | collective-permute-start | bytes 503816 | tf_op jit(solution)/shard_map/ppermute | solution.py:513
  4.8 1.5 %load.1.st_in = f32[15,14,48,128]{3,2,1,0:T(8,128)S(1)} custom-call(f32[2,12,32,128]{3,2,1,0:T(8,128)} %bitcast.6, f32[2,12,32,128]{3,2,1,0:T(8,128)} %bitcast.8, f32[12,32,128]{2,1,0:T(8,128)} %bitcast.10, f32[12,32,128]{2,1,0:T(8,128)} %bitcast.12), custom_call_target="tpu_custom_call" | custom-call | tf_op jit(solution)/shard_map/load/pallas_call | solution.py:541
  6.2 1.0 %collective-permute-done.one = f32[328,128]{1,0:T(8,128)S(1)} collective-permute-done((f32[328,128]{1,0:T(8,128)S(1)}, f32[328,128]{1,0:T(8,128)S(1)}, u32[]{:S(2)}, u32[]{:S(2)}) %collective-permute-start) | collective-permute-done | bytes 167968 | tf_op jit(solution)/shard_map/ppermute | solution.py:513
  7.3 3.2 %collective-permute-done.1.two = f32[328,128]{1,0:T(8,128)S(1)} collective-permute-done((f32[328,128]{1,0:T(8,128)S(1)}, f32[328,128]{1,0:T(8,128)S(1)}, u32[]{:S(2)}, u32[]{:S(2)}) %collective-permute-start.1) | collective-permute-done | bytes 167968 | tf_op jit(solution)/shard_map/ppermute | solution.py:513
  10.5 0.7 %first.1 = (f32[15,14,48,128]{3,2,1,0:T(8,128)S(1)}, f32[13,40,128]{2,1,0:T(8,128)S(1)}, f32[13,40,128]{2,1,0:T(8,128)S(1)}) custom-call(f32[15,14,48,128]{3,2,1,0:T(8,128)S(1)} %load.1.st_in, f32[328,128]{1,0:T(8,128)S(1)} %collective-permute-done.one, f32[328,128]{1,0:T(8,128)S(1)} %collective-permute-done.1.two), custom_call_target="tpu_custom_call", output_to_operand_aliasing={{0}: (0, {})} | custom-call | tf_op jit(solution)/shard_map/first/pallas_call | solution.py:550
  11.2 0.1 collective-permute-start.2
  11.2 0.7 %collective-permute-start.3 = (f32[13,40,128]{2,1,0:T(8,128)S(1)}, f32[13,40,128]{2,1,0:T(8,128)S(1)}, u32[]{:S(2)}, u32[]{:S(2)}) collective-permute-start(f32[13,40,128]{2,1,0:T(8,128)S(1)} %get-tuple-element.23), channel_id=1, source_target_pairs={{1,2},{2,1},{3,4},{4,3},{5,6},{6,5},{9,10},{10,9},{11,12},{12,11},... | collective-permute-start | bytes 798728 | tf_op jit(solution)/shard_map/ppermute | solution.py:511
  11.9 1.7 %inner.1 = (f32[15,14,48,128]{3,2,1,0:T(8,128)S(1)}, f32[4,6,48,128]{3,2,1,0:T(8,128)S(1)}) custom-call(f32[15,14,48,128]{3,2,1,0:T(8,128)S(1)} %get-tuple-element.19.st_in, f32[328,128]{1,0:T(8,128)S(1)} %collective-permute-done.one, f32[328,128]{1,0:T(8,128)S(1)} %collective-permute-done.1.two), custom_call_target="tpu_custom_call", output_to_operand_aliasing={{0}: (0, {})} | custom-call | tf_op jit(solution)/shard_map/inner/pallas_call | solution.py:562
  13.6 0.0 collective-permute-done.2.one
  13.7 0.0 collective-permute-done.3.two
  13.7 1.3 %second.1 = (f32[15,14,48,128]{3,2,1,0:T(8,128)S(1)}, f32[4,6,48,128]{3,2,1,0:T(8,128)S(1)}, f32[6,48,128]{2,1,0:T(8,128)S(1)}, f32[3,48,128]{2,1,0:T(8,128)S(1)}, f32[8,56,128]{2,1,0:T(8,128)S(1)}) custom-call(f32[15,14,48,128]{3,2,1,0:T(8,128)S(1)} %get-tuple-element.20.st_in, ...), custom_call_target="tpu_custom_call", output_to_operand_aliasing={{0}: (0, {}), {1}: (1, {})} | custom-call | tf_op jit(solution)/shard_map/second/pallas_call | solution.py:575
  15.0 18.0 %all_to_all.5.got = f32[8,56,128]{2,1,0:T(8,128)S(1)} all-to-all(f32[8,56,128]{2,1,0:T(8,128)S(1)} %get-tuple-element.28), channel_id=1, replica_groups=mesh['gx'=4,'gy'=8] {'gy'}, dimensions={0} | all-to-all | bytes 458752 | tf_op jit(solution)/shard_map/all_to_all | solution.py:585
  32.9 2.5 %third.1 = f32[2,12,32,128]{3,2,1,0:T(8,128)} custom-call(f32[15,14,48,128]{3,2,1,0:T(8,128)S(1)} %get-tuple-element.24.st, f32[6,48,128]{2,1,0:T(8,128)S(1)} %get-tuple-element.25.extra, f32[4,6,48,128]{3,2,1,0:T(8,128)S(1)} %get-tuple-element.26.coarse, f32[3,48,128]{2,1,0:T(8,128)S(1)} %get-tuple-element.27.sides, f32[8,56,128]{2,1,0:T(8,128)S(1)} %all_to_all.5.got), custom_call_target="tpu_custom_call" | custom-call | tf_op jit(solution)/shard_map/third/pallas_call | solution.py:587
Async XLA Ops:
  1.2 6.1 %collective-permute-start = (f32[328,128]{1,0:T(8,128)S(1)}, f32[328,128]{1,0:T(8,128)S(1)}, u32[]{:S(2)}, u32[]{:S(2)}) collective-permute-start(f32[328,128]{1,0:T(8,128)S(1)} %get-tuple-element.17), channel_id=1, source_target_pairs={{0,8},{8,0},{16,24},{24,16},{1,9},{9,1},{17,25},{25,17},{2,10},{10... | collective-permute-start | bytes 503816 | tf_op jit(solution)/shard_map/ppermute | solution.py:513
  2.8 7.6 %collective-permute-start.1 = (f32[328,128]{1,0:T(8,128)S(1)}, f32[328,128]{1,0:T(8,128)S(1)}, u32[]{:S(2)}, u32[]{:S(2)}) collective-permute-start(f32[328,128]{1,0:T(8,128)S(1)} %get-tuple-element.18), channel_id=1, source_target_pairs={{8,16},{16,8},{9,17},{17,9},{10,18},{18,10},{11,19},{19,11},{12,20... | collective-permute-start | bytes 503816 | tf_op jit(solution)/shard_map/ppermute | solution.py:513
  11.2 2.5 %collective-permute-start.2 = (f32[13,40,128]{2,1,0:T(8,128)S(1)}, f32[13,40,128]{2,1,0:T(8,128)S(1)}, u32[]{:S(2)}, u32[]{:S(2)}) collective-permute-start(f32[13,40,128]{2,1,0:T(8,128)S(1)} %get-tuple-element.22), channel_id=1, source_target_pairs={{0,1},{1,0},{2,3},{3,2},{4,5},{5,4},{6,7},{7,6},{8,9},{9,8},{10,11... | collective-permute-start | bytes 798728 | tf_op jit(solution)/shard_map/ppermute | solution.py:512
  11.2 2.4 %collective-permute-start.3 = (f32[13,40,128]{2,1,0:T(8,128)S(1)}, f32[13,40,128]{2,1,0:T(8,128)S(1)}, u32[]{:S(2)}, u32[]{:S(2)}) collective-permute-start(f32[13,40,128]{2,1,0:T(8,128)S(1)} %get-tuple-element.23), channel_id=1, source_target_pairs={{1,2},{2,1},{3,4},{4,3},{5,6},{6,5},{9,10},{10,9},{11,12},{12,11},... | collective-permute-start | bytes 798728 | tf_op jit(solution)/shard_map/ppermute | solution.py:511

commit v4 on v3

--- a/solution.py
+++ b/solution.py
@@ -15,8 +15,9 @@
 CROP = 4
 (SA, GA, SB, GB, K, C, RS, RG, FX, FZ, H, FY, ASS, ASG, AGG) = range(15)
 PLANES = 15
-(M_S, M_G, M_K, M_C, M_FY, M_C2, M_D2, M_1S, M_1G, M_2S, M_2G, M_3S, M_3G) = range(13)
-MESSAGE = 13
+(M_S, M_G, M_K, M_C, M_FY, M_1S, M_1G, M_2S, M_2G, M_C2, M_D2, M_3S, M_3G) = range(13)
+MESSAGE, SOON = 13, 9
+(R_SLOPE, R_OFFSET, R_LAST, R_FIRST, R_FIRST_OFFSET) = range(5)
 
 GROUP = 3
 
@@ -203,7 +204,48 @@
     return [(st, (target, i), s), (st, (target + 1, i), g)]
 
 
-def first_kernel(st_in, one, two, st, out_one, out_two):
+def send_planes(st, onward, planes, edge):
+    ny, ext = st.shape[1] - 2, st.shape[2]
+    e, d, f, way = (ny, ny - 1, ny - 2, -1) if onward else (1, 2, 3, 1)
+    near, far = (d, f) if onward else (e, d)
+    from_d = CONDUCT + FLOW if onward else CONDUCT
+    fy = st[FY, near]
+    out = {M_FY: fy}
+    if M_S in planes:
+        s, g = st[SA, e], st[GA, e]
+        part_s, part_g = row_inner(st, e, SA, edge)
+        out.update({M_S: s, M_G: g, M_K: st[K, e], M_C: st[C, e]})
+        out[M_1S] = st[RS, e] + part_s + fy * (st[SA, d] - s)
+        if onward:
+            out[M_1G] = st[RG, e] + part_g + CONDUCT * st[GA, d] - FLOW * (g - st[GA, d])
+        else:
+            out[M_1G] = st[RG, e] + part_g + CONDUCT * st[GA, d] - FLOW * g
+        out[M_2S] = st[RS, e] + fy * st[SB, d]
+        out[M_2G] = st[RG, e] + from_d * st[GB, d]
+    if M_C2 in planes:
+        s, g = st[SB, d], st[GB, d]
+        part_s, part_g = row_inner(st, d, SB, edge)
+        out[M_3S] = st[RS, d] + part_s - fy * s + st[FY, far] * (st[SB, f] - s)
+        if onward:
+            out[M_3G] = st[RG, d] + part_g + CONDUCT * st[GB, f] - FLOW * (g - st[GB, f])
+        else:
+            out[M_3G] = st[RG, d] + part_g + CONDUCT * st[GB, f] - FLOW * g
+        fx, fz = st[FX, d], st[FZ, d]
+        diag = st[H, d] + (fx + down_x(fx)) + (fz + down_z(fz)) + st[C, d] + fy + st[FY, far]
+        out.update({M_C2: st[C, d], M_D2: diag})
+    return [out[plane][CROP : ext - CROP] for plane in planes]
+
+
+def write_message(ref, st, onward, planes, edge):
+    for go in (True, False):
+
+        @pl.when(onward == go)
+        def _():
+            for k, value in enumerate(send_planes(st, go, planes, edge)):
+                ref[k] = value
+
+
+def first_kernel(st_in, one, two, st, across):
     del st_in
     planes, rows, ext, nz = st.shape
     ny, nx = rows - 2, ext - 2 * PAD
@@ -221,42 +263,7 @@
     ends = [2, 3, ny - 2, ny - 1]
     grouped(ends, lambda i: row_coefficients(st, i, mask))
     grouped(ends, lambda i: row_sweep(st, i, SA, SB, edge))
-
-    def diag_of(i):
-        fx, fz = st[FX, i], st[FZ, i]
-        return st[H, i] + (fx + down_x(fx)) + (fz + down_z(fz)) + st[C, i] + st[FY, i] + st[FY, i - 1]
-
-    e, d = ny, ny - 1
-    s, g, fy = st[SA, e], st[GA, e], st[FY, d]
-    part_s, part_g = row_inner(st, e, SA, edge)
-    m1s = st[RS, e] + part_s + fy * (st[SA, d] - s)
-    m1g = st[RG, e] + part_g + CONDUCT * st[GA, d] - FLOW * (g - st[GA, d])
-    s1, g1 = st[SB, d], st[GB, d]
-    m2s = st[RS, e] + fy * s1
-    m2g = st[RG, e] + (CONDUCT + FLOW) * g1
-    part_s, part_g = row_inner(st, d, SB, edge)
-    m3s = st[RS, d] + part_s - fy * s1 + st[FY, d - 1] * (st[SB, d - 1] - s1)
-    m3g = st[RG, d] + part_g + CONDUCT * st[GB, d - 1] - FLOW * (g1 - st[GB, d - 1])
-    onward = [s, g, st[K, e], st[C, e], fy, st[C, d], diag_of(d), m1s, m1g, m2s, m2g, m3s, m3g]
-
-    e, d = 1, 2
-    s, g, fy = st[SA, e], st[GA, e], st[FY, e]
-    part_s, part_g = row_inner(st, e, SA, edge)
-    m1s = st[RS, e] + part_s + fy * (st[SA, d] - s)
-    m1g = st[RG, e] + part_g + CONDUCT * st[GA, d] - FLOW * g
-    s1, g1 = st[SB, d], st[GB, d]
-    m2s = st[RS, e] + fy * s1
-    m2g = st[RG, e] + CONDUCT * g1
-    part_s, part_g = row_inner(st, d, SB, edge)
-    m3s = st[RS, d] + part_s - fy * s1 + st[FY, d] * (st[SB, d + 1] - s1)
-    m3g = st[RG, d] + part_g + CONDUCT * st[GB, d + 1] - FLOW * g1
-    back = [s, g, st[K, e], st[C, e], fy, st[C, d], diag_of(d), m1s, m1g, m2s, m2g, m3s, m3g]
-
-    even_y = lax.axis_index("gy") % 2 == 0
-    for plane, (a, b) in enumerate(zip(onward, back)):
-        a, b = a[CROP : ext - CROP], b[CROP : ext - CROP]
-        out_one[plane] = jnp.where(even_y, a, b)
-        out_two[plane] = jnp.where(even_y, b, a)
+    write_message(across, st, lax.axis_index("gy") % 2 == 1, range(SOON), edge)
 
 
 def outer_residual(st, i, s_at, rs, rg, fy_out, edge, after):
@@ -295,7 +302,7 @@
     return [(coarse, (k, j), v) for k, v in enumerate(values)]
 
 
-def inner_kernel(st_in, one, two, st, coarse):
+def inner_kernel(st_in, one, two, st, coarse, across, beside_late, beside):
     del st_in
     planes, rows, ext, nz = st.shape
     ny, nx = rows - 2, ext - 2 * PAD
@@ -310,27 +317,35 @@
     for j in range(2, ny // 2 - 2):
         for ref, at, value in coarse_row(st, coarse, j, mask, edge):
             ref[at] = value
-
-
-def second_kernel(st_in, coarse_in, one, two, st, coarse, extra, sides, message, before, after, squeeze):
+    odd = lax.axis_index("gy") % 2 == 1
+    write_message(across, st, odd, range(SOON, MESSAGE), edge)
+    write_message(beside_late, st, ~odd, range(SOON, MESSAGE), edge)
+    write_message(beside, st, ~odd, range(SOON), edge)
+
+
+def unpack(across, beside, planes, before, after, first=0):
+    even = lax.axis_index("gy") % 2 == 0
+    ext, nz = before.shape[1:]
+    zeros = jnp.zeros((PAD, nz), jnp.float32)
+    for plane in planes:
+        a, b = beside[plane - first], across[plane - first]
+        for ref, v in ((before, jnp.where(even, b, a)), (after, jnp.where(even, a, b))):
+            ref[plane, :PAD] = zeros
+            ref[plane, ext - PAD :] = zeros
+            ref[plane, CROP : ext - CROP] = v
+
+
+def second_kernel(st_in, coarse_in, across, beside, st, coarse, message, before, after, squeeze):
     del st_in, coarse_in
     planes, rows, ext, nz = st.shape
     ny, nx = rows - 2, ext - 2 * PAD
     shape = (ext, nz)
     me, count = lax.axis_index("gy"), lax.axis_size("gy")
-    even = me % 2 == 0
     mask = x_mask(shape, nx)
     low = jnp.where(me == 0, 0.0, mask)
     high = jnp.where(me == count - 1, 0.0, mask)
     edge = edge_weights(shape)
-    zeros = jnp.zeros((PAD, nz), jnp.float32)
-
-    for plane in range(MESSAGE):
-        a, b = one[plane], two[plane]
-        for ref, v in ((before, jnp.where(even, b, a)), (after, jnp.where(even, a, b))):
-            ref[plane, :PAD] = zeros
-            ref[plane, ext - PAD :] = zeros
-            ref[plane, CROP : ext - CROP] = v
+    unpack(across, beside, range(SOON), before, after)
 
     last = ny + 1
     ends = ((0, before, low), (last, after, high))
@@ -362,14 +377,6 @@
         is_after = i > 0
         res = outer_residual(st, i, SB, ref[M_2S], ref[M_2G], ref[M_FY], edge, is_after)
         st[SA, i], st[GA, i] = relaxed(st, i, SB, *res)
-        ss, sg, gg = inverse(jnp.maximum(ref[M_D2], SOLID_CAP), ref[M_C2], inside)
-        to, back = (CONDUCT + FLOW, CONDUCT) if is_after else (CONDUCT, CONDUCT + FLOW)
-        res_s = ref[M_3S] + ref[M_FY] * st[SB, i]
-        res_g = ref[M_3G] + to * st[GB, i]
-        side = 3 if is_after else 0
-        extra[side] = ref[M_2S] + ref[M_FY] * (ss * res_s + sg * res_g)
-        extra[side + 1] = ref[M_2G] + back * (sg * res_s + gg * res_g)
-        extra[side + 2] = ref[M_FY]
     grouped([1, 2, ny - 1, ny], lambda i: row_sweep(st, i, SB, SA, edge))
 
     blocks = ny // 2
@@ -383,47 +390,145 @@
         slopes, offsets = slope * slopes, slope * offsets + coarse[3, j]
         coarse[2, j], coarse[3, j] = slopes, offsets
 
-    for side, (i, ref, inside) in enumerate(ends):
+    squeeze[R_SLOPE], squeeze[R_OFFSET], squeeze[R_LAST] = slopes, offsets, coarse[0, blocks - 1]
+    squeeze[R_FIRST], squeeze[R_FIRST_OFFSET] = coarse[0, 0], first_offset
+    span = nx // 2 + 2
+    for k in range(5):
+        message[k * span : (k + 1) * span] = squeeze[k, pl.ds(PAD - 2, span, 2), :]
+
+
+def outer_kernel(st, across, beside, across_late, beside_late, extra, sides, before, after):
+    planes, rows, ext, nz = st.shape
+    ny, nx = rows - 2, ext - 2 * PAD
+    me, count = lax.axis_index("gy"), lax.axis_size("gy")
+    mask = x_mask((ext, nz), nx)
+    unpack(across, beside, (M_K, M_C, M_FY, M_2S, M_2G), before, after)
+    unpack(across_late, beside_late, range(SOON, MESSAGE), before, after, SOON)
+    low = jnp.where(me == 0, 0.0, mask)
+    high = jnp.where(me == count - 1, 0.0, mask)
+    for i, ref, inside in ((0, before, low), (ny + 1, after, high)):
+        is_after = i > 0
+        ss, sg, gg = inverse(jnp.maximum(ref[M_D2], SOLID_CAP), ref[M_C2], inside)
+        to, back = (CONDUCT + FLOW, CONDUCT) if is_after else (CONDUCT, CONDUCT + FLOW)
+        res_s = ref[M_3S] + ref[M_FY] * st[SB, i]
+        res_g = ref[M_3G] + to * st[GB, i]
+        side = 3 if is_after else 0
+        extra[side] = ref[M_2S] + ref[M_FY] * (ss * res_s + sg * res_g)
+        extra[side + 1] = ref[M_2G] + back * (sg * res_s + gg * res_g)
+        extra[side + 2] = ref[M_FY]
         k2 = 2.0 * ref[M_FY] - ref[M_K]
         solid, ratio, denominator = coarse_coefficients(pair_x(ref[M_C] + ref[M_C2]), pair_x(ref[M_K] + k2))
-        sides[side] = ratio
-        if side:
+        sides[int(is_after)] = ratio
+        if is_after:
             sides[2] = (2.0 * FLOW) / denominator
 
-    squeeze[0], squeeze[1], squeeze[2] = slopes, offsets, coarse[0, blocks - 1]
-    squeeze[3], squeeze[4] = coarse[0, 0], first_offset
-    span = nx // 2 + 2
-    pick = pl.ds(PAD - 2, span, 2)
-    thin = [squeeze[k, pick, :] for k in range(5)]
-    blank = jnp.zeros_like(thin[0])
-
-    def fill(d, carry):
-        onward = d > me
-        for k, (a, b) in enumerate(zip(thin[:3], thin[3:] + [blank])):
-            message[d, k * span : (k + 1) * span] = jnp.where(onward, a, b)
-        return carry
-
-    lax.fori_loop(0, count, fill, 0)
-
-
-def third_kernel(st, extra, coarse, sides, got, out, sc, wide, done, sems):
+
+class Group:
+    def __init__(self, radix, stride, own, others, span):
+        self.radix, self.own, self.others, self.span = radix, own, others, span
+        me = lax.axis_index("gy")
+        self.at = lax.rem(lax.div(me, stride), radix)
+        low = lax.rem(me, stride)
+        self.lowest, self.highest = low == 0, low == stride - 1
+
+    def plane(self, ref, plane):
+        return ref[plane * self.span : (plane + 1) * self.span]
+
+    def member(self, place, plane):
+        value = None if self.own is None else self.plane(self.own, plane)
+        for k, ref in enumerate(self.others, 1):
+            got = self.plane(ref, plane)
+            value = got if value is None else jnp.where(source(self.at, k, self.radix) == place, got, value)
+        return value
+
+    def lower(self, slope, offset):
+        ahead = (jnp.ones_like(slope), jnp.zeros_like(slope))
+        for place in range(self.radix - 1):
+            a, b = self.member(place, R_SLOPE), self.member(place, R_OFFSET)
+            below = place < self.at
+            ahead = tuple(jnp.where(below, new, old) for new, old in zip((a * ahead[0], a * ahead[1] + b), ahead))
+        return slope * ahead[0], slope * ahead[1] + offset
+
+    def beside(self, leads, first, first_offset):
+        last_low, lead_high, offset_high = leads
+        for place in range(self.radix):
+            low, high = self.lowest & (self.at == place + 1), self.highest & (self.at == place - 1)
+            last_low = jnp.where(low, self.member(place, R_LAST), last_low)
+            lead_high = jnp.where(high, self.member(place, first), lead_high)
+            offset_high = jnp.where(high, self.member(place, first_offset), offset_high)
+        return last_low, lead_high, offset_high
+
+
+def source(at, k, radix):
+    if radix & (radix - 1) == 0:
+        return at ^ k
+    return (at + radix - k) % radix
+
+
+def stages(count):
+    out, rest = [2], count // 2
+    if count % 2:
+        return [1, count]
+    while rest > 1:
+        radix = next((r for r in (8, 4, 2) if rest % r == 0), rest)
+        out.append(radix)
+        rest //= radix
+    return out if len(out) > 1 else out + [1]
+
+
+def exchange_stage(messages, radix, stride):
+    count, got = lax.axis_size("gy"), []
+    for k, message in enumerate(messages, 1):
+        pairs = []
+        for me in range(count):
+            at = me // stride % radix
+            pairs.append((me + (source(at, k, radix) - at) * stride, me))
+        got.append(lax.ppermute(message, "gy", pairs))
+    return got
+
+
+def join_kernel(radix, stride, final, span, *refs):
+    own, near_in, others, (near, outs) = refs[0], refs[1], refs[2 : 1 + radix + 1], (refs[radix + 1], refs[radix + 2 :])
+    group = Group(radix, stride, own, others, span)
+    old = [group.plane(near_in, k) for k in range(5)]
+    ahead = group.lower(old[0], old[1])
+    leads = group.beside(old[2:], R_FIRST, R_FIRST_OFFSET)
+    for k, value in enumerate(ahead + leads):
+        near[k * span : (k + 1) * span] = value
+    slope, offset = group.member(0, R_SLOPE), group.member(0, R_OFFSET)
+    for place in range(1, radix):
+        a = group.member(place, R_SLOPE)
+        slope, offset = a * slope, a * offset + group.member(place, R_OFFSET)
+    total = [slope, offset, group.member(radix - 1, R_LAST), group.member(0, R_FIRST), group.member(0, R_FIRST_OFFSET)]
+    if final == 0:
+        for k, value in enumerate(total):
+            outs[0][k * span : (k + 1) * span] = value
+        return
+    at = lax.axis_index("gy") // (stride * radix)
+    for k, out in enumerate(outs, 1):
+        onward = (at ^ k) > at if final & (final - 1) == 0 else (at + k) % final > at
+        for plane, (a, b) in enumerate(zip(total[:3], total[3:] + [jnp.zeros_like(slope)])):
+            out[plane * span : (plane + 1) * span] = jnp.where(onward, a, b)
+
+
+def third_kernel(radix, stride, *refs):
+    st, extra, coarse, sides, near = refs[:5]
+    others, (out, sc, wide, done, sems) = refs[5 : 4 + radix], refs[4 + radix :]
     planes, rows, ext, nz = st.shape
     ny, nx = rows - 2, ext - 2 * PAD
-    shape = (ext, nz)
     me, count = lax.axis_index("gy"), lax.axis_size("gy")
-    edge = edge_weights(shape)
+    edge = edge_weights((ext, nz))
     span = nx // 2 + 2
     blocks = ny // 2
 
-    def fold(d, gas):
-        return got[d, :span] * gas + got[d, span : 2 * span]
-
-    gas_in = lax.fori_loop(0, me, fold, jnp.zeros((span, nz), jnp.float32))
-    inside_low, inside_high = me > 0, me < count - 1
-    prev, following = jnp.maximum(me - 1, 0), jnp.minimum(me + 1, count - 1)
-    lead_low = jnp.where(inside_low, got[prev, 2 * span : 3 * span], 0.0)
-    lead_high = jnp.where(inside_high, got[following, :span], 0.0)
-    offset_high = jnp.where(inside_high, got[following, span : 2 * span], 0.0)
+    group = Group(radix, stride, None, others, span)
+    leads = [group.plane(near, k) for k in range(2, 5)]
+    gas_in = group.plane(near, 1)
+    if radix > 1:
+        gas_in = group.lower(group.plane(near, 0), gas_in)[1]
+        leads = group.beside(leads, 0, 1)
+    inside_high = me < count - 1
+    lead_low, lead_high, offset_high = leads
     for k, v in enumerate((gas_in, lead_low, lead_high, offset_high)):
         wide[k, : PAD - 2] = jnp.zeros((PAD - 2, nz), jnp.float32)
         wide[k, ext - PAD + 2 :] = jnp.zeros((PAD - 2, nz), jnp.float32)
@@ -500,17 +605,15 @@
         return (self.sc if at[0] <= GB else self.st)[at]
 
 
-def swap(one, two, axis, second_first=False):
-    def pairs(first):
-        out = []
-        for i in range(first, lax.axis_size(axis) - 1, 2):
-            out += [(i, i + 1), (i + 1, i)]
-        return out
-
-    if second_first:
-        two = lax.ppermute(two, axis, pairs(1))
-        return lax.ppermute(one, axis, pairs(0)), two
-    return lax.ppermute(one, axis, pairs(0)), lax.ppermute(two, axis, pairs(1))
+def cost(rows, cells):
+    return pl.CostEstimate(flops=50 * rows * cells, bytes_accessed=16 * 4 * rows * cells, transcendentals=0)
+
+
+def swap(x, axis, first):
+    pairs = []
+    for i in range(first, lax.axis_size(axis) - 1, 2):
+        pairs += [(i, i + 1), (i + 1, i)]
+    return lax.ppermute(x, axis, pairs)
 
 
 def shards(temps, right_side, exchange, coupling):
@@ -534,10 +637,13 @@
         compiler_params=PARAMS,
         name="pack_x",
     )(temps, right_side, exchange, coupling)
-    one, two = swap(one, two, "gx")
+    one, two = swap(one, "gx", 0), swap(two, "gx", 1)
 
     state = f32((PLANES, ny + 2, ext, nz))
-    letter = f32((MESSAGE, ext - 2 * CROP, nz))
+
+    def letter(planes):
+        return f32((planes, ext - 2 * CROP, nz))
+
     st = pl.pallas_call(
         load_kernel,
         out_shape=state,
@@ -545,49 +651,80 @@
         out_specs=VMEM,
         scratch_shapes=[pltpu.SemaphoreType.DMA((6,))],
         compiler_params=PARAMS,
+        cost_estimate=cost(2 * ny, ext * nz),
         name="load",
     )(temps, right_side, exchange, coupling)
-    st, out_one, out_two = pl.pallas_call(
+    st, across = pl.pallas_call(
         first_kernel,
-        out_shape=(state, letter, letter),
+        out_shape=(state, letter(SOON)),
         in_specs=[VMEM] * 3,
-        out_specs=(VMEM,) * 3,
+        out_specs=(VMEM,) * 2,
         input_output_aliases={0: 0},
         compiler_params=PARAMS,
         name="first",
     )(st, one, two)
-    y_one, y_two = swap(out_one, out_two, "gy", True)
+    across = swap(across, "gy", 1)
 
     rows = f32((4, ny // 2, ext, nz))
-    st, coarse = pl.pallas_call(
+    st, coarse, late, beside_late, beside = pl.pallas_call(
         inner_kernel,
-        out_shape=(state, rows),
+        out_shape=(state, rows, letter(MESSAGE - SOON), letter(MESSAGE - SOON), letter(SOON)),
         in_specs=[VMEM] * 3,
-        out_specs=(VMEM,) * 2,
+        out_specs=(VMEM,) * 5,
         input_output_aliases={0: 0},
         compiler_params=PARAMS,
+        cost_estimate=cost(4 * ny, ext * nz),
         name="inner",
     )(st, one, two)
 
-    count = lax.axis_size("gy")
+    beside = swap(beside, "gy", 0)
+    late, beside_late = swap(late, "gy", 1), swap(beside_late, "gy", 0)
+
     span = nx // 2 + 2
-    height = (3 * span + 7) // 8 * 8
-    st, coarse, extra, sides, message = pl.pallas_call(
+    five, three = (f32(((k * span + 7) // 8 * 8, nz)) for k in (5, 3))
+    letters = [pltpu.VMEM((MESSAGE, ext, nz), jnp.float32)] * 2
+    st, coarse, total = pl.pallas_call(
         second_kernel,
-        out_shape=(state, rows, f32((6, ext, nz)), f32((3, ext, nz)), f32((count, height, nz))),
+        out_shape=(state, rows, five),
         in_specs=[VMEM] * 4,
-        out_specs=(VMEM,) * 5,
-        scratch_shapes=[pltpu.VMEM((MESSAGE, ext, nz), jnp.float32)] * 2 + [pltpu.VMEM((5, ext, nz), jnp.float32)],
+        out_specs=(VMEM,) * 3,
+        scratch_shapes=letters + [pltpu.VMEM((5, ext, nz), jnp.float32)],
         input_output_aliases={0: 0, 1: 1},
         compiler_params=PARAMS,
         name="second",
-    )(st, coarse, y_one, y_two)
-    got = lax.all_to_all(message, "gy", 0, 0)
+    )(st, coarse, across, beside)
+    extra, sides = pl.pallas_call(
+        outer_kernel,
+        out_shape=(f32((6, ext, nz)), f32((3, ext, nz))),
+        in_specs=[VMEM] * 5,
+        out_specs=(VMEM,) * 2,
+        scratch_shapes=letters,
+        compiler_params=PARAMS,
+        name="outer",
+    )(st, across, beside, late, beside_late)
+
+    near = jnp.concatenate([jnp.ones((span, nz), jnp.float32), jnp.zeros((five.shape[0] - span, nz), jnp.float32)])
+    radices, stride = stages(lax.axis_size("gy")), 1
+    for place, radix in enumerate(radices[:-1]):
+        others = exchange_stage([total] * (radix - 1), radix, stride)
+        final = radices[-1] if place == len(radices) - 2 else 0
+        outs = (three,) * (final - 1) if final else (five,)
+        near, *messages = pl.pallas_call(
+            functools.partial(join_kernel, radix, stride, final, span),
+            out_shape=(five,) + outs,
+            in_specs=[VMEM] * (1 + radix),
+            out_specs=(VMEM,) * (1 + len(outs)),
+            compiler_params=PARAMS,
+            name="join",
+        )(total, near, *others)
+        total = messages[0] if messages else total
+        stride *= radix
+    got = exchange_stage(messages, radices[-1], stride)
 
     out = pl.pallas_call(
-        third_kernel,
+        functools.partial(third_kernel, radices[-1], stride),
         out_shape=f32((2, ny, nx, nz)),
-        in_specs=[VMEM] * 5,
+        in_specs=[VMEM] * (5 + len(got)),
         out_specs=HBM,
         scratch_shapes=[
             pltpu.VMEM((4, ny + 2, ext, nz), jnp.float32),
@@ -597,7 +734,7 @@
         ],
         compiler_params=PARAMS,
         name="third",
-    )(st, extra, coarse, sides, got)
+    )(st, extra, coarse, sides, near, *got)
     return jnp.transpose(out, (0, 2, 1, 3))
 
 

time: 35.6 us -> 32.8 us (0.921)
  blocking collectives: 18 us -> 0 us
  starting transfers between devices: 4.3 us -> 14.5 us
  waiting for transfers between devices: 4.22 us -> 8.28 us
  Pallas kernels: 8.86 us -> 9.42 us
    all_to_all x1 -> x0, blocking collectives: 18 us -> none  [shards(): got = lax.all_to_all(message, 'gy', 0, 0)]
    ppermute x4 -> x10, starting transfers between devices: 4.3 us -> 14.5 us  [the longest x6 10.8 us: swap(): return lax.ppermute(x, axis, pairs)]
    ppermute x4 -> x10, waiting for transfers between devices: 4.22 us -> 8.28 us  [the longest x6 4.22 us: swap(): return lax.ppermute(x, axis, pairs)]
    pallas_call x4 -> x6, Pallas kernels: 6.19 us -> 6.74 us  [the longest x1 2.62 us: shards(): pl.pallas_call(functools.partial(third_kernel, radices[-1], stride), out_...]
  transfers between devices with their start and end apart: 4 -> 10, of which waited for: 2 -> 6; matrix products, arithmetic and copies ran while one was open for 0% -> 0% of each run, Pallas kernels for 9% -> 15%
where the time goes in v4:
time: 32.8 us; the launch traced here: 32.3 us
  starting transfers between devices  14.5 us (44%)
  Pallas kernels  9.42 us (29%)
  waiting for transfers between devices  8.28 us (25%)
    ppermute x6, starting transfers between devices, swap(): return lax.ppermute(x, axis, pairs)  10.8 us
    ppermute x6, waiting for transfers between devices, swap(): return lax.ppermute(x, axis, pairs)  4.22 us
    ppermute x4, waiting for transfers between devices, exchange_stage(): got.append(lax.ppermute(message, 'gy', pairs))  4.06 us
    ppermute x4, starting transfers between devices, exchange_stage(): got.append(lax.ppermute(message, 'gy', pairs))  3.64 us
    pallas_call x1, Pallas kernels, shards(): pl.pallas_call(functools.partial(third_kernel, radices[-1], stride), out_...  2.62 us
    pallas_call x1, Pallas kernels, shards(): pl.pallas_call(inner_kernel, out_shape=(state, rows, letter(MESSAGE - SOO...  2.08 us
    pallas_call x1, Pallas kernels, shards(): pl.pallas_call(load_kernel, out_shape=state, in_specs=[HBM] * 4, out_spec...  1.49 us
    pallas_call x1, Pallas kernels, shards(): pl.pallas_call(second_kernel, out_shape=(state, rows, five), in_specs=[VM...  1.26 us
  transfers between devices with their start and end apart: 10, of which 6 were waited for; matrix products, arithmetic and copies ran while one was open for 0% of the time, Pallas kernels for 15%

profile of v4, /device:TPU:16, one launch (start us, length us, event | category | flops | bytes accessed | tf_op | source)
XLA Modules:
  0.0 32.3 jit_solution(18087699332117370391)
XLA Ops:
  0.0 1.2 %pack_x.1 = (f32[328,128]{1,0:T(8,128)S(1)}, f32[328,128]{1,0:T(8,128)S(1)}) custom-call(f32[2,12,32,128]{3,2,1,0:T(8,128)} %bitcast.5, f32[2,12,32,128]{3,2,1,0:T(8,128)} %bitcast.7, f32[12,32,128]{2,1,0:T(8,128)} %bitcast.9, f32[12,32,128]{2,1,0:T(8,128)} %bitcast.11), custom_call_target="tpu_custom_call" | custom-call | tf_op jit(solution)/shard_map/pack_x/pallas_call | solution.py:631
  1.2 1.6 %collective-permute-start = (f32[328,128]{1,0:T(8,128)S(1)}, f32[328,128]{1,0:T(8,128)S(1)}, u32[]{:S(2)}, u32[]{:S(2)}) collective-permute-start(f32[328,128]{1,0:T(8,128)S(1)} %get-tuple-element.23), channel_id=1, source_target_pairs={{0,8},{8,0},{16,24},{24,16},{1,9},{9,1},{17,25},{25,17},{2,10},{10... | collective-permute-start | bytes 503816 | tf_op jit(solution)/shard_map/ppermute | solution.py:616
  2.8 1.9 %collective-permute-start.1 = (f32[328,128]{1,0:T(8,128)S(1)}, f32[328,128]{1,0:T(8,128)S(1)}, u32[]{:S(2)}, u32[]{:S(2)}) collective-permute-start(f32[328,128]{1,0:T(8,128)S(1)} %get-tuple-element.24), channel_id=1, source_target_pairs={{8,16},{16,8},{9,17},{17,9},{10,18},{18,10},{11,19},{19,11},{12,20... | collective-permute-start | bytes 503816 | tf_op jit(solution)/shard_map/ppermute | solution.py:616
  4.8 1.5 %load.1.st_in = f32[15,14,48,128]{3,2,1,0:T(8,128)S(1)} custom-call(f32[2,12,32,128]{3,2,1,0:T(8,128)} %bitcast.6, f32[2,12,32,128]{3,2,1,0:T(8,128)} %bitcast.8, f32[12,32,128]{2,1,0:T(8,128)} %bitcast.10, f32[12,32,128]{2,1,0:T(8,128)} %bitcast.12), custom_call_target="tpu_custom_call" | custom-call | flops 7372800 | bytes 9437184 | tf_op jit(solution)/shard_map/load/pallas_call | solution.py:647
  6.2 1.0 %collective-permute-done.one = f32[328,128]{1,0:T(8,128)S(1)} collective-permute-done((f32[328,128]{1,0:T(8,128)S(1)}, f32[328,128]{1,0:T(8,128)S(1)}, u32[]{:S(2)}, u32[]{:S(2)}) %collective-permute-start) | collective-permute-done | bytes 167968 | tf_op jit(solution)/shard_map/ppermute | solution.py:616
  7.3 3.2 %collective-permute-done.1.two = f32[328,128]{1,0:T(8,128)S(1)} collective-permute-done((f32[328,128]{1,0:T(8,128)S(1)}, f32[328,128]{1,0:T(8,128)S(1)}, u32[]{:S(2)}, u32[]{:S(2)}) %collective-permute-start.1) | collective-permute-done | bytes 167968 | tf_op jit(solution)/shard_map/ppermute | solution.py:616
  10.5 0.6 %first.1 = (f32[15,14,48,128]{3,2,1,0:T(8,128)S(1)}, f32[9,40,128]{2,1,0:T(8,128)S(1)}) custom-call(f32[15,14,48,128]{3,2,1,0:T(8,128)S(1)} %load.1.st_in, f32[328,128]{1,0:T(8,128)S(1)} %collective-permute-done.one, f32[328,128]{1,0:T(8,128)S(1)} %collective-permute-done.1.two), custom_call_target="tpu_custom_call", output_to_operand_aliasing={{0}: (0, {})} | custom-call | tf_op jit(solution)/shard_map/first/pallas_call | solution.py:657
  11.1 0.7 %collective-permute-start.2 = (f32[9,40,128]{2,1,0:T(8,128)S(1)}, f32[9,40,128]{2,1,0:T(8,128)S(1)}, u32[]{:S(2)}, u32[]{:S(2)}) collective-permute-start(f32[9,40,128]{2,1,0:T(8,128)S(1)} %get-tuple-element.28), channel_id=1, source_target_pairs={{1,2},{2,1},{3,4},{4,3},{5,6},{6,5},{9,10},{10,9},{11,12},{12,11},... | collective-permute-start | bytes 552968 | tf_op jit(solution)/shard_map/ppermute | solution.py:616
  11.8 0.0 copy-start
  11.8 2.1 %inner.1 = (f32[15,14,48,128]{3,2,1,0:T(8,128)S(1)}, f32[4,6,48,128]{3,2,1,0:T(8,128)S(1)}, f32[4,40,128]{2,1,0:T(8,128)S(1)}, f32[4,40,128]{2,1,0:T(8,128)S(1)}, f32[9,40,128]{2,1,0:T(8,128)S(1)}) custom-call(f32[15,14,48,128]{3,2,1,0:T(8,128)S(1)} %get-tuple-element.25.st_in, ...), custom_call_target="tpu_custom_call", output_to_operand_aliasing={{0}: (0, {})} | custom-call | flops 14745600 | bytes 18874368 | tf_op jit(solution)/shard_map/inner/pallas_call | solution.py:669
  13.9 3.0 %collective-permute-start.3 = (f32[9,40,128]{2,1,0:T(8,128)S(1)}, f32[9,40,128]{2,1,0:T(8,128)S(1)}, u32[]{:S(2)}, u32[]{:S(2)}) collective-permute-start(f32[9,40,128]{2,1,0:T(8,128)S(1)} %get-tuple-element.29), channel_id=1, source_target_pairs={{0,1},{1,0},{2,3},{3,2},{4,5},{5,4},{6,7},{7,6},{8,9},{9,8},{10,11... | collective-permute-start | bytes 552968 | tf_op jit(solution)/shard_map/ppermute | solution.py:616
  16.9 0.7 %collective-permute-start.4 = (f32[4,40,128]{2,1,0:T(8,128)S(1)}, f32[4,40,128]{2,1,0:T(8,128)S(1)}, u32[]{:S(2)}, u32[]{:S(2)}) collective-permute-start(f32[4,40,128]{2,1,0:T(8,128)S(1)} %get-tuple-element.31), channel_id=1, source_target_pairs={{1,2},{2,1},{3,4},{4,3},{5,6},{6,5},{9,10},{10,9},{11,12},{12,11},... | collective-permute-start | bytes 245768 | tf_op jit(solution)/shard_map/ppermute | solution.py:616
  17.6 2.9 %collective-permute-start.5 = (f32[4,40,128]{2,1,0:T(8,128)S(1)}, f32[4,40,128]{2,1,0:T(8,128)S(1)}, u32[]{:S(2)}, u32[]{:S(2)}) collective-permute-start(f32[4,40,128]{2,1,0:T(8,128)S(1)} %get-tuple-element.32), channel_id=1, source_target_pairs={{0,1},{1,0},{2,3},{3,2},{4,5},{5,4},{6,7},{7,6},{8,9},{9,8},{10,11... | collective-permute-start | bytes 245768 | tf_op jit(solution)/shard_map/ppermute | solution.py:616
  20.5 1.3 %second.1 = (f32[15,14,48,128]{3,2,1,0:T(8,128)S(1)}, f32[4,6,48,128]{3,2,1,0:T(8,128)S(1)}, f32[96,128]{1,0:T(8,128)S(1)}) custom-call(f32[15,14,48,128]{3,2,1,0:T(8,128)S(1)} %get-tuple-element.26.st_in, f32[4,6,48,128]{3,2,1,0:T(8,128)S(1)} %get-tuple-element.27.coarse_in, ...), custom_call_target="tpu_custom_call", output_to_operand_aliasing={{0}: (0, {}), {1}: (1, {})} | custom-call | tf_op jit(solution)/shard_map/second/pallas_call | solution.py:686
  21.7 0.1 collective-permute-start.6
  21.8 1.2 %collective-permute-done.6.refs_2_ = f32[96,128]{1,0:T(8,128)S(1)} collective-permute-done((f32[96,128]{1,0:T(8,128)S(1)}, f32[96,128]{1,0:T(8,128)S(1)}, u32[]{:S(2)}, u32[]{:S(2)}) %collective-permute-start.6) | collective-permute-done | bytes 49184 | tf_op jit(solution)/shard_map/ppermute | solution.py:486
  23.1 1.6 %collective-permute-start.7 = (f32[56,128]{1,0:T(8,128)S(1)}, f32[56,128]{1,0:T(8,128)S(1)}, u32[]{:S(2)}, u32[]{:S(2)}) collective-permute-start(f32[56,128]{1,0:T(8,128)S(1)} %get-tuple-element.38), channel_id=1, source_target_pairs={{2,0},{3,1},{0,2},{1,3},{6,4},{7,5},{4,6},{5,7},{10,8},{11,9},{8,1... | collective-permute-start | bytes 86024 | tf_op jit(solution)/shard_map/ppermute | solution.py:486
  24.6 0.2 collective-permute-start.8
  24.9 1.8 %collective-permute-start.9 = (f32[56,128]{1,0:T(8,128)S(1)}, f32[56,128]{1,0:T(8,128)S(1)}, u32[]{:S(2)}, u32[]{:S(2)}) collective-permute-start(f32[56,128]{1,0:T(8,128)S(1)} %get-tuple-element.40), channel_id=1, source_target_pairs={{6,0},{7,1},{4,2},{5,3},{2,4},{3,5},{0,6},{1,7},{14,8},{15,9},{12,... | collective-permute-start | bytes 86024 | tf_op jit(solution)/shard_map/ppermute | solution.py:486
  26.6 0.1 outer.1
  26.8 0.2 collective-permute-done.7.refs_5_
  27.0 1.8 %collective-permute-done.8.refs_6_ = f32[56,128]{1,0:T(8,128)S(1)} collective-permute-done((f32[56,128]{1,0:T(8,128)S(1)}, f32[56,128]{1,0:T(8,128)S(1)}, u32[]{:S(2)}, u32[]{:S(2)}) %collective-permute-start.8) | collective-permute-done | bytes 28704 | tf_op jit(solution)/shard_map/ppermute | solution.py:486
  28.8 0.9 %collective-permute-done.9.refs_7_ = f32[56,128]{1,0:T(8,128)S(1)} collective-permute-done((f32[56,128]{1,0:T(8,128)S(1)}, f32[56,128]{1,0:T(8,128)S(1)}, u32[]{:S(2)}, u32[]{:S(2)}) %collective-permute-start.9) | collective-permute-done | bytes 28704 | tf_op jit(solution)/shard_map/ppermute | solution.py:486
  29.6 2.6 %third.1 = f32[2,12,32,128]{3,2,1,0:T(8,128)} custom-call(f32[15,14,48,128]{3,2,1,0:T(8,128)S(1)} %get-tuple-element.30.st.refs_0_, f32[6,48,128]{2,1,0:T(8,128)S(1)} %get-tuple-element.33.refs_1_, f32[4,6,48,128]{3,2,1,0:T(8,128)S(1)} %get-tuple-element.34.refs_2_, f32[3,48,128]{2,1,0:T(8,128)S(1)} %get-tuple-element.35.refs_3_, ...), custom_call_target="tpu_custom_call" | custom-call | tf_op jit(solution)/shard_map/third/pallas_call | solution.py:724
  (6 shorter events, 0.1 us)
Async XLA Ops:
  1.2 6.1 %collective-permute-start = (f32[328,128]{1,0:T(8,128)S(1)}, f32[328,128]{1,0:T(8,128)S(1)}, u32[]{:S(2)}, u32[]{:S(2)}) collective-permute-start(f32[328,128]{1,0:T(8,128)S(1)} %get-tuple-element.23), channel_id=1, source_target_pairs={{0,8},{8,0},{16,24},{24,16},{1,9},{9,1},{17,25},{25,17},{2,10},{10... | collective-permute-start | bytes 503816 | tf_op jit(solution)/shard_map/ppermute | solution.py:616
  2.8 7.6 %collective-permute-start.1 = (f32[328,128]{1,0:T(8,128)S(1)}, f32[328,128]{1,0:T(8,128)S(1)}, u32[]{:S(2)}, u32[]{:S(2)}) collective-permute-start(f32[328,128]{1,0:T(8,128)S(1)} %get-tuple-element.24), channel_id=1, source_target_pairs={{8,16},{16,8},{9,17},{17,9},{10,18},{18,10},{11,19},{19,11},{12,20... | collective-permute-start | bytes 503816 | tf_op jit(solution)/shard_map/ppermute | solution.py:616
  11.1 9.4 %collective-permute-start.2 = (f32[9,40,128]{2,1,0:T(8,128)S(1)}, f32[9,40,128]{2,1,0:T(8,128)S(1)}, u32[]{:S(2)}, u32[]{:S(2)}) collective-permute-start(f32[9,40,128]{2,1,0:T(8,128)S(1)} %get-tuple-element.28), channel_id=1, source_target_pairs={{1,2},{2,1},{3,4},{4,3},{5,6},{6,5},{9,10},{10,9},{11,12},{12,11},... | collective-permute-start | bytes 552968 | tf_op jit(solution)/shard_map/ppermute | solution.py:616
  11.8 11.3 %copy-start = (f32[96,128]{1,0:T(8,128)S(1)}, f32[96,128]{1,0:T(8,128)}, u32[]{:S(2)}) copy-start(f32[96,128]{1,0:T(8,128)} %constant.0.clone.1.refs_1_) | copy-start | bytes 147460
  13.9 6.6 %collective-permute-start.3 = (f32[9,40,128]{2,1,0:T(8,128)S(1)}, f32[9,40,128]{2,1,0:T(8,128)S(1)}, u32[]{:S(2)}, u32[]{:S(2)}) collective-permute-start(f32[9,40,128]{2,1,0:T(8,128)S(1)} %get-tuple-element.29), channel_id=1, source_target_pairs={{0,1},{1,0},{2,3},{3,2},{4,5},{5,4},{6,7},{7,6},{8,9},{9,8},{10,11... | collective-permute-start | bytes 552968 | tf_op jit(solution)/shard_map/ppermute | solution.py:616
  16.9 9.7 %collective-permute-start.4 = (f32[4,40,128]{2,1,0:T(8,128)S(1)}, f32[4,40,128]{2,1,0:T(8,128)S(1)}, u32[]{:S(2)}, u32[]{:S(2)}) collective-permute-start(f32[4,40,128]{2,1,0:T(8,128)S(1)} %get-tuple-element.31), channel_id=1, source_target_pairs={{1,2},{2,1},{3,4},{4,3},{5,6},{6,5},{9,10},{10,9},{11,12},{12,11},... | collective-permute-start | bytes 245768 | tf_op jit(solution)/shard_map/ppermute | solution.py:616
  17.6 9.1 %collective-permute-start.5 = (f32[4,40,128]{2,1,0:T(8,128)S(1)}, f32[4,40,128]{2,1,0:T(8,128)S(1)}, u32[]{:S(2)}, u32[]{:S(2)}) collective-permute-start(f32[4,40,128]{2,1,0:T(8,128)S(1)} %get-tuple-element.32), channel_id=1, source_target_pairs={{0,1},{1,0},{2,3},{3,2},{4,5},{5,4},{6,7},{7,6},{8,9},{9,8},{10,11... | collective-permute-start | bytes 245768 | tf_op jit(solution)/shard_map/ppermute | solution.py:616
  21.7 1.3 %collective-permute-start.6 = (f32[96,128]{1,0:T(8,128)S(1)}, f32[96,128]{1,0:T(8,128)S(1)}, u32[]{:S(2)}, u32[]{:S(2)}) collective-permute-start(f32[96,128]{1,0:T(8,128)S(1)} %get-tuple-element.36.refs_0_), channel_id=1, source_target_pairs={{1,0},{0,1},{3,2},{2,3},{5,4},{4,5},{7,6},{6,7},{9,8},{8,9},{11,10... | collective-permute-start | bytes 147464 | tf_op jit(solution)/shard_map/ppermute | solution.py:486
  23.1 3.9 %collective-permute-start.7 = (f32[56,128]{1,0:T(8,128)S(1)}, f32[56,128]{1,0:T(8,128)S(1)}, u32[]{:S(2)}, u32[]{:S(2)}) collective-permute-start(f32[56,128]{1,0:T(8,128)S(1)} %get-tuple-element.38), channel_id=1, source_target_pairs={{2,0},{3,1},{0,2},{1,3},{6,4},{7,5},{4,6},{5,7},{10,8},{11,9},{8,1... | collective-permute-start | bytes 86024 | tf_op jit(solution)/shard_map/ppermute | solution.py:486
  24.6 4.1 %collective-permute-start.8 = (f32[56,128]{1,0:T(8,128)S(1)}, f32[56,128]{1,0:T(8,128)S(1)}, u32[]{:S(2)}, u32[]{:S(2)}) collective-permute-start(f32[56,128]{1,0:T(8,128)S(1)} %get-tuple-element.39), channel_id=1, source_target_pairs={{4,0},{5,1},{6,2},{7,3},{0,4},{1,5},{2,6},{3,7},{12,8},{13,9},{14,... | collective-permute-start | bytes 86024 | tf_op jit(solution)/shard_map/ppermute | solution.py:486
  24.9 4.8 %collective-permute-start.9 = (f32[56,128]{1,0:T(8,128)S(1)}, f32[56,128]{1,0:T(8,128)S(1)}, u32[]{:S(2)}, u32[]{:S(2)}) collective-permute-start(f32[56,128]{1,0:T(8,128)S(1)} %get-tuple-element.40), channel_id=1, source_target_pairs={{6,0},{7,1},{4,2},{5,3},{2,4},{3,5},{0,6},{1,7},{14,8},{15,9},{12,... | collective-permute-start | bytes 86024 | tf_op jit(solution)/shard_map/ppermute | solution.py:486

commit v5 on v3

v5 whole, which is shorter than its diff:
```python
import functools

import jax
import jax.numpy as jnp
from jax import lax
from jax.experimental import pallas as pl
from jax.experimental.pallas import tpu as pltpu
from jax.sharding import PartitionSpec as P

SOLID_CAP, GAS_CAP, FLOW, CONDUCT, RELAX, LUMP = 0.5, 0.02, 40.0, 0.05, 0.8, 0.25
GAS_SELF = GAS_CAP + 4.5 * CONDUCT

PAD = 8
WX = 5
CROP = 4
(SA, GA, SB, GB, K, C, RS, RG, FX, FZ, H, FY, ASS, ASG, AGG) = range(15)
PLANES = 15
(M_S, M_G, M_K, M_C, M_FY, M_1S, M_1G, M_2S, M_2G) = range(9)
MESSAGE, EARLY = 9, 5

GROUP = 3

VMEM = pl.BlockSpec(memory_space=pltpu.VMEM)
HBM = pl.BlockSpec(memory_space=pltpu.HBM)
PARAMS = pltpu.CompilerParams(vmem_limit_bytes=40 * 1024 * 1024)


def up_x(v):
    return pltpu.roll(v, v.shape[0] - 1, 0)


def down_x(v):
    return pltpu.roll(v, 1, 0)


def up_z(v):
    return pltpu.roll(v, v.shape[1] - 1, 1)


def down_z(v):
    return pltpu.roll(v, 1, 1)


def lanes(shape):
    return lax.broadcasted_iota(jnp.int32, shape, 1)


def x_mask(shape, nx):
    row = lax.broadcasted_iota(jnp.int32, shape, 0)
    place, count = lax.axis_index("gx"), lax.axis_size("gx")
    low = jnp.where(place == 0, PAD, PAD - WX)
    high = jnp.where(place == count - 1, PAD + nx, PAD + nx + WX)
    return jnp.where((row >= low) & (row < high), 1.0, 0.0).astype(jnp.float32)


STRIP = ((SA, WX - 1), (GA, WX - 1), (K, WX), (RS, WX - 1), (RG, WX - 1), (C, WX - 1))
STRIP_ROWS = sum(width for plane, width in STRIP)


def conductivity_of(s, exchange):
    return 1.0 + 4.0 * exchange * s * s * s


def strip_values(s, g, k, rs, rg, c, low):
    out, inn = (WX - 1, WX - 2) if low else (8 - WX, 9 - WX)
    four = slice(0, WX - 1) if low else slice(9 - WX, 8)
    five = slice(0, WX) if low else slice(8 - WX, 8)
    row = lax.broadcasted_iota(jnp.int32, s.shape, 0)
    rs = rs + jnp.where(row == inn, 0.5 * (k[inn : inn + 1] + k[out : out + 1]) * s[out : out + 1], 0.0)
    rg = rg + jnp.where(row == inn, CONDUCT * g[out : out + 1], 0.0)
    return [s[four], g[four], k[five], rs[four], rg[four], c[four]]


def pack_kernel(temps, right, exchange, coupling, one, two, early, *scratch):
    pair_low, pair_high, single_low, single_high, rows_t, rows_e, rows_c, sems = scratch
    even = lax.axis_index("gx") % 2 == 0
    odd = lax.axis_index("gy") % 2 == 1
    ny, nx, nz = exchange.shape
    copies = []
    for k, ref in enumerate((temps, right, exchange, coupling)):
        low, high, at = (pair_low, pair_high, k) if k < 2 else (single_low, single_high, k - 2)
        lead = (slice(None),) * (ref.ndim - 2)
        copies.append(pltpu.make_async_copy(ref.at[lead + (slice(0, 8),)], low.at[at], sems.at[2 * k]))
        copies.append(pltpu.make_async_copy(ref.at[lead + (slice(nx - 8, nx),)], high.at[at], sems.at[2 * k + 1]))
    ends = pl.ds(jnp.where(odd, ny - 2, 0), 2)
    copies.append(pltpu.make_async_copy(temps.at[:, ends], rows_t, sems.at[8]))
    copies.append(pltpu.make_async_copy(exchange.at[ends], rows_e, sems.at[9]))
    copies.append(pltpu.make_async_copy(coupling.at[ends], rows_c, sems.at[10]))
    for copy in copies:
        copy.start()
    for copy in copies:
        copy.wait()
    at = 0
    for y in range(ny):
        sides = []
        for pair, single, is_low in ((pair_low, single_low, True), (pair_high, single_high, False)):
            s, g, rs, rg = (pair[i, j, y] for i in range(2) for j in range(2))
            sides.append(strip_values(s, g, conductivity_of(s, single[0, y]), rs, rg, single[1, y], is_low))
        for low, high, (plane, width) in zip(*sides, STRIP):
            one[at : at + width] = jnp.where(even, high, low)
            two[at : at + width] = jnp.where(even, low, high)
            at += width
    k = [conductivity_of(rows_t[0, i], rows_e[i]) for i in range(2)]
    pick = lambda pair: jnp.where(odd, pair[1], pair[0])
    early[M_S], early[M_G] = pick([rows_t[0, i] for i in range(2)]), pick([rows_t[1, i] for i in range(2)])
    early[M_K], early[M_C], early[M_FY] = pick(k), pick([rows_c[i] for i in range(2)]), 0.5 * (k[0] + k[1])


def load_kernel(temps, right, exchange, coupling, st, sems):
    ny, nx, nz = exchange.shape
    planes, rows, ext, nz = st.shape
    copies = []
    for k, (plane, ref) in enumerate(
        ((SA, temps.at[0]), (K, exchange), (GA, temps.at[1]), (RS, right.at[0]), (RG, right.at[1]), (C, coupling))
    ):
        to = st.at[plane, pl.ds(1, ny), pl.ds(PAD, nx)]
        copies.append(pltpu.make_async_copy(ref, to, sems.at[k]))
    for copy in copies:
        copy.start()
    zeros = jnp.zeros((PAD, nz), jnp.float32)

    def clear(i, carry):
        for plane, width in STRIP:
            st[plane, i, :PAD] = zeros
            st[plane, i, PAD + nx :] = zeros
        return carry

    lax.fori_loop(1, ny + 1, clear, 0)
    for copy in copies:
        copy.wait()

    def conduct(i, carry):
        s = st[SA, i, PAD : PAD + nx]
        st[K, i, PAD : PAD + nx] = conductivity_of(s, st[K, i, PAD : PAD + nx])
        return carry

    lax.fori_loop(1, ny + 1, conduct, 0)


def place_halo(st, one, two, y, nx):
    even = lax.axis_index("gx") % 2 == 0
    at, i = y * STRIP_ROWS, y + 1
    for plane, width in STRIP:
        a, b = one[at : at + width], two[at : at + width]
        st[plane, i, PAD - width : PAD] = jnp.where(even, b, a)
        st[plane, i, PAD + nx : PAD + nx + width] = jnp.where(even, a, b)
        at += width


def inner(s, g, c, h, fx, fz, edge):
    t = c * (s - g)
    flux_x = fx * (up_x(s) - s)
    flux_z = fz * (up_z(s) - s)
    part_s = (flux_x - down_x(flux_x)) + (flux_z - down_z(flux_z)) - h * s - t
    part_g = (
        t
        - GAS_SELF * g
        + CONDUCT * (up_x(g) + down_x(g))
        + edge[0] * up_z(g)
        + edge[1] * down_z(g)
    )
    return part_s, part_g


def edge_weights(shape):
    lane = lanes(shape)
    weight = jnp.float32(0.25 * CONDUCT)
    return jnp.where(lane == shape[1] - 1, 0.0, weight), jnp.where(lane == 0, 0.0, weight)


def row_inner(st, i, s_at, edge):
    return inner(st[s_at, i], st[s_at + 1, i], st[C, i], st[H, i], st[FX, i], st[FZ, i], edge)


def row_residual(st, i, s_at, edge):
    part_s, part_g = row_inner(st, i, s_at, edge)
    s, g, before = st[s_at, i], st[s_at + 1, i], st[s_at + 1, i - 1]
    part_s += st[FY, i] * (st[s_at, i + 1] - s) + st[FY, i - 1] * (st[s_at, i - 1] - s)
    part_g += CONDUCT * (st[s_at + 1, i + 1] + before) - FLOW * (g - before)
    return st[RS, i] + part_s, st[RG, i] + part_g


def relaxed(st, i, s_at, res_s, res_g):
    s = st[s_at, i] + st[ASS, i] * res_s + st[ASG, i] * res_g
    g = st[s_at + 1, i] + st[ASG, i] * res_s + st[AGG, i] * res_g
    return s, g


def faces(k):
    lane = lanes(k.shape)
    end = k.shape[1] - 1
    fx = 0.5 * (k + up_x(k))
    fz = jnp.where(lane == end, 0.0, 0.125 * (k + up_z(k)))
    h = SOLID_CAP + jnp.where((lane == 0) | (lane == end), 0.125 * k, 0.0)
    return fx, fz, h, h + (fx + down_x(fx)) + (fz + down_z(fz))


def inverse(diag, c, mask):
    gas_diag = (GAS_SELF + FLOW) + c
    inv = (RELAX * mask) / (diag * gas_diag - c * c)
    return inv * gas_diag, inv * c, inv * diag


def last_relaxed(st, i, s_at, edge, own):
    full_s, full_g = st[s_at, i], st[s_at + 1, i]
    s, g = full_s[own], full_g[own]
    flux_x = st[FX, i] * (up_x(full_s) - full_s)
    flux_z = st[FZ, i, own] * (up_z(s) - s)
    c, before = st[C, i, own], st[s_at + 1, i - 1, own]
    t = c * (s - g)
    res_s = st[RS, i, own] + (flux_x[own] - down_x(flux_x)[own]) + (flux_z - down_z(flux_z)) - st[H, i, own] * s - t
    res_s += st[FY, i, own] * (st[s_at, i + 1, own] - s) + st[FY, i - 1, own] * (st[s_at, i - 1, own] - s)
    res_g = st[RG, i, own] + t - GAS_SELF * g + edge[0][own] * up_z(g) + edge[1][own] * down_z(g)
    res_g += CONDUCT * (up_x(full_g)[own] + down_x(full_g)[own] + st[s_at + 1, i + 1, own] + before) - FLOW * (g - before)
    ss, sg, gg = st[ASS, i, own], st[ASG, i, own], st[AGG, i, own]
    return s + ss * res_s + sg * res_g, g + sg * res_s + gg * res_g


def grouped(rows, work):
    for start in range(0, len(rows), GROUP):
        stores = []
        for i in rows[start : start + GROUP]:
            stores += work(i)
        for ref, at, value in stores:
            ref[at] = value


def row_coefficients(st, i, mask):
    fx, fz, h, diag = faces(st[K, i])
    fy = 0.5 * (st[K, i] + st[K, i + 1])
    before = 0.5 * (st[K, i] + st[K, i - 1])
    ss, sg, gg = inverse(diag + st[C, i] + fy + before, st[C, i], mask)
    values = ((FX, fx), (FZ, fz), (H, h), (FY, fy), (ASS, ss), (ASG, sg), (AGG, gg))
    return [(st, (plane, i), v) for plane, v in values]


def row_sweep(st, i, source, target, edge):
    s, g = relaxed(st, i, source, *row_residual(st, i, source, edge))
    return [(st, (target, i), s), (st, (target + 1, i), g)]


def send_planes(st, onward, edge):
    ny = st.shape[1] - 2
    e, d, near = (ny, ny - 1, ny - 1) if onward else (1, 2, 1)
    fy, s, g, g_d = st[FY, near], st[SA, e], st[GA, e], st[GA, d]
    part_s, part_g = row_inner(st, e, SA, edge)
    m_1s = st[RS, e] + part_s + fy * (st[SA, d] - s)
    m_1g = st[RG, e] + part_g + CONDUCT * g_d - FLOW * (g - g_d if onward else g)
    m_2s = st[RS, e] + fy * st[SB, d]
    m_2g = st[RG, e] + (CONDUCT + FLOW if onward else CONDUCT) * st[GB, d]
    return [s, g, st[K, e], st[C, e], fy, m_1s, m_1g, m_2s, m_2g]


def write_across(ref, st, onward, edge):
    ext = st.shape[2]
    for k, value in enumerate(send_planes(st, onward, edge)):
        if k >= EARLY:
            ref[k - EARLY] = value[CROP : ext - CROP]
        else:
            ref[MESSAGE - EARLY, 8 * k : 8 * k + 4] = value[CROP:PAD]
            ref[MESSAGE - EARLY, 8 * k + 4 : 8 * k + 8] = value[ext - PAD : ext - CROP]


def write_beside(refs, st, onward, edge):
    ext = st.shape[2]
    for k, value in enumerate(send_planes(st, onward, edge)):
        ref, at = (refs[0], k) if k < EARLY else (refs[1], k - EARLY)
        ref[at] = value[CROP : ext - CROP]


def write_message(write, ref, st, onward, edge):
    for go in (True, False):

        @pl.when(onward == go)
        def _():
            write(ref, st, go, edge)


def first_kernel(st_in, one, two, early, st, across):
    del st_in, early
    planes, rows, ext, nz = st.shape
    ny, nx = rows - 2, ext - 2 * PAD
    shape = (ext, nz)
    mask = x_mask(shape, nx)
    edge = edge_weights(shape)

    for y in list(range(4)) + list(range(ny - 4, ny)):
        place_halo(st, one, two, y, nx)
    for i in (1, ny):
        fx, fz, h, diag = faces(st[K, i])
        st[FX, i], st[FZ, i], st[H, i] = fx, fz, h
    st[FY, 1] = 0.5 * (st[K, 1] + st[K, 2])
    st[FY, ny - 3] = 0.5 * (st[K, ny - 3] + st[K, ny - 2])
    ends = [2, 3, ny - 2, ny - 1]
    grouped(ends, lambda i: row_coefficients(st, i, mask))
    grouped(ends, lambda i: row_sweep(st, i, SA, SB, edge))
    write_message(write_across, across, st, lax.axis_index("gy") % 2 == 1, edge)


def outer_residual(st, i, s_at, rs, rg, fy_out, edge, after):
    part_s, part_g = row_inner(st, i, s_at, edge)
    s, g = st[s_at, i], st[s_at + 1, i]
    if after:
        part_s += st[FY, i - 1] * (st[s_at, i - 1] - s)
        part_g += (CONDUCT + FLOW) * st[s_at + 1, i - 1]
    else:
        part_s += st[FY, i] * (st[s_at, i + 1] - s)
        part_g += CONDUCT * st[s_at + 1, i + 1]
    return rs + part_s - fy_out * s, rg + part_g - FLOW * g


def pair_x(v):
    row = lax.broadcasted_iota(jnp.int32, v.shape, 0)
    return v + jnp.where(row % 2 == 0, up_x(v), down_x(v))


def coarse_coefficients(c_sum, k_sum):
    solid = 4.0 * SOLID_CAP + c_sum + LUMP * k_sum
    ratio = c_sum / solid
    denominator = (4.0 * GAS_CAP + 2.0 * FLOW) + c_sum - c_sum * ratio
    return solid, ratio, denominator


def coarse_row(st, coarse, j, mask, edge):
    i = 2 * j + 1
    res_s, res_g = row_residual(st, i, SA, edge)
    more_s, more_g = row_residual(st, i + 1, SA, edge)
    res_s, res_g = pair_x((res_s + more_s) * mask), pair_x((res_g + more_g) * mask)
    c_sum = pair_x(st[C, i] + st[C, i + 1])
    solid, ratio, denominator = coarse_coefficients(c_sum, pair_x(st[K, i] + st[K, i + 1]))
    lead = res_s / solid
    values = (lead, ratio, (2.0 * FLOW) / denominator, (res_g + c_sum * lead) / denominator)
    return [(coarse, (k, j), v) for k, v in enumerate(values)]


def inner_kernel(st_in, one, two, st, coarse, beside_a, beside_b):
    del st_in
    planes, rows, ext, nz = st.shape
    ny, nx = rows - 2, ext - 2 * PAD
    shape = (ext, nz)
    mask = x_mask(shape, nx)
    edge = edge_weights(shape)
    for y in range(4, ny - 4):
        place_halo(st, one, two, y, nx)
    grouped(list(range(4, ny - 2)), lambda i: row_coefficients(st, i, mask))
    grouped(list(range(4, ny - 2)), lambda i: row_sweep(st, i, SA, SB, edge))
    grouped(list(range(3, ny - 1)), lambda i: row_sweep(st, i, SB, SA, edge))
    for j in range(2, ny // 2 - 2):
        for ref, at, value in coarse_row(st, coarse, j, mask, edge):
            ref[at] = value
    write_message(write_beside, (beside_a, beside_b), st, lax.axis_index("gy") % 2 == 0, edge)


def unpack(early, across, beside_a, beside_b, before, after):
    even = lax.axis_index("gy") % 2 == 0
    ext, nz = before.shape[1:]
    zeros = jnp.zeros((PAD, nz), jnp.float32)

    def fill(far, near):
        for k in range(MESSAGE):
            for ref in (far, near):
                ref[k, :PAD] = zeros
                ref[k, ext - PAD :] = zeros
            near[k, CROP : ext - CROP] = beside_a[k] if k < EARLY else beside_b[k - EARLY]
            if k >= EARLY:
                far[k, CROP : ext - CROP] = across[k - EARLY]
            else:
                far[k, PAD : ext - PAD] = early[k]
                far[k, CROP:PAD] = across[MESSAGE - EARLY, 8 * k : 8 * k + 4]
                far[k, ext - PAD : ext - CROP] = across[MESSAGE - EARLY, 8 * k + 4 : 8 * k + 8]

    for is_even, far, near in ((True, before, after), (False, after, before)):

        @pl.when(even == is_even)
        def _():
            fill(far, near)


def second_kernel(st_in, coarse_in, early, across, beside_a, beside_b, st, coarse, extra, total, last_info, first_info, message, before, after, squeeze):
    del st_in, coarse_in
    planes, rows, ext, nz = st.shape
    ny, nx = rows - 2, ext - 2 * PAD
    shape = (ext, nz)
    me, count = lax.axis_index("gy"), lax.axis_size("gy")
    mask = x_mask(shape, nx)
    low = jnp.where(me == 0, 0.0, mask)
    high = jnp.where(me == count - 1, 0.0, mask)
    edge = edge_weights(shape)
    unpack(early, across, beside_a, beside_b, before, after)

    last = ny + 1
    ends = ((0, before, low), (last, after, high))
    for i, ref, inside in ends:
        st[SA, i], st[GA, i], st[K, i], st[C, i] = ref[M_S], ref[M_G], ref[M_K], ref[M_C]
    st[FY, 0] = 0.5 * (st[K, 0] + st[K, 1])
    st[FY, ny] = 0.5 * (st[K, ny] + st[K, last])
    for i in (1, ny):
        fx, fz = st[FX, i], st[FZ, i]
        diag = st[H, i] + (fx + down_x(fx)) + (fz + down_z(fz)) + st[C, i] + st[FY, i - 1] + st[FY, i]
        st[ASS, i], st[ASG, i], st[AGG, i] = inverse(diag, st[C, i], mask)
    for i, ref, inside in ends:
        fx, fz, h, diag = faces(st[K, i])
        st[FX, i], st[FZ, i], st[H, i] = fx, fz, h
        diag += st[C, i] + ref[M_FY] + st[FY, min(i, ny)]
        st[ASS, i], st[ASG, i], st[AGG, i] = inverse(diag, st[C, i], inside)

    res = before[M_1S] + st[FY, 0] * (st[SA, 1] - st[SA, 0]), before[M_1G] + CONDUCT * st[GA, 1]
    new_low = relaxed(st, 0, SA, *res)
    res = after[M_1S] + st[FY, ny] * (st[SA, ny] - st[SA, last]), after[M_1G] + (CONDUCT + FLOW) * st[GA, ny]
    new_high = relaxed(st, last, SA, *res)
    stores = row_sweep(st, 1, SA, SB, edge) + row_sweep(st, ny, SA, SB, edge)
    st[SB, 0], st[GB, 0] = new_low
    st[SB, last], st[GB, last] = new_high
    for ref, at, value in stores:
        ref[at] = value

    for i, ref, inside in ends:
        is_after = i > 0
        res = outer_residual(st, i, SB, ref[M_2S], ref[M_2G], ref[M_FY], edge, is_after)
        st[SA, i], st[GA, i] = relaxed(st, i, SB, *res)
    grouped([1, 2, ny - 1, ny], lambda i: row_sweep(st, i, SB, SA, edge))

    for i, ref, inside in ends:
        for k, plane in enumerate((M_2S, M_2G, M_FY)):
            extra[(3 if i else 0) + k] = ref[plane]

    blocks = ny // 2
    for j in (0, 1, blocks - 2, blocks - 1):
        for ref, at, value in coarse_row(st, coarse, j, mask, edge):
            ref[at] = value
    for k in range(4):
        squeeze[k] = coarse[k, 0]
    slopes, offsets = coarse[2, 0], coarse[3, 0]
    for j in range(1, blocks):
        slope = coarse[2, j]
        slopes, offsets = slope * slopes, slope * offsets + coarse[3, j]
        coarse[2, j], coarse[3, j] = slopes, offsets
    squeeze[4], squeeze[5], squeeze[6], squeeze[7] = slopes, offsets, coarse[0, blocks - 1], coarse[1, blocks - 1]

    span = nx // 2 + 2
    lead, ratio, slope, offset, slopes, offsets, lead_last, ratio_last = (
        squeeze[k, pl.ds(PAD - 2, span, 2), :] for k in range(8)
    )
    part = slice(PAD - 1, PAD + nx + 1)

    def increments(d, face, gas):
        return [(st[FY, face] * (st[SA, d] - st[SB, d]))[part], (gas * (st[GA, d] - st[GB, d]))[part]]

    onward = [lead_last, ratio_last] + increments(ny - 1, ny - 1, CONDUCT + FLOW)
    back = [lead, offset] + increments(2, 1, CONDUCT) + [slope, ratio]
    write_rows(total, [slopes, offsets])
    write_rows(last_info, onward)
    write_rows(first_info, back)
    for go, info in ((True, onward), (False, back)):

        @pl.when((me % 2 == 0) == go)
        def _():
            write_rows(message, [slopes, offsets] + info)


def write_rows(ref, values):
    at = 0
    for value in values:
        ref[at : at + value.shape[0]] = value
        at += value.shape[0]


class Rows:
    def __init__(self, nx):
        self.span = nx // 2 + 2
        self.map = 2 * self.span
        self.info = self.map + 2 * (nx + 2)
        self.rest = self.map
        self.final = self.map + self.info
        self.full = self.final + self.rest
        self.low = self.map
        self.high = self.low + self.info
        self.near = self.high + self.info + self.rest


def source(at, k, radix):
    if radix & (radix - 1) == 0:
        return at ^ k
    return (at + radix - k) % radix


def target(at, k, radix):
    return at ^ k if radix & (radix - 1) == 0 else (at + k) % radix


def order(radix):
    out = [(k, any(abs(source(at, k, radix) - at) == 1 for at in range(radix))) for k in range(1, radix)]
    return sorted(out, key=lambda item: (not item[1], -item[0]))


def stages(count):
    if count % 2:
        return [1, count]
    out, rest = [2], count // 2
    while rest > 1:
        radix = next((r for r in (8, 4, 2) if rest % r == 0), rest)
        out.append(radix)
        rest //= radix
    return out if len(out) > 1 else out + [1]


def exchange_stage(messages, radix, stride):
    count, got = lax.axis_size("gy"), []
    for (k, near), message in zip(order(radix), messages):
        pairs = []
        for me in range(count):
            at, low = me // stride % radix, me % stride
            sender = me - low + (source(at, k, radix) - at) * stride + (stride - 1 - low)
            pairs.append((sender, me))
        got.append(lax.ppermute(message, "gy", pairs))
    return got


class Group:
    def __init__(self, radix, stride, others, nx):
        self.radix, self.others, self.nx = radix, others, nx
        me = lax.axis_index("gy")
        self.at = lax.rem(lax.div(me, stride), radix)
        low = lax.rem(me, stride)
        self.lowest, self.highest = low == 0, low == stride - 1

    def map_of(self, place, own):
        rows = Rows(self.nx)
        out = own
        for (k, near), ref in zip(order(self.radix), self.others):
            here = source(self.at, k, self.radix) == place
            got = [ref[i * rows.span : (i + 1) * rows.span] for i in range(2)]
            out = got if out is None else [jnp.where(here, new, old) for new, old in zip(got, out)]
        return out

    def ahead(self, slope, offset):
        a, b = jnp.ones_like(slope), jnp.zeros_like(slope)
        for place in range(self.radix - 1):
            new_a, new_b = self.map_of(place, None)
            below = place < self.at
            a, b = jnp.where(below, new_a * a, a), jnp.where(below, new_a * b + new_b, b)
        return slope * a, slope * b + offset

    def total(self, own):
        a, b = self.map_of(0, own)
        for place in range(1, self.radix):
            new_a, new_b = self.map_of(place, own)
            a, b = new_a * a, new_a * b + new_b
        return a, b

    def collect(self, near, final):
        rows = Rows(self.nx)
        for (k, adjacent), ref in zip(order(self.radix), self.others):
            if not adjacent:
                continue
            place = source(self.at, k, self.radix)

            @pl.when(self.lowest & (place == self.at - 1))
            def _():
                near[rows.low : rows.low + rows.info] = ref[rows.map : rows.final]

            @pl.when(self.highest & (place == self.at + 1))
            def _():
                near[rows.high : rows.high + rows.info] = ref[rows.map : rows.final]
                rest = slice(0, rows.map) if final else slice(rows.final, rows.full)
                near[rows.high + rows.info : rows.near] = ref[rest]


def start_near(near, nx, nz):
    rows = Rows(nx)
    near[: rows.span] = jnp.ones((rows.span, nz), jnp.float32)
    near[rows.span :] = jnp.zeros((near.shape[0] - rows.span, nz), jnp.float32)


def join_kernel(radix, stride, final, nx, is_first, *refs):
    rows = Rows(nx)
    total, last_info, first_info, near_in = refs[:4]
    others, near, outs = refs[4 : 3 + radix], refs[3 + radix], refs[4 + radix :]
    nz = near.shape[1]
    if is_first:
        start_near(near, nx, nz)
    else:
        near[...] = near_in[...]
    group = Group(radix, stride, others, nx)
    own = [total[i * rows.span : (i + 1) * rows.span] for i in range(2)]
    ahead = group.ahead(near[: rows.span], near[rows.span : rows.map])
    write_rows(near, ahead)
    group.collect(near, False)
    whole = group.total(own)
    at = lax.div(lax.axis_index("gy"), stride * radix)
    if final == 0:
        write_rows(outs[0], whole)
        return
    at = lax.rem(at, final)
    for (k, adjacent), out in zip(order(final), outs):
        up = target(at, k, final) > at
        if not adjacent:
            write_rows(out, whole)
            continue

        @pl.when(up)
        def _():
            write_rows(out, whole)
            out[rows.map : rows.final] = last_info[: rows.info]

        @pl.when(jnp.logical_not(up))
        def _():
            out[: rows.map] = first_info[rows.info : rows.info + rows.rest]
            out[rows.map : rows.final] = first_info[: rows.info]


def full_message(nx, stride, radix, total, last_info, first_info, k):
    rows = Rows(nx)
    at = lax.axis_index("gy") // stride % radix
    onward = jnp.concatenate([total[: rows.map], last_info[: rows.info], first_info[rows.info : rows.info + rows.rest]])
    back = jnp.concatenate([total[: rows.map], first_info[: rows.info + rows.rest]])
    message = jnp.where(target(at, k, radix) > at, onward, back)
    return jnp.pad(message, ((0, -rows.full % 8), (0, 0)))


def third_kernel(radix, stride, *refs):
    st, extra, coarse, near_in = refs[:4]
    others, (out, sc, wide, near, done, sems) = refs[4 : 3 + radix], refs[3 + radix :]
    planes, rows, ext, nz = st.shape
    ny, nx = rows - 2, ext - 2 * PAD
    edge = edge_weights((ext, nz))
    blocks = ny // 2

    lay = Rows(nx)
    span = lay.span
    near[...] = near_in[...]
    group = Group(radix, stride, others, nx)
    if radix > 1:
        group.collect(near, True)
    gas_in = group.ahead(near[:span], near[span : lay.map])[1]
    at_high = lay.high + lay.info
    starts = [lay.low, lay.low + span, lay.high, lay.high + span, at_high, at_high + span]
    for k, v in enumerate([gas_in] + [near[start : start + span] for start in starts]):
        wide[k, : PAD - 2] = jnp.zeros((PAD - 2, nz), jnp.float32)
        wide[k, ext - PAD + 2 :] = jnp.zeros((PAD - 2, nz), jnp.float32)
        wide[k, pl.ds(PAD - 2, span, 2), :] = v
        wide[k, pl.ds(PAD - 1, span, 2), :] = v
    for k, start in enumerate((lay.low, lay.low + nx + 2, lay.high, lay.high + nx + 2)):
        start += lay.map
        wide[7 + k, :PAD] = jnp.zeros((PAD, nz), jnp.float32)
        wide[7 + k, ext - PAD :] = jnp.zeros((PAD, nz), jnp.float32)
        wide[7 + k, PAD - 1 : PAD + nx + 1] = near[start : start + nx + 2]

    gas_in = wide[0]
    last = ny + 1
    solid_low = wide[1] + wide[2] * gas_in
    sc[0, 0] = st[SA, 0] + solid_low
    sc[1, 0] = st[GA, 0] + gas_in

    def correct(j, carry):
        gas = coarse[2, j] * gas_in + coarse[3, j]
        solid = coarse[0, j] + coarse[1, j] * gas
        for i in (2 * j + 1, 2 * j + 2):
            sc[0, i] = st[SA, i] + solid
            sc[1, i] = st[GA, i] + gas
        return carry

    lax.fori_loop(0, blocks, correct, 0)
    gas = coarse[2, blocks - 1] * gas_in + coarse[3, blocks - 1]
    gas_high = wide[5] * gas + wide[4]
    solid_high = wide[3] + wide[6] * gas_high
    sc[0, last] = st[SA, last] + solid_high
    sc[1, last] = st[GA, last] + gas_high

    view = Fields(st, sc)
    for i, is_after, solid, gas in ((0, False, solid_low, gas_in), (last, True, solid_high, gas_high)):
        side = 3 if is_after else 0
        fy = extra[side + 2]
        to = 9 if is_after else 7
        rs = extra[side] + wide[to] + fy * solid
        rg = extra[side + 1] + wide[to + 1] + (CONDUCT if is_after else CONDUCT + FLOW) * gas
        res = outer_residual(view, i, SA, rs, rg, fy, edge, is_after)
        sc[2, i], sc[3, i] = relaxed(view, i, SA, *res)

    def sweep(k, carry):
        stores = []
        for r in range(GROUP):
            i = GROUP * k + 1 + r
            new_s, new_g = relaxed(view, i, SA, *row_residual(view, i, SA, edge))
            stores += [((2, i), new_s), ((3, i), new_g)]
        for at, value in stores:
            sc[at] = value
        return carry

    lax.fori_loop(0, ny // GROUP, sweep, 0)

    def leaving(k):
        part = pl.ds(GROUP * k, GROUP)
        return pltpu.make_async_copy(done.at[:, part], out.at[:, part], sems.at[k])

    def final(k, carry):
        stores = []
        for r in range(GROUP):
            i = GROUP * k + 1 + r
            new_s, new_g = last_relaxed(view, i, SB, edge, slice(PAD, PAD + nx))
            stores += [((0, i - 1), new_s), ((1, i - 1), new_g)]
        for at, value in stores:
            done[at] = value
        leaving(k).start()
        return carry

    lax.fori_loop(0, ny // GROUP, final, 0)
    for k in range(ny // GROUP):
        leaving(k).wait()


class Fields:
    def __init__(self, st, sc):
        self.st, self.sc = st, sc

    def __getitem__(self, at):
        return (self.sc if at[0] <= GB else self.st)[at]


def cost(rows, cells):
    return pl.CostEstimate(flops=50 * rows * cells, bytes_accessed=16 * 4 * rows * cells, transcendentals=0)


def swap(x, axis, first):
    pairs = []
    for i in range(first, lax.axis_size(axis) - 1, 2):
        pairs += [(i, i + 1), (i + 1, i)]
    return lax.ppermute(x, axis, pairs)


def shards(temps, right_side, exchange, coupling):
    temps, right_side = (jnp.transpose(a, (0, 2, 1, 3)) for a in (temps, right_side))
    exchange, coupling = (jnp.transpose(a, (1, 0, 2)) for a in (exchange, coupling))
    temps, right_side, exchange, coupling = (
        pltpu.with_memory_space_constraint(a, pltpu.HBM) for a in (temps, right_side, exchange, coupling)
    )
    ny, nx, nz = exchange.shape
    ext = nx + 2 * PAD
    f32 = functools.partial(jax.ShapeDtypeStruct, dtype=jnp.float32)

    strip = f32(((ny * STRIP_ROWS + 7) // 8 * 8, nz))
    scratch = [(2, 2, ny, 8, nz)] * 2 + [(2, ny, 8, nz)] * 2 + [(2, 2, nx, nz), (2, nx, nz), (2, nx, nz)]
    one, two, early = pl.pallas_call(
        pack_kernel,
        out_shape=(strip, strip, f32((EARLY, nx, nz))),
        in_specs=[HBM] * 4,
        out_specs=(VMEM,) * 3,
        scratch_shapes=[pltpu.VMEM(shape, jnp.float32) for shape in scratch] + [pltpu.SemaphoreType.DMA((11,))],
        compiler_params=PARAMS,
        name="pack_x",
    )(temps, right_side, exchange, coupling)
    one, two = swap(one, "gx", 0), swap(two, "gx", 1)
    early = swap(early, "gy", 1)

    state = f32((PLANES, ny + 2, ext, nz))

    def letter(planes):
        return f32((planes, ext - 2 * CROP, nz))

    st = pl.pallas_call(
        load_kernel,
        out_shape=state,
        in_specs=[HBM] * 4,
        out_specs=VMEM,
        scratch_shapes=[pltpu.SemaphoreType.DMA((6,))],
        compiler_params=PARAMS,
        cost_estimate=cost(2 * ny, ext * nz),
        name="load",
    )(temps, right_side, exchange, coupling)
    st, across = pl.pallas_call(
        first_kernel,
        out_shape=(state, letter(MESSAGE - EARLY + 1)),
        in_specs=[VMEM] * 4,
        out_specs=(VMEM,) * 2,
        input_output_aliases={0: 0},
        compiler_params=PARAMS,
        name="first",
    )(st, one, two, early)
    across = swap(across, "gy", 1)

    rows = f32((4, ny // 2, ext, nz))
    st, coarse, beside_a, beside_b = pl.pallas_call(
        inner_kernel,
        out_shape=(state, rows, letter(EARLY), letter(MESSAGE - EARLY)),
        in_specs=[VMEM] * 3,
        out_specs=(VMEM,) * 4,
        input_output_aliases={0: 0},
        compiler_params=PARAMS,
        cost_estimate=cost(4 * ny, ext * nz),
        name="inner",
    )(st, one, two)

    beside_a, beside_b = swap(beside_a, "gy", 0), swap(beside_b, "gy", 0)

    lay = Rows(nx)

    def tall(height):
        return f32(((height + 7) // 8 * 8, nz))

    letters = [pltpu.VMEM((MESSAGE, ext, nz), jnp.float32)] * 2
    st, coarse, extra, total, last_info, first_info, message = pl.pallas_call(
        second_kernel,
        out_shape=(
            state,
            rows,
            f32((6, ext, nz)),
            tall(lay.map),
            tall(lay.info),
            tall(lay.info + lay.rest),
            tall(lay.full),
        ),
        in_specs=[VMEM] * 6,
        out_specs=(VMEM,) * 7,
        scratch_shapes=letters + [pltpu.VMEM((8, ext, nz), jnp.float32)],
        input_output_aliases={0: 0, 1: 1},
        compiler_params=PARAMS,
        name="second",
    )(st, coarse, early, across, beside_a, beside_b)

    near, messages = total, [message]
    radices, stride = stages(lax.axis_size("gy")), 1
    for place, radix in enumerate(radices[:-1]):
        if place:
            messages = [full_message(nx, stride, radix, total, last_info, first_info, k) for k, _ in order(radix)]
        others = exchange_stage(messages, radix, stride)
        final = radices[-1] if place == len(radices) - 2 else 0
        outs = [tall(lay.final if adjacent else lay.map) for _, adjacent in order(final)] if final else [tall(lay.map)]
        near, *messages = pl.pallas_call(
            functools.partial(join_kernel, radix, stride, final, nx, place == 0),
            out_shape=(tall(lay.near), *outs),
            in_specs=[VMEM] * (3 + radix),
            out_specs=(VMEM,) * (1 + len(outs)),
            compiler_params=PARAMS,
            name="join",
        )(total, last_info, first_info, near, *others)
        total = total if final else messages[0]
        stride *= radix
    got = exchange_stage(messages, radices[-1], stride)

    out = pl.pallas_call(
        functools.partial(third_kernel, radices[-1], stride),
        out_shape=f32((2, ny, nx, nz)),
        in_specs=[VMEM] * (4 + len(got)),
        out_specs=HBM,
        scratch_shapes=[
            pltpu.VMEM((4, ny + 2, ext, nz), jnp.float32),
            pltpu.VMEM((11, ext, nz), jnp.float32),
            pltpu.VMEM(tall(lay.near).shape, jnp.float32),
            pltpu.VMEM((2, ny, nx, nz), jnp.float32),
            pltpu.SemaphoreType.DMA((ny // GROUP,)),
        ],
        compiler_params=PARAMS,
        name="third",
    )(st, extra, coarse, near, *got)
    return jnp.transpose(out, (0, 2, 1, 3))


def solution(mesh):
    return jax.shard_map(
        shards,
        mesh=mesh,
        in_specs=(
            P(None, "gx", "gy", None),
            P(None, "gx", "gy", None),
            P("gx", "gy", None),
            P("gx", "gy", None),
        ),
        out_specs=P(None, "gx", "gy", None),
        check_vma=False,
    )
```

time: 35.6 us -> 33.1 us (0.930)
  the two profiles are of different devices: /device:TPU:16 before, /device:TPU:9 now
where the time goes in v5:
time: 33.1 us; the launch traced here: 32.9 us
  starting transfers between devices  17.4 us (53%)
  Pallas kernels  9.04 us (27%)
  waiting for transfers between devices  6.38 us (19%)
    ppermute x6, starting transfers between devices, swap(): return lax.ppermute(x, axis, pairs)  13 us
    ppermute x4, waiting for transfers between devices, exchange_stage(): got.append(lax.ppermute(message, 'gy', pairs))  4.83 us
    ppermute x4, starting transfers between devices, exchange_stage(): got.append(lax.ppermute(message, 'gy', pairs))  4.39 us
    pallas_call x1, Pallas kernels, shards(): pl.pallas_call(functools.partial(third_kernel, radices[-1], stride), out_...  2.49 us
    pallas_call x1, Pallas kernels, shards(): pl.pallas_call(inner_kernel, out_shape=(state, rows, letter(EARLY), lette...  1.86 us
    ppermute x6, waiting for transfers between devices, swap(): return lax.ppermute(x, axis, pairs)  1.55 us
    pallas_call x1, Pallas kernels, shards(): pl.pallas_call(load_kernel, out_shape=state, in_specs=[HBM] * 4, out_spec...  1.49 us
    pallas_call x1, Pallas kernels, shards(): pl.pallas_call(pack_kernel, out_shape=(strip, strip, f32((EARLY, nx, nz))...  1.33 us
  transfers between devices with their start and end apart: 10, of which 5 were waited for; matrix products, arithmetic and copies ran while one was open for 0% of the time, Pallas kernels for 10%

profile of v5, /device:TPU:9, one launch (start us, length us, event | category | flops | bytes accessed | tf_op | source)
XLA Modules:
  0.0 32.9 jit_solution(5319645444326768978)
XLA Ops:
  0.0 1.3 %pack_x.1 = (f32[304,128]{1,0:T(8,128)S(1)}, f32[304,128]{1,0:T(8,128)S(1)}, f32[5,32,128]{2,1,0:T(8,128)S(1)}) custom-call(f32[2,12,32,128]{3,2,1,0:T(8,128)} %bitcast.5, f32[2,12,32,128]{3,2,1,0:T(8,128)} %bitcast.7, f32[12,32,128]{2,1,0:T(8,128)} %bitcast.9, f32[12,32,128]{2,1,0:T(8,128)} %bitcast.11), custom_call_target="tpu_custom_call" | custom-call | tf_op jit(solution)/shard_map/pack_x/pallas_call | solution.py:743
  1.3 0.1 collective-permute-start
  1.4 4.5 %collective-permute-start.1 = (f32[304,128]{1,0:T(8,128)S(1)}, f32[304,128]{1,0:T(8,128)S(1)}, u32[]{:S(2)}, u32[]{:S(2)}) collective-permute-start(f32[304,128]{1,0:T(8,128)S(1)} %get-tuple-element.26), channel_id=1, source_target_pairs={{8,16},{16,8},{9,17},{17,9},{10,18},{18,10},{11,19},{19,11},{12,20... | collective-permute-start | bytes 466952 | tf_op jit(solution)/shard_map/ppermute | solution.py:728
  5.9 4.2 %collective-permute-start.2 = (f32[5,32,128]{2,1,0:T(8,128)S(1)}, f32[5,32,128]{2,1,0:T(8,128)S(1)}, u32[]{:S(2)}, u32[]{:S(2)}) collective-permute-start(f32[5,32,128]{2,1,0:T(8,128)S(1)} %get-tuple-element.27), channel_id=1, source_target_pairs={{1,2},{2,1},{3,4},{4,3},{5,6},{6,5},{9,10},{10,9},{11,12},{12,11},... | collective-permute-start | bytes 245768 | tf_op jit(solution)/shard_map/ppermute | solution.py:728
  10.1 1.5 %load.1.st_in = f32[15,14,48,128]{3,2,1,0:T(8,128)S(1)} custom-call(f32[2,12,32,128]{3,2,1,0:T(8,128)} %bitcast.6, f32[2,12,32,128]{3,2,1,0:T(8,128)} %bitcast.8, f32[12,32,128]{2,1,0:T(8,128)} %bitcast.10, f32[12,32,128]{2,1,0:T(8,128)} %bitcast.12), custom_call_target="tpu_custom_call" | custom-call | flops 7372800 | bytes 9437184 | tf_op jit(solution)/shard_map/load/pallas_call | solution.py:760
  11.6 0.6 %collective-permute-done.2.early = f32[5,32,128]{2,1,0:T(8,128)S(1)} collective-permute-done((f32[5,32,128]{2,1,0:T(8,128)S(1)}, f32[5,32,128]{2,1,0:T(8,128)S(1)}, u32[]{:S(2)}, u32[]{:S(2)}) %collective-permute-start.2) | collective-permute-done | bytes 81952 | tf_op jit(solution)/shard_map/ppermute | solution.py:728
  12.3 0.0 collective-permute-done.one
  12.3 0.0 collective-permute-done.1.two
  12.3 0.6 %first.1 = (f32[15,14,48,128]{3,2,1,0:T(8,128)S(1)}, f32[5,40,128]{2,1,0:T(8,128)S(1)}) custom-call(f32[15,14,48,128]{3,2,1,0:T(8,128)S(1)} %load.1.st_in, f32[304,128]{1,0:T(8,128)S(1)} %collective-permute-done.one, f32[304,128]{1,0:T(8,128)S(1)} %collective-permute-done.1.two, ...), custom_call_target="tpu_custom_call", output_to_operand_aliasing={{0}: (0, {})} | custom-call | tf_op jit(solution)/shard_map/first/pallas_call | solution.py:770
  12.8 3.6 %collective-permute-start.3 = (f32[5,40,128]{2,1,0:T(8,128)S(1)}, f32[5,40,128]{2,1,0:T(8,128)S(1)}, u32[]{:S(2)}, u32[]{:S(2)}) collective-permute-start(f32[5,40,128]{2,1,0:T(8,128)S(1)} %get-tuple-element.31), channel_id=1, source_target_pairs={{1,2},{2,1},{3,4},{4,3},{5,6},{6,5},{9,10},{10,9},{11,12},{12,11},... | collective-permute-start | bytes 307208 | tf_op jit(solution)/shard_map/ppermute | solution.py:728
  16.5 1.9 %inner.1 = (f32[15,14,48,128]{3,2,1,0:T(8,128)S(1)}, f32[4,6,48,128]{3,2,1,0:T(8,128)S(1)}, f32[5,40,128]{2,1,0:T(8,128)S(1)}, f32[4,40,128]{2,1,0:T(8,128)S(1)}) custom-call(f32[15,14,48,128]{3,2,1,0:T(8,128)S(1)} %get-tuple-element.28.st_in, f32[304,128]{1,0:T(8,128)S(1)} %collective-permute-done.one, ...), custom_call_target="tpu_custom_call", output_to_operand_aliasing={{0}: (0, {})} | custom-call | flops 14745600 | bytes 18874368 | tf_op jit(solution)/shard_map/inner/pallas_call | solution.py:782
  18.4 0.1 collective-permute-start.4
  18.4 0.5 %collective-permute-start.5 = (f32[4,40,128]{2,1,0:T(8,128)S(1)}, f32[4,40,128]{2,1,0:T(8,128)S(1)}, u32[]{:S(2)}, u32[]{:S(2)}) collective-permute-start(f32[4,40,128]{2,1,0:T(8,128)S(1)} %get-tuple-element.33), channel_id=1, source_target_pairs={{0,1},{1,0},{2,3},{3,2},{4,5},{5,4},{6,7},{7,6},{8,9},{9,8},{10,11... | collective-permute-start | bytes 245768 | tf_op jit(solution)/shard_map/ppermute | solution.py:728
  18.9 0.9 %collective-permute-done.5.beside_b = f32[4,40,128]{2,1,0:T(8,128)S(1)} collective-permute-done((f32[4,40,128]{2,1,0:T(8,128)S(1)}, f32[4,40,128]{2,1,0:T(8,128)S(1)}, u32[]{:S(2)}, u32[]{:S(2)}) %collective-permute-start.5) | collective-permute-done | bytes 81952 | tf_op jit(solution)/shard_map/ppermute | solution.py:728
  19.9 0.0 collective-permute-done.3.across
  19.9 1.2 %second.1 = (f32[15,14,48,128]{3,2,1,0:T(8,128)S(1)}, f32[4,6,48,128]{3,2,1,0:T(8,128)S(1)}, f32[6,48,128]{2,1,0:T(8,128)S(1)}, f32[40,128]{1,0:T(8,128)S(1)}, f...) custom-call(f32[15,14,48,128]{3,2,1,0:T(8,128)S(1)} %get-tuple-eleme, ...), custom_call_target="tpu_custom_call", output_to_operand_aliasing={{0}: (0, {}), {1}: (1, {})} | custom-call | tf_op jit(solution)/shard_map/second/pallas_call | solution.py:801
  21.1 0.4 %collective-permute-start.6 = (f32[176,128]{1,0:T(8,128)S(1)}, f32[176,128]{1,0:T(8,128)S(1)}, u32[]{:S(2)}, u32[]{:S(2)}) collective-permute-start(f32[176,128]{1,0:T(8,128)S(1)} %get-tuple-element.40), channel_id=1, source_target_pairs={{1,0},{0,1},{3,2},{2,3},{5,4},{4,5},{7,6},{6,7},{9,8},{8,9},{11,10... | collective-permute-start | bytes 270344 | tf_op jit(solution)/shard_map/ppermute | solution.py:515
  21.5 0.9 %collective-permute-done.6.refs_4_ = f32[176,128]{1,0:T(8,128)S(1)} collective-permute-done((f32[176,128]{1,0:T(8,128)S(1)}, f32[176,128]{1,0:T(8,128)S(1)}, u32[]{:S(2)}, u32[]{:S(2)}) %collective-permute-start.6) | collective-permute-done | bytes 90144 | tf_op jit(solution)/shard_map/ppermute | solution.py:515
  22.5 2.8 %collective-permute-start.7 = (f32[144,128]{1,0:T(8,128)S(1)}, f32[144,128]{1,0:T(8,128)S(1)}, u32[]{:S(2)}, u32[]{:S(2)}) collective-permute-start(f32[144,128]{1,0:T(8,128)S(1)} %get-tuple-element.42), channel_id=1, source_target_pairs={{7,0},{6,1},{5,2},{4,3},{3,4},{2,5},{1,6},{0,7},{15,8},{14,9},{13,... | collective-permute-start | bytes 221192 | tf_op jit(solution)/shard_map/ppermute | solution.py:515
  25.3 1.0 %collective-permute-start.8 = (f32[144,128]{1,0:T(8,128)S(1)}, f32[144,128]{1,0:T(8,128)S(1)}, u32[]{:S(2)}, u32[]{:S(2)}) collective-permute-start(f32[144,128]{1,0:T(8,128)S(1)} %get-tuple-element.43), channel_id=1, source_target_pairs={{3,0},{2,1},{1,2},{0,3},{7,4},{6,5},{5,6},{4,7},{11,8},{10,9},{9,1... | collective-permute-start | bytes 221192 | tf_op jit(solution)/shard_map/ppermute | solution.py:515
  26.3 0.2 collective-permute-start.9
  26.5 3.3 %collective-permute-done.9.refs_6_ = f32[40,128]{1,0:T(8,128)S(1)} collective-permute-done((f32[40,128]{1,0:T(8,128)S(1)}, f32[40,128]{1,0:T(8,128)S(1)}, u32[]{:S(2)}, u32[]{:S(2)}) %collective-permute-start.9) | collective-permute-done | bytes 20512 | tf_op jit(solution)/shard_map/ppermute | solution.py:515
  29.9 0.5 %collective-permute-done.8.refs_5_ = f32[144,128]{1,0:T(8,128)S(1)} collective-permute-done((f32[144,128]{1,0:T(8,128)S(1)}, f32[144,128]{1,0:T(8,128)S(1)}, u32[]{:S(2)}, u32[]{:S(2)}) %collective-permute-start.8) | collective-permute-done | bytes 73760 | tf_op jit(solution)/shard_map/ppermute | solution.py:515
  30.4 2.5 %third.1 = f32[2,12,32,128]{3,2,1,0:T(8,128)} custom-call(f32[15,14,48,128]{3,2,1,0:T(8,128)S(1)} %get-tuple-element.34.refs_0_, f32[6,48,128]{2,1,0:T(8,128)S(1)} %get-tuple-element.35.refs_1_, f32[4,6,48,128]{3,2,1,0:T(8,128)S(1)} %get-tuple-element.36.refs_2_, f32[280,128]{1,0:T(8,128)S(1)} %get-tuple-element.41.refs_3_, ...), custom_call_target="tpu_custom_call" | custom-call | tf_op jit(solution)/shard_map/third/pallas_call | solution.py:840
  (3 shorter events, 0.1 us)
Async XLA Ops:
  1.3 10.9 %collective-permute-start = (f32[304,128]{1,0:T(8,128)S(1)}, f32[304,128]{1,0:T(8,128)S(1)}, u32[]{:S(2)}, u32[]{:S(2)}) collective-permute-start(f32[304,128]{1,0:T(8,128)S(1)} %get-tuple-element.25), channel_id=1, source_target_pairs={{0,8},{8,0},{16,24},{24,16},{1,9},{9,1},{17,25},{25,17},{2,10},{10... | collective-permute-start | bytes 466952 | tf_op jit(solution)/shard_map/ppermute | solution.py:728
  1.4 10.8 %collective-permute-start.1 = (f32[304,128]{1,0:T(8,128)S(1)}, f32[304,128]{1,0:T(8,128)S(1)}, u32[]{:S(2)}, u32[]{:S(2)}) collective-permute-start(f32[304,128]{1,0:T(8,128)S(1)} %get-tuple-element.26), channel_id=1, source_target_pairs={{8,16},{16,8},{9,17},{17,9},{10,18},{18,10},{11,19},{19,11},{12,20... | collective-permute-start | bytes 466952 | tf_op jit(solution)/shard_map/ppermute | solution.py:728
  5.9 6.4 %collective-permute-start.2 = (f32[5,32,128]{2,1,0:T(8,128)S(1)}, f32[5,32,128]{2,1,0:T(8,128)S(1)}, u32[]{:S(2)}, u32[]{:S(2)}) collective-permute-start(f32[5,32,128]{2,1,0:T(8,128)S(1)} %get-tuple-element.27), channel_id=1, source_target_pairs={{1,2},{2,1},{3,4},{4,3},{5,6},{6,5},{9,10},{10,9},{11,12},{12,11},... | collective-permute-start | bytes 245768 | tf_op jit(solution)/shard_map/ppermute | solution.py:728
  12.8 7.0 %collective-permute-start.3 = (f32[5,40,128]{2,1,0:T(8,128)S(1)}, f32[5,40,128]{2,1,0:T(8,128)S(1)}, u32[]{:S(2)}, u32[]{:S(2)}) collective-permute-start(f32[5,40,128]{2,1,0:T(8,128)S(1)} %get-tuple-element.31), channel_id=1, source_target_pairs={{1,2},{2,1},{3,4},{4,3},{5,6},{6,5},{9,10},{10,9},{11,12},{12,11},... | collective-permute-start | bytes 307208 | tf_op jit(solution)/shard_map/ppermute | solution.py:728
  18.4 1.5 %collective-permute-start.4 = (f32[5,40,128]{2,1,0:T(8,128)S(1)}, f32[5,40,128]{2,1,0:T(8,128)S(1)}, u32[]{:S(2)}, u32[]{:S(2)}) collective-permute-start(f32[5,40,128]{2,1,0:T(8,128)S(1)} %get-tuple-element.32), channel_id=1, source_target_pairs={{0,1},{1,0},{2,3},{3,2},{4,5},{5,4},{6,7},{7,6},{8,9},{9,8},{10,11... | collective-permute-start | bytes 307208 | tf_op jit(solution)/shard_map/ppermute | solution.py:728
  18.4 1.4 %collective-permute-start.5 = (f32[4,40,128]{2,1,0:T(8,128)S(1)}, f32[4,40,128]{2,1,0:T(8,128)S(1)}, u32[]{:S(2)}, u32[]{:S(2)}) collective-permute-start(f32[4,40,128]{2,1,0:T(8,128)S(1)} %get-tuple-element.33), channel_id=1, source_target_pairs={{0,1},{1,0},{2,3},{3,2},{4,5},{5,4},{6,7},{7,6},{8,9},{9,8},{10,11... | collective-permute-start | bytes 245768 | tf_op jit(solution)/shard_map/ppermute | solution.py:728
  21.1 1.4 %collective-permute-start.6 = (f32[176,128]{1,0:T(8,128)S(1)}, f32[176,128]{1,0:T(8,128)S(1)}, u32[]{:S(2)}, u32[]{:S(2)}) collective-permute-start(f32[176,128]{1,0:T(8,128)S(1)} %get-tuple-element.40), channel_id=1, source_target_pairs={{1,0},{0,1},{3,2},{2,3},{5,4},{4,5},{7,6},{6,7},{9,8},{8,9},{11,10... | collective-permute-start | bytes 270344 | tf_op jit(solution)/shard_map/ppermute | solution.py:515
  22.5 7.3 %collective-permute-start.7 = (f32[144,128]{1,0:T(8,128)S(1)}, f32[144,128]{1,0:T(8,128)S(1)}, u32[]{:S(2)}, u32[]{:S(2)}) collective-permute-start(f32[144,128]{1,0:T(8,128)S(1)} %get-tuple-element.42), channel_id=1, source_target_pairs={{7,0},{6,1},{5,2},{4,3},{3,4},{2,5},{1,6},{0,7},{15,8},{14,9},{13,... | collective-permute-start | bytes 221192 | tf_op jit(solution)/shard_map/ppermute | solution.py:515
  25.3 5.1 %collective-permute-start.8 = (f32[144,128]{1,0:T(8,128)S(1)}, f32[144,128]{1,0:T(8,128)S(1)}, u32[]{:S(2)}, u32[]{:S(2)}) collective-permute-start(f32[144,128]{1,0:T(8,128)S(1)} %get-tuple-element.43), channel_id=1, source_target_pairs={{3,0},{2,1},{1,2},{0,3},{7,4},{6,5},{5,6},{4,7},{11,8},{10,9},{9,1... | collective-permute-start | bytes 221192 | tf_op jit(solution)/shard_map/ppermute | solution.py:515
  26.3 3.5 %collective-permute-start.9 = (f32[40,128]{1,0:T(8,128)S(1)}, f32[40,128]{1,0:T(8,128)S(1)}, u32[]{:S(2)}, u32[]{:S(2)}) collective-permute-start(f32[40,128]{1,0:T(8,128)S(1)} %get-tuple-element.44), channel_id=1, source_target_pairs={{5,0},{4,1},{7,2},{6,3},{1,4},{0,5},{3,6},{2,7},{13,8},{12,9},{15,... | collective-permute-start | bytes 61448 | tf_op jit(solution)/shard_map/ppermute | solution.py:515

commit v6 on v5

--- a/solution.py
+++ b/solution.py
@@ -16,7 +16,7 @@
 (SA, GA, SB, GB, K, C, RS, RG, FX, FZ, H, FY, ASS, ASG, AGG) = range(15)
 PLANES = 15
 (M_S, M_G, M_K, M_C, M_FY, M_1S, M_1G, M_2S, M_2G) = range(9)
-MESSAGE, EARLY = 9, 5
+MESSAGE = 9
 
 GROUP = 3
 
@@ -71,10 +71,8 @@
     return [s[four], g[four], k[five], rs[four], rg[four], c[four]]
 
 
-def pack_kernel(temps, right, exchange, coupling, one, two, early, *scratch):
-    pair_low, pair_high, single_low, single_high, rows_t, rows_e, rows_c, sems = scratch
+def pack_kernel(temps, right, exchange, coupling, one, two, pair_low, pair_high, single_low, single_high, sems):
     even = lax.axis_index("gx") % 2 == 0
-    odd = lax.axis_index("gy") % 2 == 1
     ny, nx, nz = exchange.shape
     copies = []
     for k, ref in enumerate((temps, right, exchange, coupling)):
@@ -82,10 +80,6 @@
         lead = (slice(None),) * (ref.ndim - 2)
         copies.append(pltpu.make_async_copy(ref.at[lead + (slice(0, 8),)], low.at[at], sems.at[2 * k]))
         copies.append(pltpu.make_async_copy(ref.at[lead + (slice(nx - 8, nx),)], high.at[at], sems.at[2 * k + 1]))
-    ends = pl.ds(jnp.where(odd, ny - 2, 0), 2)
-    copies.append(pltpu.make_async_copy(temps.at[:, ends], rows_t, sems.at[8]))
-    copies.append(pltpu.make_async_copy(exchange.at[ends], rows_e, sems.at[9]))
-    copies.append(pltpu.make_async_copy(coupling.at[ends], rows_c, sems.at[10]))
     for copy in copies:
         copy.start()
     for copy in copies:
@@ -100,10 +94,7 @@
             one[at : at + width] = jnp.where(even, high, low)
             two[at : at + width] = jnp.where(even, low, high)
             at += width
-    k = [conductivity_of(rows_t[0, i], rows_e[i]) for i in range(2)]
-    pick = lambda pair: jnp.where(odd, pair[1], pair[0])
-    early[M_S], early[M_G] = pick([rows_t[0, i] for i in range(2)]), pick([rows_t[1, i] for i in range(2)])
-    early[M_K], early[M_C], early[M_FY] = pick(k), pick([rows_c[i] for i in range(2)]), 0.5 * (k[0] + k[1])
+    two[one.shape[0] :] = jnp.zeros((8, nz), jnp.float32)
 
 
 def load_kernel(temps, right, exchange, coupling, st, sems):
@@ -251,33 +242,18 @@
     return [s, g, st[K, e], st[C, e], fy, m_1s, m_1g, m_2s, m_2g]
 
 
-def write_across(ref, st, onward, edge):
+def write_message(ref, st, onward, edge):
     ext = st.shape[2]
-    for k, value in enumerate(send_planes(st, onward, edge)):
-        if k >= EARLY:
-            ref[k - EARLY] = value[CROP : ext - CROP]
-        else:
-            ref[MESSAGE - EARLY, 8 * k : 8 * k + 4] = value[CROP:PAD]
-            ref[MESSAGE - EARLY, 8 * k + 4 : 8 * k + 8] = value[ext - PAD : ext - CROP]
-
-
-def write_beside(refs, st, onward, edge):
-    ext = st.shape[2]
-    for k, value in enumerate(send_planes(st, onward, edge)):
-        ref, at = (refs[0], k) if k < EARLY else (refs[1], k - EARLY)
-        ref[at] = value[CROP : ext - CROP]
-
-
-def write_message(write, ref, st, onward, edge):
     for go in (True, False):
 
         @pl.when(onward == go)
         def _():
-            write(ref, st, go, edge)
-
-
-def first_kernel(st_in, one, two, early, st, across):
-    del st_in, early
+            for k, value in enumerate(send_planes(st, go, edge)):
+                ref[k] = value[CROP : ext - CROP]
+
+
+def first_kernel(st_in, one, two, st, across):
+    del st_in
     planes, rows, ext, nz = st.shape
     ny, nx = rows - 2, ext - 2 * PAD
     shape = (ext, nz)
@@ -294,7 +270,7 @@
     ends = [2, 3, ny - 2, ny - 1]
     grouped(ends, lambda i: row_coefficients(st, i, mask))
     grouped(ends, lambda i: row_sweep(st, i, SA, SB, edge))
-    write_message(write_across, across, st, lax.axis_index("gy") % 2 == 1, edge)
+    write_message(across, st, lax.axis_index("gy") % 2 == 1, edge)
 
 
 def outer_residual(st, i, s_at, rs, rg, fy_out, edge, after):
@@ -333,7 +309,7 @@
     return [(coarse, (k, j), v) for k, v in enumerate(values)]
 
 
-def inner_kernel(st_in, one, two, st, coarse, beside_a, beside_b):
+def inner_kernel(st_in, one, two, st, coarse, beside):
     del st_in
     planes, rows, ext, nz = st.shape
     ny, nx = rows - 2, ext - 2 * PAD
@@ -348,35 +324,25 @@
     for j in range(2, ny // 2 - 2):
         for ref, at, value in coarse_row(st, coarse, j, mask, edge):
             ref[at] = value
-    write_message(write_beside, (beside_a, beside_b), st, lax.axis_index("gy") % 2 == 0, edge)
-
-
-def unpack(early, across, beside_a, beside_b, before, after):
+    write_message(beside, st, lax.axis_index("gy") % 2 == 0, edge)
+
+
+def unpack(across, beside, before, after):
     even = lax.axis_index("gy") % 2 == 0
     ext, nz = before.shape[1:]
     zeros = jnp.zeros((PAD, nz), jnp.float32)
-
-    def fill(far, near):
-        for k in range(MESSAGE):
-            for ref in (far, near):
-                ref[k, :PAD] = zeros
-                ref[k, ext - PAD :] = zeros
-            near[k, CROP : ext - CROP] = beside_a[k] if k < EARLY else beside_b[k - EARLY]
-            if k >= EARLY:
-                far[k, CROP : ext - CROP] = across[k - EARLY]
-            else:
-                far[k, PAD : ext - PAD] = early[k]
-                far[k, CROP:PAD] = across[MESSAGE - EARLY, 8 * k : 8 * k + 4]
-                far[k, ext - PAD : ext - CROP] = across[MESSAGE - EARLY, 8 * k + 4 : 8 * k + 8]
-
     for is_even, far, near in ((True, before, after), (False, after, before)):
 
         @pl.when(even == is_even)
         def _():
-            fill(far, near)
-
-
-def second_kernel(st_in, coarse_in, early, across, beside_a, beside_b, st, coarse, extra, total, last_info, first_info, message, before, after, squeeze):
+            for k in range(MESSAGE):
+                for ref, got in ((far, across), (near, beside)):
+                    ref[k, :PAD] = zeros
+                    ref[k, ext - PAD :] = zeros
+                    ref[k, CROP : ext - CROP] = got[k]
+
+
+def second_kernel(st_in, coarse_in, across, beside, st, coarse, extra, total, last_info, first_info, message, before, after, squeeze):
     del st_in, coarse_in
     planes, rows, ext, nz = st.shape
     ny, nx = rows - 2, ext - 2 * PAD
@@ -386,7 +352,7 @@
     low = jnp.where(me == 0, 0.0, mask)
     high = jnp.where(me == count - 1, 0.0, mask)
     edge = edge_weights(shape)
-    unpack(early, across, beside_a, beside_b, before, after)
+    unpack(across, beside, before, after)
 
     last = ny + 1
     ends = ((0, before, low), (last, after, high))
@@ -738,19 +704,20 @@
     ext = nx + 2 * PAD
     f32 = functools.partial(jax.ShapeDtypeStruct, dtype=jnp.float32)
 
-    strip = f32(((ny * STRIP_ROWS + 7) // 8 * 8, nz))
-    scratch = [(2, 2, ny, 8, nz)] * 2 + [(2, ny, 8, nz)] * 2 + [(2, 2, nx, nz), (2, nx, nz), (2, nx, nz)]
-    one, two, early = pl.pallas_call(
+    height = (ny * STRIP_ROWS + 7) // 8 * 8
+    strips = f32((height, nz)), f32((height + 8, nz))
+    scratch = [(2, 2, ny, 8, nz)] * 2 + [(2, ny, 8, nz)] * 2
+    one, two = pl.pallas_call(
         pack_kernel,
-        out_shape=(strip, strip, f32((EARLY, nx, nz))),
+        out_shape=strips,
         in_specs=[HBM] * 4,
-        out_specs=(VMEM,) * 3,
-        scratch_shapes=[pltpu.VMEM(shape, jnp.float32) for shape in scratch] + [pltpu.SemaphoreType.DMA((11,))],
+        out_specs=(VMEM,) * 2,
+        scratch_shapes=[pltpu.VMEM(shape, jnp.float32) for shape in scratch] + [pltpu.SemaphoreType.DMA((8,))],
         compiler_params=PARAMS,
         name="pack_x",
     )(temps, right_side, exchange, coupling)
-    one, two = swap(one, "gx", 0), swap(two, "gx", 1)
-    early = swap(early, "gy", 1)
+    two = swap(two, "gx", 1)
+    one = swap(one, "gx", 0)
 
     state = f32((PLANES, ny + 2, ext, nz))
 
@@ -769,28 +736,28 @@
     )(temps, right_side, exchange, coupling)
     st, across = pl.pallas_call(
         first_kernel,
-        out_shape=(state, letter(MESSAGE - EARLY + 1)),
-        in_specs=[VMEM] * 4,
+        out_shape=(state, letter(MESSAGE)),
+        in_specs=[VMEM] * 3,
         out_specs=(VMEM,) * 2,
         input_output_aliases={0: 0},
         compiler_params=PARAMS,
         name="first",
-    )(st, one, two, early)
+    )(st, one, two)
     across = swap(across, "gy", 1)
 
     rows = f32((4, ny // 2, ext, nz))
-    st, coarse, beside_a, beside_b = pl.pallas_call(
+    st, coarse, beside = pl.pallas_call(
         inner_kernel,
-        out_shape=(state, rows, letter(EARLY), letter(MESSAGE - EARLY)),
+        out_shape=(state, rows, letter(MESSAGE)),
         in_specs=[VMEM] * 3,
-        out_specs=(VMEM,) * 4,
+        out_specs=(VMEM,) * 3,
         input_output_aliases={0: 0},
         compiler_params=PARAMS,
         cost_estimate=cost(4 * ny, ext * nz),
         name="inner",
     )(st, one, two)
 
-    beside_a, beside_b = swap(beside_a, "gy", 0), swap(beside_b, "gy", 0)
+    beside = swap(beside, "gy", 0)
 
     lay = Rows(nx)
 
@@ -809,13 +776,13 @@
             tall(lay.info + lay.rest),
             tall(lay.full),
         ),
-        in_specs=[VMEM] * 6,
+        in_specs=[VMEM] * 4,
         out_specs=(VMEM,) * 7,
         scratch_shapes=letters + [pltpu.VMEM((8, ext, nz), jnp.float32)],
         input_output_aliases={0: 0, 1: 1},
         compiler_params=PARAMS,
         name="second",
-    )(st, coarse, early, across, beside_a, beside_b)
+    )(st, coarse, across, beside)
 
     near, messages = total, [message]
     radices, stride = stages(lax.axis_size("gy")), 1

time: 33.1 us -> 33.2 us (level)
  the two profiles are of different devices: /device:TPU:9 before, /device:TPU:0 now
where the time goes in v6:
time: 33.2 us; the launch traced here: 33 us
  starting transfers between devices  15.7 us (47%)
  Pallas kernels  8.94 us (27%)
  waiting for transfers between devices  8.31 us (25%)
    ppermute x4, starting transfers between devices, swap(): return lax.ppermute(x, axis, pairs)  10.1 us
    ppermute x4, starting transfers between devices, exchange_stage(): got.append(lax.ppermute(message, 'gy', pairs))  5.51 us
    ppermute x4, waiting for transfers between devices, exchange_stage(): got.append(lax.ppermute(message, 'gy', pairs))  5 us
    ppermute x4, waiting for transfers between devices, swap(): return lax.ppermute(x, axis, pairs)  3.31 us
    pallas_call x1, Pallas kernels, shards(): pl.pallas_call(functools.partial(third_kernel, radices[-1], stride), out_...  2.5 us
    pallas_call x1, Pallas kernels, shards(): pl.pallas_call(inner_kernel, out_shape=(state, rows, letter(MESSAGE)), in...  1.86 us
    pallas_call x1, Pallas kernels, shards(): pl.pallas_call(load_kernel, out_shape=state, in_specs=[HBM] * 4, out_spec...  1.48 us
    pallas_call x1, Pallas kernels, shards(): pl.pallas_call(second_kernel, out_shape=(state, rows, f32((6, ext, nz)),...  1.24 us
  transfers between devices with their start and end apart: 8, of which 5 were waited for; matrix products, arithmetic and copies ran while one was open for 0% of the time, Pallas kernels for 10%

profile of v6, /device:TPU:0, one launch (start us, length us, event | category | flops | bytes accessed | tf_op | source)
XLA Modules:
  0.0 33.0 jit_solution(12749278175544785534)
XLA Ops:
  0.0 1.2 %pack_x.1 = (f32[304,128]{1,0:T(8,128)S(1)}, f32[312,128]{1,0:T(8,128)S(1)}) custom-call(f32[2,12,32,128]{3,2,1,0:T(8,128)} %bitcast.5, f32[2,12,32,128]{3,2,1,0:T(8,128)} %bitcast.7, f32[12,32,128]{2,1,0:T(8,128)} %bitcast.9, f32[12,32,128]{2,1,0:T(8,128)} %bitcast.11), custom_call_target="tpu_custom_call" | custom-call | tf_op jit(solution)/shard_map/pack_x/pallas_call | solution.py:710
  1.2 0.7 %collective-permute-start.1 = (f32[312,128]{1,0:T(8,128)S(1)}, f32[312,128]{1,0:T(8,128)S(1)}, u32[]{:S(2)}, u32[]{:S(2)}) collective-permute-start(f32[312,128]{1,0:T(8,128)S(1)} %get-tuple-element.24), channel_id=1, source_target_pairs={{8,16},{16,8},{9,17},{17,9},{10,18},{18,10},{11,19},{19,11},{12,20... | collective-permute-start | bytes 479240 | tf_op jit(solution)/shard_map/ppermute | solution.py:694
  1.9 5.9 %collective-permute-start = (f32[304,128]{1,0:T(8,128)S(1)}, f32[304,128]{1,0:T(8,128)S(1)}, u32[]{:S(2)}, u32[]{:S(2)}) collective-permute-start(f32[304,128]{1,0:T(8,128)S(1)} %get-tuple-element.23), channel_id=1, source_target_pairs={{0,8},{8,0},{16,24},{24,16},{1,9},{9,1},{17,25},{25,17},{2,10},{10... | collective-permute-start | bytes 466952 | tf_op jit(solution)/shard_map/ppermute | solution.py:694
  7.8 1.5 %load.1.st_in = f32[15,14,48,128]{3,2,1,0:T(8,128)S(1)} custom-call(f32[2,12,32,128]{3,2,1,0:T(8,128)} %bitcast.6, f32[2,12,32,128]{3,2,1,0:T(8,128)} %bitcast.8, f32[12,32,128]{2,1,0:T(8,128)} %bitcast.10, f32[12,32,128]{2,1,0:T(8,128)} %bitcast.12), custom_call_target="tpu_custom_call" | custom-call | flops 7372800 | bytes 9437184 | tf_op jit(solution)/shard_map/load/pallas_call | solution.py:727
  9.3 2.3 %collective-permute-done.one = f32[304,128]{1,0:T(8,128)S(1)} collective-permute-done((f32[304,128]{1,0:T(8,128)S(1)}, f32[304,128]{1,0:T(8,128)S(1)}, u32[]{:S(2)}, u32[]{:S(2)}) %collective-permute-start) | collective-permute-done | bytes 155680 | tf_op jit(solution)/shard_map/ppermute | solution.py:694
  11.6 0.0 collective-permute-done.1.two
  11.6 0.6 %first.1 = (f32[15,14,48,128]{3,2,1,0:T(8,128)S(1)}, f32[9,40,128]{2,1,0:T(8,128)S(1)}) custom-call(f32[15,14,48,128]{3,2,1,0:T(8,128)S(1)} %load.1.st_in, f32[304,128]{1,0:T(8,128)S(1)} %collective-permute-done.one, f32[312,128]{1,0:T(8,128)S(1)} %collective-permute-done.1.two), custom_call_target="tpu_custom_call", output_to_operand_aliasing={{0}: (0, {})} | custom-call | tf_op jit(solution)/shard_map/first/pallas_call | solution.py:737
  12.2 0.7 %collective-permute-start.2 = (f32[9,40,128]{2,1,0:T(8,128)S(1)}, f32[9,40,128]{2,1,0:T(8,128)S(1)}, u32[]{:S(2)}, u32[]{:S(2)}) collective-permute-start(f32[9,40,128]{2,1,0:T(8,128)S(1)} %get-tuple-element.28), channel_id=1, source_target_pairs={{1,2},{2,1},{3,4},{4,3},{5,6},{6,5},{9,10},{10,9},{11,12},{12,11},... | collective-permute-start | bytes 552968 | tf_op jit(solution)/shard_map/ppermute | solution.py:694
  12.8 1.9 %inner.1 = (f32[15,14,48,128]{3,2,1,0:T(8,128)S(1)}, f32[4,6,48,128]{3,2,1,0:T(8,128)S(1)}, f32[9,40,128]{2,1,0:T(8,128)S(1)}) custom-call(f32[15,14,48,128]{3,2,1,0:T(8,128)S(1)} %get-tuple-element.25.st_in, f32[304,128]{1,0:T(8,128)S(1)} %collective-permute-done.one, f32[312,128]{1,0:T(8,128)S(1)} %collective-permute-done.1.two), custom_call_target="tpu_custom_call", output_to_operand_aliasing={{0}: (0, {})} | custom-call | flops 14745600 | bytes 18874368 | tf_op jit(solution)/shard_map/inner/pallas_call | solution.py:749
  14.7 2.9 %collective-permute-start.3 = (f32[9,40,128]{2,1,0:T(8,128)S(1)}, f32[9,40,128]{2,1,0:T(8,128)S(1)}, u32[]{:S(2)}, u32[]{:S(2)}) collective-permute-start(f32[9,40,128]{2,1,0:T(8,128)S(1)} %get-tuple-element.29), channel_id=1, source_target_pairs={{0,1},{1,0},{2,3},{3,2},{4,5},{5,4},{6,7},{7,6},{8,9},{9,8},{10,11... | collective-permute-start | bytes 552968 | tf_op jit(solution)/shard_map/ppermute | solution.py:694
  17.6 0.0 collective-permute-done.2.across
  17.6 1.1 %collective-permute-done.3.beside = f32[9,40,128]{2,1,0:T(8,128)S(1)} collective-permute-done((f32[9,40,128]{2,1,0:T(8,128)S(1)}, f32[9,40,128]{2,1,0:T(8,128)S(1)}, u32[]{:S(2)}, u32[]{:S(2)}) %collective-permute-start.3) | collective-permute-done | bytes 184352 | tf_op jit(solution)/shard_map/ppermute | solution.py:694
  18.7 1.2 %second.1 = (f32[15,14,48,128]{3,2,1,0:T(8,128)S(1)}, f32[4,6,48,128]{3,2,1,0:T(8,128)S(1)}, f32[6,48,128]{2,1,0:T(8,128)S(1)}, f32[40,128]{1,0:T(8,128)S(1)}, f...) custom-call(f32[15,14,48,128]{3,2,1,0:T(8,128)S(1)} %get-tuple-eleme, ...), custom_call_target="tpu_custom_call", output_to_operand_aliasing={{0}: (0, {}), {1}: (1, {})} | custom-call | tf_op jit(solution)/shard_map/second/pallas_call | solution.py:768
  19.9 1.4 %collective-permute-start.4 = (f32[176,128]{1,0:T(8,128)S(1)}, f32[176,128]{1,0:T(8,128)S(1)}, u32[]{:S(2)}, u32[]{:S(2)}) collective-permute-start(f32[176,128]{1,0:T(8,128)S(1)} %get-tuple-element.36), channel_id=1, source_target_pairs={{1,0},{0,1},{3,2},{2,3},{5,4},{4,5},{7,6},{6,7},{9,8},{8,9},{11,10... | collective-permute-start | bytes 270344 | tf_op jit(solution)/shard_map/ppermute | solution.py:481
  21.3 0.9 %collective-permute-done.4.refs_4_ = f32[176,128]{1,0:T(8,128)S(1)} collective-permute-done((f32[176,128]{1,0:T(8,128)S(1)}, f32[176,128]{1,0:T(8,128)S(1)}, u32[]{:S(2)}, u32[]{:S(2)}) %collective-permute-start.4) | collective-permute-done | bytes 90144 | tf_op jit(solution)/shard_map/ppermute | solution.py:481
  22.3 2.7 %collective-permute-start.5 = (f32[144,128]{1,0:T(8,128)S(1)}, f32[144,128]{1,0:T(8,128)S(1)}, u32[]{:S(2)}, u32[]{:S(2)}) collective-permute-start(f32[144,128]{1,0:T(8,128)S(1)} %get-tuple-element.38), channel_id=1, source_target_pairs={{7,0},{6,1},{5,2},{4,3},{3,4},{2,5},{1,6},{0,7},{15,8},{14,9},{13,... | collective-permute-start | bytes 221192 | tf_op jit(solution)/shard_map/ppermute | solution.py:481
  25.0 1.4 %collective-permute-start.6 = (f32[144,128]{1,0:T(8,128)S(1)}, f32[144,128]{1,0:T(8,128)S(1)}, u32[]{:S(2)}, u32[]{:S(2)}) collective-permute-start(f32[144,128]{1,0:T(8,128)S(1)} %get-tuple-element.39), channel_id=1, source_target_pairs={{3,0},{2,1},{1,2},{0,3},{7,4},{6,5},{5,6},{4,7},{11,8},{10,9},{9,1... | collective-permute-start | bytes 221192 | tf_op jit(solution)/shard_map/ppermute | solution.py:481
  26.4 0.0 collective-permute-start.7
  26.4 3.2 %collective-permute-done.7.refs_6_ = f32[40,128]{1,0:T(8,128)S(1)} collective-permute-done((f32[40,128]{1,0:T(8,128)S(1)}, f32[40,128]{1,0:T(8,128)S(1)}, u32[]{:S(2)}, u32[]{:S(2)}) %collective-permute-start.7) | collective-permute-done | bytes 20512 | tf_op jit(solution)/shard_map/ppermute | solution.py:481
  29.6 0.0 collective-permute-done.5.refs_4_
  29.6 0.9 %collective-permute-done.6.refs_5_ = f32[144,128]{1,0:T(8,128)S(1)} collective-permute-done((f32[144,128]{1,0:T(8,128)S(1)}, f32[144,128]{1,0:T(8,128)S(1)}, u32[]{:S(2)}, u32[]{:S(2)}) %collective-permute-start.6) | collective-permute-done | bytes 73760 | tf_op jit(solution)/shard_map/ppermute | solution.py:481
  30.5 2.5 %third.1 = f32[2,12,32,128]{3,2,1,0:T(8,128)} custom-call(f32[15,14,48,128]{3,2,1,0:T(8,128)S(1)} %get-tuple-element.30.refs_0_, f32[6,48,128]{2,1,0:T(8,128)S(1)} %get-tuple-element.31.refs_1_, f32[4,6,48,128]{3,2,1,0:T(8,128)S(1)} %get-tuple-element.32.refs_2_, f32[280,128]{1,0:T(8,128)S(1)} %get-tuple-element.37.refs_3_, ...), custom_call_target="tpu_custom_call" | custom-call | tf_op jit(solution)/shard_map/third/pallas_call | solution.py:807
  (1 shorter events, 0.0 us)
Async XLA Ops:
  1.2 10.3 %collective-permute-start.1 = (f32[312,128]{1,0:T(8,128)S(1)}, f32[312,128]{1,0:T(8,128)S(1)}, u32[]{:S(2)}, u32[]{:S(2)}) collective-permute-start(f32[312,128]{1,0:T(8,128)S(1)} %get-tuple-element.24), channel_id=1, source_target_pairs={{8,16},{16,8},{9,17},{17,9},{10,18},{18,10},{11,19},{19,11},{12,20... | collective-permute-start | bytes 479240 | tf_op jit(solution)/shard_map/ppermute | solution.py:694
  1.9 9.6 %collective-permute-start = (f32[304,128]{1,0:T(8,128)S(1)}, f32[304,128]{1,0:T(8,128)S(1)}, u32[]{:S(2)}, u32[]{:S(2)}) collective-permute-start(f32[304,128]{1,0:T(8,128)S(1)} %get-tuple-element.23), channel_id=1, source_target_pairs={{0,8},{8,0},{16,24},{24,16},{1,9},{9,1},{17,25},{25,17},{2,10},{10... | collective-permute-start | bytes 466952 | tf_op jit(solution)/shard_map/ppermute | solution.py:694
  12.2 5.5 %collective-permute-start.2 = (f32[9,40,128]{2,1,0:T(8,128)S(1)}, f32[9,40,128]{2,1,0:T(8,128)S(1)}, u32[]{:S(2)}, u32[]{:S(2)}) collective-permute-start(f32[9,40,128]{2,1,0:T(8,128)S(1)} %get-tuple-element.28), channel_id=1, source_target_pairs={{1,2},{2,1},{3,4},{4,3},{5,6},{6,5},{9,10},{10,9},{11,12},{12,11},... | collective-permute-start | bytes 552968 | tf_op jit(solution)/shard_map/ppermute | solution.py:694
  14.7 4.0 %collective-permute-start.3 = (f32[9,40,128]{2,1,0:T(8,128)S(1)}, f32[9,40,128]{2,1,0:T(8,128)S(1)}, u32[]{:S(2)}, u32[]{:S(2)}) collective-permute-start(f32[9,40,128]{2,1,0:T(8,128)S(1)} %get-tuple-element.29), channel_id=1, source_target_pairs={{0,1},{1,0},{2,3},{3,2},{4,5},{5,4},{6,7},{7,6},{8,9},{9,8},{10,11... | collective-permute-start | bytes 552968 | tf_op jit(solution)/shard_map/ppermute | solution.py:694
  19.9 2.3 %collective-permute-start.4 = (f32[176,128]{1,0:T(8,128)S(1)}, f32[176,128]{1,0:T(8,128)S(1)}, u32[]{:S(2)}, u32[]{:S(2)}) collective-permute-start(f32[176,128]{1,0:T(8,128)S(1)} %get-tuple-element.36), channel_id=1, source_target_pairs={{1,0},{0,1},{3,2},{2,3},{5,4},{4,5},{7,6},{6,7},{9,8},{8,9},{11,10... | collective-permute-start | bytes 270344 | tf_op jit(solution)/shard_map/ppermute | solution.py:481
  22.3 7.3 %collective-permute-start.5 = (f32[144,128]{1,0:T(8,128)S(1)}, f32[144,128]{1,0:T(8,128)S(1)}, u32[]{:S(2)}, u32[]{:S(2)}) collective-permute-start(f32[144,128]{1,0:T(8,128)S(1)} %get-tuple-element.38), channel_id=1, source_target_pairs={{7,0},{6,1},{5,2},{4,3},{3,4},{2,5},{1,6},{0,7},{15,8},{14,9},{13,... | collective-permute-start | bytes 221192 | tf_op jit(solution)/shard_map/ppermute | solution.py:481
  25.0 5.5 %collective-permute-start.6 = (f32[144,128]{1,0:T(8,128)S(1)}, f32[144,128]{1,0:T(8,128)S(1)}, u32[]{:S(2)}, u32[]{:S(2)}) collective-permute-start(f32[144,128]{1,0:T(8,128)S(1)} %get-tuple-element.39), channel_id=1, source_target_pairs={{3,0},{2,1},{1,2},{0,3},{7,4},{6,5},{5,6},{4,7},{11,8},{10,9},{9,1... | collective-permute-start | bytes 221192 | tf_op jit(solution)/shard_map/ppermute | solution.py:481
  26.4 3.2 %collective-permute-start.7 = (f32[40,128]{1,0:T(8,128)S(1)}, f32[40,128]{1,0:T(8,128)S(1)}, u32[]{:S(2)}, u32[]{:S(2)}) collective-permute-start(f32[40,128]{1,0:T(8,128)S(1)} %get-tuple-element.40), channel_id=1, source_target_pairs={{5,0},{4,1},{7,2},{6,3},{1,4},{0,5},{3,6},{2,7},{13,8},{12,9},{15,... | collective-permute-start | bytes 61448 | tf_op jit(solution)/shard_map/ppermute | solution.py:481

commit v7 on v6

--- a/solution.py
+++ b/solution.py
@@ -16,7 +16,7 @@
 (SA, GA, SB, GB, K, C, RS, RG, FX, FZ, H, FY, ASS, ASG, AGG) = range(15)
 PLANES = 15
 (M_S, M_G, M_K, M_C, M_FY, M_1S, M_1G, M_2S, M_2G) = range(9)
-MESSAGE = 9
+MESSAGE, HALF = 9, 5
 
 GROUP = 3
 
@@ -94,7 +94,6 @@
             one[at : at + width] = jnp.where(even, high, low)
             two[at : at + width] = jnp.where(even, low, high)
             at += width
-    two[one.shape[0] :] = jnp.zeros((8, nz), jnp.float32)
 
 
 def load_kernel(temps, right, exchange, coupling, st, sems):
@@ -242,14 +241,19 @@
     return [s, g, st[K, e], st[C, e], fy, m_1s, m_1g, m_2s, m_2g]
 
 
-def write_message(ref, st, onward, edge):
+def write_message(refs, st, onward, edge):
     ext = st.shape[2]
     for go in (True, False):
 
         @pl.when(onward == go)
         def _():
             for k, value in enumerate(send_planes(st, go, edge)):
-                ref[k] = value[CROP : ext - CROP]
+                ref, at = message_plane(refs, k)
+                ref[at] = value[CROP : ext - CROP]
+
+
+def message_plane(refs, plane):
+    return (refs[0], plane) if len(refs) == 1 or plane < HALF else (refs[1], plane - HALF)
 
 
 def first_kernel(st_in, one, two, st, across):
@@ -270,7 +274,7 @@
     ends = [2, 3, ny - 2, ny - 1]
     grouped(ends, lambda i: row_coefficients(st, i, mask))
     grouped(ends, lambda i: row_sweep(st, i, SA, SB, edge))
-    write_message(across, st, lax.axis_index("gy") % 2 == 1, edge)
+    write_message([across], st, lax.axis_index("gy") % 2 == 1, edge)
 
 
 def outer_residual(st, i, s_at, rs, rg, fy_out, edge, after):
@@ -309,7 +313,7 @@
     return [(coarse, (k, j), v) for k, v in enumerate(values)]
 
 
-def inner_kernel(st_in, one, two, st, coarse, beside):
+def inner_kernel(st_in, one, two, st, coarse, beside_a, beside_b):
     del st_in
     planes, rows, ext, nz = st.shape
     ny, nx = rows - 2, ext - 2 * PAD
@@ -324,76 +328,81 @@
     for j in range(2, ny // 2 - 2):
         for ref, at, value in coarse_row(st, coarse, j, mask, edge):
             ref[at] = value
-    write_message(beside, st, lax.axis_index("gy") % 2 == 0, edge)
-
-
-def unpack(across, beside, before, after):
-    even = lax.axis_index("gy") % 2 == 0
-    ext, nz = before.shape[1:]
-    zeros = jnp.zeros((PAD, nz), jnp.float32)
-    for is_even, far, near in ((True, before, after), (False, after, before)):
-
-        @pl.when(even == is_even)
-        def _():
-            for k in range(MESSAGE):
-                for ref, got in ((far, across), (near, beside)):
-                    ref[k, :PAD] = zeros
-                    ref[k, ext - PAD :] = zeros
-                    ref[k, CROP : ext - CROP] = got[k]
-
-
-def second_kernel(st_in, coarse_in, across, beside, st, coarse, extra, total, last_info, first_info, message, before, after, squeeze):
-    del st_in, coarse_in
+    write_message([beside_a, beside_b], st, lax.axis_index("gy") % 2 == 0, edge)
+
+
+def end_work(st, coarse, extra, got, outer, is_after):
     planes, rows, ext, nz = st.shape
     ny, nx = rows - 2, ext - 2 * PAD
-    shape = (ext, nz)
     me, count = lax.axis_index("gy"), lax.axis_size("gy")
-    mask = x_mask(shape, nx)
-    low = jnp.where(me == 0, 0.0, mask)
-    high = jnp.where(me == count - 1, 0.0, mask)
-    edge = edge_weights(shape)
-    unpack(across, beside, before, after)
-
-    last = ny + 1
-    ends = ((0, before, low), (last, after, high))
-    for i, ref, inside in ends:
-        st[SA, i], st[GA, i], st[K, i], st[C, i] = ref[M_S], ref[M_G], ref[M_K], ref[M_C]
-    st[FY, 0] = 0.5 * (st[K, 0] + st[K, 1])
-    st[FY, ny] = 0.5 * (st[K, ny] + st[K, last])
-    for i in (1, ny):
-        fx, fz = st[FX, i], st[FZ, i]
-        diag = st[H, i] + (fx + down_x(fx)) + (fz + down_z(fz)) + st[C, i] + st[FY, i - 1] + st[FY, i]
-        st[ASS, i], st[ASG, i], st[AGG, i] = inverse(diag, st[C, i], mask)
-    for i, ref, inside in ends:
-        fx, fz, h, diag = faces(st[K, i])
-        st[FX, i], st[FZ, i], st[H, i] = fx, fz, h
-        diag += st[C, i] + ref[M_FY] + st[FY, min(i, ny)]
-        st[ASS, i], st[ASG, i], st[AGG, i] = inverse(diag, st[C, i], inside)
-
-    res = before[M_1S] + st[FY, 0] * (st[SA, 1] - st[SA, 0]), before[M_1G] + CONDUCT * st[GA, 1]
-    new_low = relaxed(st, 0, SA, *res)
-    res = after[M_1S] + st[FY, ny] * (st[SA, ny] - st[SA, last]), after[M_1G] + (CONDUCT + FLOW) * st[GA, ny]
-    new_high = relaxed(st, last, SA, *res)
-    stores = row_sweep(st, 1, SA, SB, edge) + row_sweep(st, ny, SA, SB, edge)
-    st[SB, 0], st[GB, 0] = new_low
-    st[SB, last], st[GB, last] = new_high
+    mask = x_mask((ext, nz), nx)
+    inside = jnp.where(me == (count - 1 if is_after else 0), 0.0, mask)
+    edge = edge_weights((ext, nz))
+    zeros = jnp.zeros((PAD, nz), jnp.float32)
+    for k in range(MESSAGE):
+        outer[k, :PAD] = zeros
+        outer[k, ext - PAD :] = zeros
+        ref, at = message_plane(got, k)
+        outer[k, CROP : ext - CROP] = ref[at]
+
+    o, e, near = (ny + 1, ny, ny) if is_after else (0, 1, 0)
+    to_o = CONDUCT + FLOW if is_after else CONDUCT
+    s_o, g_o, k_o, c_o, fy_out = (outer[plane] for plane in (M_S, M_G, M_K, M_C, M_FY))
+    fy = 0.5 * (k_o + st[K, e])
+    fx, fz, h, diag = faces(k_o)
+    inv_o = inverse(diag + c_o + fy_out + fy, c_o, inside)
+    fx_e, fz_e = st[FX, e], st[FZ, e]
+    diag = st[H, e] + (fx_e + down_x(fx_e)) + (fz_e + down_z(fz_e)) + st[C, e] + fy
+    inv_e = inverse(diag + st[FY, near - 1 if is_after else near + 1], st[C, e], mask)
+    for plane, value in ((SA, s_o), (GA, g_o), (K, k_o), (C, c_o), (FX, fx), (FZ, fz), (H, h)):
+        st[plane, o] = value
+    st[FY, near] = fy
+    for k in range(3):
+        st[ASS + k, o], st[ASS + k, e] = inv_o[k], inv_e[k]
+
+    res = outer[M_1S] + fy * (st[SA, e] - s_o), outer[M_1G] + to_o * st[GA, e]
+    new_o = relaxed(st, o, SA, *res)
+    stores = row_sweep(st, e, SA, SB, edge)
+    st[SB, o], st[GB, o] = new_o
     for ref, at, value in stores:
         ref[at] = value
-
-    for i, ref, inside in ends:
-        is_after = i > 0
-        res = outer_residual(st, i, SB, ref[M_2S], ref[M_2G], ref[M_FY], edge, is_after)
-        st[SA, i], st[GA, i] = relaxed(st, i, SB, *res)
-    grouped([1, 2, ny - 1, ny], lambda i: row_sweep(st, i, SB, SA, edge))
-
-    for i, ref, inside in ends:
-        for k, plane in enumerate((M_2S, M_2G, M_FY)):
-            extra[(3 if i else 0) + k] = ref[plane]
-
+    res = outer_residual(st, o, SB, outer[M_2S], outer[M_2G], fy_out, edge, is_after)
+    new_o = relaxed(st, o, SB, *res)
+    ends = [e - 1, e] if is_after else [e, e + 1]
+    grouped(ends, lambda i: row_sweep(st, i, SB, SA, edge))
+    st[SA, o], st[GA, o] = new_o
+    for k, plane in enumerate((M_2S, M_2G, M_FY)):
+        extra[(3 if is_after else 0) + k] = outer[plane]
     blocks = ny // 2
-    for j in (0, 1, blocks - 2, blocks - 1):
-        for ref, at, value in coarse_row(st, coarse, j, mask, edge):
-            ref[at] = value
+    stores = []
+    for j in (blocks - 2, blocks - 1) if is_after else (0, 1):
+        stores += coarse_row(st, coarse, j, mask, edge)
+    for ref, at, value in stores:
+        ref[at] = value
+
+
+def either_end(after, st, coarse, extra, got, outer):
+    for is_after in (True, False):
+
+        @pl.when(after == is_after)
+        def _():
+            end_work(st, coarse, extra, got, outer, is_after)
+
+
+def near_kernel(st_in, coarse_in, beside_a, beside_b, st, coarse, extra, outer):
+    del st_in, coarse_in
+    either_end(lax.axis_index("gy") % 2 == 0, st, coarse, extra, [beside_a, beside_b], outer)
+
+
+def second_kernel(st_in, coarse_in, extra_in, across, *refs):
+    st, coarse, extra, total, last_info, first_info, message, outer, squeeze = refs
+    del st_in, coarse_in, extra_in
+    planes, rows, ext, nz = st.shape
+    ny, nx = rows - 2, ext - 2 * PAD
+    me = lax.axis_index("gy")
+    either_end(me % 2 == 1, st, coarse, extra, [across], outer)
+
+    blocks = ny // 2
     for k in range(4):
         squeeze[k] = coarse[k, 0]
     slopes, offsets = coarse[2, 0], coarse[3, 0]
@@ -705,7 +714,7 @@
     f32 = functools.partial(jax.ShapeDtypeStruct, dtype=jnp.float32)
 
     height = (ny * STRIP_ROWS + 7) // 8 * 8
-    strips = f32((height, nz)), f32((height + 8, nz))
+    strips = f32((height, nz)), f32((height, nz))
     scratch = [(2, 2, ny, 8, nz)] * 2 + [(2, ny, 8, nz)] * 2
     one, two = pl.pallas_call(
         pack_kernel,
@@ -716,8 +725,7 @@
         compiler_params=PARAMS,
         name="pack_x",
     )(temps, right_side, exchange, coupling)
-    two = swap(two, "gx", 1)
-    one = swap(one, "gx", 0)
+    one, two = swap(one, "gx", 0), swap(two, "gx", 1)
 
     state = f32((PLANES, ny + 2, ext, nz))
 
@@ -746,43 +754,46 @@
     across = swap(across, "gy", 1)
 
     rows = f32((4, ny // 2, ext, nz))
-    st, coarse, beside = pl.pallas_call(
+    st, coarse, beside_a, beside_b = pl.pallas_call(
         inner_kernel,
-        out_shape=(state, rows, letter(MESSAGE)),
+        out_shape=(state, rows, letter(HALF), letter(MESSAGE - HALF)),
         in_specs=[VMEM] * 3,
-        out_specs=(VMEM,) * 3,
+        out_specs=(VMEM,) * 4,
         input_output_aliases={0: 0},
         compiler_params=PARAMS,
         cost_estimate=cost(4 * ny, ext * nz),
         name="inner",
     )(st, one, two)
 
-    beside = swap(beside, "gy", 0)
+    beside_a, beside_b = swap(beside_a, "gy", 0), swap(beside_b, "gy", 0)
 
     lay = Rows(nx)
 
     def tall(height):
         return f32(((height + 7) // 8 * 8, nz))
 
-    letters = [pltpu.VMEM((MESSAGE, ext, nz), jnp.float32)] * 2
+    letter_room = pltpu.VMEM((MESSAGE, ext, nz), jnp.float32)
+    more = f32((6, ext, nz))
+    st, coarse, extra = pl.pallas_call(
+        near_kernel,
+        out_shape=(state, rows, more),
+        in_specs=[VMEM] * 4,
+        out_specs=(VMEM,) * 3,
+        scratch_shapes=[letter_room],
+        input_output_aliases={0: 0, 1: 1},
+        compiler_params=PARAMS,
+        name="near",
+    )(st, coarse, beside_a, beside_b)
     st, coarse, extra, total, last_info, first_info, message = pl.pallas_call(
         second_kernel,
-        out_shape=(
-            state,
-            rows,
-            f32((6, ext, nz)),
-            tall(lay.map),
-            tall(lay.info),
-            tall(lay.info + lay.rest),
-            tall(lay.full),
-        ),
+        out_shape=(state, rows, more, tall(lay.map), tall(lay.info), tall(lay.info + lay.rest), tall(lay.full)),
         in_specs=[VMEM] * 4,
         out_specs=(VMEM,) * 7,
-        scratch_shapes=letters + [pltpu.VMEM((8, ext, nz), jnp.float32)],
-        input_output_aliases={0: 0, 1: 1},
+        scratch_shapes=[letter_room, pltpu.VMEM((8, ext, nz), jnp.float32)],
+        input_output_aliases={0: 0, 1: 1, 2: 2},
         compiler_params=PARAMS,
         name="second",
-    )(st, coarse, across, beside)
+    )(st, coarse, extra, across)
 
     near, messages = total, [message]
     radices, stride = stages(lax.axis_size("gy")), 1

time: 33.2 us -> 31.7 us (0.955)
  the two profiles are of different devices: /device:TPU:0 before, /device:TPU:16 now
where the time goes in v7:
time: 31.7 us; the launch traced here: 31.2 us
  starting transfers between devices  11.8 us (37%)
  waiting for transfers between devices  10.2 us (32%)
  Pallas kernels  9.2 us (29%)
    ppermute x5, starting transfers between devices, swap(): return lax.ppermute(x, axis, pairs)  7.2 us
    ppermute x5, waiting for transfers between devices, swap(): return lax.ppermute(x, axis, pairs)  5.16 us
    ppermute x4, waiting for transfers between devices, exchange_stage(): got.append(lax.ppermute(message, 'gy', pairs))  5 us
    ppermute x4, starting transfers between devices, exchange_stage(): got.append(lax.ppermute(message, 'gy', pairs))  4.56 us
    pallas_call x1, Pallas kernels, shards(): pl.pallas_call(functools.partial(third_kernel, radices[-1], stride), out_...  2.61 us
    pallas_call x1, Pallas kernels, shards(): pl.pallas_call(inner_kernel, out_shape=(state, rows, letter(HALF), letter...  1.92 us
    pallas_call x1, Pallas kernels, shards(): pl.pallas_call(load_kernel, out_shape=state, in_specs=[HBM] * 4, out_spec...  1.49 us
    pallas_call x1, Pallas kernels, shards(): pl.pallas_call(pack_kernel, out_shape=strips, in_specs=[HBM] * 4, out_spe...  1.24 us
  transfers between devices with their start and end apart: 9, of which 6 were waited for; matrix products, arithmetic and copies ran while one was open for 0% of the time, Pallas kernels for 13%

profile of v7, /device:TPU:16, one launch (start us, length us, event | category | flops | bytes accessed | tf_op | source)
XLA Modules:
  0.0 31.2 jit_solution(9548007779784187487)
XLA Ops:
  0.0 1.2 %pack_x.1 = (f32[304,128]{1,0:T(8,128)S(1)}, f32[304,128]{1,0:T(8,128)S(1)}) custom-call(f32[2,12,32,128]{3,2,1,0:T(8,128)} %bitcast.5, f32[2,12,32,128]{3,2,1,0:T(8,128)} %bitcast.7, f32[12,32,128]{2,1,0:T(8,128)} %bitcast.9, f32[12,32,128]{2,1,0:T(8,128)} %bitcast.11), custom_call_target="tpu_custom_call" | custom-call | tf_op jit(solution)/shard_map/pack_x/pallas_call | solution.py:719
  1.2 1.6 %collective-permute-start = (f32[304,128]{1,0:T(8,128)S(1)}, f32[304,128]{1,0:T(8,128)S(1)}, u32[]{:S(2)}, u32[]{:S(2)}) collective-permute-start(f32[304,128]{1,0:T(8,128)S(1)} %get-tuple-element.27), channel_id=1, source_target_pairs={{0,8},{8,0},{16,24},{24,16},{1,9},{9,1},{17,25},{25,17},{2,10},{10... | collective-permute-start | bytes 466952 | tf_op jit(solution)/shard_map/ppermute | solution.py:703
  2.9 1.9 %collective-permute-start.1 = (f32[304,128]{1,0:T(8,128)S(1)}, f32[304,128]{1,0:T(8,128)S(1)}, u32[]{:S(2)}, u32[]{:S(2)}) collective-permute-start(f32[304,128]{1,0:T(8,128)S(1)} %get-tuple-element.28), channel_id=1, source_target_pairs={{8,16},{16,8},{9,17},{17,9},{10,18},{18,10},{11,19},{19,11},{12,20... | collective-permute-start | bytes 466952 | tf_op jit(solution)/shard_map/ppermute | solution.py:703
  4.8 1.5 %load.1.st_in = f32[15,14,48,128]{3,2,1,0:T(8,128)S(1)} custom-call(f32[2,12,32,128]{3,2,1,0:T(8,128)} %bitcast.6, f32[2,12,32,128]{3,2,1,0:T(8,128)} %bitcast.8, f32[12,32,128]{2,1,0:T(8,128)} %bitcast.10, f32[12,32,128]{2,1,0:T(8,128)} %bitcast.12), custom_call_target="tpu_custom_call" | custom-call | flops 7372800 | bytes 9437184 | tf_op jit(solution)/shard_map/load/pallas_call | solution.py:735
  6.3 0.8 %collective-permute-done.one = f32[304,128]{1,0:T(8,128)S(1)} collective-permute-done((f32[304,128]{1,0:T(8,128)S(1)}, f32[304,128]{1,0:T(8,128)S(1)}, u32[]{:S(2)}, u32[]{:S(2)}) %collective-permute-start) | collective-permute-done | bytes 155680 | tf_op jit(solution)/shard_map/ppermute | solution.py:703
  7.1 3.2 %collective-permute-done.1.two = f32[304,128]{1,0:T(8,128)S(1)} collective-permute-done((f32[304,128]{1,0:T(8,128)S(1)}, f32[304,128]{1,0:T(8,128)S(1)}, u32[]{:S(2)}, u32[]{:S(2)}) %collective-permute-start.1) | collective-permute-done | bytes 155680 | tf_op jit(solution)/shard_map/ppermute | solution.py:703
  10.3 0.6 %first.1 = (f32[15,14,48,128]{3,2,1,0:T(8,128)S(1)}, f32[9,40,128]{2,1,0:T(8,128)S(1)}) custom-call(f32[15,14,48,128]{3,2,1,0:T(8,128)S(1)} %load.1.st_in, f32[304,128]{1,0:T(8,128)S(1)} %collective-permute-done.one, f32[304,128]{1,0:T(8,128)S(1)} %collective-permute-done.1.two), custom_call_target="tpu_custom_call", output_to_operand_aliasing={{0}: (0, {})} | custom-call | tf_op jit(solution)/shard_map/first/pallas_call | solution.py:745
  10.9 0.7 %collective-permute-start.4 = (f32[9,40,128]{2,1,0:T(8,128)S(1)}, f32[9,40,128]{2,1,0:T(8,128)S(1)}, u32[]{:S(2)}, u32[]{:S(2)}) collective-permute-start(f32[9,40,128]{2,1,0:T(8,128)S(1)} %get-tuple-element.37), channel_id=1, source_target_pairs={{1,2},{2,1},{3,4},{4,3},{5,6},{6,5},{9,10},{10,9},{11,12},{12,11},... | collective-permute-start | bytes 552968 | tf_op jit(solution)/shard_map/ppermute | solution.py:703
  11.5 1.9 %inner.1 = (f32[15,14,48,128]{3,2,1,0:T(8,128)S(1)}, f32[4,6,48,128]{3,2,1,0:T(8,128)S(1)}, f32[5,40,128]{2,1,0:T(8,128)S(1)}, f32[4,40,128]{2,1,0:T(8,128)S(1)}) custom-call(f32[15,14,48,128]{3,2,1,0:T(8,128)S(1)} %get-tuple-element.29.st_in, f32[304,128]{1,0:T(8,128)S(1)} %collective-permute-done.one, ...), custom_call_target="tpu_custom_call", output_to_operand_aliasing={{0}: (0, {})} | custom-call | flops 14745600 | bytes 18874368 | tf_op jit(solution)/shard_map/inner/pallas_call | solution.py:757
  13.5 2.9 %collective-permute-start.2 = (f32[5,40,128]{2,1,0:T(8,128)S(1)}, f32[5,40,128]{2,1,0:T(8,128)S(1)}, u32[]{:S(2)}, u32[]{:S(2)}) collective-permute-start(f32[5,40,128]{2,1,0:T(8,128)S(1)} %get-tuple-element.32), channel_id=1, source_target_pairs={{0,1},{1,0},{2,3},{3,2},{4,5},{5,4},{6,7},{7,6},{8,9},{9,8},{10,11... | collective-permute-start | bytes 307208 | tf_op jit(solution)/shard_map/ppermute | solution.py:703
  16.4 0.1 collective-permute-start.3
  16.4 1.2 %collective-permute-done.3.beside_b = f32[4,40,128]{2,1,0:T(8,128)S(1)} collective-permute-done((f32[4,40,128]{2,1,0:T(8,128)S(1)}, f32[4,40,128]{2,1,0:T(8,128)S(1)}, u32[]{:S(2)}, u32[]{:S(2)}) %collective-permute-start.3) | collective-permute-done | bytes 81952 | tf_op jit(solution)/shard_map/ppermute | solution.py:703
  17.6 0.6 %near.1 = (f32[15,14,48,128]{3,2,1,0:T(8,128)S(1)}, f32[4,6,48,128]{3,2,1,0:T(8,128)S(1)}, f32[6,48,128]{2,1,0:T(8,128)S(1)}) custom-call(f32[15,14,48,128]{3,2,1,0:T(8,128)S(1)} %get-tuple-element.30.st_in, f32[4,6,48,128]{3,2,1,0:T(8,128)S(1)} %get-tuple-element.31.coarse_in, ...), custom_call_target="tpu_custom_call", output_to_operand_aliasing={{0}: (0, {}), {1}: (1, {})} | custom-call | tf_op jit(solution)/shard_map/near/pallas_call | solution.py:777
  18.3 0.0 collective-permute-done.4.across
  18.3 0.7 %second.1 = (f32[15,14,48,128]{3,2,1,0:T(8,128)S(1)}, f32[4,6,48,128]{3,2,1,0:T(8,128)S(1)}, f32[6,48,128]{2,1,0:T(8,128)S(1)}, f32[40,128]{1,0:T(8,128)S(1)}, f...) custom-call(f32[15,14,48,128]{3,2,1,0:T(8,128)S(1)} %get-tuple-eleme, ...), custom_call_target="tpu_custom_call", output_to_operand_aliasing={{0}: (0, {}), {1}: (1, {}), {2}: (2, {})} | custom-call | tf_op jit(solution)/shard_map/second/pallas_call | solution.py:787
  19.0 0.5 %collective-permute-start.5 = (f32[176,128]{1,0:T(8,128)S(1)}, f32[176,128]{1,0:T(8,128)S(1)}, u32[]{:S(2)}, u32[]{:S(2)}) collective-permute-start(f32[176,128]{1,0:T(8,128)S(1)} %get-tuple-element.44), channel_id=1, source_target_pairs={{1,0},{0,1},{3,2},{2,3},{5,4},{4,5},{7,6},{6,7},{9,8},{8,9},{11,10... | collective-permute-start | bytes 270344 | tf_op jit(solution)/shard_map/ppermute | solution.py:490
  19.4 0.9 %collective-permute-done.5.refs_4_ = f32[176,128]{1,0:T(8,128)S(1)} collective-permute-done((f32[176,128]{1,0:T(8,128)S(1)}, f32[176,128]{1,0:T(8,128)S(1)}, u32[]{:S(2)}, u32[]{:S(2)}) %collective-permute-start.5) | collective-permute-done | bytes 90144 | tf_op jit(solution)/shard_map/ppermute | solution.py:490
  20.4 2.7 %collective-permute-start.6 = (f32[144,128]{1,0:T(8,128)S(1)}, f32[144,128]{1,0:T(8,128)S(1)}, u32[]{:S(2)}, u32[]{:S(2)}) collective-permute-start(f32[144,128]{1,0:T(8,128)S(1)} %get-tuple-element.46), channel_id=1, source_target_pairs={{7,0},{6,1},{5,2},{4,3},{3,4},{2,5},{1,6},{0,7},{15,8},{14,9},{13,... | collective-permute-start | bytes 221192 | tf_op jit(solution)/shard_map/ppermute | solution.py:490
  23.1 1.4 %collective-permute-start.7 = (f32[144,128]{1,0:T(8,128)S(1)}, f32[144,128]{1,0:T(8,128)S(1)}, u32[]{:S(2)}, u32[]{:S(2)}) collective-permute-start(f32[144,128]{1,0:T(8,128)S(1)} %get-tuple-element.47), channel_id=1, source_target_pairs={{3,0},{2,1},{1,2},{0,3},{7,4},{6,5},{5,6},{4,7},{11,8},{10,9},{9,1... | collective-permute-start | bytes 221192 | tf_op jit(solution)/shard_map/ppermute | solution.py:490
  24.5 0.0 collective-permute-start.8
  24.5 3.2 %collective-permute-done.8.refs_6_ = f32[40,128]{1,0:T(8,128)S(1)} collective-permute-done((f32[40,128]{1,0:T(8,128)S(1)}, f32[40,128]{1,0:T(8,128)S(1)}, u32[]{:S(2)}, u32[]{:S(2)}) %collective-permute-start.8) | collective-permute-done | bytes 20512 | tf_op jit(solution)/shard_map/ppermute | solution.py:490
  27.7 0.0 collective-permute-done.6.refs_4_
  27.7 0.9 %collective-permute-done.7.refs_5_ = f32[144,128]{1,0:T(8,128)S(1)} collective-permute-done((f32[144,128]{1,0:T(8,128)S(1)}, f32[144,128]{1,0:T(8,128)S(1)}, u32[]{:S(2)}, u32[]{:S(2)}) %collective-permute-start.7) | collective-permute-done | bytes 73760 | tf_op jit(solution)/shard_map/ppermute | solution.py:490
  28.6 2.6 %third.1 = f32[2,12,32,128]{3,2,1,0:T(8,128)} custom-call(f32[15,14,48,128]{3,2,1,0:T(8,128)S(1)} %get-tuple-element.38.refs_0_, f32[6,48,128]{2,1,0:T(8,128)S(1)} %get-tuple-element.39.refs_1_, f32[4,6,48,128]{3,2,1,0:T(8,128)S(1)} %get-tuple-element.40.refs_2_, f32[280,128]{1,0:T(8,128)S(1)} %get-tuple-element.45.refs_3_, ...), custom_call_target="tpu_custom_call" | custom-call | tf_op jit(solution)/shard_map/third/pallas_call | solution.py:818
  (2 shorter events, 0.1 us)
Async XLA Ops:
  1.2 5.8 %collective-permute-start = (f32[304,128]{1,0:T(8,128)S(1)}, f32[304,128]{1,0:T(8,128)S(1)}, u32[]{:S(2)}, u32[]{:S(2)}) collective-permute-start(f32[304,128]{1,0:T(8,128)S(1)} %get-tuple-element.27), channel_id=1, source_target_pairs={{0,8},{8,0},{16,24},{24,16},{1,9},{9,1},{17,25},{25,17},{2,10},{10... | collective-permute-start | bytes 466952 | tf_op jit(solution)/shard_map/ppermute | solution.py:703
  2.9 7.4 %collective-permute-start.1 = (f32[304,128]{1,0:T(8,128)S(1)}, f32[304,128]{1,0:T(8,128)S(1)}, u32[]{:S(2)}, u32[]{:S(2)}) collective-permute-start(f32[304,128]{1,0:T(8,128)S(1)} %get-tuple-element.28), channel_id=1, source_target_pairs={{8,16},{16,8},{9,17},{17,9},{10,18},{18,10},{11,19},{19,11},{12,20... | collective-permute-start | bytes 466952 | tf_op jit(solution)/shard_map/ppermute | solution.py:703
  10.9 7.4 %collective-permute-start.4 = (f32[9,40,128]{2,1,0:T(8,128)S(1)}, f32[9,40,128]{2,1,0:T(8,128)S(1)}, u32[]{:S(2)}, u32[]{:S(2)}) collective-permute-start(f32[9,40,128]{2,1,0:T(8,128)S(1)} %get-tuple-element.37), channel_id=1, source_target_pairs={{1,2},{2,1},{3,4},{4,3},{5,6},{6,5},{9,10},{10,9},{11,12},{12,11},... | collective-permute-start | bytes 552968 | tf_op jit(solution)/shard_map/ppermute | solution.py:703
  13.5 4.2 %collective-permute-start.2 = (f32[5,40,128]{2,1,0:T(8,128)S(1)}, f32[5,40,128]{2,1,0:T(8,128)S(1)}, u32[]{:S(2)}, u32[]{:S(2)}) collective-permute-start(f32[5,40,128]{2,1,0:T(8,128)S(1)} %get-tuple-element.32), channel_id=1, source_target_pairs={{0,1},{1,0},{2,3},{3,2},{4,5},{5,4},{6,7},{7,6},{8,9},{9,8},{10,11... | collective-permute-start | bytes 307208 | tf_op jit(solution)/shard_map/ppermute | solution.py:703
  16.4 1.3 %collective-permute-start.3 = (f32[4,40,128]{2,1,0:T(8,128)S(1)}, f32[4,40,128]{2,1,0:T(8,128)S(1)}, u32[]{:S(2)}, u32[]{:S(2)}) collective-permute-start(f32[4,40,128]{2,1,0:T(8,128)S(1)} %get-tuple-element.33), channel_id=1, source_target_pairs={{0,1},{1,0},{2,3},{3,2},{4,5},{5,4},{6,7},{7,6},{8,9},{9,8},{10,11... | collective-permute-start | bytes 245768 | tf_op jit(solution)/shard_map/ppermute | solution.py:703
  19.0 1.4 %collective-permute-start.5 = (f32[176,128]{1,0:T(8,128)S(1)}, f32[176,128]{1,0:T(8,128)S(1)}, u32[]{:S(2)}, u32[]{:S(2)}) collective-permute-start(f32[176,128]{1,0:T(8,128)S(1)} %get-tuple-element.44), channel_id=1, source_target_pairs={{1,0},{0,1},{3,2},{2,3},{5,4},{4,5},{7,6},{6,7},{9,8},{8,9},{11,10... | collective-permute-start | bytes 270344 | tf_op jit(solution)/shard_map/ppermute | solution.py:490
  20.4 7.3 %collective-permute-start.6 = (f32[144,128]{1,0:T(8,128)S(1)}, f32[144,128]{1,0:T(8,128)S(1)}, u32[]{:S(2)}, u32[]{:S(2)}) collective-permute-start(f32[144,128]{1,0:T(8,128)S(1)} %get-tuple-element.46), channel_id=1, source_target_pairs={{7,0},{6,1},{5,2},{4,3},{3,4},{2,5},{1,6},{0,7},{15,8},{14,9},{13,... | collective-permute-start | bytes 221192 | tf_op jit(solution)/shard_map/ppermute | solution.py:490
  23.1 5.5 %collective-permute-start.7 = (f32[144,128]{1,0:T(8,128)S(1)}, f32[144,128]{1,0:T(8,128)S(1)}, u32[]{:S(2)}, u32[]{:S(2)}) collective-permute-start(f32[144,128]{1,0:T(8,128)S(1)} %get-tuple-element.47), channel_id=1, source_target_pairs={{3,0},{2,1},{1,2},{0,3},{7,4},{6,5},{5,6},{4,7},{11,8},{10,9},{9,1... | collective-permute-start | bytes 221192 | tf_op jit(solution)/shard_map/ppermute | solution.py:490
  24.5 3.2 %collective-permute-start.8 = (f32[40,128]{1,0:T(8,128)S(1)}, f32[40,128]{1,0:T(8,128)S(1)}, u32[]{:S(2)}, u32[]{:S(2)}) collective-permute-start(f32[40,128]{1,0:T(8,128)S(1)} %get-tuple-element.48), channel_id=1, source_target_pairs={{5,0},{4,1},{7,2},{6,3},{1,4},{0,5},{3,6},{2,7},{13,8},{12,9},{15,... | collective-permute-start | bytes 61448 | tf_op jit(solution)/shard_map/ppermute | solution.py:490

commit v8 on v7

--- a/solution.py
+++ b/solution.py
@@ -16,7 +16,7 @@
 (SA, GA, SB, GB, K, C, RS, RG, FX, FZ, H, FY, ASS, ASG, AGG) = range(15)
 PLANES = 15
 (M_S, M_G, M_K, M_C, M_FY, M_1S, M_1G, M_2S, M_2G) = range(9)
-MESSAGE, HALF = 9, 5
+MESSAGE, EARLY, THIRD = 9, 5, 3
 
 GROUP = 3
 
@@ -71,8 +71,10 @@
     return [s[four], g[four], k[five], rs[four], rg[four], c[four]]
 
 
-def pack_kernel(temps, right, exchange, coupling, one, two, pair_low, pair_high, single_low, single_high, sems):
+def pack_kernel(temps, right, exchange, coupling, one, two, early, *scratch):
+    pair_low, pair_high, single_low, single_high, rows_t, rows_e, rows_c, sems = scratch
     even = lax.axis_index("gx") % 2 == 0
+    odd = lax.axis_index("gy") % 2 == 1
     ny, nx, nz = exchange.shape
     copies = []
     for k, ref in enumerate((temps, right, exchange, coupling)):
@@ -80,6 +82,10 @@
         lead = (slice(None),) * (ref.ndim - 2)
         copies.append(pltpu.make_async_copy(ref.at[lead + (slice(0, 8),)], low.at[at], sems.at[2 * k]))
         copies.append(pltpu.make_async_copy(ref.at[lead + (slice(nx - 8, nx),)], high.at[at], sems.at[2 * k + 1]))
+    ends = pl.ds(jnp.where(odd, ny - 2, 0), 2)
+    copies.append(pltpu.make_async_copy(temps.at[:, ends], rows_t, sems.at[8]))
+    copies.append(pltpu.make_async_copy(exchange.at[ends], rows_e, sems.at[9]))
+    copies.append(pltpu.make_async_copy(coupling.at[ends], rows_c, sems.at[10]))
     for copy in copies:
         copy.start()
     for copy in copies:
@@ -94,6 +100,10 @@
             one[at : at + width] = jnp.where(even, high, low)
             two[at : at + width] = jnp.where(even, low, high)
             at += width
+    k = [conductivity_of(rows_t[0, i], rows_e[i]) for i in range(2)]
+    pick = lambda pair: jnp.where(odd, pair[1], pair[0])
+    early[M_S], early[M_G] = pick([rows_t[0, i] for i in range(2)]), pick([rows_t[1, i] for i in range(2)])
+    early[M_K], early[M_C], early[M_FY] = pick(k), pick([rows_c[i] for i in range(2)]), 0.5 * (k[0] + k[1])
 
 
 def load_kernel(temps, right, exchange, coupling, st, sems):
@@ -241,19 +251,40 @@
     return [s, g, st[K, e], st[C, e], fy, m_1s, m_1g, m_2s, m_2g]
 
 
-def write_message(refs, st, onward, edge):
-    ext = st.shape[2]
+def write_across(ref, k, value):
+    ext = value.shape[0]
+    if k >= EARLY:
+        ref[k - EARLY] = value[CROP : ext - CROP]
+    else:
+        ref[MESSAGE - EARLY, 8 * k : 8 * k + 4] = value[CROP:PAD]
+        ref[MESSAGE - EARLY, 8 * k + 4 : 8 * k + 8] = value[ext - PAD : ext - CROP]
+
+
+def read_across(early, across, outer, k):
+    ext = outer.shape[1]
+    if k >= EARLY:
+        outer[k, CROP : ext - CROP] = across[k - EARLY]
+    else:
+        outer[k, PAD : ext - PAD] = early[k]
+        outer[k, CROP:PAD] = across[MESSAGE - EARLY, 8 * k : 8 * k + 4]
+        outer[k, ext - PAD : ext - CROP] = across[MESSAGE - EARLY, 8 * k + 4 : 8 * k + 8]
+
+
+def write_beside(refs, k, value):
+    refs[k // THIRD][k % THIRD] = value[CROP : value.shape[0] - CROP]
+
+
+def read_beside(refs, outer, k):
+    outer[k, CROP : outer.shape[1] - CROP] = refs[k // THIRD][k % THIRD]
+
+
+def write_message(write, st, onward, edge):
     for go in (True, False):
 
         @pl.when(onward == go)
         def _():
             for k, value in enumerate(send_planes(st, go, edge)):
-                ref, at = message_plane(refs, k)
-                ref[at] = value[CROP : ext - CROP]
-
-
-def message_plane(refs, plane):
-    return (refs[0], plane) if len(refs) == 1 or plane < HALF else (refs[1], plane - HALF)
+                write(k, value)
 
 
 def first_kernel(st_in, one, two, st, across):
@@ -274,7 +305,7 @@
     ends = [2, 3, ny - 2, ny - 1]
     grouped(ends, lambda i: row_coefficients(st, i, mask))
     grouped(ends, lambda i: row_sweep(st, i, SA, SB, edge))
-    write_message([across], st, lax.axis_index("gy") % 2 == 1, edge)
+    write_message(functools.partial(write_across, across), st, lax.axis_index("gy") % 2 == 1, edge)
 
 
 def outer_residual(st, i, s_at, rs, rg, fy_out, edge, after):
@@ -313,8 +344,8 @@
     return [(coarse, (k, j), v) for k, v in enumerate(values)]
 
 
-def inner_kernel(st_in, one, two, st, coarse, beside_a, beside_b):
-    del st_in
+def inner_kernel(st_in, one, two, early, st, coarse, *beside):
+    del st_in, early
     planes, rows, ext, nz = st.shape
     ny, nx = rows - 2, ext - 2 * PAD
     shape = (ext, nz)
@@ -328,10 +359,10 @@
     for j in range(2, ny // 2 - 2):
         for ref, at, value in coarse_row(st, coarse, j, mask, edge):
             ref[at] = value
-    write_message([beside_a, beside_b], st, lax.axis_index("gy") % 2 == 0, edge)
-
-
-def end_work(st, coarse, extra, got, outer, is_after):
+    write_message(functools.partial(write_beside, beside), st, lax.axis_index("gy") % 2 == 0, edge)
+
+
+def end_work(st, coarse, extra, read, outer, is_after):
     planes, rows, ext, nz = st.shape
     ny, nx = rows - 2, ext - 2 * PAD
     me, count = lax.axis_index("gy"), lax.axis_size("gy")
@@ -342,8 +373,7 @@
     for k in range(MESSAGE):
         outer[k, :PAD] = zeros
         outer[k, ext - PAD :] = zeros
-        ref, at = message_plane(got, k)
-        outer[k, CROP : ext - CROP] = ref[at]
+        read(outer, k)
 
     o, e, near = (ny + 1, ny, ny) if is_after else (0, 1, 0)
     to_o = CONDUCT + FLOW if is_after else CONDUCT
@@ -381,26 +411,27 @@
         ref[at] = value
 
 
-def either_end(after, st, coarse, extra, got, outer):
+def either_end(after, st, coarse, extra, read, outer):
     for is_after in (True, False):
 
         @pl.when(after == is_after)
         def _():
-            end_work(st, coarse, extra, got, outer, is_after)
-
-
-def near_kernel(st_in, coarse_in, beside_a, beside_b, st, coarse, extra, outer):
+            end_work(st, coarse, extra, read, outer, is_after)
+
+
+def near_kernel(st_in, coarse_in, *refs):
+    beside, (st, coarse, extra, outer) = refs[:-4], refs[-4:]
     del st_in, coarse_in
-    either_end(lax.axis_index("gy") % 2 == 0, st, coarse, extra, [beside_a, beside_b], outer)
-
-
-def second_kernel(st_in, coarse_in, extra_in, across, *refs):
+    either_end(lax.axis_index("gy") % 2 == 0, st, coarse, extra, functools.partial(read_beside, beside), outer)
+
+
+def second_kernel(st_in, coarse_in, extra_in, early, across, *refs):
     st, coarse, extra, total, last_info, first_info, message, outer, squeeze = refs
     del st_in, coarse_in, extra_in
     planes, rows, ext, nz = st.shape
     ny, nx = rows - 2, ext - 2 * PAD
     me = lax.axis_index("gy")
-    either_end(me % 2 == 1, st, coarse, extra, [across], outer)
+    either_end(me % 2 == 1, st, coarse, extra, functools.partial(read_across, early, across), outer)
 
     blocks = ny // 2
     for k in range(4):
@@ -713,19 +744,19 @@
     ext = nx + 2 * PAD
     f32 = functools.partial(jax.ShapeDtypeStruct, dtype=jnp.float32)
 
-    height = (ny * STRIP_ROWS + 7) // 8 * 8
-    strips = f32((height, nz)), f32((height, nz))
-    scratch = [(2, 2, ny, 8, nz)] * 2 + [(2, ny, 8, nz)] * 2
-    one, two = pl.pallas_call(
+    strip = f32(((ny * STRIP_ROWS + 7) // 8 * 8, nz))
+    scratch = [(2, 2, ny, 8, nz)] * 2 + [(2, ny, 8, nz)] * 2 + [(2, 2, nx, nz), (2, nx, nz), (2, nx, nz)]
+    one, two, early = pl.pallas_call(
         pack_kernel,
-        out_shape=strips,
+        out_shape=(strip, strip, f32((EARLY, nx, nz))),
         in_specs=[HBM] * 4,
-        out_specs=(VMEM,) * 2,
-        scratch_shapes=[pltpu.VMEM(shape, jnp.float32) for shape in scratch] + [pltpu.SemaphoreType.DMA((8,))],
+        out_specs=(VMEM,) * 3,
+        scratch_shapes=[pltpu.VMEM(shape, jnp.float32) for shape in scratch] + [pltpu.SemaphoreType.DMA((11,))],
         compiler_params=PARAMS,
         name="pack_x",
     )(temps, right_side, exchange, coupling)
     one, two = swap(one, "gx", 0), swap(two, "gx", 1)
+    early = swap(early, "gy", 1)
 
     state = f32((PLANES, ny + 2, ext, nz))
 
@@ -744,7 +775,7 @@
     )(temps, right_side, exchange, coupling)
     st, across = pl.pallas_call(
         first_kernel,
-        out_shape=(state, letter(MESSAGE)),
+        out_shape=(state, letter(MESSAGE - EARLY + 1)),
         in_specs=[VMEM] * 3,
         out_specs=(VMEM,) * 2,
         input_output_aliases={0: 0},
@@ -754,18 +785,18 @@
     across = swap(across, "gy", 1)
 
     rows = f32((4, ny // 2, ext, nz))
-    st, coarse, beside_a, beside_b = pl.pallas_call(
+    st, coarse, *beside = pl.pallas_call(
         inner_kernel,
-        out_shape=(state, rows, letter(HALF), letter(MESSAGE - HALF)),
-        in_specs=[VMEM] * 3,
-        out_specs=(VMEM,) * 4,
+        out_shape=(state, rows) + (letter(THIRD),) * (MESSAGE // THIRD),
+        in_specs=[VMEM] * 4,
+        out_specs=(VMEM,) * (2 + MESSAGE // THIRD),
         input_output_aliases={0: 0},
         compiler_params=PARAMS,
         cost_estimate=cost(4 * ny, ext * nz),
         name="inner",
-    )(st, one, two)
-
-    beside_a, beside_b = swap(beside_a, "gy", 0), swap(beside_b, "gy", 0)
+    )(st, one, two, early)
+
+    beside = [swap(part, "gy", 0) for part in beside]
 
     lay = Rows(nx)
 
@@ -777,23 +808,23 @@
     st, coarse, extra = pl.pallas_call(
         near_kernel,
         out_shape=(state, rows, more),
-        in_specs=[VMEM] * 4,
+        in_specs=[VMEM] * (2 + len(beside)),
         out_specs=(VMEM,) * 3,
         scratch_shapes=[letter_room],
         input_output_aliases={0: 0, 1: 1},
         compiler_params=PARAMS,
         name="near",
-    )(st, coarse, beside_a, beside_b)
+    )(st, coarse, *beside)
     st, coarse, extra, total, last_info, first_info, message = pl.pallas_call(
         second_kernel,
         out_shape=(state, rows, more, tall(lay.map), tall(lay.info), tall(lay.info + lay.rest), tall(lay.full)),
-        in_specs=[VMEM] * 4,
+        in_specs=[VMEM] * 5,
         out_specs=(VMEM,) * 7,
         scratch_shapes=[letter_room, pltpu.VMEM((8, ext, nz), jnp.float32)],
         input_output_aliases={0: 0, 1: 1, 2: 2},
         compiler_params=PARAMS,
         name="second",
-    )(st, coarse, extra, across)
+    )(st, coarse, extra, early, across)
 
     near, messages = total, [message]
     radices, stride = stages(lax.axis_size("gy")), 1

time: 31.7 us -> 31.5 us (level)
  the two profiles are of different devices: /device:TPU:16 before, /device:TPU:9 now
where the time goes in v8:
time: 31.5 us; the launch traced here: 31.3 us
  starting transfers between devices  15.5 us (49%)
  Pallas kernels  9.27 us (29%)
  waiting for transfers between devices  6.37 us (20%)
    ppermute x7, starting transfers between devices, swap(): return lax.ppermute(x, axis, pairs)  11.6 us
    ppermute x4, waiting for transfers between devices, exchange_stage(): got.append(lax.ppermute(message, 'gy', pairs))  5.19 us
    ppermute x4, starting transfers between devices, exchange_stage(): got.append(lax.ppermute(message, 'gy', pairs))  3.9 us
    pallas_call x1, Pallas kernels, shards(): pl.pallas_call(functools.partial(third_kernel, radices[-1], stride), out_...  2.6 us
    pallas_call x1, Pallas kernels, shards(): pl.pallas_call(inner_kernel, out_shape=(state, rows) + (letter(THIRD),) *...  1.92 us
    pallas_call x1, Pallas kernels, shards(): pl.pallas_call(load_kernel, out_shape=state, in_specs=[HBM] * 4, out_spec...  1.49 us
    pallas_call x1, Pallas kernels, shards(): pl.pallas_call(pack_kernel, out_shape=(strip, strip, f32((EARLY, nx, nz))...  1.33 us
    ppermute x7, waiting for transfers between devices, swap(): return lax.ppermute(x, axis, pairs)  1.18 us
  transfers between devices with their start and end apart: 11, of which 6 were waited for; matrix products, arithmetic and copies ran while one was open for 0% of the time, Pallas kernels for 15%

profile of v8, /device:TPU:9, one launch (start us, length us, event | category | flops | bytes accessed | tf_op | source)
XLA Modules:
  0.0 31.3 jit_solution(1139945374749822425)
XLA Ops:
  0.0 1.3 %pack_x.1 = (f32[304,128]{1,0:T(8,128)S(1)}, f32[304,128]{1,0:T(8,128)S(1)}, f32[5,32,128]{2,1,0:T(8,128)S(1)}) custom-call(f32[2,12,32,128]{3,2,1,0:T(8,128)} %bitcast.5, f32[2,12,32,128]{3,2,1,0:T(8,128)} %bitcast.7, f32[12,32,128]{2,1,0:T(8,128)} %bitcast.9, f32[12,32,128]{2,1,0:T(8,128)} %bitcast.11), custom_call_target="tpu_custom_call" | custom-call | tf_op jit(solution)/shard_map/pack_x/pallas_call | solution.py:749
  1.3 0.1 collective-permute-start
  1.4 4.5 %collective-permute-start.1 = (f32[304,128]{1,0:T(8,128)S(1)}, f32[304,128]{1,0:T(8,128)S(1)}, u32[]{:S(2)}, u32[]{:S(2)}) collective-permute-start(f32[304,128]{1,0:T(8,128)S(1)} %get-tuple-element.30), channel_id=1, source_target_pairs={{8,16},{16,8},{9,17},{17,9},{10,18},{18,10},{11,19},{19,11},{12,20... | collective-permute-start | bytes 466952 | tf_op jit(solution)/shard_map/ppermute | solution.py:734
  5.9 4.2 %collective-permute-start.2 = (f32[5,32,128]{2,1,0:T(8,128)S(1)}, f32[5,32,128]{2,1,0:T(8,128)S(1)}, u32[]{:S(2)}, u32[]{:S(2)}) collective-permute-start(f32[5,32,128]{2,1,0:T(8,128)S(1)} %get-tuple-element.32), channel_id=1, source_target_pairs={{1,2},{2,1},{3,4},{4,3},{5,6},{6,5},{9,10},{10,9},{11,12},{12,11},... | collective-permute-start | bytes 245768 | tf_op jit(solution)/shard_map/ppermute | solution.py:734
  10.1 1.5 %load.1.st_in = f32[15,14,48,128]{3,2,1,0:T(8,128)S(1)} custom-call(f32[2,12,32,128]{3,2,1,0:T(8,128)} %bitcast.6, f32[2,12,32,128]{3,2,1,0:T(8,128)} %bitcast.8, f32[12,32,128]{2,1,0:T(8,128)} %bitcast.10, f32[12,32,128]{2,1,0:T(8,128)} %bitcast.12), custom_call_target="tpu_custom_call" | custom-call | flops 7372800 | bytes 9437184 | tf_op jit(solution)/shard_map/load/pallas_call | solution.py:766
  11.7 0.0 collective-permute-done.1.two
  11.7 0.6 %first.1 = (f32[15,14,48,128]{3,2,1,0:T(8,128)S(1)}, f32[5,40,128]{2,1,0:T(8,128)S(1)}) custom-call(f32[15,14,48,128]{3,2,1,0:T(8,128)S(1)} %load.1.st_in, f32[304,128]{1,0:T(8,128)S(1)} %collective-permute-done.one, f32[304,128]{1,0:T(8,128)S(1)} %collective-permute-done.1.two), custom_call_target="tpu_custom_call", output_to_operand_aliasing={{0}: (0, {})} | custom-call | tf_op jit(solution)/shard_map/first/pallas_call | solution.py:776
  12.3 2.2 %collective-permute-start.6 = (f32[5,40,128]{2,1,0:T(8,128)S(1)}, f32[5,40,128]{2,1,0:T(8,128)S(1)}, u32[]{:S(2)}, u32[]{:S(2)}) collective-permute-start(f32[5,40,128]{2,1,0:T(8,128)S(1)} %get-tuple-element.41), channel_id=1, source_target_pairs={{1,2},{2,1},{3,4},{4,3},{5,6},{6,5},{9,10},{10,9},{11,12},{12,11},... | collective-permute-start | bytes 307208 | tf_op jit(solution)/shard_map/ppermute | solution.py:734
  14.5 1.9 %inner.1 = (f32[15,14,48,128]{3,2,1,0:T(8,128)S(1)}, f32[4,6,48,128]{3,2,1,0:T(8,128)S(1)}, f32[3,40,128]{2,1,0:T(8,128)S(1)}, f32[3,40,128]{2,1,0:T(8,128)S(1)}, f32[3,40,128]{2,1,0:T(8,128)S(1)}) custom-call(f32[15,14,48,128]{3,2,1,0:T(8,128)S(1)} %get-tuple-element.31.st_in, ...), custom_call_target="tpu_custom_call", output_to_operand_aliasing={{0}: (0, {})} | custom-call | flops 14745600 | bytes 18874368 | tf_op jit(solution)/shard_map/inner/pallas_call | solution.py:788
  16.4 0.1 collective-permute-start.3
  16.5 0.5 %collective-permute-start.4 = (f32[3,40,128]{2,1,0:T(8,128)S(1)}, f32[3,40,128]{2,1,0:T(8,128)S(1)}, u32[]{:S(2)}, u32[]{:S(2)}) collective-permute-start(f32[3,40,128]{2,1,0:T(8,128)S(1)} %get-tuple-element.36), channel_id=1, source_target_pairs={{0,1},{1,0},{2,3},{3,2},{4,5},{5,4},{6,7},{7,6},{8,9},{9,8},{10,11... | collective-permute-start | bytes 184328 | tf_op jit(solution)/shard_map/ppermute | solution.py:734
  17.0 0.1 collective-permute-start.5
  17.1 0.7 %collective-permute-done.3.refs_0_ = f32[3,40,128]{2,1,0:T(8,128)S(1)} collective-permute-done((f32[3,40,128]{2,1,0:T(8,128)S(1)}, f32[3,40,128]{2,1,0:T(8,128)S(1)}, u32[]{:S(2)}, u32[]{:S(2)}) %collective-permute-start.3) | collective-permute-done | bytes 61472 | tf_op jit(solution)/shard_map/ppermute | solution.py:734
  17.7 0.2 collective-permute-done.4.refs_1_
  17.9 0.4 %collective-permute-done.5.refs_2_ = f32[3,40,128]{2,1,0:T(8,128)S(1)} collective-permute-done((f32[3,40,128]{2,1,0:T(8,128)S(1)}, f32[3,40,128]{2,1,0:T(8,128)S(1)}, u32[]{:S(2)}, u32[]{:S(2)}) %collective-permute-start.5) | collective-permute-done | bytes 61472 | tf_op jit(solution)/shard_map/ppermute | solution.py:734
  18.2 0.6 %near.1 = (f32[15,14,48,128]{3,2,1,0:T(8,128)S(1)}, f32[4,6,48,128]{3,2,1,0:T(8,128)S(1)}, f32[6,48,128]{2,1,0:T(8,128)S(1)}) custom-call(f32[15,14,48,128]{3,2,1,0:T(8,128)S(1)} %get-tuple-element.33.st_in, f32[4,6,48,128]{3,2,1,0:T(8,128)S(1)} %get-tuple-element.34.coarse_in, ...), custom_call_target="tpu_custom_call", output_to_operand_aliasing={{0}: (0, {}), {1}: (1, {})} | custom-call | tf_op jit(solution)/shard_map/near/pallas_call | solution.py:808
  18.8 0.7 %second.1 = (f32[15,14,48,128]{3,2,1,0:T(8,128)S(1)}, f32[4,6,48,128]{3,2,1,0:T(8,128)S(1)}, f32[6,48,128]{2,1,0:T(8,128)S(1)}, f32[40,128]{1,0:T(8,128)S(1)}, f...) custom-call(f32[15,14,48,128]{3,2,1,0:T(8,128)S(1)} %get-tuple-eleme, ...), custom_call_target="tpu_custom_call", output_to_operand_aliasing={{0}: (0, {}), {1}: (1, {}), {2}: (2, {})} | custom-call | tf_op jit(solution)/shard_map/second/pallas_call | solution.py:818
  19.6 0.2 collective-permute-start.7
  19.8 1.1 %collective-permute-done.7.refs_4_ = f32[176,128]{1,0:T(8,128)S(1)} collective-permute-done((f32[176,128]{1,0:T(8,128)S(1)}, f32[176,128]{1,0:T(8,128)S(1)}, u32[]{:S(2)}, u32[]{:S(2)}) %collective-permute-start.7) | collective-permute-done | bytes 90144 | tf_op jit(solution)/shard_map/ppermute | solution.py:521
  21.0 2.5 %collective-permute-start.8 = (f32[144,128]{1,0:T(8,128)S(1)}, f32[144,128]{1,0:T(8,128)S(1)}, u32[]{:S(2)}, u32[]{:S(2)}) collective-permute-start(f32[144,128]{1,0:T(8,128)S(1)} %get-tuple-element.50), channel_id=1, source_target_pairs={{7,0},{6,1},{5,2},{4,3},{3,4},{2,5},{1,6},{0,7},{15,8},{14,9},{13,... | collective-permute-start | bytes 221192 | tf_op jit(solution)/shard_map/ppermute | solution.py:521
  23.4 1.2 %collective-permute-start.9 = (f32[144,128]{1,0:T(8,128)S(1)}, f32[144,128]{1,0:T(8,128)S(1)}, u32[]{:S(2)}, u32[]{:S(2)}) collective-permute-start(f32[144,128]{1,0:T(8,128)S(1)} %get-tuple-element.51), channel_id=1, source_target_pairs={{3,0},{2,1},{1,2},{0,3},{7,4},{6,5},{5,6},{4,7},{11,8},{10,9},{9,1... | collective-permute-start | bytes 221192 | tf_op jit(solution)/shard_map/ppermute | solution.py:521
  24.6 3.5 %collective-permute-done.10.refs_6_ = f32[40,128]{1,0:T(8,128)S(1)} collective-permute-done((f32[40,128]{1,0:T(8,128)S(1)}, f32[40,128]{1,0:T(8,128)S(1)}, u32[]{:S(2)}, u32[]{:S(2)}) %collective-permute-start.10) | collective-permute-done | bytes 20512 | tf_op jit(solution)/shard_map/ppermute | solution.py:521
  28.2 0.6 %collective-permute-done.9.refs_5_ = f32[144,128]{1,0:T(8,128)S(1)} collective-permute-done((f32[144,128]{1,0:T(8,128)S(1)}, f32[144,128]{1,0:T(8,128)S(1)}, u32[]{:S(2)}, u32[]{:S(2)}) %collective-permute-start.9) | collective-permute-done | bytes 73760 | tf_op jit(solution)/shard_map/ppermute | solution.py:521
  28.7 2.6 %third.1 = f32[2,12,32,128]{3,2,1,0:T(8,128)} custom-call(f32[15,14,48,128]{3,2,1,0:T(8,128)S(1)} %get-tuple-element.42.refs_0_, f32[6,48,128]{2,1,0:T(8,128)S(1)} %get-tuple-element.43.refs_1_, f32[4,6,48,128]{3,2,1,0:T(8,128)S(1)} %get-tuple-element.44.refs_2_, f32[280,128]{1,0:T(8,128)S(1)} %get-tuple-element.49.refs_3_, ...), custom_call_target="tpu_custom_call" | custom-call | tf_op jit(solution)/shard_map/third/pallas_call | solution.py:849
  (6 shorter events, 0.1 us)
Async XLA Ops:
  1.3 10.3 %collective-permute-start = (f32[304,128]{1,0:T(8,128)S(1)}, f32[304,128]{1,0:T(8,128)S(1)}, u32[]{:S(2)}, u32[]{:S(2)}) collective-permute-start(f32[304,128]{1,0:T(8,128)S(1)} %get-tuple-element.29), channel_id=1, source_target_pairs={{0,8},{8,0},{16,24},{24,16},{1,9},{9,1},{17,25},{25,17},{2,10},{10... | collective-permute-start | bytes 466952 | tf_op jit(solution)/shard_map/ppermute | solution.py:734
  1.4 10.2 %collective-permute-start.1 = (f32[304,128]{1,0:T(8,128)S(1)}, f32[304,128]{1,0:T(8,128)S(1)}, u32[]{:S(2)}, u32[]{:S(2)}) collective-permute-start(f32[304,128]{1,0:T(8,128)S(1)} %get-tuple-element.30), channel_id=1, source_target_pairs={{8,16},{16,8},{9,17},{17,9},{10,18},{18,10},{11,19},{19,11},{12,20... | collective-permute-start | bytes 466952 | tf_op jit(solution)/shard_map/ppermute | solution.py:734
  5.9 8.6 %collective-permute-start.2 = (f32[5,32,128]{2,1,0:T(8,128)S(1)}, f32[5,32,128]{2,1,0:T(8,128)S(1)}, u32[]{:S(2)}, u32[]{:S(2)}) collective-permute-start(f32[5,32,128]{2,1,0:T(8,128)S(1)} %get-tuple-element.32), channel_id=1, source_target_pairs={{1,2},{2,1},{3,4},{4,3},{5,6},{6,5},{9,10},{10,9},{11,12},{12,11},... | collective-permute-start | bytes 245768 | tf_op jit(solution)/shard_map/ppermute | solution.py:734
  12.3 6.6 %collective-permute-start.6 = (f32[5,40,128]{2,1,0:T(8,128)S(1)}, f32[5,40,128]{2,1,0:T(8,128)S(1)}, u32[]{:S(2)}, u32[]{:S(2)}) collective-permute-start(f32[5,40,128]{2,1,0:T(8,128)S(1)} %get-tuple-element.41), channel_id=1, source_target_pairs={{1,2},{2,1},{3,4},{4,3},{5,6},{6,5},{9,10},{10,9},{11,12},{12,11},... | collective-permute-start | bytes 307208 | tf_op jit(solution)/shard_map/ppermute | solution.py:734
  16.4 1.3 %collective-permute-start.3 = (f32[3,40,128]{2,1,0:T(8,128)S(1)}, f32[3,40,128]{2,1,0:T(8,128)S(1)}, u32[]{:S(2)}, u32[]{:S(2)}) collective-permute-start(f32[3,40,128]{2,1,0:T(8,128)S(1)} %get-tuple-element.35), channel_id=1, source_target_pairs={{0,1},{1,0},{2,3},{3,2},{4,5},{5,4},{6,7},{7,6},{8,9},{9,8},{10,11... | collective-permute-start | bytes 184328 | tf_op jit(solution)/shard_map/ppermute | solution.py:734
  16.5 1.4 %collective-permute-start.4 = (f32[3,40,128]{2,1,0:T(8,128)S(1)}, f32[3,40,128]{2,1,0:T(8,128)S(1)}, u32[]{:S(2)}, u32[]{:S(2)}) collective-permute-start(f32[3,40,128]{2,1,0:T(8,128)S(1)} %get-tuple-element.36), channel_id=1, source_target_pairs={{0,1},{1,0},{2,3},{3,2},{4,5},{5,4},{6,7},{7,6},{8,9},{9,8},{10,11... | collective-permute-start | bytes 184328 | tf_op jit(solution)/shard_map/ppermute | solution.py:734
  17.0 1.2 %collective-permute-start.5 = (f32[3,40,128]{2,1,0:T(8,128)S(1)}, f32[3,40,128]{2,1,0:T(8,128)S(1)}, u32[]{:S(2)}, u32[]{:S(2)}) collective-permute-start(f32[3,40,128]{2,1,0:T(8,128)S(1)} %get-tuple-element.37), channel_id=1, source_target_pairs={{0,1},{1,0},{2,3},{3,2},{4,5},{5,4},{6,7},{7,6},{8,9},{9,8},{10,11... | collective-permute-start | bytes 184328 | tf_op jit(solution)/shard_map/ppermute | solution.py:734
  19.6 1.4 %collective-permute-start.7 = (f32[176,128]{1,0:T(8,128)S(1)}, f32[176,128]{1,0:T(8,128)S(1)}, u32[]{:S(2)}, u32[]{:S(2)}) collective-permute-start(f32[176,128]{1,0:T(8,128)S(1)} %get-tuple-element.48), channel_id=1, source_target_pairs={{1,0},{0,1},{3,2},{2,3},{5,4},{4,5},{7,6},{6,7},{9,8},{8,9},{11,10... | collective-permute-start | bytes 270344 | tf_op jit(solution)/shard_map/ppermute | solution.py:521
  21.0 7.2 %collective-permute-start.8 = (f32[144,128]{1,0:T(8,128)S(1)}, f32[144,128]{1,0:T(8,128)S(1)}, u32[]{:S(2)}, u32[]{:S(2)}) collective-permute-start(f32[144,128]{1,0:T(8,128)S(1)} %get-tuple-element.50), channel_id=1, source_target_pairs={{7,0},{6,1},{5,2},{4,3},{3,4},{2,5},{1,6},{0,7},{15,8},{14,9},{13,... | collective-permute-start | bytes 221192 | tf_op jit(solution)/shard_map/ppermute | solution.py:521
  23.4 5.3 %collective-permute-start.9 = (f32[144,128]{1,0:T(8,128)S(1)}, f32[144,128]{1,0:T(8,128)S(1)}, u32[]{:S(2)}, u32[]{:S(2)}) collective-permute-start(f32[144,128]{1,0:T(8,128)S(1)} %get-tuple-element.51), channel_id=1, source_target_pairs={{3,0},{2,1},{1,2},{0,3},{7,4},{6,5},{5,6},{4,7},{11,8},{10,9},{9,1... | collective-permute-start | bytes 221192 | tf_op jit(solution)/shard_map/ppermute | solution.py:521
  24.6 3.5 %collective-permute-start.10 = (f32[40,128]{1,0:T(8,128)S(1)}, f32[40,128]{1,0:T(8,128)S(1)}, u32[]{:S(2)}, u32[]{:S(2)}) collective-permute-start(f32[40,128]{1,0:T(8,128)S(1)} %get-tuple-element.52), channel_id=1, source_target_pairs={{5,0},{4,1},{7,2},{6,3},{1,4},{0,5},{3,6},{2,7},{13,8},{12,9},{15,... | collective-permute-start | bytes 61448 | tf_op jit(solution)/shard_map/ppermute | solution.py:521

commit v9 on v8

--- a/solution.py
+++ b/solution.py
@@ -18,7 +18,7 @@
 (M_S, M_G, M_K, M_C, M_FY, M_1S, M_1G, M_2S, M_2G) = range(9)
 MESSAGE, EARLY, THIRD = 9, 5, 3
 
-GROUP = 3
+GROUP = 4
 
 VMEM = pl.BlockSpec(memory_space=pltpu.VMEM)
 HBM = pl.BlockSpec(memory_space=pltpu.HBM)
@@ -71,7 +71,7 @@
     return [s[four], g[four], k[five], rs[four], rg[four], c[four]]
 
 
-def pack_kernel(temps, right, exchange, coupling, one, two, early, *scratch):
+def pack_kernel(temps, right, exchange, coupling, one, two, early, st, *scratch):
     pair_low, pair_high, single_low, single_high, rows_t, rows_e, rows_c, sems = scratch
     even = lax.axis_index("gx") % 2 == 0
     odd = lax.axis_index("gy") % 2 == 1
@@ -86,7 +86,13 @@
     copies.append(pltpu.make_async_copy(temps.at[:, ends], rows_t, sems.at[8]))
     copies.append(pltpu.make_async_copy(exchange.at[ends], rows_e, sems.at[9]))
     copies.append(pltpu.make_async_copy(coupling.at[ends], rows_c, sems.at[10]))
-    for copy in copies:
+    loads = []
+    for k, (plane, ref) in enumerate(
+        ((SA, temps.at[0]), (K, exchange), (GA, temps.at[1]), (RS, right.at[0]), (RG, right.at[1]), (C, coupling))
+    ):
+        to = st.at[plane, pl.ds(1, ny), pl.ds(PAD, nx)]
+        loads.append(pltpu.make_async_copy(ref, to, sems.at[11 + k]))
+    for copy in copies + loads:
         copy.start()
     for copy in copies:
         copy.wait()
@@ -104,37 +110,20 @@
     pick = lambda pair: jnp.where(odd, pair[1], pair[0])
     early[M_S], early[M_G] = pick([rows_t[0, i] for i in range(2)]), pick([rows_t[1, i] for i in range(2)])
     early[M_K], early[M_C], early[M_FY] = pick(k), pick([rows_c[i] for i in range(2)]), 0.5 * (k[0] + k[1])
-
-
-def load_kernel(temps, right, exchange, coupling, st, sems):
-    ny, nx, nz = exchange.shape
+    for copy in loads:
+        copy.wait()
+
+
+def conduct_kernel(st_in, st):
+    del st_in
     planes, rows, ext, nz = st.shape
-    copies = []
-    for k, (plane, ref) in enumerate(
-        ((SA, temps.at[0]), (K, exchange), (GA, temps.at[1]), (RS, right.at[0]), (RG, right.at[1]), (C, coupling))
-    ):
-        to = st.at[plane, pl.ds(1, ny), pl.ds(PAD, nx)]
-        copies.append(pltpu.make_async_copy(ref, to, sems.at[k]))
-    for copy in copies:
-        copy.start()
+    own = slice(PAD, ext - PAD)
     zeros = jnp.zeros((PAD, nz), jnp.float32)
-
-    def clear(i, carry):
+    for i in range(1, rows - 1):
+        st[K, i, own] = conductivity_of(st[SA, i, own], st[K, i, own])
         for plane, width in STRIP:
             st[plane, i, :PAD] = zeros
-            st[plane, i, PAD + nx :] = zeros
-        return carry
-
-    lax.fori_loop(1, ny + 1, clear, 0)
-    for copy in copies:
-        copy.wait()
-
-    def conduct(i, carry):
-        s = st[SA, i, PAD : PAD + nx]
-        st[K, i, PAD : PAD + nx] = conductivity_of(s, st[K, i, PAD : PAD + nx])
-        return carry
-
-    lax.fori_loop(1, ny + 1, conduct, 0)
+            st[plane, i, ext - PAD :] = zeros
 
 
 def place_halo(st, one, two, y, nx):
@@ -746,33 +735,32 @@
 
     strip = f32(((ny * STRIP_ROWS + 7) // 8 * 8, nz))
     scratch = [(2, 2, ny, 8, nz)] * 2 + [(2, ny, 8, nz)] * 2 + [(2, 2, nx, nz), (2, nx, nz), (2, nx, nz)]
-    one, two, early = pl.pallas_call(
+    state = f32((PLANES, ny + 2, ext, nz))
+    one, two, early, st = pl.pallas_call(
         pack_kernel,
-        out_shape=(strip, strip, f32((EARLY, nx, nz))),
+        out_shape=(strip, strip, f32((EARLY, nx, nz)), state),
         in_specs=[HBM] * 4,
-        out_specs=(VMEM,) * 3,
-        scratch_shapes=[pltpu.VMEM(shape, jnp.float32) for shape in scratch] + [pltpu.SemaphoreType.DMA((11,))],
+        out_specs=(VMEM,) * 4,
+        scratch_shapes=[pltpu.VMEM(shape, jnp.float32) for shape in scratch] + [pltpu.SemaphoreType.DMA((17,))],
         compiler_params=PARAMS,
         name="pack_x",
     )(temps, right_side, exchange, coupling)
     one, two = swap(one, "gx", 0), swap(two, "gx", 1)
     early = swap(early, "gy", 1)
 
-    state = f32((PLANES, ny + 2, ext, nz))
-
     def letter(planes):
         return f32((planes, ext - 2 * CROP, nz))
 
     st = pl.pallas_call(
-        load_kernel,
+        conduct_kernel,
         out_shape=state,
-        in_specs=[HBM] * 4,
+        in_specs=[VMEM],
         out_specs=VMEM,
-        scratch_shapes=[pltpu.SemaphoreType.DMA((6,))],
+        input_output_aliases={0: 0},
         compiler_params=PARAMS,
         cost_estimate=cost(2 * ny, ext * nz),
-        name="load",
-    )(temps, right_side, exchange, coupling)
+        name="conduct",
+    )(st)
     st, across = pl.pallas_call(
         first_kernel,
         out_shape=(state, letter(MESSAGE - EARLY + 1)),

time: 31.5 us -> 30.7 us (0.975)
  the two profiles are of different devices: /device:TPU:9 before, /device:TPU:17 now
where the time goes in v9:
time: 30.7 us; the launch traced here: 30.5 us
  starting transfers between devices  16 us (52%)
  Pallas kernels  7.99 us (26%)
  waiting for transfers between devices  6.4 us (21%)
    ppermute x7, starting transfers between devices, swap(): return lax.ppermute(x, axis, pairs)  12.7 us
    ppermute x4, waiting for transfers between devices, exchange_stage(): got.append(lax.ppermute(message, 'gy', pairs))  4.74 us
    ppermute x4, starting transfers between devices, exchange_stage(): got.append(lax.ppermute(message, 'gy', pairs))  3.25 us
    pallas_call x1, Pallas kernels, shards(): pl.pallas_call(functools.partial(third_kernel, radices[-1], stride), out_...  2.37 us
    pallas_call x1, Pallas kernels, shards(): pl.pallas_call(inner_kernel, out_shape=(state, rows) + (letter(THIRD),) *...  1.93 us
    pallas_call x1, Pallas kernels, shards(): pl.pallas_call(pack_kernel, out_shape=(strip, strip, f32((EARLY, nx, nz))...  1.7 us
    ppermute x7, waiting for transfers between devices, swap(): return lax.ppermute(x, axis, pairs)  1.67 us
    pallas_call x1, Pallas kernels, shards(): pl.pallas_call(second_kernel, out_shape=(state, rows, more, tall(lay.map)...  0.7 us
  transfers between devices with their start and end apart: 11, of which 7 were waited for; matrix products, arithmetic and copies ran while one was open for 0% of the time, Pallas kernels for 10%

profile of v9, /device:TPU:17, one launch (start us, length us, event | category | flops | bytes accessed | tf_op | source)
XLA Modules:
  0.0 30.5 jit_solution(696742676661816236)
XLA Ops:
  0.0 1.7 %pack_x.1 = (f32[304,128]{1,0:T(8,128)S(1)}, f32[304,128]{1,0:T(8,128)S(1)}, f32[5,32,128]{2,1,0:T(8,128)S(1)}, f32[15,14,48,128]{3,2,1,0:T(8,128)S(1)}) custom-call(f32[2,12,32,128]{3,2,1,0:T(8,128)} %bitcast.5, f32[2,12,32,128]{3,2,1,0:T(8,128)} %bitcast.6, f32[12,32,128]{2,1,0:T(8,128)} %bitcast.7, f32[12,32,128]{2,1,0:T(8,128)} %bitcast.8), custom_call_target="tpu_custom_call" | custom-call | tf_op jit(solution)/shard_map/pack_x/pallas_call | solution.py:739
  1.7 1.4 %collective-permute-start = (f32[304,128]{1,0:T(8,128)S(1)}, f32[304,128]{1,0:T(8,128)S(1)}, u32[]{:S(2)}, u32[]{:S(2)}) collective-permute-start(f32[304,128]{1,0:T(8,128)S(1)} %get-tuple-element.31), channel_id=1, source_target_pairs={{0,8},{8,0},{16,24},{24,16},{1,9},{9,1},{17,25},{25,17},{2,10},{10... | collective-permute-start | bytes 466952 | tf_op jit(solution)/shard_map/ppermute | solution.py:723
  3.1 1.9 %collective-permute-start.1 = (f32[304,128]{1,0:T(8,128)S(1)}, f32[304,128]{1,0:T(8,128)S(1)}, u32[]{:S(2)}, u32[]{:S(2)}) collective-permute-start(f32[304,128]{1,0:T(8,128)S(1)} %get-tuple-element.32), channel_id=1, source_target_pairs={{8,16},{16,8},{9,17},{17,9},{10,18},{18,10},{11,19},{19,11},{12,20... | collective-permute-start | bytes 466952 | tf_op jit(solution)/shard_map/ppermute | solution.py:723
  5.0 4.0 %collective-permute-start.2 = (f32[5,32,128]{2,1,0:T(8,128)S(1)}, f32[5,32,128]{2,1,0:T(8,128)S(1)}, u32[]{:S(2)}, u32[]{:S(2)}) collective-permute-start(f32[5,32,128]{2,1,0:T(8,128)S(1)} %get-tuple-element.34), channel_id=1, source_target_pairs={{1,2},{2,1},{3,4},{4,3},{5,6},{6,5},{9,10},{10,9},{11,12},{12,11},... | collective-permute-start | bytes 245768 | tf_op jit(solution)/shard_map/ppermute | solution.py:723
  9.0 0.5 %collective-permute-done.1.two = f32[304,128]{1,0:T(8,128)S(1)} collective-permute-done((f32[304,128]{1,0:T(8,128)S(1)}, f32[304,128]{1,0:T(8,128)S(1)}, u32[]{:S(2)}, u32[]{:S(2)}) %collective-permute-start.1) | collective-permute-done | bytes 155680 | tf_op jit(solution)/shard_map/ppermute | solution.py:723
  9.5 0.6 %first.1 = (f32[15,14,48,128]{3,2,1,0:T(8,128)S(1)}, f32[5,40,128]{2,1,0:T(8,128)S(1)}) custom-call(f32[15,14,48,128]{3,2,1,0:T(8,128)S(1)} %conduct.1.st_in, f32[304,128]{1,0:T(8,128)S(1)} %collective-permute-done.one, f32[304,128]{1,0:T(8,128)S(1)} %collective-permute-done.1.two), custom_call_target="tpu_custom_call", output_to_operand_aliasing={{0}: (0, {})} | custom-call | tf_op jit(solution)/shard_map/first/pallas_call | solution.py:764
  10.1 4.9 %collective-permute-start.6 = (f32[5,40,128]{2,1,0:T(8,128)S(1)}, f32[5,40,128]{2,1,0:T(8,128)S(1)}, u32[]{:S(2)}, u32[]{:S(2)}) collective-permute-start(f32[5,40,128]{2,1,0:T(8,128)S(1)} %get-tuple-element.43), channel_id=1, source_target_pairs={{1,2},{2,1},{3,4},{4,3},{5,6},{6,5},{9,10},{10,9},{11,12},{12,11},... | collective-permute-start | bytes 307208 | tf_op jit(solution)/shard_map/ppermute | solution.py:723
  15.0 1.9 %inner.1 = (f32[15,14,48,128]{3,2,1,0:T(8,128)S(1)}, f32[4,6,48,128]{3,2,1,0:T(8,128)S(1)}, f32[3,40,128]{2,1,0:T(8,128)S(1)}, f32[3,40,128]{2,1,0:T(8,128)S(1)}, f32[3,40,128]{2,1,0:T(8,128)S(1)}) custom-call(f32[15,14,48,128]{3,2,1,0:T(8,128)S(1)} %get-tuple-element.33.st_in, ...), custom_call_target="tpu_custom_call", output_to_operand_aliasing={{0}: (0, {})} | custom-call | flops 14745600 | bytes 18874368 | tf_op jit(solution)/shard_map/inner/pallas_call | solution.py:776
  16.9 0.1 collective-permute-start.3
  17.0 0.5 %collective-permute-start.4 = (f32[3,40,128]{2,1,0:T(8,128)S(1)}, f32[3,40,128]{2,1,0:T(8,128)S(1)}, u32[]{:S(2)}, u32[]{:S(2)}) collective-permute-start(f32[3,40,128]{2,1,0:T(8,128)S(1)} %get-tuple-element.38), channel_id=1, source_target_pairs={{0,1},{1,0},{2,3},{3,2},{4,5},{5,4},{6,7},{7,6},{8,9},{9,8},{10,11... | collective-permute-start | bytes 184328 | tf_op jit(solution)/shard_map/ppermute | solution.py:723
  17.5 0.1 collective-permute-start.5
  17.6 0.7 %collective-permute-done.3.refs_0_ = f32[3,40,128]{2,1,0:T(8,128)S(1)} collective-permute-done((f32[3,40,128]{2,1,0:T(8,128)S(1)}, f32[3,40,128]{2,1,0:T(8,128)S(1)}, u32[]{:S(2)}, u32[]{:S(2)}) %collective-permute-start.3) | collective-permute-done | bytes 61472 | tf_op jit(solution)/shard_map/ppermute | solution.py:723
  18.3 0.2 collective-permute-done.4.refs_1_
  18.4 0.4 %collective-permute-done.5.refs_2_ = f32[3,40,128]{2,1,0:T(8,128)S(1)} collective-permute-done((f32[3,40,128]{2,1,0:T(8,128)S(1)}, f32[3,40,128]{2,1,0:T(8,128)S(1)}, u32[]{:S(2)}, u32[]{:S(2)}) %collective-permute-start.5) | collective-permute-done | bytes 61472 | tf_op jit(solution)/shard_map/ppermute | solution.py:723
  18.8 0.6 %near.1 = (f32[15,14,48,128]{3,2,1,0:T(8,128)S(1)}, f32[4,6,48,128]{3,2,1,0:T(8,128)S(1)}, f32[6,48,128]{2,1,0:T(8,128)S(1)}) custom-call(f32[15,14,48,128]{3,2,1,0:T(8,128)S(1)} %get-tuple-element.35.st_in, f32[4,6,48,128]{3,2,1,0:T(8,128)S(1)} %get-tuple-element.36.coarse_in, ...), custom_call_target="tpu_custom_call", output_to_operand_aliasing={{0}: (0, {}), {1}: (1, {})} | custom-call | tf_op jit(solution)/shard_map/near/pallas_call | solution.py:796
  19.4 0.7 %second.1 = (f32[15,14,48,128]{3,2,1,0:T(8,128)S(1)}, f32[4,6,48,128]{3,2,1,0:T(8,128)S(1)}, f32[6,48,128]{2,1,0:T(8,128)S(1)}, f32[40,128]{1,0:T(8,128)S(1)}, f...) custom-call(f32[15,14,48,128]{3,2,1,0:T(8,128)S(1)} %get-tuple-eleme, ...), custom_call_target="tpu_custom_call", output_to_operand_aliasing={{0}: (0, {}), {1}: (1, {}), {2}: (2, {})} | custom-call | tf_op jit(solution)/shard_map/second/pallas_call | solution.py:806
  20.1 0.2 collective-permute-start.7
  20.3 1.1 %collective-permute-done.7.refs_4_ = f32[176,128]{1,0:T(8,128)S(1)} collective-permute-done((f32[176,128]{1,0:T(8,128)S(1)}, f32[176,128]{1,0:T(8,128)S(1)}, u32[]{:S(2)}, u32[]{:S(2)}) %collective-permute-start.7) | collective-permute-done | bytes 90144 | tf_op jit(solution)/shard_map/ppermute | solution.py:510
  21.5 1.0 %collective-permute-start.8 = (f32[144,128]{1,0:T(8,128)S(1)}, f32[144,128]{1,0:T(8,128)S(1)}, u32[]{:S(2)}, u32[]{:S(2)}) collective-permute-start(f32[144,128]{1,0:T(8,128)S(1)} %get-tuple-element.52), channel_id=1, source_target_pairs={{7,0},{6,1},{5,2},{4,3},{3,4},{2,5},{1,6},{0,7},{15,8},{14,9},{13,... | collective-permute-start | bytes 221192 | tf_op jit(solution)/shard_map/ppermute | solution.py:510
  22.5 1.7 %collective-permute-start.9 = (f32[144,128]{1,0:T(8,128)S(1)}, f32[144,128]{1,0:T(8,128)S(1)}, u32[]{:S(2)}, u32[]{:S(2)}) collective-permute-start(f32[144,128]{1,0:T(8,128)S(1)} %get-tuple-element.53), channel_id=1, source_target_pairs={{3,0},{2,1},{1,2},{0,3},{7,4},{6,5},{5,6},{4,7},{11,8},{10,9},{9,1... | collective-permute-start | bytes 221192 | tf_op jit(solution)/shard_map/ppermute | solution.py:510
  24.3 0.3 collective-permute-start.10
  24.5 3.2 %collective-permute-done.10.refs_6_ = f32[40,128]{1,0:T(8,128)S(1)} collective-permute-done((f32[40,128]{1,0:T(8,128)S(1)}, f32[40,128]{1,0:T(8,128)S(1)}, u32[]{:S(2)}, u32[]{:S(2)}) %collective-permute-start.10) | collective-permute-done | bytes 20512 | tf_op jit(solution)/shard_map/ppermute | solution.py:510
  27.8 0.4 %collective-permute-done.9.refs_5_ = f32[144,128]{1,0:T(8,128)S(1)} collective-permute-done((f32[144,128]{1,0:T(8,128)S(1)}, f32[144,128]{1,0:T(8,128)S(1)}, u32[]{:S(2)}, u32[]{:S(2)}) %collective-permute-start.9) | collective-permute-done | bytes 73760 | tf_op jit(solution)/shard_map/ppermute | solution.py:510
  28.1 2.4 %third.1 = f32[2,12,32,128]{3,2,1,0:T(8,128)} custom-call(f32[15,14,48,128]{3,2,1,0:T(8,128)S(1)} %get-tuple-element.44.refs_0_, f32[6,48,128]{2,1,0:T(8,128)S(1)} %get-tuple-element.45.refs_1_, f32[4,6,48,128]{3,2,1,0:T(8,128)S(1)} %get-tuple-element.46.refs_2_, f32[280,128]{1,0:T(8,128)S(1)} %get-tuple-element.51.refs_3_, ...), custom_call_target="tpu_custom_call" | custom-call | tf_op jit(solution)/shard_map/third/pallas_call | solution.py:837
  (6 shorter events, 0.1 us)
Async XLA Ops:
  1.7 7.3 %collective-permute-start = (f32[304,128]{1,0:T(8,128)S(1)}, f32[304,128]{1,0:T(8,128)S(1)}, u32[]{:S(2)}, u32[]{:S(2)}) collective-permute-start(f32[304,128]{1,0:T(8,128)S(1)} %get-tuple-element.31), channel_id=1, source_target_pairs={{0,8},{8,0},{16,24},{24,16},{1,9},{9,1},{17,25},{25,17},{2,10},{10... | collective-permute-start | bytes 466952 | tf_op jit(solution)/shard_map/ppermute | solution.py:723
  3.1 6.5 %collective-permute-start.1 = (f32[304,128]{1,0:T(8,128)S(1)}, f32[304,128]{1,0:T(8,128)S(1)}, u32[]{:S(2)}, u32[]{:S(2)}) collective-permute-start(f32[304,128]{1,0:T(8,128)S(1)} %get-tuple-element.32), channel_id=1, source_target_pairs={{8,16},{16,8},{9,17},{17,9},{10,18},{18,10},{11,19},{19,11},{12,20... | collective-permute-start | bytes 466952 | tf_op jit(solution)/shard_map/ppermute | solution.py:723
  5.0 10.0 %collective-permute-start.2 = (f32[5,32,128]{2,1,0:T(8,128)S(1)}, f32[5,32,128]{2,1,0:T(8,128)S(1)}, u32[]{:S(2)}, u32[]{:S(2)}) collective-permute-start(f32[5,32,128]{2,1,0:T(8,128)S(1)} %get-tuple-element.34), channel_id=1, source_target_pairs={{1,2},{2,1},{3,4},{4,3},{5,6},{6,5},{9,10},{10,9},{11,12},{12,11},... | collective-permute-start | bytes 245768 | tf_op jit(solution)/shard_map/ppermute | solution.py:723
  10.1 9.2 %collective-permute-start.6 = (f32[5,40,128]{2,1,0:T(8,128)S(1)}, f32[5,40,128]{2,1,0:T(8,128)S(1)}, u32[]{:S(2)}, u32[]{:S(2)}) collective-permute-start(f32[5,40,128]{2,1,0:T(8,128)S(1)} %get-tuple-element.43), channel_id=1, source_target_pairs={{1,2},{2,1},{3,4},{4,3},{5,6},{6,5},{9,10},{10,9},{11,12},{12,11},... | collective-permute-start | bytes 307208 | tf_op jit(solution)/shard_map/ppermute | solution.py:723
  16.9 1.3 %collective-permute-start.3 = (f32[3,40,128]{2,1,0:T(8,128)S(1)}, f32[3,40,128]{2,1,0:T(8,128)S(1)}, u32[]{:S(2)}, u32[]{:S(2)}) collective-permute-start(f32[3,40,128]{2,1,0:T(8,128)S(1)} %get-tuple-element.37), channel_id=1, source_target_pairs={{0,1},{1,0},{2,3},{3,2},{4,5},{5,4},{6,7},{7,6},{8,9},{9,8},{10,11... | collective-permute-start | bytes 184328 | tf_op jit(solution)/shard_map/ppermute | solution.py:723
  17.0 1.4 %collective-permute-start.4 = (f32[3,40,128]{2,1,0:T(8,128)S(1)}, f32[3,40,128]{2,1,0:T(8,128)S(1)}, u32[]{:S(2)}, u32[]{:S(2)}) collective-permute-start(f32[3,40,128]{2,1,0:T(8,128)S(1)} %get-tuple-element.38), channel_id=1, source_target_pairs={{0,1},{1,0},{2,3},{3,2},{4,5},{5,4},{6,7},{7,6},{8,9},{9,8},{10,11... | collective-permute-start | bytes 184328 | tf_op jit(solution)/shard_map/ppermute | solution.py:723
  17.5 1.2 %collective-permute-start.5 = (f32[3,40,128]{2,1,0:T(8,128)S(1)}, f32[3,40,128]{2,1,0:T(8,128)S(1)}, u32[]{:S(2)}, u32[]{:S(2)}) collective-permute-start(f32[3,40,128]{2,1,0:T(8,128)S(1)} %get-tuple-element.39), channel_id=1, source_target_pairs={{0,1},{1,0},{2,3},{3,2},{4,5},{5,4},{6,7},{7,6},{8,9},{9,8},{10,11... | collective-permute-start | bytes 184328 | tf_op jit(solution)/shard_map/ppermute | solution.py:723
  20.1 1.4 %collective-permute-start.7 = (f32[176,128]{1,0:T(8,128)S(1)}, f32[176,128]{1,0:T(8,128)S(1)}, u32[]{:S(2)}, u32[]{:S(2)}) collective-permute-start(f32[176,128]{1,0:T(8,128)S(1)} %get-tuple-element.50), channel_id=1, source_target_pairs={{1,0},{0,1},{3,2},{2,3},{5,4},{4,5},{7,6},{6,7},{9,8},{8,9},{11,10... | collective-permute-start | bytes 270344 | tf_op jit(solution)/shard_map/ppermute | solution.py:510
  21.5 6.3 %collective-permute-start.8 = (f32[144,128]{1,0:T(8,128)S(1)}, f32[144,128]{1,0:T(8,128)S(1)}, u32[]{:S(2)}, u32[]{:S(2)}) collective-permute-start(f32[144,128]{1,0:T(8,128)S(1)} %get-tuple-element.52), channel_id=1, source_target_pairs={{7,0},{6,1},{5,2},{4,3},{3,4},{2,5},{1,6},{0,7},{15,8},{14,9},{13,... | collective-permute-start | bytes 221192 | tf_op jit(solution)/shard_map/ppermute | solution.py:510
  22.5 5.6 %collective-permute-start.9 = (f32[144,128]{1,0:T(8,128)S(1)}, f32[144,128]{1,0:T(8,128)S(1)}, u32[]{:S(2)}, u32[]{:S(2)}) collective-permute-start(f32[144,128]{1,0:T(8,128)S(1)} %get-tuple-element.53), channel_id=1, source_target_pairs={{3,0},{2,1},{1,2},{0,3},{7,4},{6,5},{5,6},{4,7},{11,8},{10,9},{9,1... | collective-permute-start | bytes 221192 | tf_op jit(solution)/shard_map/ppermute | solution.py:510
  24.3 3.5 %collective-permute-start.10 = (f32[40,128]{1,0:T(8,128)S(1)}, f32[40,128]{1,0:T(8,128)S(1)}, u32[]{:S(2)}, u32[]{:S(2)}) collective-permute-start(f32[40,128]{1,0:T(8,128)S(1)} %get-tuple-element.54), channel_id=1, source_target_pairs={{5,0},{4,1},{7,2},{6,3},{1,4},{0,5},{3,6},{2,7},{13,8},{12,9},{15,... | collective-permute-start | bytes 61448 | tf_op jit(solution)/shard_map/ppermute | solution.py:510

commit v10 on v9

--- a/solution.py
+++ b/solution.py
@@ -16,7 +16,7 @@
 (SA, GA, SB, GB, K, C, RS, RG, FX, FZ, H, FY, ASS, ASG, AGG) = range(15)
 PLANES = 15
 (M_S, M_G, M_K, M_C, M_FY, M_1S, M_1G, M_2S, M_2G) = range(9)
-MESSAGE, EARLY, THIRD = 9, 5, 3
+MESSAGE, EARLY, THIRD = 9, 7, 3
 
 GROUP = 4
 
@@ -71,47 +71,43 @@
     return [s[four], g[four], k[five], rs[four], rg[four], c[four]]
 
 
-def pack_kernel(temps, right, exchange, coupling, one, two, early, st, *scratch):
-    pair_low, pair_high, single_low, single_high, rows_t, rows_e, rows_c, sems = scratch
+def pack_kernel(temps, right, exchange, coupling, one, two, early, st, sems):
     even = lax.axis_index("gx") % 2 == 0
     odd = lax.axis_index("gy") % 2 == 1
     ny, nx, nz = exchange.shape
     copies = []
-    for k, ref in enumerate((temps, right, exchange, coupling)):
-        low, high, at = (pair_low, pair_high, k) if k < 2 else (single_low, single_high, k - 2)
-        lead = (slice(None),) * (ref.ndim - 2)
-        copies.append(pltpu.make_async_copy(ref.at[lead + (slice(0, 8),)], low.at[at], sems.at[2 * k]))
-        copies.append(pltpu.make_async_copy(ref.at[lead + (slice(nx - 8, nx),)], high.at[at], sems.at[2 * k + 1]))
-    ends = pl.ds(jnp.where(odd, ny - 2, 0), 2)
-    copies.append(pltpu.make_async_copy(temps.at[:, ends], rows_t, sems.at[8]))
-    copies.append(pltpu.make_async_copy(exchange.at[ends], rows_e, sems.at[9]))
-    copies.append(pltpu.make_async_copy(coupling.at[ends], rows_c, sems.at[10]))
-    loads = []
     for k, (plane, ref) in enumerate(
-        ((SA, temps.at[0]), (K, exchange), (GA, temps.at[1]), (RS, right.at[0]), (RG, right.at[1]), (C, coupling))
+        ((SA, temps.at[0]), (K, exchange), (GA, temps.at[1]), (C, coupling), (RS, right.at[0]), (RG, right.at[1]))
     ):
         to = st.at[plane, pl.ds(1, ny), pl.ds(PAD, nx)]
-        loads.append(pltpu.make_async_copy(ref, to, sems.at[11 + k]))
-    for copy in copies + loads:
+        copies.append(pltpu.make_async_copy(ref, to, sems.at[k]))
+    for copy in copies:
         copy.start()
     for copy in copies:
         copy.wait()
     at = 0
-    for y in range(ny):
+    for i in range(1, ny + 1):
         sides = []
-        for pair, single, is_low in ((pair_low, single_low, True), (pair_high, single_high, False)):
-            s, g, rs, rg = (pair[i, j, y] for i in range(2) for j in range(2))
-            sides.append(strip_values(s, g, conductivity_of(s, single[0, y]), rs, rg, single[1, y], is_low))
+        for start in (PAD, PAD + nx - 8):
+            s, g, e, rs, rg, c = (st[plane, i, start : start + 8] for plane in (SA, GA, K, RS, RG, C))
+            sides.append(strip_values(s, g, conductivity_of(s, e), rs, rg, c, start == PAD))
         for low, high, (plane, width) in zip(*sides, STRIP):
             one[at : at + width] = jnp.where(even, high, low)
             two[at : at + width] = jnp.where(even, low, high)
             at += width
-    k = [conductivity_of(rows_t[0, i], rows_e[i]) for i in range(2)]
-    pick = lambda pair: jnp.where(odd, pair[1], pair[0])
-    early[M_S], early[M_G] = pick([rows_t[0, i] for i in range(2)]), pick([rows_t[1, i] for i in range(2)])
-    early[M_K], early[M_C], early[M_FY] = pick(k), pick([rows_c[i] for i in range(2)]), 0.5 * (k[0] + k[1])
-    for copy in loads:
-        copy.wait()
+    own = slice(PAD, PAD + nx)
+    for is_odd, e, d in ((True, ny, ny - 1), (False, 1, 2)):
+
+        @pl.when(odd == is_odd)
+        def _():
+            s, s_d, g, g_d = st[SA, e, own], st[SA, d, own], st[GA, e, own], st[GA, d, own]
+            c, k, k_d = st[C, e, own], conductivity_of(s, st[K, e, own]), conductivity_of(s_d, st[K, d, own])
+            fx, fz, h, _ = faces(k)
+            fy = 0.5 * (k + k_d)
+            part_s, part_g = inner(s, g, c, h, fx, fz, edge_weights((nx, nz)))
+            m_1s, m_1g = first_partial(st[RS, e, own] + part_s, st[RG, e, own] + part_g, s, s_d, g, g_d, fy, is_odd)
+            for plane, value in enumerate((s, g, k, c, fy, m_1s, m_1g)):
+                early[plane] = value
 
 
 def conduct_kernel(st_in, st):
@@ -228,35 +224,47 @@
     return [(st, (target, i), s), (st, (target + 1, i), g)]
 
 
+def first_partial(res_s, res_g, s, s_d, g, g_d, fy, onward):
+    return res_s + fy * (s_d - s), res_g + CONDUCT * g_d - FLOW * (g - g_d if onward else g)
+
+
 def send_planes(st, onward, edge):
     ny = st.shape[1] - 2
     e, d, near = (ny, ny - 1, ny - 1) if onward else (1, 2, 1)
     fy, s, g, g_d = st[FY, near], st[SA, e], st[GA, e], st[GA, d]
     part_s, part_g = row_inner(st, e, SA, edge)
-    m_1s = st[RS, e] + part_s + fy * (st[SA, d] - s)
-    m_1g = st[RG, e] + part_g + CONDUCT * g_d - FLOW * (g - g_d if onward else g)
+    m_1s, m_1g = first_partial(st[RS, e] + part_s, st[RG, e] + part_g, s, st[SA, d], g, g_d, fy, onward)
     m_2s = st[RS, e] + fy * st[SB, d]
     m_2g = st[RG, e] + (CONDUCT + FLOW if onward else CONDUCT) * st[GB, d]
     return [s, g, st[K, e], st[C, e], fy, m_1s, m_1g, m_2s, m_2g]
 
 
+def across_parts(ext):
+    parts, at = [], 0
+    for k in range(EARLY, MESSAGE):
+        parts.append((k, CROP, ext - CROP, at))
+        at += ext - 2 * CROP
+    for k in range(EARLY):
+        more = 1 if k in (M_1S, M_1G) else 0
+        for low, high in ((CROP, PAD + more), (ext - PAD - more, ext - CROP)):
+            parts.append((k, low, high, at))
+            at += high - low
+    return parts, (at + 7) // 8 * 8
+
+
 def write_across(ref, k, value):
-    ext = value.shape[0]
-    if k >= EARLY:
-        ref[k - EARLY] = value[CROP : ext - CROP]
-    else:
-        ref[MESSAGE - EARLY, 8 * k : 8 * k + 4] = value[CROP:PAD]
-        ref[MESSAGE - EARLY, 8 * k + 4 : 8 * k + 8] = value[ext - PAD : ext - CROP]
+    for plane, low, high, at in across_parts(value.shape[0])[0]:
+        if plane == k:
+            ref[at : at + high - low] = value[low:high]
 
 
 def read_across(early, across, outer, k):
     ext = outer.shape[1]
-    if k >= EARLY:
-        outer[k, CROP : ext - CROP] = across[k - EARLY]
-    else:
+    if k < EARLY:
         outer[k, PAD : ext - PAD] = early[k]
-        outer[k, CROP:PAD] = across[MESSAGE - EARLY, 8 * k : 8 * k + 4]
-        outer[k, ext - PAD : ext - CROP] = across[MESSAGE - EARLY, 8 * k + 4 : 8 * k + 8]
+    for plane, low, high, at in across_parts(ext)[0]:
+        if plane == k:
+            outer[k, low:high] = across[at : at + high - low]
 
 
 def write_beside(refs, k, value):
@@ -276,7 +284,7 @@
                 write(k, value)
 
 
-def first_kernel(st_in, one, two, st, across):
+def first_kernel(st_in, one, two, st, across, *beside):
     del st_in
     planes, rows, ext, nz = st.shape
     ny, nx = rows - 2, ext - 2 * PAD
@@ -294,7 +302,9 @@
     ends = [2, 3, ny - 2, ny - 1]
     grouped(ends, lambda i: row_coefficients(st, i, mask))
     grouped(ends, lambda i: row_sweep(st, i, SA, SB, edge))
-    write_message(functools.partial(write_across, across), st, lax.axis_index("gy") % 2 == 1, edge)
+    odd = lax.axis_index("gy") % 2 == 1
+    write_message(functools.partial(write_across, across), st, odd, edge)
+    write_message(functools.partial(write_beside, beside), st, jnp.logical_not(odd), edge)
 
 
 def outer_residual(st, i, s_at, rs, rg, fy_out, edge, after):
@@ -333,7 +343,7 @@
     return [(coarse, (k, j), v) for k, v in enumerate(values)]
 
 
-def inner_kernel(st_in, one, two, early, st, coarse, *beside):
+def inner_kernel(st_in, one, two, early, st, coarse):
     del st_in, early
     planes, rows, ext, nz = st.shape
     ny, nx = rows - 2, ext - 2 * PAD
@@ -348,7 +358,6 @@
     for j in range(2, ny // 2 - 2):
         for ref, at, value in coarse_row(st, coarse, j, mask, edge):
             ref[at] = value
-    write_message(functools.partial(write_beside, beside), st, lax.axis_index("gy") % 2 == 0, edge)
 
 
 def end_work(st, coarse, extra, read, outer, is_after):
@@ -734,14 +743,13 @@
     f32 = functools.partial(jax.ShapeDtypeStruct, dtype=jnp.float32)
 
     strip = f32(((ny * STRIP_ROWS + 7) // 8 * 8, nz))
-    scratch = [(2, 2, ny, 8, nz)] * 2 + [(2, ny, 8, nz)] * 2 + [(2, 2, nx, nz), (2, nx, nz), (2, nx, nz)]
     state = f32((PLANES, ny + 2, ext, nz))
     one, two, early, st = pl.pallas_call(
         pack_kernel,
         out_shape=(strip, strip, f32((EARLY, nx, nz)), state),
         in_specs=[HBM] * 4,
         out_specs=(VMEM,) * 4,
-        scratch_shapes=[pltpu.VMEM(shape, jnp.float32) for shape in scratch] + [pltpu.SemaphoreType.DMA((17,))],
+        scratch_shapes=[pltpu.SemaphoreType.DMA((6,))],
         compiler_params=PARAMS,
         name="pack_x",
     )(temps, right_side, exchange, coupling)
@@ -761,11 +769,11 @@
         cost_estimate=cost(2 * ny, ext * nz),
         name="conduct",
     )(st)
-    st, across = pl.pallas_call(
+    st, across, *beside = pl.pallas_call(
         first_kernel,
-        out_shape=(state, letter(MESSAGE - EARLY + 1)),
+        out_shape=(state, f32((across_parts(ext)[1], nz))) + (letter(THIRD),) * (MESSAGE // THIRD),
         in_specs=[VMEM] * 3,
-        out_specs=(VMEM,) * 2,
+        out_specs=(VMEM,) * (2 + MESSAGE // THIRD),
         input_output_aliases={0: 0},
         compiler_params=PARAMS,
         name="first",
@@ -773,11 +781,11 @@
     across = swap(across, "gy", 1)
 
     rows = f32((4, ny // 2, ext, nz))
-    st, coarse, *beside = pl.pallas_call(
+    st, coarse = pl.pallas_call(
         inner_kernel,
-        out_shape=(state, rows) + (letter(THIRD),) * (MESSAGE // THIRD),
+        out_shape=(state, rows),
         in_specs=[VMEM] * 4,
-        out_specs=(VMEM,) * (2 + MESSAGE // THIRD),
+        out_specs=(VMEM,) * 2,
         input_output_aliases={0: 0},
         compiler_params=PARAMS,
         cost_estimate=cost(4 * ny, ext * nz),

time: 30.7 us -> 29.4 us (0.958)
  the two profiles are of different devices: /device:TPU:17 before, /device:TPU:16 now
where the time goes in v10:
time: 29.4 us; the launch traced here: 28.9 us
  starting transfers between devices  11.5 us (39%)
  waiting for transfers between devices  9.81 us (33%)
  Pallas kernels  7.45 us (25%)
    ppermute x7, starting transfers between devices, swap(): return lax.ppermute(x, axis, pairs)  8.31 us
    ppermute x4, waiting for transfers between devices, exchange_stage(): got.append(lax.ppermute(message, 'gy', pairs))  5.11 us
    ppermute x7, waiting for transfers between devices, swap(): return lax.ppermute(x, axis, pairs)  4.71 us
    ppermute x4, starting transfers between devices, exchange_stage(): got.append(lax.ppermute(message, 'gy', pairs))  3.19 us
    pallas_call x1, Pallas kernels, shards(): pl.pallas_call(functools.partial(third_kernel, radices[-1], stride), out_...  2.22 us
    pallas_call x1, Pallas kernels, shards(): pl.pallas_call(inner_kernel, out_shape=(state, rows), in_specs=[VMEM] * 4...  1.7 us
    pallas_call x1, Pallas kernels, shards(): pl.pallas_call(pack_kernel, out_shape=(strip, strip, f32((EARLY, nx, nz))...  1.65 us
    pallas_call x1, Pallas kernels, shards(): pl.pallas_call(second_kernel, out_shape=(state, rows, more, tall(lay.map)...  0.62 us
  transfers between devices with their start and end apart: 11, of which 5 were waited for; matrix products, arithmetic and copies ran while one was open for 0% of the time, Pallas kernels for 10%

profile of v10, /device:TPU:16, one launch (start us, length us, event | category | flops | bytes accessed | tf_op | source)
XLA Modules:
  0.0 28.9 jit_solution(3990564321192383411)
XLA Ops:
  0.0 1.6 %pack_x.1 = (f32[304,128]{1,0:T(8,128)S(1)}, f32[304,128]{1,0:T(8,128)S(1)}, f32[7,32,128]{2,1,0:T(8,128)S(1)}, f32[15,14,48,128]{3,2,1,0:T(8,128)S(1)}) custom-call(f32[2,12,32,128]{3,2,1,0:T(8,128)} %bitcast.5, f32[2,12,32,128]{3,2,1,0:T(8,128)} %bitcast.6, f32[12,32,128]{2,1,0:T(8,128)} %bitcast.7, f32[12,32,128]{2,1,0:T(8,128)} %bitcast.8), custom_call_target="tpu_custom_call" | custom-call | tf_op jit(solution)/shard_map/pack_x/pallas_call | solution.py:747
  1.7 1.6 %collective-permute-start = (f32[304,128]{1,0:T(8,128)S(1)}, f32[304,128]{1,0:T(8,128)S(1)}, u32[]{:S(2)}, u32[]{:S(2)}) collective-permute-start(f32[304,128]{1,0:T(8,128)S(1)} %get-tuple-element.31), channel_id=1, source_target_pairs={{0,8},{8,0},{16,24},{24,16},{1,9},{9,1},{17,25},{25,17},{2,10},{10... | collective-permute-start | bytes 466952 | tf_op jit(solution)/shard_map/ppermute | solution.py:732
  3.3 1.9 %collective-permute-start.1 = (f32[304,128]{1,0:T(8,128)S(1)}, f32[304,128]{1,0:T(8,128)S(1)}, u32[]{:S(2)}, u32[]{:S(2)}) collective-permute-start(f32[304,128]{1,0:T(8,128)S(1)} %get-tuple-element.32), channel_id=1, source_target_pairs={{8,16},{16,8},{9,17},{17,9},{10,18},{18,10},{11,19},{19,11},{12,20... | collective-permute-start | bytes 466952 | tf_op jit(solution)/shard_map/ppermute | solution.py:732
  5.2 0.7 %collective-permute-start.2 = (f32[7,32,128]{2,1,0:T(8,128)S(1)}, f32[7,32,128]{2,1,0:T(8,128)S(1)}, u32[]{:S(2)}, u32[]{:S(2)}) collective-permute-start(f32[7,32,128]{2,1,0:T(8,128)S(1)} %get-tuple-element.34), channel_id=1, source_target_pairs={{1,2},{2,1},{3,4},{4,3},{5,6},{6,5},{9,10},{10,9},{11,12},{12,11},... | collective-permute-start | bytes 344072 | tf_op jit(solution)/shard_map/ppermute | solution.py:732
  5.9 0.1 conduct.1.st_in
  6.0 1.5 %collective-permute-done.one = f32[304,128]{1,0:T(8,128)S(1)} collective-permute-done((f32[304,128]{1,0:T(8,128)S(1)}, f32[304,128]{1,0:T(8,128)S(1)}, u32[]{:S(2)}, u32[]{:S(2)}) %collective-permute-start) | collective-permute-done | bytes 155680 | tf_op jit(solution)/shard_map/ppermute | solution.py:732
  7.5 3.2 %collective-permute-done.1.two = f32[304,128]{1,0:T(8,128)S(1)} collective-permute-done((f32[304,128]{1,0:T(8,128)S(1)}, f32[304,128]{1,0:T(8,128)S(1)}, u32[]{:S(2)}, u32[]{:S(2)}) %collective-permute-start.1) | collective-permute-done | bytes 155680 | tf_op jit(solution)/shard_map/ppermute | solution.py:732
  10.7 0.6 %first.1 = (f32[15,14,48,128]{3,2,1,0:T(8,128)S(1)}, f32[144,128]{1,0:T(8,128)S(1)}, f32[3,40,128]{2,1,0:T(8,128)S(1)}, f32[3,40,128]{2,1,0:T(8,128)S(1)}, f32[3,40,128]{2,1,0:T(8,128)S(1)}) custom-call(f32[15,14,48,128]{3,2,1,0:T(8,128)S(1)} %conduct.1.st_in, f32[304,128]{1,0:T(8,128)S(1)} %collective-permute-done.one, ...), custom_call_target="tpu_custom_call", output_to_operand_aliasing={{0}: (0, {})} | custom-call | tf_op jit(solution)/shard_map/first/pallas_call | solution.py:772
  11.2 0.7 %collective-permute-start.6 = (f32[144,128]{1,0:T(8,128)S(1)}, f32[144,128]{1,0:T(8,128)S(1)}, u32[]{:S(2)}, u32[]{:S(2)}) collective-permute-start(f32[144,128]{1,0:T(8,128)S(1)} %get-tuple-element.43), channel_id=1, source_target_pairs={{1,2},{2,1},{3,4},{4,3},{5,6},{6,5},{9,10},{10,9},{11,12},{12,11},... | collective-permute-start | bytes 221192 | tf_op jit(solution)/shard_map/ppermute | solution.py:732
  11.9 2.9 %collective-permute-start.3 = (f32[3,40,128]{2,1,0:T(8,128)S(1)}, f32[3,40,128]{2,1,0:T(8,128)S(1)}, u32[]{:S(2)}, u32[]{:S(2)}) collective-permute-start(f32[3,40,128]{2,1,0:T(8,128)S(1)} %get-tuple-element.37), channel_id=1, source_target_pairs={{0,1},{1,0},{2,3},{3,2},{4,5},{5,4},{6,7},{7,6},{8,9},{9,8},{10,11... | collective-permute-start | bytes 184328 | tf_op jit(solution)/shard_map/ppermute | solution.py:732
  14.8 0.1 collective-permute-start.4
  14.9 0.4 %collective-permute-start.5 = (f32[3,40,128]{2,1,0:T(8,128)S(1)}, f32[3,40,128]{2,1,0:T(8,128)S(1)}, u32[]{:S(2)}, u32[]{:S(2)}) collective-permute-start(f32[3,40,128]{2,1,0:T(8,128)S(1)} %get-tuple-element.39), channel_id=1, source_target_pairs={{0,1},{1,0},{2,3},{3,2},{4,5},{5,4},{6,7},{7,6},{8,9},{9,8},{10,11... | collective-permute-start | bytes 184328 | tf_op jit(solution)/shard_map/ppermute | solution.py:732
  15.3 0.0 collective-permute-done.2.early
  15.3 1.7 %inner.1 = (f32[15,14,48,128]{3,2,1,0:T(8,128)S(1)}, f32[4,6,48,128]{3,2,1,0:T(8,128)S(1)}) custom-call(f32[15,14,48,128]{3,2,1,0:T(8,128)S(1)} %get-tuple-element.33.st_in, f32[304,128]{1,0:T(8,128)S(1)} %collective-permute-done.one, f32[304,128]{1,0:T(8,128)S(1)} %collective-permute-done.1.two, ...), custom_call_target="tpu_custom_call", output_to_operand_aliasing={{0}: (0, {})} | custom-call | flops 14745600 | bytes 18874368 | tf_op jit(solution)/shard_map/inner/pallas_call | solution.py:784
  17.1 0.6 %near.1 = (f32[15,14,48,128]{3,2,1,0:T(8,128)S(1)}, f32[4,6,48,128]{3,2,1,0:T(8,128)S(1)}, f32[6,48,128]{2,1,0:T(8,128)S(1)}) custom-call(f32[15,14,48,128]{3,2,1,0:T(8,128)S(1)} %get-tuple-element.35.st_in, f32[4,6,48,128]{3,2,1,0:T(8,128)S(1)} %get-tuple-element.36.coarse_in, ...), custom_call_target="tpu_custom_call", output_to_operand_aliasing={{0}: (0, {}), {1}: (1, {})} | custom-call | tf_op jit(solution)/shard_map/near/pallas_call | solution.py:804
  17.7 0.6 %second.1 = (f32[15,14,48,128]{3,2,1,0:T(8,128)S(1)}, f32[4,6,48,128]{3,2,1,0:T(8,128)S(1)}, f32[6,48,128]{2,1,0:T(8,128)S(1)}, f32[40,128]{1,0:T(8,128)S(1)}, f...) custom-call(f32[15,14,48,128]{3,2,1,0:T(8,128)S(1)} %get-tuple-eleme, ...), custom_call_target="tpu_custom_call", output_to_operand_aliasing={{0}: (0, {}), {1}: (1, {}), {2}: (2, {})} | custom-call | tf_op jit(solution)/shard_map/second/pallas_call | solution.py:814
  18.3 0.1 collective-permute-start.7
  18.4 1.2 %collective-permute-done.7.refs_4_ = f32[176,128]{1,0:T(8,128)S(1)} collective-permute-done((f32[176,128]{1,0:T(8,128)S(1)}, f32[176,128]{1,0:T(8,128)S(1)}, u32[]{:S(2)}, u32[]{:S(2)}) %collective-permute-start.7) | collective-permute-done | bytes 90144 | tf_op jit(solution)/shard_map/ppermute | solution.py:519
  19.7 1.5 %collective-permute-start.8 = (f32[144,128]{1,0:T(8,128)S(1)}, f32[144,128]{1,0:T(8,128)S(1)}, u32[]{:S(2)}, u32[]{:S(2)}) collective-permute-start(f32[144,128]{1,0:T(8,128)S(1)} %get-tuple-element.52), channel_id=1, source_target_pairs={{7,0},{6,1},{5,2},{4,3},{3,4},{2,5},{1,6},{0,7},{15,8},{14,9},{13,... | collective-permute-start | bytes 221192 | tf_op jit(solution)/shard_map/ppermute | solution.py:519
  21.2 1.4 %collective-permute-start.9 = (f32[144,128]{1,0:T(8,128)S(1)}, f32[144,128]{1,0:T(8,128)S(1)}, u32[]{:S(2)}, u32[]{:S(2)}) collective-permute-start(f32[144,128]{1,0:T(8,128)S(1)} %get-tuple-element.53), channel_id=1, source_target_pairs={{3,0},{2,1},{1,2},{0,3},{7,4},{6,5},{5,6},{4,7},{11,8},{10,9},{9,1... | collective-permute-start | bytes 221192 | tf_op jit(solution)/shard_map/ppermute | solution.py:519
  22.6 0.2 collective-permute-start.10
  22.8 3.0 %collective-permute-done.10.refs_6_ = f32[40,128]{1,0:T(8,128)S(1)} collective-permute-done((f32[40,128]{1,0:T(8,128)S(1)}, f32[40,128]{1,0:T(8,128)S(1)}, u32[]{:S(2)}, u32[]{:S(2)}) %collective-permute-start.10) | collective-permute-done | bytes 20512 | tf_op jit(solution)/shard_map/ppermute | solution.py:519
  25.8 0.9 %collective-permute-done.9.refs_5_ = f32[144,128]{1,0:T(8,128)S(1)} collective-permute-done((f32[144,128]{1,0:T(8,128)S(1)}, f32[144,128]{1,0:T(8,128)S(1)}, u32[]{:S(2)}, u32[]{:S(2)}) %collective-permute-start.9) | collective-permute-done | bytes 73760 | tf_op jit(solution)/shard_map/ppermute | solution.py:519
  26.7 2.2 %third.1 = f32[2,12,32,128]{3,2,1,0:T(8,128)} custom-call(f32[15,14,48,128]{3,2,1,0:T(8,128)S(1)} %get-tuple-element.44.refs_0_, f32[6,48,128]{2,1,0:T(8,128)S(1)} %get-tuple-element.45.refs_1_, f32[4,6,48,128]{3,2,1,0:T(8,128)S(1)} %get-tuple-element.46.refs_2_, f32[280,128]{1,0:T(8,128)S(1)} %get-tuple-element.51.refs_3_, ...), custom_call_target="tpu_custom_call" | custom-call | tf_op jit(solution)/shard_map/third/pallas_call | solution.py:845
  (6 shorter events, 0.1 us)
Async XLA Ops:
  1.7 5.8 %collective-permute-start = (f32[304,128]{1,0:T(8,128)S(1)}, f32[304,128]{1,0:T(8,128)S(1)}, u32[]{:S(2)}, u32[]{:S(2)}) collective-permute-start(f32[304,128]{1,0:T(8,128)S(1)} %get-tuple-element.31), channel_id=1, source_target_pairs={{0,8},{8,0},{16,24},{24,16},{1,9},{9,1},{17,25},{25,17},{2,10},{10... | collective-permute-start | bytes 466952 | tf_op jit(solution)/shard_map/ppermute | solution.py:732
  3.3 7.4 %collective-permute-start.1 = (f32[304,128]{1,0:T(8,128)S(1)}, f32[304,128]{1,0:T(8,128)S(1)}, u32[]{:S(2)}, u32[]{:S(2)}) collective-permute-start(f32[304,128]{1,0:T(8,128)S(1)} %get-tuple-element.32), channel_id=1, source_target_pairs={{8,16},{16,8},{9,17},{17,9},{10,18},{18,10},{11,19},{19,11},{12,20... | collective-permute-start | bytes 466952 | tf_op jit(solution)/shard_map/ppermute | solution.py:732
  5.2 10.1 %collective-permute-start.2 = (f32[7,32,128]{2,1,0:T(8,128)S(1)}, f32[7,32,128]{2,1,0:T(8,128)S(1)}, u32[]{:S(2)}, u32[]{:S(2)}) collective-permute-start(f32[7,32,128]{2,1,0:T(8,128)S(1)} %get-tuple-element.34), channel_id=1, source_target_pairs={{1,2},{2,1},{3,4},{4,3},{5,6},{6,5},{9,10},{10,9},{11,12},{12,11},... | collective-permute-start | bytes 344072 | tf_op jit(solution)/shard_map/ppermute | solution.py:732
  11.2 6.4 %collective-permute-start.6 = (f32[144,128]{1,0:T(8,128)S(1)}, f32[144,128]{1,0:T(8,128)S(1)}, u32[]{:S(2)}, u32[]{:S(2)}) collective-permute-start(f32[144,128]{1,0:T(8,128)S(1)} %get-tuple-element.43), channel_id=1, source_target_pairs={{1,2},{2,1},{3,4},{4,3},{5,6},{6,5},{9,10},{10,9},{11,12},{12,11},... | collective-permute-start | bytes 221192 | tf_op jit(solution)/shard_map/ppermute | solution.py:732
  11.9 5.1 %collective-permute-start.3 = (f32[3,40,128]{2,1,0:T(8,128)S(1)}, f32[3,40,128]{2,1,0:T(8,128)S(1)}, u32[]{:S(2)}, u32[]{:S(2)}) collective-permute-start(f32[3,40,128]{2,1,0:T(8,128)S(1)} %get-tuple-element.37), channel_id=1, source_target_pairs={{0,1},{1,0},{2,3},{3,2},{4,5},{5,4},{6,7},{7,6},{8,9},{9,8},{10,11... | collective-permute-start | bytes 184328 | tf_op jit(solution)/shard_map/ppermute | solution.py:732
  14.8 2.2 %collective-permute-start.4 = (f32[3,40,128]{2,1,0:T(8,128)S(1)}, f32[3,40,128]{2,1,0:T(8,128)S(1)}, u32[]{:S(2)}, u32[]{:S(2)}) collective-permute-start(f32[3,40,128]{2,1,0:T(8,128)S(1)} %get-tuple-element.38), channel_id=1, source_target_pairs={{0,1},{1,0},{2,3},{3,2},{4,5},{5,4},{6,7},{7,6},{8,9},{9,8},{10,11... | collective-permute-start | bytes 184328 | tf_op jit(solution)/shard_map/ppermute | solution.py:732
  14.9 2.2 %collective-permute-start.5 = (f32[3,40,128]{2,1,0:T(8,128)S(1)}, f32[3,40,128]{2,1,0:T(8,128)S(1)}, u32[]{:S(2)}, u32[]{:S(2)}) collective-permute-start(f32[3,40,128]{2,1,0:T(8,128)S(1)} %get-tuple-element.39), channel_id=1, source_target_pairs={{0,1},{1,0},{2,3},{3,2},{4,5},{5,4},{6,7},{7,6},{8,9},{9,8},{10,11... | collective-permute-start | bytes 184328 | tf_op jit(solution)/shard_map/ppermute | solution.py:732
  18.3 1.4 %collective-permute-start.7 = (f32[176,128]{1,0:T(8,128)S(1)}, f32[176,128]{1,0:T(8,128)S(1)}, u32[]{:S(2)}, u32[]{:S(2)}) collective-permute-start(f32[176,128]{1,0:T(8,128)S(1)} %get-tuple-element.50), channel_id=1, source_target_pairs={{1,0},{0,1},{3,2},{2,3},{5,4},{4,5},{7,6},{6,7},{9,8},{8,9},{11,10... | collective-permute-start | bytes 270344 | tf_op jit(solution)/shard_map/ppermute | solution.py:519
  19.7 6.1 %collective-permute-start.8 = (f32[144,128]{1,0:T(8,128)S(1)}, f32[144,128]{1,0:T(8,128)S(1)}, u32[]{:S(2)}, u32[]{:S(2)}) collective-permute-start(f32[144,128]{1,0:T(8,128)S(1)} %get-tuple-element.52), channel_id=1, source_target_pairs={{7,0},{6,1},{5,2},{4,3},{3,4},{2,5},{1,6},{0,7},{15,8},{14,9},{13,... | collective-permute-start | bytes 221192 | tf_op jit(solution)/shard_map/ppermute | solution.py:519
  21.2 5.5 %collective-permute-start.9 = (f32[144,128]{1,0:T(8,128)S(1)}, f32[144,128]{1,0:T(8,128)S(1)}, u32[]{:S(2)}, u32[]{:S(2)}) collective-permute-start(f32[144,128]{1,0:T(8,128)S(1)} %get-tuple-element.53), channel_id=1, source_target_pairs={{3,0},{2,1},{1,2},{0,3},{7,4},{6,5},{5,6},{4,7},{11,8},{10,9},{9,1... | collective-permute-start | bytes 221192 | tf_op jit(solution)/shard_map/ppermute | solution.py:519
  22.6 3.2 %collective-permute-start.10 = (f32[40,128]{1,0:T(8,128)S(1)}, f32[40,128]{1,0:T(8,128)S(1)}, u32[]{:S(2)}, u32[]{:S(2)}) collective-permute-start(f32[40,128]{1,0:T(8,128)S(1)} %get-tuple-element.54), channel_id=1, source_target_pairs={{5,0},{4,1},{7,2},{6,3},{1,4},{0,5},{3,6},{2,7},{13,8},{12,9},{15,... | collective-permute-start | bytes 61448 | tf_op jit(solution)/shard_map/ppermute | solution.py:519

commit v11 on v10

--- a/solution.py
+++ b/solution.py
@@ -424,7 +424,7 @@
 
 
 def second_kernel(st_in, coarse_in, extra_in, early, across, *refs):
-    st, coarse, extra, total, last_info, first_info, message, outer, squeeze = refs
+    st, coarse, extra, total, info_far, info_near, outer, squeeze = refs
     del st_in, coarse_in, extra_in
     planes, rows, ext, nz = st.shape
     ny, nx = rows - 2, ext - 2 * PAD
@@ -453,13 +453,12 @@
     onward = [lead_last, ratio_last] + increments(ny - 1, ny - 1, CONDUCT + FLOW)
     back = [lead, offset] + increments(2, 1, CONDUCT) + [slope, ratio]
     write_rows(total, [slopes, offsets])
-    write_rows(last_info, onward)
-    write_rows(first_info, back)
-    for go, info in ((True, onward), (False, back)):
-
-        @pl.when((me % 2 == 0) == go)
+    for odd in (True, False):
+
+        @pl.when((me % 2 == 1) == odd)
         def _():
-            write_rows(message, [slopes, offsets] + info)
+            write_rows(info_far, onward if odd else back)
+            write_rows(info_near, back if odd else onward)
 
 
 def write_rows(ref, values):
@@ -469,32 +468,20 @@
         at += value.shape[0]
 
 
-class Rows:
+class Info:
     def __init__(self, nx):
-        self.span = nx // 2 + 2
-        self.map = 2 * self.span
-        self.info = self.map + 2 * (nx + 2)
-        self.rest = self.map
-        self.final = self.map + self.info
-        self.full = self.final + self.rest
-        self.low = self.map
-        self.high = self.low + self.info
-        self.near = self.high + self.info + self.rest
+        span = self.span = nx // 2 + 2
+        self.lead, self.second = 0, span
+        self.solid, self.gas = 2 * span, 2 * span + nx + 2
+        self.slope = 2 * span + 2 * (nx + 2)
+        self.ratio = self.slope + span
+        self.height = (self.ratio + span + 7) // 8 * 8
 
 
 def source(at, k, radix):
     if radix & (radix - 1) == 0:
         return at ^ k
     return (at + radix - k) % radix
-
-
-def target(at, k, radix):
-    return at ^ k if radix & (radix - 1) == 0 else (at + k) % radix
-
-
-def order(radix):
-    out = [(k, any(abs(source(at, k, radix) - at) == 1 for at in range(radix))) for k in range(1, radix)]
-    return sorted(out, key=lambda item: (not item[1], -item[0]))
 
 
 def stages(count):
@@ -508,32 +495,27 @@
     return out if len(out) > 1 else out + [1]
 
 
-def exchange_stage(messages, radix, stride):
+def exchange_stage(message, radix, stride):
     count, got = lax.axis_size("gy"), []
-    for (k, near), message in zip(order(radix), messages):
+    for k in range(1, radix):
         pairs = []
         for me in range(count):
-            at, low = me // stride % radix, me % stride
-            sender = me - low + (source(at, k, radix) - at) * stride + (stride - 1 - low)
-            pairs.append((sender, me))
+            at = me // stride % radix
+            pairs.append((me + (source(at, k, radix) - at) * stride, me))
         got.append(lax.ppermute(message, "gy", pairs))
     return got
 
 
 class Group:
-    def __init__(self, radix, stride, others, nx):
-        self.radix, self.others, self.nx = radix, others, nx
-        me = lax.axis_index("gy")
-        self.at = lax.rem(lax.div(me, stride), radix)
-        low = lax.rem(me, stride)
-        self.lowest, self.highest = low == 0, low == stride - 1
+    def __init__(self, radix, stride, others, span):
+        self.radix, self.others, self.span = radix, others, span
+        self.at = lax.rem(lax.div(lax.axis_index("gy"), stride), radix)
 
     def map_of(self, place, own):
-        rows = Rows(self.nx)
         out = own
-        for (k, near), ref in zip(order(self.radix), self.others):
+        for k, ref in enumerate(self.others, 1):
             here = source(self.at, k, self.radix) == place
-            got = [ref[i * rows.span : (i + 1) * rows.span] for i in range(2)]
+            got = read_map(ref, self.span)
             out = got if out is None else [jnp.where(here, new, old) for new, old in zip(got, out)]
         return out
 
@@ -552,103 +534,50 @@
             a, b = new_a * a, new_a * b + new_b
         return a, b
 
-    def collect(self, near, final):
-        rows = Rows(self.nx)
-        for (k, adjacent), ref in zip(order(self.radix), self.others):
-            if not adjacent:
-                continue
-            place = source(self.at, k, self.radix)
-
-            @pl.when(self.lowest & (place == self.at - 1))
-            def _():
-                near[rows.low : rows.low + rows.info] = ref[rows.map : rows.final]
-
-            @pl.when(self.highest & (place == self.at + 1))
-            def _():
-                near[rows.high : rows.high + rows.info] = ref[rows.map : rows.final]
-                rest = slice(0, rows.map) if final else slice(rows.final, rows.full)
-                near[rows.high + rows.info : rows.near] = ref[rest]
-
-
-def start_near(near, nx, nz):
-    rows = Rows(nx)
-    near[: rows.span] = jnp.ones((rows.span, nz), jnp.float32)
-    near[rows.span :] = jnp.zeros((near.shape[0] - rows.span, nz), jnp.float32)
-
-
-def join_kernel(radix, stride, final, nx, is_first, *refs):
-    rows = Rows(nx)
-    total, last_info, first_info, near_in = refs[:4]
-    others, near, outs = refs[4 : 3 + radix], refs[3 + radix], refs[4 + radix :]
-    nz = near.shape[1]
-    if is_first:
-        start_near(near, nx, nz)
-    else:
-        near[...] = near_in[...]
-    group = Group(radix, stride, others, nx)
-    own = [total[i * rows.span : (i + 1) * rows.span] for i in range(2)]
-    ahead = group.ahead(near[: rows.span], near[rows.span : rows.map])
-    write_rows(near, ahead)
-    group.collect(near, False)
-    whole = group.total(own)
-    at = lax.div(lax.axis_index("gy"), stride * radix)
-    if final == 0:
-        write_rows(outs[0], whole)
-        return
-    at = lax.rem(at, final)
-    for (k, adjacent), out in zip(order(final), outs):
-        up = target(at, k, final) > at
-        if not adjacent:
-            write_rows(out, whole)
-            continue
-
-        @pl.when(up)
-        def _():
-            write_rows(out, whole)
-            out[rows.map : rows.final] = last_info[: rows.info]
-
-        @pl.when(jnp.logical_not(up))
-        def _():
-            out[: rows.map] = first_info[rows.info : rows.info + rows.rest]
-            out[rows.map : rows.final] = first_info[: rows.info]
-
-
-def full_message(nx, stride, radix, total, last_info, first_info, k):
-    rows = Rows(nx)
-    at = lax.axis_index("gy") // stride % radix
-    onward = jnp.concatenate([total[: rows.map], last_info[: rows.info], first_info[rows.info : rows.info + rows.rest]])
-    back = jnp.concatenate([total[: rows.map], first_info[: rows.info + rows.rest]])
-    message = jnp.where(target(at, k, radix) > at, onward, back)
-    return jnp.pad(message, ((0, -rows.full % 8), (0, 0)))
+
+def read_map(ref, span):
+    return [ref[i * span : (i + 1) * span] for i in range(2)]
+
+
+def join_kernel(radix, stride, span, is_first, *refs):
+    total, ahead_in, info_far, info_near = refs[:4]
+    others, (ahead, whole, far_out, near_out) = refs[4 : 3 + radix], refs[3 + radix :]
+    own = read_map(total, span)
+    before = (jnp.ones_like(own[0]), jnp.zeros_like(own[0])) if is_first else read_map(ahead_in, span)
+    group = Group(radix, stride, others, span)
+    write_rows(ahead, group.ahead(*before))
+    write_rows(whole, group.total(own))
+    far_out[...] = info_far[...]
+    near_out[...] = info_near[...]
 
 
 def third_kernel(radix, stride, *refs):
-    st, extra, coarse, near_in = refs[:4]
-    others, (out, sc, wide, near, done, sems) = refs[4 : 3 + radix], refs[3 + radix :]
+    st, extra, coarse, ahead, info_far, info_near = refs[:6]
+    others, (out, sc, wide, done, sems) = refs[6 : 5 + radix], refs[5 + radix :]
     planes, rows, ext, nz = st.shape
     ny, nx = rows - 2, ext - 2 * PAD
     edge = edge_weights((ext, nz))
     blocks = ny // 2
 
-    lay = Rows(nx)
-    span = lay.span
-    near[...] = near_in[...]
-    group = Group(radix, stride, others, nx)
-    if radix > 1:
-        group.collect(near, True)
-    gas_in = group.ahead(near[:span], near[span : lay.map])[1]
-    at_high = lay.high + lay.info
-    starts = [lay.low, lay.low + span, lay.high, lay.high + span, at_high, at_high + span]
-    for k, v in enumerate([gas_in] + [near[start : start + span] for start in starts]):
+    info = Info(nx)
+    span = info.span
+    gas_in = Group(radix, stride, others, span).ahead(*read_map(ahead, span))[1]
+    odd = lax.axis_index("gy") % 2 == 1
+
+    def from_beside(after, start, height):
+        part = slice(start, start + height)
+        return jnp.where(odd, info_far[part], info_near[part]) if after else jnp.where(odd, info_near[part], info_far[part])
+
+    starts = ((False, info.lead), (False, info.second), (True, info.lead), (True, info.second), (True, info.slope), (True, info.ratio))
+    for k, v in enumerate([gas_in] + [from_beside(after, start, span) for after, start in starts]):
         wide[k, : PAD - 2] = jnp.zeros((PAD - 2, nz), jnp.float32)
         wide[k, ext - PAD + 2 :] = jnp.zeros((PAD - 2, nz), jnp.float32)
         wide[k, pl.ds(PAD - 2, span, 2), :] = v
         wide[k, pl.ds(PAD - 1, span, 2), :] = v
-    for k, start in enumerate((lay.low, lay.low + nx + 2, lay.high, lay.high + nx + 2)):
-        start += lay.map
+    for k, (after, start) in enumerate(((False, info.solid), (False, info.gas), (True, info.solid), (True, info.gas))):
         wide[7 + k, :PAD] = jnp.zeros((PAD, nz), jnp.float32)
         wide[7 + k, ext - PAD :] = jnp.zeros((PAD, nz), jnp.float32)
-        wide[7 + k, PAD - 1 : PAD + nx + 1] = near[start : start + nx + 2]
+        wide[7 + k, PAD - 1 : PAD + nx + 1] = from_beside(after, start, nx + 2)
 
     gas_in = wide[0]
     last = ny + 1
@@ -794,11 +723,9 @@
 
     beside = [swap(part, "gy", 0) for part in beside]
 
-    lay = Rows(nx)
-
-    def tall(height):
-        return f32(((height + 7) // 8 * 8, nz))
-
+    info = f32((Info(nx).height, nz))
+    span = Info(nx).span
+    map_shape = f32(((2 * span + 7) // 8 * 8, nz))
     letter_room = pltpu.VMEM((MESSAGE, ext, nz), jnp.float32)
     more = f32((6, ext, nz))
     st, coarse, extra = pl.pallas_call(
@@ -811,52 +738,46 @@
         compiler_params=PARAMS,
         name="near",
     )(st, coarse, *beside)
-    st, coarse, extra, total, last_info, first_info, message = pl.pallas_call(
+    st, coarse, extra, total, info_far, info_near = pl.pallas_call(
         second_kernel,
-        out_shape=(state, rows, more, tall(lay.map), tall(lay.info), tall(lay.info + lay.rest), tall(lay.full)),
+        out_shape=(state, rows, more, map_shape, info, info),
         in_specs=[VMEM] * 5,
-        out_specs=(VMEM,) * 7,
+        out_specs=(VMEM,) * 6,
         scratch_shapes=[letter_room, pltpu.VMEM((8, ext, nz), jnp.float32)],
         input_output_aliases={0: 0, 1: 1, 2: 2},
         compiler_params=PARAMS,
         name="second",
     )(st, coarse, extra, early, across)
 
-    near, messages = total, [message]
-    radices, stride = stages(lax.axis_size("gy")), 1
+    ahead, radices, stride = total, stages(lax.axis_size("gy")), 1
     for place, radix in enumerate(radices[:-1]):
-        if place:
-            messages = [full_message(nx, stride, radix, total, last_info, first_info, k) for k, _ in order(radix)]
-        others = exchange_stage(messages, radix, stride)
-        final = radices[-1] if place == len(radices) - 2 else 0
-        outs = [tall(lay.final if adjacent else lay.map) for _, adjacent in order(final)] if final else [tall(lay.map)]
-        near, *messages = pl.pallas_call(
-            functools.partial(join_kernel, radix, stride, final, nx, place == 0),
-            out_shape=(tall(lay.near), *outs),
+        others = exchange_stage(total, radix, stride)
+        ahead, total, info_far, info_near = pl.pallas_call(
+            functools.partial(join_kernel, radix, stride, span, place == 0),
+            out_shape=(map_shape, map_shape, info, info),
             in_specs=[VMEM] * (3 + radix),
-            out_specs=(VMEM,) * (1 + len(outs)),
+            out_specs=(VMEM,) * 4,
             compiler_params=PARAMS,
             name="join",
-        )(total, last_info, first_info, near, *others)
-        total = total if final else messages[0]
+        )(total, ahead, info_far, info_near, *others)
         stride *= radix
-    got = exchange_stage(messages, radices[-1], stride)
+    info_far, info_near = swap(info_far, "gy", 1), swap(info_near, "gy", 0)
+    got = exchange_stage(total, radices[-1], stride)
 
     out = pl.pallas_call(
         functools.partial(third_kernel, radices[-1], stride),
         out_shape=f32((2, ny, nx, nz)),
-        in_specs=[VMEM] * (4 + len(got)),
+        in_specs=[VMEM] * (6 + len(got)),
         out_specs=HBM,
         scratch_shapes=[
             pltpu.VMEM((4, ny + 2, ext, nz), jnp.float32),
             pltpu.VMEM((11, ext, nz), jnp.float32),
-            pltpu.VMEM(tall(lay.near).shape, jnp.float32),
             pltpu.VMEM((2, ny, nx, nz), jnp.float32),
             pltpu.SemaphoreType.DMA((ny // GROUP,)),
         ],
         compiler_params=PARAMS,
         name="third",
-    )(st, extra, coarse, near, *got)
+    )(st, extra, coarse, ahead, info_far, info_near, *got)
     return jnp.transpose(out, (0, 2, 1, 3))
 
 

time: 29.4 us -> 32.7 us (1.11)
  starting transfers between devices: 11.5 us -> 15.5 us
  waiting for transfers between devices: 9.81 us -> 9.08 us
    ppermute x7 -> x9, starting transfers between devices: 8.31 us -> 11.9 us  [swap(): return lax.ppermute(x, axis, pairs)]
    ppermute x4, waiting for transfers between devices: 5.11 us -> 4.37 us  [exchange_stage(): got.append(lax.ppermute(message, 'gy', pairs))]
    ppermute x4, starting transfers between devices: 3.19 us -> 3.62 us  [exchange_stage(): got.append(lax.ppermute(message, 'gy', pairs))]
    ppermute x7 -> x9, waiting for transfers between devices: 4.71 us -> 4.71 us  [swap(): return lax.ppermute(x, axis, pairs)]
  transfers between devices with their start and end apart: 11 -> 13, of which waited for: 5 -> 6; matrix products, arithmetic and copies ran while one was open for 0% -> 0% of each run, Pallas kernels for 10% -> 9%
where the time goes in v11:
time: 32.7 us; the launch traced here: 32.5 us
  starting transfers between devices  15.5 us (47%)
  waiting for transfers between devices  9.08 us (28%)
  Pallas kernels  7.74 us (24%)
    ppermute x9, starting transfers between devices, swap(): return lax.ppermute(x, axis, pairs)  11.9 us
    ppermute x9, waiting for transfers between devices, swap(): return lax.ppermute(x, axis, pairs)  4.71 us
    ppermute x4, waiting for transfers between devices, exchange_stage(): got.append(lax.ppermute(message, 'gy', pairs))  4.37 us
    ppermute x4, starting transfers between devices, exchange_stage(): got.append(lax.ppermute(message, 'gy', pairs))  3.62 us
    pallas_call x1, Pallas kernels, shards(): pl.pallas_call(functools.partial(third_kernel, radices[-1], stride), out_...  2.34 us
    pallas_call x1, Pallas kernels, shards(): pl.pallas_call(inner_kernel, out_shape=(state, rows), in_specs=[VMEM] * 4...  1.77 us
    pallas_call x1, Pallas kernels, shards(): pl.pallas_call(pack_kernel, out_shape=(strip, strip, f32((EARLY, nx, nz))...  1.65 us
    pallas_call x1, Pallas kernels, shards(): pl.pallas_call(second_kernel, out_shape=(state, rows, more, map_shape, in...  0.67 us
  transfers between devices with their start and end apart: 13, of which 6 were waited for; matrix products, arithmetic and copies ran while one was open for 0% of the time, Pallas kernels for 9%

profile of v11, /device:TPU:16, one launch (start us, length us, event | category | flops | bytes accessed | tf_op | source)
XLA Modules:
  0.0 32.5 jit_solution(11193212698710168794)
XLA Ops:
  0.0 1.6 %pack_x.1 = (f32[304,128]{1,0:T(8,128)S(1)}, f32[304,128]{1,0:T(8,128)S(1)}, f32[7,32,128]{2,1,0:T(8,128)S(1)}, f32[15,14,48,128]{3,2,1,0:T(8,128)S(1)}) custom-call(f32[2,12,32,128]{3,2,1,0:T(8,128)} %bitcast.5, f32[2,12,32,128]{3,2,1,0:T(8,128)} %bitcast.6, f32[12,32,128]{2,1,0:T(8,128)} %bitcast.7, f32[12,32,128]{2,1,0:T(8,128)} %bitcast.8), custom_call_target="tpu_custom_call" | custom-call | tf_op jit(solution)/shard_map/pack_x/pallas_call | solution.py:676
  1.7 1.6 %collective-permute-start = (f32[304,128]{1,0:T(8,128)S(1)}, f32[304,128]{1,0:T(8,128)S(1)}, u32[]{:S(2)}, u32[]{:S(2)}) collective-permute-start(f32[304,128]{1,0:T(8,128)S(1)} %get-tuple-element.30), channel_id=1, source_target_pairs={{0,8},{8,0},{16,24},{24,16},{1,9},{9,1},{17,25},{25,17},{2,10},{10... | collective-permute-start | bytes 466952 | tf_op jit(solution)/shard_map/ppermute | solution.py:661
  3.3 1.9 %collective-permute-start.1 = (f32[304,128]{1,0:T(8,128)S(1)}, f32[304,128]{1,0:T(8,128)S(1)}, u32[]{:S(2)}, u32[]{:S(2)}) collective-permute-start(f32[304,128]{1,0:T(8,128)S(1)} %get-tuple-element.31), channel_id=1, source_target_pairs={{8,16},{16,8},{9,17},{17,9},{10,18},{18,10},{11,19},{19,11},{12,20... | collective-permute-start | bytes 466952 | tf_op jit(solution)/shard_map/ppermute | solution.py:661
  5.2 0.7 %collective-permute-start.2 = (f32[7,32,128]{2,1,0:T(8,128)S(1)}, f32[7,32,128]{2,1,0:T(8,128)S(1)}, u32[]{:S(2)}, u32[]{:S(2)}) collective-permute-start(f32[7,32,128]{2,1,0:T(8,128)S(1)} %get-tuple-element.33), channel_id=1, source_target_pairs={{1,2},{2,1},{3,4},{4,3},{5,6},{6,5},{9,10},{10,9},{11,12},{12,11},... | collective-permute-start | bytes 344072 | tf_op jit(solution)/shard_map/ppermute | solution.py:661
  6.0 1.5 %collective-permute-done.one = f32[304,128]{1,0:T(8,128)S(1)} collective-permute-done((f32[304,128]{1,0:T(8,128)S(1)}, f32[304,128]{1,0:T(8,128)S(1)}, u32[]{:S(2)}, u32[]{:S(2)}) %collective-permute-start) | collective-permute-done | bytes 155680 | tf_op jit(solution)/shard_map/ppermute | solution.py:661
  7.5 3.2 %collective-permute-done.1.two = f32[304,128]{1,0:T(8,128)S(1)} collective-permute-done((f32[304,128]{1,0:T(8,128)S(1)}, f32[304,128]{1,0:T(8,128)S(1)}, u32[]{:S(2)}, u32[]{:S(2)}) %collective-permute-start.1) | collective-permute-done | bytes 155680 | tf_op jit(solution)/shard_map/ppermute | solution.py:661
  10.7 0.6 %first.1 = (f32[15,14,48,128]{3,2,1,0:T(8,128)S(1)}, f32[144,128]{1,0:T(8,128)S(1)}, f32[3,40,128]{2,1,0:T(8,128)S(1)}, f32[3,40,128]{2,1,0:T(8,128)S(1)}, f32[3,40,128]{2,1,0:T(8,128)S(1)}) custom-call(f32[15,14,48,128]{3,2,1,0:T(8,128)S(1)} %conduct.1.st_in, f32[304,128]{1,0:T(8,128)S(1)} %collective-permute-done.one, ...), custom_call_target="tpu_custom_call", output_to_operand_aliasing={{0}: (0, {})} | custom-call | tf_op jit(solution)/shard_map/first/pallas_call | solution.py:701
  11.3 0.7 %collective-permute-start.6 = (f32[144,128]{1,0:T(8,128)S(1)}, f32[144,128]{1,0:T(8,128)S(1)}, u32[]{:S(2)}, u32[]{:S(2)}) collective-permute-start(f32[144,128]{1,0:T(8,128)S(1)} %get-tuple-element.42), channel_id=1, source_target_pairs={{1,2},{2,1},{3,4},{4,3},{5,6},{6,5},{9,10},{10,9},{11,12},{12,11},... | collective-permute-start | bytes 221192 | tf_op jit(solution)/shard_map/ppermute | solution.py:661
  11.9 2.9 %collective-permute-start.3 = (f32[3,40,128]{2,1,0:T(8,128)S(1)}, f32[3,40,128]{2,1,0:T(8,128)S(1)}, u32[]{:S(2)}, u32[]{:S(2)}) collective-permute-start(f32[3,40,128]{2,1,0:T(8,128)S(1)} %get-tuple-element.36), channel_id=1, source_target_pairs={{0,1},{1,0},{2,3},{3,2},{4,5},{5,4},{6,7},{7,6},{8,9},{9,8},{10,11... | collective-permute-start | bytes 184328 | tf_op jit(solution)/shard_map/ppermute | solution.py:661
  14.9 0.4 %collective-permute-start.5 = (f32[3,40,128]{2,1,0:T(8,128)S(1)}, f32[3,40,128]{2,1,0:T(8,128)S(1)}, u32[]{:S(2)}, u32[]{:S(2)}) collective-permute-start(f32[3,40,128]{2,1,0:T(8,128)S(1)} %get-tuple-element.38), channel_id=1, source_target_pairs={{0,1},{1,0},{2,3},{3,2},{4,5},{5,4},{6,7},{7,6},{8,9},{9,8},{10,11... | collective-permute-start | bytes 184328 | tf_op jit(solution)/shard_map/ppermute | solution.py:661
  15.4 1.8 %inner.1 = (f32[15,14,48,128]{3,2,1,0:T(8,128)S(1)}, f32[4,6,48,128]{3,2,1,0:T(8,128)S(1)}) custom-call(f32[15,14,48,128]{3,2,1,0:T(8,128)S(1)} %get-tuple-element.32.st_in, f32[304,128]{1,0:T(8,128)S(1)} %collective-permute-done.one, f32[304,128]{1,0:T(8,128)S(1)} %collective-permute-done.1.two, ...), custom_call_target="tpu_custom_call", output_to_operand_aliasing={{0}: (0, {})} | custom-call | flops 14745600 | bytes 18874368 | tf_op jit(solution)/shard_map/inner/pallas_call | solution.py:713
  17.2 0.6 %near.1 = (f32[15,14,48,128]{3,2,1,0:T(8,128)S(1)}, f32[4,6,48,128]{3,2,1,0:T(8,128)S(1)}, f32[6,48,128]{2,1,0:T(8,128)S(1)}) custom-call(f32[15,14,48,128]{3,2,1,0:T(8,128)S(1)} %get-tuple-element.34.st_in, f32[4,6,48,128]{3,2,1,0:T(8,128)S(1)} %get-tuple-element.35.coarse_in, ...), custom_call_target="tpu_custom_call", output_to_operand_aliasing={{0}: (0, {}), {1}: (1, {})} | custom-call | tf_op jit(solution)/shard_map/near/pallas_call | solution.py:731
  17.8 0.7 %second.1 = (f32[15,14,48,128]{3,2,1,0:T(8,128)S(1)}, f32[4,6,48,128]{3,2,1,0:T(8,128)S(1)}, f32[6,48,128]{2,1,0:T(8,128)S(1)}, f32[40,128]{1,0:T(8,128)S(1)}, f...) custom-call(f32[15,14,48,128]{3,2,1,0:T(8,128)S(1)} %get-tuple-element.3, ...), custom_call_target="tpu_custom_call", output_to_operand_aliasing={{0}: (0, {}), {1}: (1, {}), {2}: (2, {})} | custom-call | tf_op jit(solution)/shard_map/second/pallas_call | solution.py:741
  18.5 0.1 collective-permute-start.7
  18.6 1.1 %collective-permute-done.7.refs_4_ = f32[40,128]{1,0:T(8,128)S(1)} collective-permute-done((f32[40,128]{1,0:T(8,128)S(1)}, f32[40,128]{1,0:T(8,128)S(1)}, u32[]{:S(2)}, u32[]{:S(2)}) %collective-permute-start.7) | collective-permute-done | bytes 20512 | tf_op jit(solution)/shard_map/ppermute | solution.py:505
  19.8 0.7 %collective-permute-start.8 = (f32[144,128]{1,0:T(8,128)S(1)}, f32[144,128]{1,0:T(8,128)S(1)}, u32[]{:S(2)}, u32[]{:S(2)}) collective-permute-start(f32[144,128]{1,0:T(8,128)S(1)} %get-tuple-element.50), channel_id=1, source_target_pairs={{1,2},{2,1},{3,4},{4,3},{5,6},{6,5},{9,10},{10,9},{11,12},{12,11},... | collective-permute-start | bytes 221192 | tf_op jit(solution)/shard_map/ppermute | solution.py:661
  20.5 2.9 %collective-permute-start.9 = (f32[144,128]{1,0:T(8,128)S(1)}, f32[144,128]{1,0:T(8,128)S(1)}, u32[]{:S(2)}, u32[]{:S(2)}) collective-permute-start(f32[144,128]{1,0:T(8,128)S(1)} %get-tuple-element.51), channel_id=1, source_target_pairs={{0,1},{1,0},{2,3},{3,2},{4,5},{5,4},{6,7},{7,6},{8,9},{9,8},{10,11... | collective-permute-start | bytes 221192 | tf_op jit(solution)/shard_map/ppermute | solution.py:661
  23.4 1.2 %collective-permute-start.12 = (f32[40,128]{1,0:T(8,128)S(1)}, f32[40,128]{1,0:T(8,128)S(1)}, u32[]{:S(2)}, u32[]{:S(2)}) collective-permute-start(f32[40,128]{1,0:T(8,128)S(1)} %get-tuple-element.52), channel_id=1, source_target_pairs={{6,0},{7,1},{4,2},{5,3},{2,4},{3,5},{0,6},{1,7},{14,8},{15,9},{12,... | collective-permute-start | bytes 61448 | tf_op jit(solution)/shard_map/ppermute | solution.py:505
  24.6 1.7 %collective-permute-start.11 = (f32[40,128]{1,0:T(8,128)S(1)}, f32[40,128]{1,0:T(8,128)S(1)}, u32[]{:S(2)}, u32[]{:S(2)}) collective-permute-start(f32[40,128]{1,0:T(8,128)S(1)} %get-tuple-element.52), channel_id=1, source_target_pairs={{4,0},{5,1},{6,2},{7,3},{0,4},{1,5},{2,6},{3,7},{12,8},{13,9},{14,... | collective-permute-start | bytes 61448 | tf_op jit(solution)/shard_map/ppermute | solution.py:505
  26.3 0.5 %collective-permute-start.10 = (f32[40,128]{1,0:T(8,128)S(1)}, f32[40,128]{1,0:T(8,128)S(1)}, u32[]{:S(2)}, u32[]{:S(2)}) collective-permute-start(f32[40,128]{1,0:T(8,128)S(1)} %get-tuple-element.52), channel_id=1, source_target_pairs={{2,0},{3,1},{0,2},{1,3},{6,4},{7,5},{4,6},{5,7},{10,8},{11,9},{8,1... | collective-permute-start | bytes 61448 | tf_op jit(solution)/shard_map/ppermute | solution.py:505
  26.9 1.2 %collective-permute-done.12.refs_8_ = f32[40,128]{1,0:T(8,128)S(1)} collective-permute-done((f32[40,128]{1,0:T(8,128)S(1)}, f32[40,128]{1,0:T(8,128)S(1)}, u32[]{:S(2)}, u32[]{:S(2)}) %collective-permute-start.12) | collective-permute-done | bytes 20512 | tf_op jit(solution)/shard_map/ppermute | solution.py:505
  28.1 0.3 collective-permute-done.11.refs_7_
  28.4 1.7 %collective-permute-done.10.refs_6_ = f32[40,128]{1,0:T(8,128)S(1)} collective-permute-done((f32[40,128]{1,0:T(8,128)S(1)}, f32[40,128]{1,0:T(8,128)S(1)}, u32[]{:S(2)}, u32[]{:S(2)}) %collective-permute-start.10) | collective-permute-done | bytes 20512 | tf_op jit(solution)/shard_map/ppermute | solution.py:505
  30.1 2.3 %third.1 = f32[2,12,32,128]{3,2,1,0:T(8,128)} custom-call(f32[15,14,48,128]{3,2,1,0:T(8,128)S(1)} %get-tuple-element.43.refs_0_, f32[6,48,128]{2,1,0:T(8,128)S(1)} %get-tuple-element.44.refs_1_, f32[4,6,48,128]{3,2,1,0:T(8,128)S(1)} %get-tuple-element.45.refs_2_, f32[40,128]{1,0:T(8,128)S(1)} %get-tuple-element.49.refs_3_, ...), custom_call_target="tpu_custom_call" | custom-call | tf_op jit(solution)/shard_map/third/pallas_call | solution.py:767
  (10 shorter events, 0.2 us)
Async XLA Ops:
  1.7 5.8 %collective-permute-start = (f32[304,128]{1,0:T(8,128)S(1)}, f32[304,128]{1,0:T(8,128)S(1)}, u32[]{:S(2)}, u32[]{:S(2)}) collective-permute-start(f32[304,128]{1,0:T(8,128)S(1)} %get-tuple-element.30), channel_id=1, source_target_pairs={{0,8},{8,0},{16,24},{24,16},{1,9},{9,1},{17,25},{25,17},{2,10},{10... | collective-permute-start | bytes 466952 | tf_op jit(solution)/shard_map/ppermute | solution.py:661
  3.3 7.4 %collective-permute-start.1 = (f32[304,128]{1,0:T(8,128)S(1)}, f32[304,128]{1,0:T(8,128)S(1)}, u32[]{:S(2)}, u32[]{:S(2)}) collective-permute-start(f32[304,128]{1,0:T(8,128)S(1)} %get-tuple-element.31), channel_id=1, source_target_pairs={{8,16},{16,8},{9,17},{17,9},{10,18},{18,10},{11,19},{19,11},{12,20... | collective-permute-start | bytes 466952 | tf_op jit(solution)/shard_map/ppermute | solution.py:661
  5.2 10.2 %collective-permute-start.2 = (f32[7,32,128]{2,1,0:T(8,128)S(1)}, f32[7,32,128]{2,1,0:T(8,128)S(1)}, u32[]{:S(2)}, u32[]{:S(2)}) collective-permute-start(f32[7,32,128]{2,1,0:T(8,128)S(1)} %get-tuple-element.33), channel_id=1, source_target_pairs={{1,2},{2,1},{3,4},{4,3},{5,6},{6,5},{9,10},{10,9},{11,12},{12,11},... | collective-permute-start | bytes 344072 | tf_op jit(solution)/shard_map/ppermute | solution.py:661
  11.3 6.6 %collective-permute-start.6 = (f32[144,128]{1,0:T(8,128)S(1)}, f32[144,128]{1,0:T(8,128)S(1)}, u32[]{:S(2)}, u32[]{:S(2)}) collective-permute-start(f32[144,128]{1,0:T(8,128)S(1)} %get-tuple-element.42), channel_id=1, source_target_pairs={{1,2},{2,1},{3,4},{4,3},{5,6},{6,5},{9,10},{10,9},{11,12},{12,11},... | collective-permute-start | bytes 221192 | tf_op jit(solution)/shard_map/ppermute | solution.py:661
  11.9 5.2 %collective-permute-start.3 = (f32[3,40,128]{2,1,0:T(8,128)S(1)}, f32[3,40,128]{2,1,0:T(8,128)S(1)}, u32[]{:S(2)}, u32[]{:S(2)}) collective-permute-start(f32[3,40,128]{2,1,0:T(8,128)S(1)} %get-tuple-element.36), channel_id=1, source_target_pairs={{0,1},{1,0},{2,3},{3,2},{4,5},{5,4},{6,7},{7,6},{8,9},{9,8},{10,11... | collective-permute-start | bytes 184328 | tf_op jit(solution)/shard_map/ppermute | solution.py:661
  14.8 2.3 %collective-permute-start.4 = (f32[3,40,128]{2,1,0:T(8,128)S(1)}, f32[3,40,128]{2,1,0:T(8,128)S(1)}, u32[]{:S(2)}, u32[]{:S(2)}) collective-permute-start(f32[3,40,128]{2,1,0:T(8,128)S(1)} %get-tuple-element.37), channel_id=1, source_target_pairs={{0,1},{1,0},{2,3},{3,2},{4,5},{5,4},{6,7},{7,6},{8,9},{9,8},{10,11... | collective-permute-start | bytes 184328 | tf_op jit(solution)/shard_map/ppermute | solution.py:661
  14.9 2.2 %collective-permute-start.5 = (f32[3,40,128]{2,1,0:T(8,128)S(1)}, f32[3,40,128]{2,1,0:T(8,128)S(1)}, u32[]{:S(2)}, u32[]{:S(2)}) collective-permute-start(f32[3,40,128]{2,1,0:T(8,128)S(1)} %get-tuple-element.38), channel_id=1, source_target_pairs={{0,1},{1,0},{2,3},{3,2},{4,5},{5,4},{6,7},{7,6},{8,9},{9,8},{10,11... | collective-permute-start | bytes 184328 | tf_op jit(solution)/shard_map/ppermute | solution.py:661
  18.5 1.3 %collective-permute-start.7 = (f32[40,128]{1,0:T(8,128)S(1)}, f32[40,128]{1,0:T(8,128)S(1)}, u32[]{:S(2)}, u32[]{:S(2)}) collective-permute-start(f32[40,128]{1,0:T(8,128)S(1)} %get-tuple-element.46.refs_0_.refs_1_), channel_id=1, source_target_pairs={{1,0},{0,1},{3,2},{2,3},{5,4},{4,5},{7,6},{6,7},{9,8},{8,9},{11,10... | collective-permute-start | bytes 61448 | tf_op jit(solution)/shard_map/ppermute | solution.py:505
  19.8 10.3 %collective-permute-start.8 = (f32[144,128]{1,0:T(8,128)S(1)}, f32[144,128]{1,0:T(8,128)S(1)}, u32[]{:S(2)}, u32[]{:S(2)}) collective-permute-start(f32[144,128]{1,0:T(8,128)S(1)} %get-tuple-element.50), channel_id=1, source_target_pairs={{1,2},{2,1},{3,4},{4,3},{5,6},{6,5},{9,10},{10,9},{11,12},{12,11},... | collective-permute-start | bytes 221192 | tf_op jit(solution)/shard_map/ppermute | solution.py:661
  20.5 9.7 %collective-permute-start.9 = (f32[144,128]{1,0:T(8,128)S(1)}, f32[144,128]{1,0:T(8,128)S(1)}, u32[]{:S(2)}, u32[]{:S(2)}) collective-permute-start(f32[144,128]{1,0:T(8,128)S(1)} %get-tuple-element.51), channel_id=1, source_target_pairs={{0,1},{1,0},{2,3},{3,2},{4,5},{5,4},{6,7},{7,6},{8,9},{9,8},{10,11... | collective-permute-start | bytes 221192 | tf_op jit(solution)/shard_map/ppermute | solution.py:661
  23.4 4.7 %collective-permute-start.12 = (f32[40,128]{1,0:T(8,128)S(1)}, f32[40,128]{1,0:T(8,128)S(1)}, u32[]{:S(2)}, u32[]{:S(2)}) collective-permute-start(f32[40,128]{1,0:T(8,128)S(1)} %get-tuple-element.52), channel_id=1, source_target_pairs={{6,0},{7,1},{4,2},{5,3},{2,4},{3,5},{0,6},{1,7},{14,8},{15,9},{12,... | collective-permute-start | bytes 61448 | tf_op jit(solution)/shard_map/ppermute | solution.py:505
  24.6 3.8 %collective-permute-start.11 = (f32[40,128]{1,0:T(8,128)S(1)}, f32[40,128]{1,0:T(8,128)S(1)}, u32[]{:S(2)}, u32[]{:S(2)}) collective-permute-start(f32[40,128]{1,0:T(8,128)S(1)} %get-tuple-element.52), channel_id=1, source_target_pairs={{4,0},{5,1},{6,2},{7,3},{0,4},{1,5},{2,6},{3,7},{12,8},{13,9},{14,... | collective-permute-start | bytes 61448 | tf_op jit(solution)/shard_map/ppermute | solution.py:505
  26.3 3.8 %collective-permute-start.10 = (f32[40,128]{1,0:T(8,128)S(1)}, f32[40,128]{1,0:T(8,128)S(1)}, u32[]{:S(2)}, u32[]{:S(2)}) collective-permute-start(f32[40,128]{1,0:T(8,128)S(1)} %get-tuple-element.52), channel_id=1, source_target_pairs={{2,0},{3,1},{0,2},{1,3},{6,4},{7,5},{4,6},{5,7},{10,8},{11,9},{8,1... | collective-permute-start | bytes 61448 | tf_op jit(solution)/shard_map/ppermute | solution.py:505

commit v12 on v10

--- a/solution.py
+++ b/solution.py
@@ -488,13 +488,31 @@
     return (at + radix - k) % radix
 
 
-def target(at, k, radix):
-    return at ^ k if radix & (radix - 1) == 0 else (at + k) % radix
-
-
-def order(radix):
-    out = [(k, any(abs(source(at, k, radix) - at) == 1 for at in range(radix))) for k in range(1, radix)]
-    return sorted(out, key=lambda item: (not item[1], -item[0]))
+def matchings(count, radix, stride):
+    if (count, radix, stride) == (8, 4, 2):
+        swaps = ((1, 2), (3, 4), (5, 6), (0, 7)), ((0, 3), (1, 5), (2, 6), (4, 7)), ((0, 4), (1, 6), (2, 5), (3, 7))
+        out = []
+        for pairs in swaps:
+            senders = [0] * count
+            for a, b in pairs:
+                senders[a], senders[b] = b, a
+            out.append((senders, len(out) == 0))
+        return out
+    out = []
+    for k in range(1, radix):
+        senders = []
+        for me in range(count):
+            at, low = me // stride % radix, me % stride
+            senders.append(me - low + (source(at, k, radix) - at) * stride + (stride - 1 - low))
+        out.append((senders, any(abs(source(at, k, radix) - at) == 1 for at in range(radix))))
+    return sorted(out, key=lambda item: not item[1])
+
+
+def look_up(table):
+    me, value = lax.axis_index("gy"), jnp.int32(table[0])
+    for k in range(1, len(table)):
+        value = jnp.where(me == k, table[k], value)
+    return value
 
 
 def stages(count):
@@ -508,22 +526,21 @@
     return out if len(out) > 1 else out + [1]
 
 
-def exchange_stage(messages, radix, stride):
-    count, got = lax.axis_size("gy"), []
-    for (k, near), message in zip(order(radix), messages):
-        pairs = []
-        for me in range(count):
-            at, low = me // stride % radix, me % stride
-            sender = me - low + (source(at, k, radix) - at) * stride + (stride - 1 - low)
-            pairs.append((sender, me))
-        got.append(lax.ppermute(message, "gy", pairs))
-    return got
+def exchange_stage(messages, swaps):
+    return [
+        lax.ppermute(message, "gy", [(sender, me) for me, sender in enumerate(senders)])
+        for (senders, near), message in zip(swaps, messages)
+    ]
 
 
 class Group:
     def __init__(self, radix, stride, others, nx):
         self.radix, self.others, self.nx = radix, others, nx
         me = lax.axis_index("gy")
+        self.swaps = [
+            (look_up([sender // stride % radix for sender in senders]), near)
+            for senders, near in matchings(lax.axis_size("gy"), radix, stride)
+        ]
         self.at = lax.rem(lax.div(me, stride), radix)
         low = lax.rem(me, stride)
         self.lowest, self.highest = low == 0, low == stride - 1
@@ -531,8 +548,8 @@
     def map_of(self, place, own):
         rows = Rows(self.nx)
         out = own
-        for (k, near), ref in zip(order(self.radix), self.others):
-            here = source(self.at, k, self.radix) == place
+        for (sender, near), ref in zip(self.swaps, self.others):
+            here = sender == place
             got = [ref[i * rows.span : (i + 1) * rows.span] for i in range(2)]
             out = got if out is None else [jnp.where(here, new, old) for new, old in zip(got, out)]
         return out
@@ -554,10 +571,9 @@
 
     def collect(self, near, final):
         rows = Rows(self.nx)
-        for (k, adjacent), ref in zip(order(self.radix), self.others):
+        for (place, adjacent), ref in zip(self.swaps, self.others):
             if not adjacent:
                 continue
-            place = source(self.at, k, self.radix)
 
             @pl.when(self.lowest & (place == self.at - 1))
             def _():
@@ -591,13 +607,12 @@
     write_rows(near, ahead)
     group.collect(near, False)
     whole = group.total(own)
-    at = lax.div(lax.axis_index("gy"), stride * radix)
     if final == 0:
         write_rows(outs[0], whole)
         return
-    at = lax.rem(at, final)
-    for (k, adjacent), out in zip(order(final), outs):
-        up = target(at, k, final) > at
+    me, count = lax.axis_index("gy"), lax.axis_size("gy")
+    for (senders, adjacent), out in zip(matchings(count, final, stride * radix), outs):
+        up = look_up(senders) > me
         if not adjacent:
             write_rows(out, whole)
             continue
@@ -613,12 +628,11 @@
             out[rows.map : rows.final] = first_info[: rows.info]
 
 
-def full_message(nx, stride, radix, total, last_info, first_info, k):
+def full_message(nx, total, last_info, first_info, senders):
     rows = Rows(nx)
-    at = lax.axis_index("gy") // stride % radix
     onward = jnp.concatenate([total[: rows.map], last_info[: rows.info], first_info[rows.info : rows.info + rows.rest]])
     back = jnp.concatenate([total[: rows.map], first_info[: rows.info + rows.rest]])
-    message = jnp.where(target(at, k, radix) > at, onward, back)
+    message = jnp.where(look_up(senders) > lax.axis_index("gy"), onward, back)
     return jnp.pad(message, ((0, -rows.full % 8), (0, 0)))
 
 
@@ -823,13 +837,16 @@
     )(st, coarse, extra, early, across)
 
     near, messages = total, [message]
-    radices, stride = stages(lax.axis_size("gy")), 1
+    count = lax.axis_size("gy")
+    radices, stride = stages(count), 1
     for place, radix in enumerate(radices[:-1]):
+        swaps = matchings(count, radix, stride)
         if place:
-            messages = [full_message(nx, stride, radix, total, last_info, first_info, k) for k, _ in order(radix)]
-        others = exchange_stage(messages, radix, stride)
+            messages = [full_message(nx, total, last_info, first_info, senders) for senders, _ in swaps]
+        others = exchange_stage(messages, swaps)
         final = radices[-1] if place == len(radices) - 2 else 0
-        outs = [tall(lay.final if adjacent else lay.map) for _, adjacent in order(final)] if final else [tall(lay.map)]
+        following = matchings(count, final, stride * radix) if final else []
+        outs = [tall(lay.final if adjacent else lay.map) for _, adjacent in following] if final else [tall(lay.map)]
         near, *messages = pl.pallas_call(
             functools.partial(join_kernel, radix, stride, final, nx, place == 0),
             out_shape=(tall(lay.near), *outs),
@@ -840,7 +857,7 @@
         )(total, last_info, first_info, near, *others)
         total = total if final else messages[0]
         stride *= radix
-    got = exchange_stage(messages, radices[-1], stride)
+    got = exchange_stage(messages, matchings(count, radices[-1], stride))
 
     out = pl.pallas_call(
         functools.partial(third_kernel, radices[-1], stride),

time: 29.4 us -> 29 us (0.986)
  waiting for transfers between devices: 9.81 us -> 9.3 us
    ppermute x4, waiting for transfers between devices: 5.11 us -> 4.6 us  [exchange_stage(): lax.ppermute(message, 'gy', [(sender, me) for me, sender in enumerate(sen...]
where the time goes in v12:
time: 29 us; the launch traced here: 28.6 us
  starting transfers between devices  11.7 us (40%)
  waiting for transfers between devices  9.3 us (32%)
  Pallas kernels  7.44 us (26%)
    ppermute x7, starting transfers between devices, swap(): return lax.ppermute(x, axis, pairs)  8.31 us
    ppermute x7, waiting for transfers between devices, swap(): return lax.ppermute(x, axis, pairs)  4.71 us
    ppermute x4, waiting for transfers between devices, exchange_stage(): lax.ppermute(message, 'gy', [(sender, me) for me, sender in enumerate(sen...  4.6 us
    ppermute x4, starting transfers between devices, exchange_stage(): lax.ppermute(message, 'gy', [(sender, me) for me, sender in enumerate(sen...  3.42 us
    pallas_call x1, Pallas kernels, shards(): pl.pallas_call(functools.partial(third_kernel, radices[-1], stride), out_...  2.22 us
    pallas_call x1, Pallas kernels, shards(): pl.pallas_call(inner_kernel, out_shape=(state, rows), in_specs=[VMEM] * 4...  1.7 us
    pallas_call x1, Pallas kernels, shards(): pl.pallas_call(pack_kernel, out_shape=(strip, strip, f32((EARLY, nx, nz))...  1.65 us
    pallas_call x1, Pallas kernels, shards(): pl.pallas_call(second_kernel, out_shape=(state, rows, more, tall(lay.map)...  0.62 us
  transfers between devices with their start and end apart: 11, of which 5 were waited for; matrix products, arithmetic and copies ran while one was open for 0% of the time, Pallas kernels for 10%

profile of v12, /device:TPU:16, one launch (start us, length us, event | category | flops | bytes accessed | tf_op | source)
XLA Modules:
  0.0 28.6 jit_solution(2447623399269931297)
XLA Ops:
  0.0 1.6 %pack_x.1 = (f32[304,128]{1,0:T(8,128)S(1)}, f32[304,128]{1,0:T(8,128)S(1)}, f32[7,32,128]{2,1,0:T(8,128)S(1)}, f32[15,14,48,128]{3,2,1,0:T(8,128)S(1)}) custom-call(f32[2,12,32,128]{3,2,1,0:T(8,128)} %bitcast.5, f32[2,12,32,128]{3,2,1,0:T(8,128)} %bitcast.6, f32[12,32,128]{2,1,0:T(8,128)} %bitcast.7, f32[12,32,128]{2,1,0:T(8,128)} %bitcast.8), custom_call_target="tpu_custom_call" | custom-call | tf_op jit(solution)/shard_map/pack_x/pallas_call | solution.py:761
  1.7 1.6 %collective-permute-start = (f32[304,128]{1,0:T(8,128)S(1)}, f32[304,128]{1,0:T(8,128)S(1)}, u32[]{:S(2)}, u32[]{:S(2)}) collective-permute-start(f32[304,128]{1,0:T(8,128)S(1)} %get-tuple-element.31), channel_id=1, source_target_pairs={{0,8},{8,0},{16,24},{24,16},{1,9},{9,1},{17,25},{25,17},{2,10},{10... | collective-permute-start | bytes 466952 | tf_op jit(solution)/shard_map/ppermute | solution.py:746
  3.3 1.9 %collective-permute-start.1 = (f32[304,128]{1,0:T(8,128)S(1)}, f32[304,128]{1,0:T(8,128)S(1)}, u32[]{:S(2)}, u32[]{:S(2)}) collective-permute-start(f32[304,128]{1,0:T(8,128)S(1)} %get-tuple-element.32), channel_id=1, source_target_pairs={{8,16},{16,8},{9,17},{17,9},{10,18},{18,10},{11,19},{19,11},{12,20... | collective-permute-start | bytes 466952 | tf_op jit(solution)/shard_map/ppermute | solution.py:746
  5.2 0.7 %collective-permute-start.2 = (f32[7,32,128]{2,1,0:T(8,128)S(1)}, f32[7,32,128]{2,1,0:T(8,128)S(1)}, u32[]{:S(2)}, u32[]{:S(2)}) collective-permute-start(f32[7,32,128]{2,1,0:T(8,128)S(1)} %get-tuple-element.34), channel_id=1, source_target_pairs={{1,2},{2,1},{3,4},{4,3},{5,6},{6,5},{9,10},{10,9},{11,12},{12,11},... | collective-permute-start | bytes 344072 | tf_op jit(solution)/shard_map/ppermute | solution.py:746
  5.9 0.1 conduct.1.st_in
  6.0 1.5 %collective-permute-done.one = f32[304,128]{1,0:T(8,128)S(1)} collective-permute-done((f32[304,128]{1,0:T(8,128)S(1)}, f32[304,128]{1,0:T(8,128)S(1)}, u32[]{:S(2)}, u32[]{:S(2)}) %collective-permute-start) | collective-permute-done | bytes 155680 | tf_op jit(solution)/shard_map/ppermute | solution.py:746
  7.5 3.2 %collective-permute-done.1.two = f32[304,128]{1,0:T(8,128)S(1)} collective-permute-done((f32[304,128]{1,0:T(8,128)S(1)}, f32[304,128]{1,0:T(8,128)S(1)}, u32[]{:S(2)}, u32[]{:S(2)}) %collective-permute-start.1) | collective-permute-done | bytes 155680 | tf_op jit(solution)/shard_map/ppermute | solution.py:746
  10.7 0.6 %first.1 = (f32[15,14,48,128]{3,2,1,0:T(8,128)S(1)}, f32[144,128]{1,0:T(8,128)S(1)}, f32[3,40,128]{2,1,0:T(8,128)S(1)}, f32[3,40,128]{2,1,0:T(8,128)S(1)}, f32[3,40,128]{2,1,0:T(8,128)S(1)}) custom-call(f32[15,14,48,128]{3,2,1,0:T(8,128)S(1)} %conduct.1.st_in, f32[304,128]{1,0:T(8,128)S(1)} %collective-permute-done.one, ...), custom_call_target="tpu_custom_call", output_to_operand_aliasing={{0}: (0, {})} | custom-call | tf_op jit(solution)/shard_map/first/pallas_call | solution.py:786
  11.2 0.7 %collective-permute-start.6 = (f32[144,128]{1,0:T(8,128)S(1)}, f32[144,128]{1,0:T(8,128)S(1)}, u32[]{:S(2)}, u32[]{:S(2)}) collective-permute-start(f32[144,128]{1,0:T(8,128)S(1)} %get-tuple-element.43), channel_id=1, source_target_pairs={{1,2},{2,1},{3,4},{4,3},{5,6},{6,5},{9,10},{10,9},{11,12},{12,11},... | collective-permute-start | bytes 221192 | tf_op jit(solution)/shard_map/ppermute | solution.py:746
  11.9 2.9 %collective-permute-start.3 = (f32[3,40,128]{2,1,0:T(8,128)S(1)}, f32[3,40,128]{2,1,0:T(8,128)S(1)}, u32[]{:S(2)}, u32[]{:S(2)}) collective-permute-start(f32[3,40,128]{2,1,0:T(8,128)S(1)} %get-tuple-element.37), channel_id=1, source_target_pairs={{0,1},{1,0},{2,3},{3,2},{4,5},{5,4},{6,7},{7,6},{8,9},{9,8},{10,11... | collective-permute-start | bytes 184328 | tf_op jit(solution)/shard_map/ppermute | solution.py:746
  14.8 0.1 collective-permute-start.4
  14.9 0.4 %collective-permute-start.5 = (f32[3,40,128]{2,1,0:T(8,128)S(1)}, f32[3,40,128]{2,1,0:T(8,128)S(1)}, u32[]{:S(2)}, u32[]{:S(2)}) collective-permute-start(f32[3,40,128]{2,1,0:T(8,128)S(1)} %get-tuple-element.39), channel_id=1, source_target_pairs={{0,1},{1,0},{2,3},{3,2},{4,5},{5,4},{6,7},{7,6},{8,9},{9,8},{10,11... | collective-permute-start | bytes 184328 | tf_op jit(solution)/shard_map/ppermute | solution.py:746
  15.3 0.0 collective-permute-done.2.early
  15.3 1.7 %inner.1 = (f32[15,14,48,128]{3,2,1,0:T(8,128)S(1)}, f32[4,6,48,128]{3,2,1,0:T(8,128)S(1)}) custom-call(f32[15,14,48,128]{3,2,1,0:T(8,128)S(1)} %get-tuple-element.33.st_in, f32[304,128]{1,0:T(8,128)S(1)} %collective-permute-done.one, f32[304,128]{1,0:T(8,128)S(1)} %collective-permute-done.1.two, ...), custom_call_target="tpu_custom_call", output_to_operand_aliasing={{0}: (0, {})} | custom-call | flops 14745600 | bytes 18874368 | tf_op jit(solution)/shard_map/inner/pallas_call | solution.py:798
  17.1 0.6 %near.1 = (f32[15,14,48,128]{3,2,1,0:T(8,128)S(1)}, f32[4,6,48,128]{3,2,1,0:T(8,128)S(1)}, f32[6,48,128]{2,1,0:T(8,128)S(1)}) custom-call(f32[15,14,48,128]{3,2,1,0:T(8,128)S(1)} %get-tuple-element.35.st_in, f32[4,6,48,128]{3,2,1,0:T(8,128)S(1)} %get-tuple-element.36.coarse_in, ...), custom_call_target="tpu_custom_call", output_to_operand_aliasing={{0}: (0, {}), {1}: (1, {})} | custom-call | tf_op jit(solution)/shard_map/near/pallas_call | solution.py:818
  17.7 0.6 %second.1 = (f32[15,14,48,128]{3,2,1,0:T(8,128)S(1)}, f32[4,6,48,128]{3,2,1,0:T(8,128)S(1)}, f32[6,48,128]{2,1,0:T(8,128)S(1)}, f32[40,128]{1,0:T(8,128)S(1)}, f...) custom-call(f32[15,14,48,128]{3,2,1,0:T(8,128)S(1)} %get-tuple-eleme, ...), custom_call_target="tpu_custom_call", output_to_operand_aliasing={{0}: (0, {}), {1}: (1, {}), {2}: (2, {})} | custom-call | tf_op jit(solution)/shard_map/second/pallas_call | solution.py:828
  18.3 0.1 collective-permute-start.7
  18.4 1.2 %collective-permute-done.7.refs_4_ = f32[176,128]{1,0:T(8,128)S(1)} collective-permute-done((f32[176,128]{1,0:T(8,128)S(1)}, f32[176,128]{1,0:T(8,128)S(1)}, u32[]{:S(2)}, u32[]{:S(2)}) %collective-permute-start.7) | collective-permute-done | bytes 90144 | tf_op jit(solution)/shard_map/ppermute | solution.py:531
  19.7 1.5 %collective-permute-start.8 = (f32[144,128]{1,0:T(8,128)S(1)}, f32[144,128]{1,0:T(8,128)S(1)}, u32[]{:S(2)}, u32[]{:S(2)}) collective-permute-start(f32[144,128]{1,0:T(8,128)S(1)} %get-tuple-element.52), channel_id=1, source_target_pairs={{7,0},{2,1},{1,2},{4,3},{3,4},{6,5},{5,6},{0,7},{15,8},{10,9},{9,1... | collective-permute-start | bytes 221192 | tf_op jit(solution)/shard_map/ppermute | solution.py:531
  21.2 1.4 %collective-permute-start.9 = (f32[40,128]{1,0:T(8,128)S(1)}, f32[40,128]{1,0:T(8,128)S(1)}, u32[]{:S(2)}, u32[]{:S(2)}) collective-permute-start(f32[40,128]{1,0:T(8,128)S(1)} %get-tuple-element.53), channel_id=1, source_target_pairs={{3,0},{5,1},{6,2},{0,3},{7,4},{1,5},{2,6},{4,7},{11,8},{13,9},{14,... | collective-permute-start | bytes 61448 | tf_op jit(solution)/shard_map/ppermute | solution.py:531
  22.6 0.4 %collective-permute-start.10 = (f32[40,128]{1,0:T(8,128)S(1)}, f32[40,128]{1,0:T(8,128)S(1)}, u32[]{:S(2)}, u32[]{:S(2)}) collective-permute-start(f32[40,128]{1,0:T(8,128)S(1)} %get-tuple-element.54), channel_id=1, source_target_pairs={{4,0},{6,1},{5,2},{7,3},{0,4},{2,5},{1,6},{3,7},{12,8},{14,9},{13,... | collective-permute-start | bytes 61448 | tf_op jit(solution)/shard_map/ppermute | solution.py:531
  23.0 1.9 %collective-permute-done.9.refs_5_ = f32[40,128]{1,0:T(8,128)S(1)} collective-permute-done((f32[40,128]{1,0:T(8,128)S(1)}, f32[40,128]{1,0:T(8,128)S(1)}, u32[]{:S(2)}, u32[]{:S(2)}) %collective-permute-start.9) | collective-permute-done | bytes 20512 | tf_op jit(solution)/shard_map/ppermute | solution.py:531
  24.9 1.5 %collective-permute-done.10.refs_6_ = f32[40,128]{1,0:T(8,128)S(1)} collective-permute-done((f32[40,128]{1,0:T(8,128)S(1)}, f32[40,128]{1,0:T(8,128)S(1)}, u32[]{:S(2)}, u32[]{:S(2)}) %collective-permute-start.10) | collective-permute-done | bytes 20512 | tf_op jit(solution)/shard_map/ppermute | solution.py:531
  26.4 2.2 %third.1 = f32[2,12,32,128]{3,2,1,0:T(8,128)} custom-call(f32[15,14,48,128]{3,2,1,0:T(8,128)S(1)} %get-tuple-element.44.refs_0_, f32[6,48,128]{2,1,0:T(8,128)S(1)} %get-tuple-element.45.refs_1_, f32[4,6,48,128]{3,2,1,0:T(8,128)S(1)} %get-tuple-element.46.refs_2_, f32[280,128]{1,0:T(8,128)S(1)} %get-tuple-element.51.refs_3_, ...), custom_call_target="tpu_custom_call" | custom-call | tf_op jit(solution)/shard_map/third/pallas_call | solution.py:862
  (6 shorter events, 0.1 us)
Async XLA Ops:
  1.7 5.8 %collective-permute-start = (f32[304,128]{1,0:T(8,128)S(1)}, f32[304,128]{1,0:T(8,128)S(1)}, u32[]{:S(2)}, u32[]{:S(2)}) collective-permute-start(f32[304,128]{1,0:T(8,128)S(1)} %get-tuple-element.31), channel_id=1, source_target_pairs={{0,8},{8,0},{16,24},{24,16},{1,9},{9,1},{17,25},{25,17},{2,10},{10... | collective-permute-start | bytes 466952 | tf_op jit(solution)/shard_map/ppermute | solution.py:746
  3.3 7.4 %collective-permute-start.1 = (f32[304,128]{1,0:T(8,128)S(1)}, f32[304,128]{1,0:T(8,128)S(1)}, u32[]{:S(2)}, u32[]{:S(2)}) collective-permute-start(f32[304,128]{1,0:T(8,128)S(1)} %get-tuple-element.32), channel_id=1, source_target_pairs={{8,16},{16,8},{9,17},{17,9},{10,18},{18,10},{11,19},{19,11},{12,20... | collective-permute-start | bytes 466952 | tf_op jit(solution)/shard_map/ppermute | solution.py:746
  5.2 10.1 %collective-permute-start.2 = (f32[7,32,128]{2,1,0:T(8,128)S(1)}, f32[7,32,128]{2,1,0:T(8,128)S(1)}, u32[]{:S(2)}, u32[]{:S(2)}) collective-permute-start(f32[7,32,128]{2,1,0:T(8,128)S(1)} %get-tuple-element.34), channel_id=1, source_target_pairs={{1,2},{2,1},{3,4},{4,3},{5,6},{6,5},{9,10},{10,9},{11,12},{12,11},... | collective-permute-start | bytes 344072 | tf_op jit(solution)/shard_map/ppermute | solution.py:746
  11.2 6.4 %collective-permute-start.6 = (f32[144,128]{1,0:T(8,128)S(1)}, f32[144,128]{1,0:T(8,128)S(1)}, u32[]{:S(2)}, u32[]{:S(2)}) collective-permute-start(f32[144,128]{1,0:T(8,128)S(1)} %get-tuple-element.43), channel_id=1, source_target_pairs={{1,2},{2,1},{3,4},{4,3},{5,6},{6,5},{9,10},{10,9},{11,12},{12,11},... | collective-permute-start | bytes 221192 | tf_op jit(solution)/shard_map/ppermute | solution.py:746
  11.9 5.1 %collective-permute-start.3 = (f32[3,40,128]{2,1,0:T(8,128)S(1)}, f32[3,40,128]{2,1,0:T(8,128)S(1)}, u32[]{:S(2)}, u32[]{:S(2)}) collective-permute-start(f32[3,40,128]{2,1,0:T(8,128)S(1)} %get-tuple-element.37), channel_id=1, source_target_pairs={{0,1},{1,0},{2,3},{3,2},{4,5},{5,4},{6,7},{7,6},{8,9},{9,8},{10,11... | collective-permute-start | bytes 184328 | tf_op jit(solution)/shard_map/ppermute | solution.py:746
  14.8 2.2 %collective-permute-start.4 = (f32[3,40,128]{2,1,0:T(8,128)S(1)}, f32[3,40,128]{2,1,0:T(8,128)S(1)}, u32[]{:S(2)}, u32[]{:S(2)}) collective-permute-start(f32[3,40,128]{2,1,0:T(8,128)S(1)} %get-tuple-element.38), channel_id=1, source_target_pairs={{0,1},{1,0},{2,3},{3,2},{4,5},{5,4},{6,7},{7,6},{8,9},{9,8},{10,11... | collective-permute-start | bytes 184328 | tf_op jit(solution)/shard_map/ppermute | solution.py:746
  14.9 2.2 %collective-permute-start.5 = (f32[3,40,128]{2,1,0:T(8,128)S(1)}, f32[3,40,128]{2,1,0:T(8,128)S(1)}, u32[]{:S(2)}, u32[]{:S(2)}) collective-permute-start(f32[3,40,128]{2,1,0:T(8,128)S(1)} %get-tuple-element.39), channel_id=1, source_target_pairs={{0,1},{1,0},{2,3},{3,2},{4,5},{5,4},{6,7},{7,6},{8,9},{9,8},{10,11... | collective-permute-start | bytes 184328 | tf_op jit(solution)/shard_map/ppermute | solution.py:746
  18.3 1.4 %collective-permute-start.7 = (f32[176,128]{1,0:T(8,128)S(1)}, f32[176,128]{1,0:T(8,128)S(1)}, u32[]{:S(2)}, u32[]{:S(2)}) collective-permute-start(f32[176,128]{1,0:T(8,128)S(1)} %get-tuple-element.50), channel_id=1, source_target_pairs={{1,0},{0,1},{3,2},{2,3},{5,4},{4,5},{7,6},{6,7},{9,8},{8,9},{11,10... | collective-permute-start | bytes 270344 | tf_op jit(solution)/shard_map/ppermute | solution.py:531
  19.7 6.7 %collective-permute-start.8 = (f32[144,128]{1,0:T(8,128)S(1)}, f32[144,128]{1,0:T(8,128)S(1)}, u32[]{:S(2)}, u32[]{:S(2)}) collective-permute-start(f32[144,128]{1,0:T(8,128)S(1)} %get-tuple-element.52), channel_id=1, source_target_pairs={{7,0},{2,1},{1,2},{4,3},{3,4},{6,5},{5,6},{0,7},{15,8},{10,9},{9,1... | collective-permute-start | bytes 221192 | tf_op jit(solution)/shard_map/ppermute | solution.py:531
  21.2 3.7 %collective-permute-start.9 = (f32[40,128]{1,0:T(8,128)S(1)}, f32[40,128]{1,0:T(8,128)S(1)}, u32[]{:S(2)}, u32[]{:S(2)}) collective-permute-start(f32[40,128]{1,0:T(8,128)S(1)} %get-tuple-element.53), channel_id=1, source_target_pairs={{3,0},{5,1},{6,2},{0,3},{7,4},{1,5},{2,6},{4,7},{11,8},{13,9},{14,... | collective-permute-start | bytes 61448 | tf_op jit(solution)/shard_map/ppermute | solution.py:531
  22.6 3.8 %collective-permute-start.10 = (f32[40,128]{1,0:T(8,128)S(1)}, f32[40,128]{1,0:T(8,128)S(1)}, u32[]{:S(2)}, u32[]{:S(2)}) collective-permute-start(f32[40,128]{1,0:T(8,128)S(1)} %get-tuple-element.54), channel_id=1, source_target_pairs={{4,0},{6,1},{5,2},{7,3},{0,4},{2,5},{1,6},{3,7},{12,8},{14,9},{13,... | collective-permute-start | bytes 61448 | tf_op jit(solution)/shard_map/ppermute | solution.py:531

commit v13 on v12

--- a/solution.py
+++ b/solution.py
@@ -71,8 +71,12 @@
     return [s[four], g[four], k[five], rs[four], rg[four], c[four]]
 
 
+def x_order():
+    return (lax.axis_index("gx") % 2 == 0) == (lax.axis_index("gy") % 2 == 1)
+
+
 def pack_kernel(temps, right, exchange, coupling, one, two, early, st, sems):
-    even = lax.axis_index("gx") % 2 == 0
+    high_first = x_order()
     odd = lax.axis_index("gy") % 2 == 1
     ny, nx, nz = exchange.shape
     copies = []
@@ -92,8 +96,8 @@
             s, g, e, rs, rg, c = (st[plane, i, start : start + 8] for plane in (SA, GA, K, RS, RG, C))
             sides.append(strip_values(s, g, conductivity_of(s, e), rs, rg, c, start == PAD))
         for low, high, (plane, width) in zip(*sides, STRIP):
-            one[at : at + width] = jnp.where(even, high, low)
-            two[at : at + width] = jnp.where(even, low, high)
+            one[at : at + width] = jnp.where(high_first, high, low)
+            two[at : at + width] = jnp.where(high_first, low, high)
             at += width
     own = slice(PAD, PAD + nx)
     for is_odd, e, d in ((True, ny, ny - 1), (False, 1, 2)):
@@ -123,12 +127,12 @@
 
 
 def place_halo(st, one, two, y, nx):
-    even = lax.axis_index("gx") % 2 == 0
+    high_first = x_order()
     at, i = y * STRIP_ROWS, y + 1
     for plane, width in STRIP:
         a, b = one[at : at + width], two[at : at + width]
-        st[plane, i, PAD - width : PAD] = jnp.where(even, b, a)
-        st[plane, i, PAD + nx : PAD + nx + width] = jnp.where(even, a, b)
+        st[plane, i, PAD - width : PAD] = jnp.where(high_first, b, a)
+        st[plane, i, PAD + nx : PAD + nx + width] = jnp.where(high_first, a, b)
         at += width
 
 
@@ -746,6 +750,16 @@
     return lax.ppermute(x, axis, pairs)
 
 
+def swap_x(x, place):
+    columns = lax.axis_size("gy")
+    pairs = []
+    for column in range(columns):
+        for i in range((column + 1 + place) % 2, lax.axis_size("gx") - 1, 2):
+            a, b = i * columns + column, (i + 1) * columns + column
+            pairs += [(a, b), (b, a)]
+    return lax.ppermute(x, ("gx", "gy"), pairs)
+
+
 def shards(temps, right_side, exchange, coupling):
     temps, right_side = (jnp.transpose(a, (0, 2, 1, 3)) for a in (temps, right_side))
     exchange, coupling = (jnp.transpose(a, (1, 0, 2)) for a in (exchange, coupling))
@@ -767,7 +781,7 @@
         compiler_params=PARAMS,
         name="pack_x",
     )(temps, right_side, exchange, coupling)
-    one, two = swap(one, "gx", 0), swap(two, "gx", 1)
+    one, two = swap_x(one, 0), swap_x(two, 1)
     early = swap(early, "gy", 1)
 
     def letter(planes):

time: 29 us -> 32 us (1.10)
  the two profiles are of different devices: /device:TPU:16 before, /device:TPU:0 now
where the time goes in v13:
time: 32 us; the launch traced here: 31.8 us
  starting transfers between devices  17 us (53%)
  Pallas kernels  7.44 us (23%)
  waiting for transfers between devices  7.17 us (22%)
    ppermute x2, starting transfers between devices, swap_x(): return lax.ppermute(x, ('gx', 'gy'), pairs)  8.42 us
    ppermute x5, starting transfers between devices, swap(): return lax.ppermute(x, axis, pairs)  4.76 us
    ppermute x4, waiting for transfers between devices, exchange_stage(): lax.ppermute(message, 'gy', [(sender, me) for me, sender in enumerate(sen...  4.72 us
    ppermute x4, starting transfers between devices, exchange_stage(): lax.ppermute(message, 'gy', [(sender, me) for me, sender in enumerate(sen...  3.87 us
    ppermute x2, waiting for transfers between devices, swap_x(): return lax.ppermute(x, ('gx', 'gy'), pairs)  2.44 us
    pallas_call x1, Pallas kernels, shards(): pl.pallas_call(functools.partial(third_kernel, radices[-1], stride), out_...  2.22 us
    pallas_call x1, Pallas kernels, shards(): pl.pallas_call(inner_kernel, out_shape=(state, rows), in_specs=[VMEM] * 4...  1.7 us
    pallas_call x1, Pallas kernels, shards(): pl.pallas_call(pack_kernel, out_shape=(strip, strip, f32((EARLY, nx, nz))...  1.65 us
  transfers between devices with their start and end apart: 11, of which 4 were waited for; matrix products, arithmetic and copies ran while one was open for 0% of the time, Pallas kernels for 9%

profile of v13, /device:TPU:0, one launch (start us, length us, event | category | flops | bytes accessed | tf_op | source)
XLA Modules:
  0.0 31.8 jit_solution(10469334922053461270)
XLA Ops:
  0.0 1.6 %pack_x.1 = (f32[304,128]{1,0:T(8,128)S(1)}, f32[304,128]{1,0:T(8,128)S(1)}, f32[7,32,128]{2,1,0:T(8,128)S(1)}, f32[15,14,48,128]{3,2,1,0:T(8,128)S(1)}) custom-call(f32[2,12,32,128]{3,2,1,0:T(8,128)} %bitcast.5, f32[2,12,32,128]{3,2,1,0:T(8,128)} %bitcast.6, f32[12,32,128]{2,1,0:T(8,128)} %bitcast.7, f32[12,32,128]{2,1,0:T(8,128)} %bitcast.8), custom_call_target="tpu_custom_call" | custom-call | tf_op jit(solution)/shard_map/pack_x/pallas_call | solution.py:775
  1.7 0.7 %collective-permute-start = (f32[304,128]{1,0:T(8,128)S(1)}, f32[304,128]{1,0:T(8,128)S(1)}, u32[]{:S(2)}, u32[]{:S(2)}) collective-permute-start(f32[304,128]{1,0:T(8,128)S(1)} %get-tuple-element.31), channel_id=1, source_target_pairs={{8,16},{16,8},{1,9},{9,1},{17,25},{25,17},{10,18},{18,10},{3,11},{... | collective-permute-start | bytes 466952 | tf_op jit(solution)/shard_map/ppermute | solution.py:760
  2.3 7.7 %collective-permute-start.1 = (f32[304,128]{1,0:T(8,128)S(1)}, f32[304,128]{1,0:T(8,128)S(1)}, u32[]{:S(2)}, u32[]{:S(2)}) collective-permute-start(f32[304,128]{1,0:T(8,128)S(1)} %get-tuple-element.32), channel_id=1, source_target_pairs={{0,8},{8,0},{16,24},{24,16},{9,17},{17,9},{2,10},{10,2},{18,26},{2... | collective-permute-start | bytes 466952 | tf_op jit(solution)/shard_map/ppermute | solution.py:760
  10.1 0.7 %collective-permute-start.2 = (f32[7,32,128]{2,1,0:T(8,128)S(1)}, f32[7,32,128]{2,1,0:T(8,128)S(1)}, u32[]{:S(2)}, u32[]{:S(2)}) collective-permute-start(f32[7,32,128]{2,1,0:T(8,128)S(1)} %get-tuple-element.34), channel_id=1, source_target_pairs={{1,2},{2,1},{3,4},{4,3},{5,6},{6,5},{9,10},{10,9},{11,12},{12,11},... | collective-permute-start | bytes 344072 | tf_op jit(solution)/shard_map/ppermute | solution.py:750
  10.8 0.1 conduct.1.st_in
  10.8 0.0 collective-permute-done.one
  10.8 2.4 %collective-permute-done.1.two = f32[304,128]{1,0:T(8,128)S(1)} collective-permute-done((f32[304,128]{1,0:T(8,128)S(1)}, f32[304,128]{1,0:T(8,128)S(1)}, u32[]{:S(2)}, u32[]{:S(2)}) %collective-permute-start.1) | collective-permute-done | bytes 155680 | tf_op jit(solution)/shard_map/ppermute | solution.py:760
  13.3 0.6 %first.1 = (f32[15,14,48,128]{3,2,1,0:T(8,128)S(1)}, f32[144,128]{1,0:T(8,128)S(1)}, f32[3,40,128]{2,1,0:T(8,128)S(1)}, f32[3,40,128]{2,1,0:T(8,128)S(1)}, f32[3,40,128]{2,1,0:T(8,128)S(1)}) custom-call(f32[15,14,48,128]{3,2,1,0:T(8,128)S(1)} %conduct.1.st_in, f32[304,128]{1,0:T(8,128)S(1)} %collective-permute-done.one, ...), custom_call_target="tpu_custom_call", output_to_operand_aliasing={{0}: (0, {})} | custom-call | tf_op jit(solution)/shard_map/first/pallas_call | solution.py:800
  13.9 0.7 %collective-permute-start.6 = (f32[144,128]{1,0:T(8,128)S(1)}, f32[144,128]{1,0:T(8,128)S(1)}, u32[]{:S(2)}, u32[]{:S(2)}) collective-permute-start(f32[144,128]{1,0:T(8,128)S(1)} %get-tuple-element.43), channel_id=1, source_target_pairs={{1,2},{2,1},{3,4},{4,3},{5,6},{6,5},{9,10},{10,9},{11,12},{12,11},... | collective-permute-start | bytes 221192 | tf_op jit(solution)/shard_map/ppermute | solution.py:750
  14.5 2.9 %collective-permute-start.3 = (f32[3,40,128]{2,1,0:T(8,128)S(1)}, f32[3,40,128]{2,1,0:T(8,128)S(1)}, u32[]{:S(2)}, u32[]{:S(2)}) collective-permute-start(f32[3,40,128]{2,1,0:T(8,128)S(1)} %get-tuple-element.37), channel_id=1, source_target_pairs={{0,1},{1,0},{2,3},{3,2},{4,5},{5,4},{6,7},{7,6},{8,9},{9,8},{10,11... | collective-permute-start | bytes 184328 | tf_op jit(solution)/shard_map/ppermute | solution.py:750
  17.4 0.1 collective-permute-start.4
  17.5 0.4 %collective-permute-start.5 = (f32[3,40,128]{2,1,0:T(8,128)S(1)}, f32[3,40,128]{2,1,0:T(8,128)S(1)}, u32[]{:S(2)}, u32[]{:S(2)}) collective-permute-start(f32[3,40,128]{2,1,0:T(8,128)S(1)} %get-tuple-element.39), channel_id=1, source_target_pairs={{0,1},{1,0},{2,3},{3,2},{4,5},{5,4},{6,7},{7,6},{8,9},{9,8},{10,11... | collective-permute-start | bytes 184328 | tf_op jit(solution)/shard_map/ppermute | solution.py:750
  18.0 1.7 %inner.1 = (f32[15,14,48,128]{3,2,1,0:T(8,128)S(1)}, f32[4,6,48,128]{3,2,1,0:T(8,128)S(1)}) custom-call(f32[15,14,48,128]{3,2,1,0:T(8,128)S(1)} %get-tuple-element.33.st_in, f32[304,128]{1,0:T(8,128)S(1)} %collective-permute-done.one, f32[304,128]{1,0:T(8,128)S(1)} %collective-permute-done.1.two, ...), custom_call_target="tpu_custom_call", output_to_operand_aliasing={{0}: (0, {})} | custom-call | flops 14745600 | bytes 18874368 | tf_op jit(solution)/shard_map/inner/pallas_call | solution.py:812
  19.7 0.0 collective-permute-done.3.refs_0_
  19.7 0.0 collective-permute-done.4.refs_1_
  19.7 0.6 %near.1 = (f32[15,14,48,128]{3,2,1,0:T(8,128)S(1)}, f32[4,6,48,128]{3,2,1,0:T(8,128)S(1)}, f32[6,48,128]{2,1,0:T(8,128)S(1)}) custom-call(f32[15,14,48,128]{3,2,1,0:T(8,128)S(1)} %get-tuple-element.35.st_in, f32[4,6,48,128]{3,2,1,0:T(8,128)S(1)} %get-tuple-element.36.coarse_in, ...), custom_call_target="tpu_custom_call", output_to_operand_aliasing={{0}: (0, {}), {1}: (1, {})} | custom-call | tf_op jit(solution)/shard_map/near/pallas_call | solution.py:832
  20.3 0.6 %second.1 = (f32[15,14,48,128]{3,2,1,0:T(8,128)S(1)}, f32[4,6,48,128]{3,2,1,0:T(8,128)S(1)}, f32[6,48,128]{2,1,0:T(8,128)S(1)}, f32[40,128]{1,0:T(8,128)S(1)}, f...) custom-call(f32[15,14,48,128]{3,2,1,0:T(8,128)S(1)} %get-tuple-eleme, ...), custom_call_target="tpu_custom_call", output_to_operand_aliasing={{0}: (0, {}), {1}: (1, {}), {2}: (2, {})} | custom-call | tf_op jit(solution)/shard_map/second/pallas_call | solution.py:842
  20.9 0.4 %collective-permute-start.7 = (f32[176,128]{1,0:T(8,128)S(1)}, f32[176,128]{1,0:T(8,128)S(1)}, u32[]{:S(2)}, u32[]{:S(2)}) collective-permute-start(f32[176,128]{1,0:T(8,128)S(1)} %get-tuple-element.50), channel_id=1, source_target_pairs={{1,0},{0,1},{3,2},{2,3},{5,4},{4,5},{7,6},{6,7},{9,8},{8,9},{11,10... | collective-permute-start | bytes 270344 | tf_op jit(solution)/shard_map/ppermute | solution.py:535
  21.4 0.9 %collective-permute-done.7.refs_4_ = f32[176,128]{1,0:T(8,128)S(1)} collective-permute-done((f32[176,128]{1,0:T(8,128)S(1)}, f32[176,128]{1,0:T(8,128)S(1)}, u32[]{:S(2)}, u32[]{:S(2)}) %collective-permute-start.7) | collective-permute-done | bytes 90144 | tf_op jit(solution)/shard_map/ppermute | solution.py:535
  22.3 1.7 %collective-permute-start.8 = (f32[144,128]{1,0:T(8,128)S(1)}, f32[144,128]{1,0:T(8,128)S(1)}, u32[]{:S(2)}, u32[]{:S(2)}) collective-permute-start(f32[144,128]{1,0:T(8,128)S(1)} %get-tuple-element.52), channel_id=1, source_target_pairs={{7,0},{2,1},{1,2},{4,3},{3,4},{6,5},{5,6},{0,7},{15,8},{10,9},{9,1... | collective-permute-start | bytes 221192 | tf_op jit(solution)/shard_map/ppermute | solution.py:535
  24.1 1.7 %collective-permute-start.9 = (f32[40,128]{1,0:T(8,128)S(1)}, f32[40,128]{1,0:T(8,128)S(1)}, u32[]{:S(2)}, u32[]{:S(2)}) collective-permute-start(f32[40,128]{1,0:T(8,128)S(1)} %get-tuple-element.53), channel_id=1, source_target_pairs={{3,0},{5,1},{6,2},{0,3},{7,4},{1,5},{2,6},{4,7},{11,8},{13,9},{14,... | collective-permute-start | bytes 61448 | tf_op jit(solution)/shard_map/ppermute | solution.py:535
  25.8 2.2 %collective-permute-done.9.refs_5_ = f32[40,128]{1,0:T(8,128)S(1)} collective-permute-done((f32[40,128]{1,0:T(8,128)S(1)}, f32[40,128]{1,0:T(8,128)S(1)}, u32[]{:S(2)}, u32[]{:S(2)}) %collective-permute-start.9) | collective-permute-done | bytes 20512 | tf_op jit(solution)/shard_map/ppermute | solution.py:535
  28.0 1.5 %collective-permute-done.10.refs_6_ = f32[40,128]{1,0:T(8,128)S(1)} collective-permute-done((f32[40,128]{1,0:T(8,128)S(1)}, f32[40,128]{1,0:T(8,128)S(1)}, u32[]{:S(2)}, u32[]{:S(2)}) %collective-permute-start.10) | collective-permute-done | bytes 20512 | tf_op jit(solution)/shard_map/ppermute | solution.py:535
  29.6 2.2 %third.1 = f32[2,12,32,128]{3,2,1,0:T(8,128)} custom-call(f32[15,14,48,128]{3,2,1,0:T(8,128)S(1)} %get-tuple-element.44.refs_0_, f32[6,48,128]{2,1,0:T(8,128)S(1)} %get-tuple-element.45.refs_1_, f32[4,6,48,128]{3,2,1,0:T(8,128)S(1)} %get-tuple-element.46.refs_2_, f32[280,128]{1,0:T(8,128)S(1)} %get-tuple-element.51.refs_3_, ...), custom_call_target="tpu_custom_call" | custom-call | tf_op jit(solution)/shard_map/third/pallas_call | solution.py:876
  (6 shorter events, 0.1 us)
Async XLA Ops:
  1.7 9.2 %collective-permute-start = (f32[304,128]{1,0:T(8,128)S(1)}, f32[304,128]{1,0:T(8,128)S(1)}, u32[]{:S(2)}, u32[]{:S(2)}) collective-permute-start(f32[304,128]{1,0:T(8,128)S(1)} %get-tuple-element.31), channel_id=1, source_target_pairs={{8,16},{16,8},{1,9},{9,1},{17,25},{25,17},{10,18},{18,10},{3,11},{... | collective-permute-start | bytes 466952 | tf_op jit(solution)/shard_map/ppermute | solution.py:760
  2.3 10.9 %collective-permute-start.1 = (f32[304,128]{1,0:T(8,128)S(1)}, f32[304,128]{1,0:T(8,128)S(1)}, u32[]{:S(2)}, u32[]{:S(2)}) collective-permute-start(f32[304,128]{1,0:T(8,128)S(1)} %get-tuple-element.32), channel_id=1, source_target_pairs={{0,8},{8,0},{16,24},{24,16},{9,17},{17,9},{2,10},{10,2},{18,26},{2... | collective-permute-start | bytes 466952 | tf_op jit(solution)/shard_map/ppermute | solution.py:760
  10.1 7.9 %collective-permute-start.2 = (f32[7,32,128]{2,1,0:T(8,128)S(1)}, f32[7,32,128]{2,1,0:T(8,128)S(1)}, u32[]{:S(2)}, u32[]{:S(2)}) collective-permute-start(f32[7,32,128]{2,1,0:T(8,128)S(1)} %get-tuple-element.34), channel_id=1, source_target_pairs={{1,2},{2,1},{3,4},{4,3},{5,6},{6,5},{9,10},{10,9},{11,12},{12,11},... | collective-permute-start | bytes 344072 | tf_op jit(solution)/shard_map/ppermute | solution.py:750
  13.9 6.4 %collective-permute-start.6 = (f32[144,128]{1,0:T(8,128)S(1)}, f32[144,128]{1,0:T(8,128)S(1)}, u32[]{:S(2)}, u32[]{:S(2)}) collective-permute-start(f32[144,128]{1,0:T(8,128)S(1)} %get-tuple-element.43), channel_id=1, source_target_pairs={{1,2},{2,1},{3,4},{4,3},{5,6},{6,5},{9,10},{10,9},{11,12},{12,11},... | collective-permute-start | bytes 221192 | tf_op jit(solution)/shard_map/ppermute | solution.py:750
  14.5 5.1 %collective-permute-start.3 = (f32[3,40,128]{2,1,0:T(8,128)S(1)}, f32[3,40,128]{2,1,0:T(8,128)S(1)}, u32[]{:S(2)}, u32[]{:S(2)}) collective-permute-start(f32[3,40,128]{2,1,0:T(8,128)S(1)} %get-tuple-element.37), channel_id=1, source_target_pairs={{0,1},{1,0},{2,3},{3,2},{4,5},{5,4},{6,7},{7,6},{8,9},{9,8},{10,11... | collective-permute-start | bytes 184328 | tf_op jit(solution)/shard_map/ppermute | solution.py:750
  17.4 2.2 %collective-permute-start.4 = (f32[3,40,128]{2,1,0:T(8,128)S(1)}, f32[3,40,128]{2,1,0:T(8,128)S(1)}, u32[]{:S(2)}, u32[]{:S(2)}) collective-permute-start(f32[3,40,128]{2,1,0:T(8,128)S(1)} %get-tuple-element.38), channel_id=1, source_target_pairs={{0,1},{1,0},{2,3},{3,2},{4,5},{5,4},{6,7},{7,6},{8,9},{9,8},{10,11... | collective-permute-start | bytes 184328 | tf_op jit(solution)/shard_map/ppermute | solution.py:750
  17.5 2.2 %collective-permute-start.5 = (f32[3,40,128]{2,1,0:T(8,128)S(1)}, f32[3,40,128]{2,1,0:T(8,128)S(1)}, u32[]{:S(2)}, u32[]{:S(2)}) collective-permute-start(f32[3,40,128]{2,1,0:T(8,128)S(1)} %get-tuple-element.39), channel_id=1, source_target_pairs={{0,1},{1,0},{2,3},{3,2},{4,5},{5,4},{6,7},{7,6},{8,9},{9,8},{10,11... | collective-permute-start | bytes 184328 | tf_op jit(solution)/shard_map/ppermute | solution.py:750
  20.9 1.4 %collective-permute-start.7 = (f32[176,128]{1,0:T(8,128)S(1)}, f32[176,128]{1,0:T(8,128)S(1)}, u32[]{:S(2)}, u32[]{:S(2)}) collective-permute-start(f32[176,128]{1,0:T(8,128)S(1)} %get-tuple-element.50), channel_id=1, source_target_pairs={{1,0},{0,1},{3,2},{2,3},{5,4},{4,5},{7,6},{6,7},{9,8},{8,9},{11,10... | collective-permute-start | bytes 270344 | tf_op jit(solution)/shard_map/ppermute | solution.py:535
  22.3 7.2 %collective-permute-start.8 = (f32[144,128]{1,0:T(8,128)S(1)}, f32[144,128]{1,0:T(8,128)S(1)}, u32[]{:S(2)}, u32[]{:S(2)}) collective-permute-start(f32[144,128]{1,0:T(8,128)S(1)} %get-tuple-element.52), channel_id=1, source_target_pairs={{7,0},{2,1},{1,2},{4,3},{3,4},{6,5},{5,6},{0,7},{15,8},{10,9},{9,1... | collective-permute-start | bytes 221192 | tf_op jit(solution)/shard_map/ppermute | solution.py:535
  24.1 4.0 %collective-permute-start.9 = (f32[40,128]{1,0:T(8,128)S(1)}, f32[40,128]{1,0:T(8,128)S(1)}, u32[]{:S(2)}, u32[]{:S(2)}) collective-permute-start(f32[40,128]{1,0:T(8,128)S(1)} %get-tuple-element.53), channel_id=1, source_target_pairs={{3,0},{5,1},{6,2},{0,3},{7,4},{1,5},{2,6},{4,7},{11,8},{13,9},{14,... | collective-permute-start | bytes 61448 | tf_op jit(solution)/shard_map/ppermute | solution.py:535
  25.8 3.8 %collective-permute-start.10 = (f32[40,128]{1,0:T(8,128)S(1)}, f32[40,128]{1,0:T(8,128)S(1)}, u32[]{:S(2)}, u32[]{:S(2)}) collective-permute-start(f32[40,128]{1,0:T(8,128)S(1)} %get-tuple-element.54), channel_id=1, source_target_pairs={{4,0},{6,1},{5,2},{7,3},{0,4},{2,5},{1,6},{3,7},{12,8},{14,9},{13,... | collective-permute-start | bytes 61448 | tf_op jit(solution)/shard_map/ppermute | solution.py:535

commit v14 on v12

--- a/solution.py
+++ b/solution.py
@@ -18,7 +18,7 @@
 (M_S, M_G, M_K, M_C, M_FY, M_1S, M_1G, M_2S, M_2G) = range(9)
 MESSAGE, EARLY, THIRD = 9, 7, 3
 
-GROUP = 4
+GROUP = 6
 
 VMEM = pl.BlockSpec(memory_space=pltpu.VMEM)
 HBM = pl.BlockSpec(memory_space=pltpu.HBM)
@@ -53,7 +53,7 @@
     return jnp.where((row >= low) & (row < high), 1.0, 0.0).astype(jnp.float32)
 
 
-STRIP = ((SA, WX - 1), (GA, WX - 1), (K, WX), (RS, WX - 1), (RG, WX - 1), (C, WX - 1))
+STRIP = ((SA, WX - 1), (GA, WX - 1), (K, WX), (C, WX - 1), (RS, WX - 1), (RG, WX - 1))
 STRIP_ROWS = sum(width for plane, width in STRIP)
 
 
@@ -61,14 +61,23 @@
     return 1.0 + 4.0 * exchange * s * s * s
 
 
-def strip_values(s, g, k, rs, rg, c, low):
-    out, inn = (WX - 1, WX - 2) if low else (8 - WX, 9 - WX)
-    four = slice(0, WX - 1) if low else slice(9 - WX, 8)
-    five = slice(0, WX) if low else slice(8 - WX, 8)
+def strip_rows(low):
+    if low:
+        return WX - 1, WX - 2, slice(0, WX - 1), slice(0, WX)
+    return 8 - WX, 9 - WX, slice(9 - WX, 8), slice(8 - WX, 8)
+
+
+def strip_values(s, g, k, c, low):
+    _, _, four, five = strip_rows(low)
+    return [s[four], g[four], k[five], c[four]]
+
+
+def strip_sides(s, g, k, rs, rg, low):
+    out, inn, four, _ = strip_rows(low)
     row = lax.broadcasted_iota(jnp.int32, s.shape, 0)
     rs = rs + jnp.where(row == inn, 0.5 * (k[inn : inn + 1] + k[out : out + 1]) * s[out : out + 1], 0.0)
     rg = rg + jnp.where(row == inn, CONDUCT * g[out : out + 1], 0.0)
-    return [s[four], g[four], k[five], rs[four], rg[four], c[four]]
+    return [rs[four], rg[four]]
 
 
 def pack_kernel(temps, right, exchange, coupling, one, two, early, st, sems):
@@ -83,18 +92,29 @@
         copies.append(pltpu.make_async_copy(ref, to, sems.at[k]))
     for copy in copies:
         copy.start()
-    for copy in copies:
+    def put(i, at, sides):
+        at += (i - 1) * STRIP_ROWS
+        for low, high in zip(*sides):
+            one[at : at + low.shape[0]] = jnp.where(even, high, low)
+            two[at : at + low.shape[0]] = jnp.where(even, low, high)
+            at += low.shape[0]
+
+    for copy in copies[:4]:
         copy.wait()
-    at = 0
     for i in range(1, ny + 1):
         sides = []
         for start in (PAD, PAD + nx - 8):
-            s, g, e, rs, rg, c = (st[plane, i, start : start + 8] for plane in (SA, GA, K, RS, RG, C))
-            sides.append(strip_values(s, g, conductivity_of(s, e), rs, rg, c, start == PAD))
-        for low, high, (plane, width) in zip(*sides, STRIP):
-            one[at : at + width] = jnp.where(even, high, low)
-            two[at : at + width] = jnp.where(even, low, high)
-            at += width
+            s, g, e, c = (st[plane, i, start : start + 8] for plane in (SA, GA, K, C))
+            sides.append(strip_values(s, g, conductivity_of(s, e), c, start == PAD))
+        put(i, 0, sides)
+    for copy in copies[4:]:
+        copy.wait()
+    for i in range(1, ny + 1):
+        sides = []
+        for start in (PAD, PAD + nx - 8):
+            s, g, e, rs, rg = (st[plane, i, start : start + 8] for plane in (SA, GA, K, RS, RG))
+            sides.append(strip_sides(s, g, conductivity_of(s, e), rs, rg, start == PAD))
+        put(i, STRIP_ROWS - 2 * (WX - 1), sides)
     own = slice(PAD, PAD + nx)
     for is_odd, e, d in ((True, ny, ny - 1), (False, 1, 2)):
 
@@ -275,36 +295,40 @@
     outer[k, CROP : outer.shape[1] - CROP] = refs[k // THIRD][k % THIRD]
 
 
-def write_message(write, st, onward, edge):
-    for go in (True, False):
-
-        @pl.when(onward == go)
-        def _():
-            for k, value in enumerate(send_planes(st, go, edge)):
-                write(k, value)
-
-
-def first_kernel(st_in, one, two, st, across, *beside):
-    del st_in
+def first_end(st, one, two, after, write):
     planes, rows, ext, nz = st.shape
     ny, nx = rows - 2, ext - 2 * PAD
-    shape = (ext, nz)
-    mask = x_mask(shape, nx)
-    edge = edge_weights(shape)
-
-    for y in list(range(4)) + list(range(ny - 4, ny)):
-        place_halo(st, one, two, y, nx)
-    for i in (1, ny):
-        fx, fz, h, diag = faces(st[K, i])
-        st[FX, i], st[FZ, i], st[H, i] = fx, fz, h
-    st[FY, 1] = 0.5 * (st[K, 1] + st[K, 2])
-    st[FY, ny - 3] = 0.5 * (st[K, ny - 3] + st[K, ny - 2])
-    ends = [2, 3, ny - 2, ny - 1]
-    grouped(ends, lambda i: row_coefficients(st, i, mask))
-    grouped(ends, lambda i: row_sweep(st, i, SA, SB, edge))
-    odd = lax.axis_index("gy") % 2 == 1
-    write_message(functools.partial(write_across, across), st, odd, edge)
-    write_message(functools.partial(write_beside, beside), st, jnp.logical_not(odd), edge)
+    mask = x_mask((ext, nz), nx)
+    edge = edge_weights((ext, nz))
+    e, d, f = (ny, ny - 1, ny - 2) if after else (1, 2, 3)
+    for i in (e, d, f):
+        place_halo(st, one, two, i - 1, nx)
+    fx, fz, h, diag = faces(st[K, e])
+    st[FX, e], st[FZ, e], st[H, e] = fx, fz, h
+    st[FY, min(e, d)] = 0.5 * (st[K, e] + st[K, d])
+    st[FY, min(d, f)] = 0.5 * (st[K, d] + st[K, f])
+    grouped([d], lambda i: row_coefficients(st, i, mask))
+    grouped([d], lambda i: row_sweep(st, i, SA, SB, edge))
+    for k, value in enumerate(send_planes(st, after, edge)):
+        write(k, value)
+
+
+def either_first(st, one, two, after, write):
+    for is_after in (True, False):
+
+        @pl.when(after == is_after)
+        def _():
+            first_end(st, one, two, is_after, write)
+
+
+def first_kernel(st_in, one, two, st, across):
+    del st_in
+    either_first(st, one, two, lax.axis_index("gy") % 2 == 1, functools.partial(write_across, across))
+
+
+def other_kernel(st_in, one, two, st, *beside):
+    del st_in
+    either_first(st, one, two, lax.axis_index("gy") % 2 == 0, functools.partial(write_beside, beside))
 
 
 def outer_residual(st, i, s_at, rs, rg, fy_out, edge, after):
@@ -350,10 +374,10 @@
     shape = (ext, nz)
     mask = x_mask(shape, nx)
     edge = edge_weights(shape)
-    for y in range(4, ny - 4):
+    for y in range(3, ny - 3):
         place_halo(st, one, two, y, nx)
-    grouped(list(range(4, ny - 2)), lambda i: row_coefficients(st, i, mask))
-    grouped(list(range(4, ny - 2)), lambda i: row_sweep(st, i, SA, SB, edge))
+    grouped(list(range(3, ny - 1)), lambda i: row_coefficients(st, i, mask))
+    grouped(list(range(3, ny - 1)), lambda i: row_sweep(st, i, SA, SB, edge))
     grouped(list(range(3, ny - 1)), lambda i: row_sweep(st, i, SB, SA, edge))
     for j in range(2, ny // 2 - 2):
         for ref, at, value in coarse_row(st, coarse, j, mask, edge):
@@ -783,14 +807,23 @@
         cost_estimate=cost(2 * ny, ext * nz),
         name="conduct",
     )(st)
-    st, across, *beside = pl.pallas_call(
+    st, across = pl.pallas_call(
         first_kernel,
-        out_shape=(state, f32((across_parts(ext)[1], nz))) + (letter(THIRD),) * (MESSAGE // THIRD),
+        out_shape=(state, f32((across_parts(ext)[1], nz))),
         in_specs=[VMEM] * 3,
-        out_specs=(VMEM,) * (2 + MESSAGE // THIRD),
+        out_specs=(VMEM,) * 2,
         input_output_aliases={0: 0},
         compiler_params=PARAMS,
         name="first",
+    )(st, one, two)
+    st, *beside = pl.pallas_call(
+        other_kernel,
+        out_shape=(state,) + (letter(THIRD),) * (MESSAGE // THIRD),
+        in_specs=[VMEM] * 3,
+        out_specs=(VMEM,) * (1 + MESSAGE // THIRD),
+        input_output_aliases={0: 0},
+        compiler_params=PARAMS,
+        name="other",
     )(st, one, two)
     across = swap(across, "gy", 1)
 

time: 29 us -> 28.7 us (0.990)
    pallas_call x1, Pallas kernels: 0.57 us -> 0.2 us  [shards(): pl.pallas_call(first_kernel, out_shape=(state, f32((across_parts(ext)[1],...]
  transfers between devices with their start and end apart: 11 -> 11, of which waited for: 5 -> 5; matrix products, arithmetic and copies ran while one was open for 0% -> 0% of each run, Pallas kernels for 10% -> 11%
where the time goes in v14:
time: 28.7 us; the launch traced here: 28.5 us
  starting transfers between devices  11.7 us (41%)
  waiting for transfers between devices  9.19 us (32%)
  Pallas kernels  7.47 us (26%)
    ppermute x7, starting transfers between devices, swap(): return lax.ppermute(x, axis, pairs)  8.3 us
    ppermute x7, waiting for transfers between devices, swap(): return lax.ppermute(x, axis, pairs)  4.7 us
    ppermute x4, waiting for transfers between devices, exchange_stage(): lax.ppermute(message, 'gy', [(sender, me) for me, sender in enumerate(sen...  4.49 us
    ppermute x4, starting transfers between devices, exchange_stage(): lax.ppermute(message, 'gy', [(sender, me) for me, sender in enumerate(sen...  3.42 us
    pallas_call x1, Pallas kernels, shards(): pl.pallas_call(functools.partial(third_kernel, radices[-1], stride), out_...  2.14 us
    pallas_call x1, Pallas kernels, shards(): pl.pallas_call(inner_kernel, out_shape=(state, rows), in_specs=[VMEM] * 4...  1.97 us
    pallas_call x1, Pallas kernels, shards(): pl.pallas_call(pack_kernel, out_shape=(strip, strip, f32((EARLY, nx, nz))...  1.62 us
    pallas_call x1, Pallas kernels, shards(): pl.pallas_call(second_kernel, out_shape=(state, rows, more, tall(lay.map)...  0.62 us
  transfers between devices with their start and end apart: 11, of which 5 were waited for; matrix products, arithmetic and copies ran while one was open for 0% of the time, Pallas kernels for 11%

profile of v14, /device:TPU:16, one launch (start us, length us, event | category | flops | bytes accessed | tf_op | source)
XLA Modules:
  0.0 28.5 jit_solution(17321260437326622378)
XLA Ops:
  0.0 1.6 %pack_x.1 = (f32[304,128]{1,0:T(8,128)S(1)}, f32[304,128]{1,0:T(8,128)S(1)}, f32[7,32,128]{2,1,0:T(8,128)S(1)}, f32[15,14,48,128]{3,2,1,0:T(8,128)S(1)}) custom-call(f32[2,12,32,128]{3,2,1,0:T(8,128)} %bitcast.5, f32[2,12,32,128]{3,2,1,0:T(8,128)} %bitcast.6, f32[12,32,128]{2,1,0:T(8,128)} %bitcast.7, f32[12,32,128]{2,1,0:T(8,128)} %bitcast.8), custom_call_target="tpu_custom_call" | custom-call | tf_op jit(solution)/shard_map/pack_x/pallas_call | solution.py:785
  1.6 1.6 %collective-permute-start = (f32[304,128]{1,0:T(8,128)S(1)}, f32[304,128]{1,0:T(8,128)S(1)}, u32[]{:S(2)}, u32[]{:S(2)}) collective-permute-start(f32[304,128]{1,0:T(8,128)S(1)} %get-tuple-element.32), channel_id=1, source_target_pairs={{0,8},{8,0},{16,24},{24,16},{1,9},{9,1},{17,25},{25,17},{2,10},{10... | collective-permute-start | bytes 466952 | tf_op jit(solution)/shard_map/ppermute | solution.py:770
  3.3 1.9 %collective-permute-start.1 = (f32[304,128]{1,0:T(8,128)S(1)}, f32[304,128]{1,0:T(8,128)S(1)}, u32[]{:S(2)}, u32[]{:S(2)}) collective-permute-start(f32[304,128]{1,0:T(8,128)S(1)} %get-tuple-element.33), channel_id=1, source_target_pairs={{8,16},{16,8},{9,17},{17,9},{10,18},{18,10},{11,19},{19,11},{12,20... | collective-permute-start | bytes 466952 | tf_op jit(solution)/shard_map/ppermute | solution.py:770
  5.2 0.7 %collective-permute-start.2 = (f32[7,32,128]{2,1,0:T(8,128)S(1)}, f32[7,32,128]{2,1,0:T(8,128)S(1)}, u32[]{:S(2)}, u32[]{:S(2)}) collective-permute-start(f32[7,32,128]{2,1,0:T(8,128)S(1)} %get-tuple-element.36), channel_id=1, source_target_pairs={{1,2},{2,1},{3,4},{4,3},{5,6},{6,5},{9,10},{10,9},{11,12},{12,11},... | collective-permute-start | bytes 344072 | tf_op jit(solution)/shard_map/ppermute | solution.py:770
  5.9 0.1 conduct.1.st_in
  5.9 1.5 %collective-permute-done.one = f32[304,128]{1,0:T(8,128)S(1)} collective-permute-done((f32[304,128]{1,0:T(8,128)S(1)}, f32[304,128]{1,0:T(8,128)S(1)}, u32[]{:S(2)}, u32[]{:S(2)}) %collective-permute-start) | collective-permute-done | bytes 155680 | tf_op jit(solution)/shard_map/ppermute | solution.py:770
  7.4 3.2 %collective-permute-done.1.two = f32[304,128]{1,0:T(8,128)S(1)} collective-permute-done((f32[304,128]{1,0:T(8,128)S(1)}, f32[304,128]{1,0:T(8,128)S(1)}, u32[]{:S(2)}, u32[]{:S(2)}) %collective-permute-start.1) | collective-permute-done | bytes 155680 | tf_op jit(solution)/shard_map/ppermute | solution.py:770
  10.6 0.2 first.1
  10.8 0.7 %collective-permute-start.6 = (f32[144,128]{1,0:T(8,128)S(1)}, f32[144,128]{1,0:T(8,128)S(1)}, u32[]{:S(2)}, u32[]{:S(2)}) collective-permute-start(f32[144,128]{1,0:T(8,128)S(1)} %get-tuple-element.45), channel_id=1, source_target_pairs={{1,2},{2,1},{3,4},{4,3},{5,6},{6,5},{9,10},{10,9},{11,12},{12,11},... | collective-permute-start | bytes 221192 | tf_op jit(solution)/shard_map/ppermute | solution.py:770
  11.5 0.2 other.1
  11.7 2.9 %collective-permute-start.3 = (f32[3,40,128]{2,1,0:T(8,128)S(1)}, f32[3,40,128]{2,1,0:T(8,128)S(1)}, u32[]{:S(2)}, u32[]{:S(2)}) collective-permute-start(f32[3,40,128]{2,1,0:T(8,128)S(1)} %get-tuple-element.39), channel_id=1, source_target_pairs={{0,1},{1,0},{2,3},{3,2},{4,5},{5,4},{6,7},{7,6},{8,9},{9,8},{10,11... | collective-permute-start | bytes 184328 | tf_op jit(solution)/shard_map/ppermute | solution.py:770
  14.7 0.1 collective-permute-start.4
  14.7 0.4 %collective-permute-start.5 = (f32[3,40,128]{2,1,0:T(8,128)S(1)}, f32[3,40,128]{2,1,0:T(8,128)S(1)}, u32[]{:S(2)}, u32[]{:S(2)}) collective-permute-start(f32[3,40,128]{2,1,0:T(8,128)S(1)} %get-tuple-element.41), channel_id=1, source_target_pairs={{0,1},{1,0},{2,3},{3,2},{4,5},{5,4},{6,7},{7,6},{8,9},{9,8},{10,11... | collective-permute-start | bytes 184328 | tf_op jit(solution)/shard_map/ppermute | solution.py:770
  15.2 2.0 %inner.1 = (f32[15,14,48,128]{3,2,1,0:T(8,128)S(1)}, f32[4,6,48,128]{3,2,1,0:T(8,128)S(1)}) custom-call(f32[15,14,48,128]{3,2,1,0:T(8,128)S(1)} %get-tuple-element.35.st_in, f32[304,128]{1,0:T(8,128)S(1)} %collective-permute-done.one, f32[304,128]{1,0:T(8,128)S(1)} %collective-permute-done.1.two, ...), custom_call_target="tpu_custom_call", output_to_operand_aliasing={{0}: (0, {})} | custom-call | flops 14745600 | bytes 18874368 | tf_op jit(solution)/shard_map/inner/pallas_call | solution.py:831
  17.2 0.6 %near.1 = (f32[15,14,48,128]{3,2,1,0:T(8,128)S(1)}, f32[4,6,48,128]{3,2,1,0:T(8,128)S(1)}, f32[6,48,128]{2,1,0:T(8,128)S(1)}) custom-call(f32[15,14,48,128]{3,2,1,0:T(8,128)S(1)} %get-tuple-element.37.st_in, f32[4,6,48,128]{3,2,1,0:T(8,128)S(1)} %get-tuple-element.38.coarse_in, ...), custom_call_target="tpu_custom_call", output_to_operand_aliasing={{0}: (0, {}), {1}: (1, {})} | custom-call | tf_op jit(solution)/shard_map/near/pallas_call | solution.py:851
  17.8 0.6 %second.1 = (f32[15,14,48,128]{3,2,1,0:T(8,128)S(1)}, f32[4,6,48,128]{3,2,1,0:T(8,128)S(1)}, f32[6,48,128]{2,1,0:T(8,128)S(1)}, f32[40,128]{1,0:T(8,128)S(1)}, f...) custom-call(f32[15,14,48,128]{3,2,1,0:T(8,128)S(1)} %get-tuple-eleme, ...), custom_call_target="tpu_custom_call", output_to_operand_aliasing={{0}: (0, {}), {1}: (1, {}), {2}: (2, {})} | custom-call | tf_op jit(solution)/shard_map/second/pallas_call | solution.py:861
  18.4 0.1 collective-permute-start.7
  18.6 1.2 %collective-permute-done.7.refs_4_ = f32[176,128]{1,0:T(8,128)S(1)} collective-permute-done((f32[176,128]{1,0:T(8,128)S(1)}, f32[176,128]{1,0:T(8,128)S(1)}, u32[]{:S(2)}, u32[]{:S(2)}) %collective-permute-start.7) | collective-permute-done | bytes 90144 | tf_op jit(solution)/shard_map/ppermute | solution.py:555
  19.8 1.0 %collective-permute-start.8 = (f32[144,128]{1,0:T(8,128)S(1)}, f32[144,128]{1,0:T(8,128)S(1)}, u32[]{:S(2)}, u32[]{:S(2)}) collective-permute-start(f32[144,128]{1,0:T(8,128)S(1)} %get-tuple-element.54), channel_id=1, source_target_pairs={{7,0},{2,1},{1,2},{4,3},{3,4},{6,5},{5,6},{0,7},{15,8},{10,9},{9,1... | collective-permute-start | bytes 221192 | tf_op jit(solution)/shard_map/ppermute | solution.py:555
  20.9 1.7 %collective-permute-start.9 = (f32[40,128]{1,0:T(8,128)S(1)}, f32[40,128]{1,0:T(8,128)S(1)}, u32[]{:S(2)}, u32[]{:S(2)}) collective-permute-start(f32[40,128]{1,0:T(8,128)S(1)} %get-tuple-element.55), channel_id=1, source_target_pairs={{3,0},{5,1},{6,2},{0,3},{7,4},{1,5},{2,6},{4,7},{11,8},{13,9},{14,... | collective-permute-start | bytes 61448 | tf_op jit(solution)/shard_map/ppermute | solution.py:555
  22.6 0.5 %collective-permute-start.10 = (f32[40,128]{1,0:T(8,128)S(1)}, f32[40,128]{1,0:T(8,128)S(1)}, u32[]{:S(2)}, u32[]{:S(2)}) collective-permute-start(f32[40,128]{1,0:T(8,128)S(1)} %get-tuple-element.56), channel_id=1, source_target_pairs={{4,0},{6,1},{5,2},{7,3},{0,4},{2,5},{1,6},{3,7},{12,8},{14,9},{13,... | collective-permute-start | bytes 61448 | tf_op jit(solution)/shard_map/ppermute | solution.py:555
  23.1 1.9 %collective-permute-done.9.refs_5_ = f32[40,128]{1,0:T(8,128)S(1)} collective-permute-done((f32[40,128]{1,0:T(8,128)S(1)}, f32[40,128]{1,0:T(8,128)S(1)}, u32[]{:S(2)}, u32[]{:S(2)}) %collective-permute-start.9) | collective-permute-done | bytes 20512 | tf_op jit(solution)/shard_map/ppermute | solution.py:555
  25.0 1.4 %collective-permute-done.10.refs_6_ = f32[40,128]{1,0:T(8,128)S(1)} collective-permute-done((f32[40,128]{1,0:T(8,128)S(1)}, f32[40,128]{1,0:T(8,128)S(1)}, u32[]{:S(2)}, u32[]{:S(2)}) %collective-permute-start.10) | collective-permute-done | bytes 20512 | tf_op jit(solution)/shard_map/ppermute | solution.py:555
  26.4 2.1 %third.1 = f32[2,12,32,128]{3,2,1,0:T(8,128)} custom-call(f32[15,14,48,128]{3,2,1,0:T(8,128)S(1)} %get-tuple-element.46.refs_0_, f32[6,48,128]{2,1,0:T(8,128)S(1)} %get-tuple-element.47.refs_1_, f32[4,6,48,128]{3,2,1,0:T(8,128)S(1)} %get-tuple-element.48.refs_2_, f32[280,128]{1,0:T(8,128)S(1)} %get-tuple-element.53.refs_3_, ...), custom_call_target="tpu_custom_call" | custom-call | tf_op jit(solution)/shard_map/third/pallas_call | solution.py:895
  (7 shorter events, 0.1 us)
Async XLA Ops:
  1.6 5.8 %collective-permute-start = (f32[304,128]{1,0:T(8,128)S(1)}, f32[304,128]{1,0:T(8,128)S(1)}, u32[]{:S(2)}, u32[]{:S(2)}) collective-permute-start(f32[304,128]{1,0:T(8,128)S(1)} %get-tuple-element.32), channel_id=1, source_target_pairs={{0,8},{8,0},{16,24},{24,16},{1,9},{9,1},{17,25},{25,17},{2,10},{10... | collective-permute-start | bytes 466952 | tf_op jit(solution)/shard_map/ppermute | solution.py:770
  3.3 7.4 %collective-permute-start.1 = (f32[304,128]{1,0:T(8,128)S(1)}, f32[304,128]{1,0:T(8,128)S(1)}, u32[]{:S(2)}, u32[]{:S(2)}) collective-permute-start(f32[304,128]{1,0:T(8,128)S(1)} %get-tuple-element.33), channel_id=1, source_target_pairs={{8,16},{16,8},{9,17},{17,9},{10,18},{18,10},{11,19},{19,11},{12,20... | collective-permute-start | bytes 466952 | tf_op jit(solution)/shard_map/ppermute | solution.py:770
  5.2 10.0 %collective-permute-start.2 = (f32[7,32,128]{2,1,0:T(8,128)S(1)}, f32[7,32,128]{2,1,0:T(8,128)S(1)}, u32[]{:S(2)}, u32[]{:S(2)}) collective-permute-start(f32[7,32,128]{2,1,0:T(8,128)S(1)} %get-tuple-element.36), channel_id=1, source_target_pairs={{1,2},{2,1},{3,4},{4,3},{5,6},{6,5},{9,10},{10,9},{11,12},{12,11},... | collective-permute-start | bytes 344072 | tf_op jit(solution)/shard_map/ppermute | solution.py:770
  10.8 6.9 %collective-permute-start.6 = (f32[144,128]{1,0:T(8,128)S(1)}, f32[144,128]{1,0:T(8,128)S(1)}, u32[]{:S(2)}, u32[]{:S(2)}) collective-permute-start(f32[144,128]{1,0:T(8,128)S(1)} %get-tuple-element.45), channel_id=1, source_target_pairs={{1,2},{2,1},{3,4},{4,3},{5,6},{6,5},{9,10},{10,9},{11,12},{12,11},... | collective-permute-start | bytes 221192 | tf_op jit(solution)/shard_map/ppermute | solution.py:770
  11.7 5.4 %collective-permute-start.3 = (f32[3,40,128]{2,1,0:T(8,128)S(1)}, f32[3,40,128]{2,1,0:T(8,128)S(1)}, u32[]{:S(2)}, u32[]{:S(2)}) collective-permute-start(f32[3,40,128]{2,1,0:T(8,128)S(1)} %get-tuple-element.39), channel_id=1, source_target_pairs={{0,1},{1,0},{2,3},{3,2},{4,5},{5,4},{6,7},{7,6},{8,9},{9,8},{10,11... | collective-permute-start | bytes 184328 | tf_op jit(solution)/shard_map/ppermute | solution.py:770
  14.7 2.5 %collective-permute-start.4 = (f32[3,40,128]{2,1,0:T(8,128)S(1)}, f32[3,40,128]{2,1,0:T(8,128)S(1)}, u32[]{:S(2)}, u32[]{:S(2)}) collective-permute-start(f32[3,40,128]{2,1,0:T(8,128)S(1)} %get-tuple-element.40), channel_id=1, source_target_pairs={{0,1},{1,0},{2,3},{3,2},{4,5},{5,4},{6,7},{7,6},{8,9},{9,8},{10,11... | collective-permute-start | bytes 184328 | tf_op jit(solution)/shard_map/ppermute | solution.py:770
  14.7 2.4 %collective-permute-start.5 = (f32[3,40,128]{2,1,0:T(8,128)S(1)}, f32[3,40,128]{2,1,0:T(8,128)S(1)}, u32[]{:S(2)}, u32[]{:S(2)}) collective-permute-start(f32[3,40,128]{2,1,0:T(8,128)S(1)} %get-tuple-element.41), channel_id=1, source_target_pairs={{0,1},{1,0},{2,3},{3,2},{4,5},{5,4},{6,7},{7,6},{8,9},{9,8},{10,11... | collective-permute-start | bytes 184328 | tf_op jit(solution)/shard_map/ppermute | solution.py:770
  18.4 1.4 %collective-permute-start.7 = (f32[176,128]{1,0:T(8,128)S(1)}, f32[176,128]{1,0:T(8,128)S(1)}, u32[]{:S(2)}, u32[]{:S(2)}) collective-permute-start(f32[176,128]{1,0:T(8,128)S(1)} %get-tuple-element.52), channel_id=1, source_target_pairs={{1,0},{0,1},{3,2},{2,3},{5,4},{4,5},{7,6},{6,7},{9,8},{8,9},{11,10... | collective-permute-start | bytes 270344 | tf_op jit(solution)/shard_map/ppermute | solution.py:555
  19.8 6.6 %collective-permute-start.8 = (f32[144,128]{1,0:T(8,128)S(1)}, f32[144,128]{1,0:T(8,128)S(1)}, u32[]{:S(2)}, u32[]{:S(2)}) collective-permute-start(f32[144,128]{1,0:T(8,128)S(1)} %get-tuple-element.54), channel_id=1, source_target_pairs={{7,0},{2,1},{1,2},{4,3},{3,4},{6,5},{5,6},{0,7},{15,8},{10,9},{9,1... | collective-permute-start | bytes 221192 | tf_op jit(solution)/shard_map/ppermute | solution.py:555
  20.9 4.1 %collective-permute-start.9 = (f32[40,128]{1,0:T(8,128)S(1)}, f32[40,128]{1,0:T(8,128)S(1)}, u32[]{:S(2)}, u32[]{:S(2)}) collective-permute-start(f32[40,128]{1,0:T(8,128)S(1)} %get-tuple-element.55), channel_id=1, source_target_pairs={{3,0},{5,1},{6,2},{0,3},{7,4},{1,5},{2,6},{4,7},{11,8},{13,9},{14,... | collective-permute-start | bytes 61448 | tf_op jit(solution)/shard_map/ppermute | solution.py:555
  22.6 3.8 %collective-permute-start.10 = (f32[40,128]{1,0:T(8,128)S(1)}, f32[40,128]{1,0:T(8,128)S(1)}, u32[]{:S(2)}, u32[]{:S(2)}) collective-permute-start(f32[40,128]{1,0:T(8,128)S(1)} %get-tuple-element.56), channel_id=1, source_target_pairs={{4,0},{6,1},{5,2},{7,3},{0,4},{2,5},{1,6},{3,7},{12,8},{14,9},{13,... | collective-permute-start | bytes 61448 | tf_op jit(solution)/shard_map/ppermute | solution.py:555

commit v15 on v14

--- a/solution.py
+++ b/solution.py
@@ -53,31 +53,35 @@
     return jnp.where((row >= low) & (row < high), 1.0, 0.0).astype(jnp.float32)
 
 
-STRIP = ((SA, WX - 1), (GA, WX - 1), (K, WX), (C, WX - 1), (RS, WX - 1), (RG, WX - 1))
-STRIP_ROWS = sum(width for plane, width in STRIP)
+PAIRS = ((SA, GA), (C, RS), (RG, K))
+STRIP_ROWS = 8 * len(PAIRS)
+
+
+def strip_height(ny):
+    return ny * STRIP_ROWS + (ny + 7) // 8 * 8
+
+
+def sublanes(nz):
+    return lax.broadcasted_iota(jnp.int32, (8, nz), 0)
 
 
 def conductivity_of(s, exchange):
     return 1.0 + 4.0 * exchange * s * s * s
 
 
-def strip_rows(low):
-    if low:
-        return WX - 1, WX - 2, slice(0, WX - 1), slice(0, WX)
-    return 8 - WX, 9 - WX, slice(9 - WX, 8), slice(8 - WX, 8)
-
-
-def strip_values(s, g, k, c, low):
-    _, _, four, five = strip_rows(low)
-    return [s[four], g[four], k[five], c[four]]
-
-
-def strip_sides(s, g, k, rs, rg, low):
-    out, inn, four, _ = strip_rows(low)
-    row = lax.broadcasted_iota(jnp.int32, s.shape, 0)
-    rs = rs + jnp.where(row == inn, 0.5 * (k[inn : inn + 1] + k[out : out + 1]) * s[out : out + 1], 0.0)
-    rg = rg + jnp.where(row == inn, CONDUCT * g[out : out + 1], 0.0)
-    return [rs[four], rg[four]]
+def strip_side(s, g, k, rs, rg, c, low):
+    row = sublanes(s.shape[1])
+    inn, shift = (3, 7) if low else (4, 1)
+    k_out, s_out, g_out = (pltpu.roll(v, shift, 0) for v in (k, s, g))
+    rs = rs + jnp.where(row == inn, 0.5 * (k + k_out) * s_out, 0.0)
+    rg = rg + jnp.where(row == inn, CONDUCT * g_out, 0.0)
+    values = {SA: s, GA: g, K: k, RS: rs, RG: rg, C: c}
+    tiles = []
+    for a, b in PAIRS:
+        a, b = values[a], values[b]
+        a, b = (a, pltpu.roll(b, 4, 0)) if low else (pltpu.roll(a, 4, 0), b)
+        tiles.append(jnp.where(row < 4, a, b))
+    return tiles, (k[4:5] if low else k[3:4])
 
 
 def pack_kernel(temps, right, exchange, coupling, one, two, early, st, sems):
@@ -92,29 +96,21 @@
         copies.append(pltpu.make_async_copy(ref, to, sems.at[k]))
     for copy in copies:
         copy.start()
-    def put(i, at, sides):
-        at += (i - 1) * STRIP_ROWS
-        for low, high in zip(*sides):
-            one[at : at + low.shape[0]] = jnp.where(even, high, low)
-            two[at : at + low.shape[0]] = jnp.where(even, low, high)
-            at += low.shape[0]
-
-    for copy in copies[:4]:
+    for copy in copies:
         copy.wait()
     for i in range(1, ny + 1):
         sides = []
         for start in (PAD, PAD + nx - 8):
-            s, g, e, c = (st[plane, i, start : start + 8] for plane in (SA, GA, K, C))
-            sides.append(strip_values(s, g, conductivity_of(s, e), c, start == PAD))
-        put(i, 0, sides)
-    for copy in copies[4:]:
-        copy.wait()
-    for i in range(1, ny + 1):
-        sides = []
-        for start in (PAD, PAD + nx - 8):
-            s, g, e, rs, rg = (st[plane, i, start : start + 8] for plane in (SA, GA, K, RS, RG))
-            sides.append(strip_sides(s, g, conductivity_of(s, e), rs, rg, start == PAD))
-        put(i, STRIP_ROWS - 2 * (WX - 1), sides)
+            s, g, e, rs, rg, c = (st[plane, i, start : start + 8] for plane in (SA, GA, K, RS, RG, C))
+            sides.append(strip_side(s, g, conductivity_of(s, e), rs, rg, c, start == PAD))
+        (low, low_k), (high, high_k) = sides
+        for p in range(len(PAIRS)):
+            part = slice((i - 1) * STRIP_ROWS + 8 * p, (i - 1) * STRIP_ROWS + 8 * p + 8)
+            one[part] = jnp.where(even, high[p], low[p])
+            two[part] = jnp.where(even, low[p], high[p])
+        part = slice(ny * STRIP_ROWS + i - 1, ny * STRIP_ROWS + i)
+        one[part] = jnp.where(even, high_k, low_k)
+        two[part] = jnp.where(even, low_k, high_k)
     own = slice(PAD, PAD + nx)
     for is_odd, e, d in ((True, ny, ny - 1), (False, 1, 2)):
 
@@ -134,22 +130,30 @@
     del st_in
     planes, rows, ext, nz = st.shape
     own = slice(PAD, ext - PAD)
-    zeros = jnp.zeros((PAD, nz), jnp.float32)
     for i in range(1, rows - 1):
         st[K, i, own] = conductivity_of(st[SA, i, own], st[K, i, own])
-        for plane, width in STRIP:
-            st[plane, i, :PAD] = zeros
-            st[plane, i, ext - PAD :] = zeros
 
 
 def place_halo(st, one, two, y, nx):
     even = lax.axis_index("gx") % 2 == 0
-    at, i = y * STRIP_ROWS, y + 1
-    for plane, width in STRIP:
-        a, b = one[at : at + width], two[at : at + width]
-        st[plane, i, PAD - width : PAD] = jnp.where(even, b, a)
-        st[plane, i, PAD + nx : PAD + nx + width] = jnp.where(even, a, b)
-        at += width
+    ny, row = st.shape[1] - 2, sublanes(st.shape[3])
+    i = y + 1
+
+    def received(part):
+        a, b = one[part], two[part]
+        return jnp.where(even, b, a), jnp.where(even, a, b)
+
+    for p, (plane_a, plane_b) in enumerate(PAIRS):
+        before, after = received(slice(y * STRIP_ROWS + 8 * p, y * STRIP_ROWS + 8 * p + 8))
+        before = {plane_a: pltpu.roll(before, 4, 0), plane_b: before}
+        after = {plane_a: after, plane_b: pltpu.roll(after, 4, 0)}
+        for plane in (plane_a, plane_b):
+            low, high = jnp.where(row >= 4, before[plane], 0.0), jnp.where(row < 4, after[plane], 0.0)
+            if plane == K:
+                k_low, k_high = received(slice(ny * STRIP_ROWS + y, ny * STRIP_ROWS + y + 1))
+                low, high = jnp.where(row == 3, k_low, low), jnp.where(row == 4, k_high, high)
+            st[plane, i, :PAD] = low
+            st[plane, i, PAD + nx :] = high
 
 
 def inner(s, g, c, h, fx, fz, edge):
@@ -329,6 +333,12 @@
 def other_kernel(st_in, one, two, st, *beside):
     del st_in
     either_first(st, one, two, lax.axis_index("gy") % 2 == 0, functools.partial(write_beside, beside))
+    planes, rows, ext, nz = st.shape
+    ny, nx = rows - 2, ext - 2 * PAD
+    mask = x_mask((ext, nz), nx)
+    for y in range(3, ny - 3):
+        place_halo(st, one, two, y, nx)
+    grouped(list(range(3, ny - 1)), lambda i: row_coefficients(st, i, mask))
 
 
 def outer_residual(st, i, s_at, rs, rg, fy_out, edge, after):
@@ -349,10 +359,9 @@
 
 
 def coarse_coefficients(c_sum, k_sum):
-    solid = 4.0 * SOLID_CAP + c_sum + LUMP * k_sum
-    ratio = c_sum / solid
-    denominator = (4.0 * GAS_CAP + 2.0 * FLOW) + c_sum - c_sum * ratio
-    return solid, ratio, denominator
+    per_solid = 1.0 / (4.0 * SOLID_CAP + c_sum + LUMP * k_sum)
+    ratio = c_sum * per_solid
+    return per_solid, ratio, 1.0 / ((4.0 * GAS_CAP + 2.0 * FLOW) + c_sum - c_sum * ratio)
 
 
 def coarse_row(st, coarse, j, mask, edge):
@@ -361,22 +370,19 @@
     more_s, more_g = row_residual(st, i + 1, SA, edge)
     res_s, res_g = pair_x((res_s + more_s) * mask), pair_x((res_g + more_g) * mask)
     c_sum = pair_x(st[C, i] + st[C, i + 1])
-    solid, ratio, denominator = coarse_coefficients(c_sum, pair_x(st[K, i] + st[K, i + 1]))
-    lead = res_s / solid
-    values = (lead, ratio, (2.0 * FLOW) / denominator, (res_g + c_sum * lead) / denominator)
+    per_solid, ratio, per_gas = coarse_coefficients(c_sum, pair_x(st[K, i] + st[K, i + 1]))
+    lead = res_s * per_solid
+    values = (lead, ratio, (2.0 * FLOW) * per_gas, (res_g + c_sum * lead) * per_gas)
     return [(coarse, (k, j), v) for k, v in enumerate(values)]
 
 
-def inner_kernel(st_in, one, two, early, st, coarse):
+def inner_kernel(st_in, early, st, coarse):
     del st_in, early
     planes, rows, ext, nz = st.shape
     ny, nx = rows - 2, ext - 2 * PAD
     shape = (ext, nz)
     mask = x_mask(shape, nx)
     edge = edge_weights(shape)
-    for y in range(3, ny - 3):
-        place_halo(st, one, two, y, nx)
-    grouped(list(range(3, ny - 1)), lambda i: row_coefficients(st, i, mask))
     grouped(list(range(3, ny - 1)), lambda i: row_sweep(st, i, SA, SB, edge))
     grouped(list(range(3, ny - 1)), lambda i: row_sweep(st, i, SB, SA, edge))
     for j in range(2, ny // 2 - 2):
@@ -780,7 +786,7 @@
     ext = nx + 2 * PAD
     f32 = functools.partial(jax.ShapeDtypeStruct, dtype=jnp.float32)
 
-    strip = f32(((ny * STRIP_ROWS + 7) // 8 * 8, nz))
+    strip = f32((strip_height(ny), nz))
     state = f32((PLANES, ny + 2, ext, nz))
     one, two, early, st = pl.pallas_call(
         pack_kernel,
@@ -831,13 +837,13 @@
     st, coarse = pl.pallas_call(
         inner_kernel,
         out_shape=(state, rows),
-        in_specs=[VMEM] * 4,
+        in_specs=[VMEM] * 2,
         out_specs=(VMEM,) * 2,
         input_output_aliases={0: 0},
         compiler_params=PARAMS,
         cost_estimate=cost(4 * ny, ext * nz),
         name="inner",
-    )(st, one, two, early)
+    )(st, early)
 
     beside = [swap(part, "gy", 0) for part in beside]
 

time: 28.7 us -> 28.7 us (level)
    pallas_call x1, Pallas kernels: 1.97 us -> 1.59 us  [shards(): pl.pallas_call(inner_kernel, out_shape=(state, rows), in_specs=[VMEM] * 2...]
  transfers between devices with their start and end apart: 11 -> 11, of which waited for: 5 -> 5; matrix products, arithmetic and copies ran while one was open for 0% -> 0% of each run, Pallas kernels for 11% -> 10%
where the time goes in v15:
time: 28.7 us; the launch traced here: 28.4 us
  starting transfers between devices  11.7 us (41%)
  waiting for transfers between devices  9.23 us (32%)
  Pallas kernels  7.35 us (26%)
    ppermute x7, starting transfers between devices, swap(): return lax.ppermute(x, axis, pairs)  8.31 us
    ppermute x7, waiting for transfers between devices, swap(): return lax.ppermute(x, axis, pairs)  4.74 us
    ppermute x4, waiting for transfers between devices, exchange_stage(): lax.ppermute(message, 'gy', [(sender, me) for me, sender in enumerate(sen...  4.49 us
    ppermute x4, starting transfers between devices, exchange_stage(): lax.ppermute(message, 'gy', [(sender, me) for me, sender in enumerate(sen...  3.41 us
    pallas_call x1, Pallas kernels, shards(): pl.pallas_call(functools.partial(third_kernel, radices[-1], stride), out_...  2.14 us
    pallas_call x1, Pallas kernels, shards(): pl.pallas_call(pack_kernel, out_shape=(strip, strip, f32((EARLY, nx, nz))...  1.63 us
    pallas_call x1, Pallas kernels, shards(): pl.pallas_call(inner_kernel, out_shape=(state, rows), in_specs=[VMEM] * 2...  1.59 us
    pallas_call x1, Pallas kernels, shards(): pl.pallas_call(second_kernel, out_shape=(state, rows, more, tall(lay.map)...  0.62 us
  transfers between devices with their start and end apart: 11, of which 5 were waited for; matrix products, arithmetic and copies ran while one was open for 0% of the time, Pallas kernels for 10%

profile of v15, /device:TPU:16, one launch (start us, length us, event | category | flops | bytes accessed | tf_op | source)
XLA Modules:
  0.0 28.4 jit_solution(3036909522306588024)
XLA Ops:
  0.0 1.6 %pack_x.1 = (f32[304,128]{1,0:T(8,128)S(1)}, f32[304,128]{1,0:T(8,128)S(1)}, f32[7,32,128]{2,1,0:T(8,128)S(1)}, f32[15,14,48,128]{3,2,1,0:T(8,128)S(1)}) custom-call(f32[2,12,32,128]{3,2,1,0:T(8,128)} %bitcast.5, f32[2,12,32,128]{3,2,1,0:T(8,128)} %bitcast.6, f32[12,32,128]{2,1,0:T(8,128)} %bitcast.7, f32[12,32,128]{2,1,0:T(8,128)} %bitcast.8), custom_call_target="tpu_custom_call" | custom-call | tf_op jit(solution)/shard_map/pack_x/pallas_call | solution.py:791
  1.6 1.6 %collective-permute-start = (f32[304,128]{1,0:T(8,128)S(1)}, f32[304,128]{1,0:T(8,128)S(1)}, u32[]{:S(2)}, u32[]{:S(2)}) collective-permute-start(f32[304,128]{1,0:T(8,128)S(1)} %get-tuple-element.32), channel_id=1, source_target_pairs={{0,8},{8,0},{16,24},{24,16},{1,9},{9,1},{17,25},{25,17},{2,10},{10... | collective-permute-start | bytes 466952 | tf_op jit(solution)/shard_map/ppermute | solution.py:776
  3.3 1.9 %collective-permute-start.1 = (f32[304,128]{1,0:T(8,128)S(1)}, f32[304,128]{1,0:T(8,128)S(1)}, u32[]{:S(2)}, u32[]{:S(2)}) collective-permute-start(f32[304,128]{1,0:T(8,128)S(1)} %get-tuple-element.33), channel_id=1, source_target_pairs={{8,16},{16,8},{9,17},{17,9},{10,18},{18,10},{11,19},{19,11},{12,20... | collective-permute-start | bytes 466952 | tf_op jit(solution)/shard_map/ppermute | solution.py:776
  5.2 0.7 %collective-permute-start.2 = (f32[7,32,128]{2,1,0:T(8,128)S(1)}, f32[7,32,128]{2,1,0:T(8,128)S(1)}, u32[]{:S(2)}, u32[]{:S(2)}) collective-permute-start(f32[7,32,128]{2,1,0:T(8,128)S(1)} %get-tuple-element.36), channel_id=1, source_target_pairs={{1,2},{2,1},{3,4},{4,3},{5,6},{6,5},{9,10},{10,9},{11,12},{12,11},... | collective-permute-start | bytes 344072 | tf_op jit(solution)/shard_map/ppermute | solution.py:776
  5.9 1.5 %collective-permute-done.one = f32[304,128]{1,0:T(8,128)S(1)} collective-permute-done((f32[304,128]{1,0:T(8,128)S(1)}, f32[304,128]{1,0:T(8,128)S(1)}, u32[]{:S(2)}, u32[]{:S(2)}) %collective-permute-start) | collective-permute-done | bytes 155680 | tf_op jit(solution)/shard_map/ppermute | solution.py:776
  7.5 3.2 %collective-permute-done.1.two = f32[304,128]{1,0:T(8,128)S(1)} collective-permute-done((f32[304,128]{1,0:T(8,128)S(1)}, f32[304,128]{1,0:T(8,128)S(1)}, u32[]{:S(2)}, u32[]{:S(2)}) %collective-permute-start.1) | collective-permute-done | bytes 155680 | tf_op jit(solution)/shard_map/ppermute | solution.py:776
  10.6 0.2 first.1
  10.8 0.7 %collective-permute-start.6 = (f32[144,128]{1,0:T(8,128)S(1)}, f32[144,128]{1,0:T(8,128)S(1)}, u32[]{:S(2)}, u32[]{:S(2)}) collective-permute-start(f32[144,128]{1,0:T(8,128)S(1)} %get-tuple-element.45), channel_id=1, source_target_pairs={{1,2},{2,1},{3,4},{4,3},{5,6},{6,5},{9,10},{10,9},{11,12},{12,11},... | collective-permute-start | bytes 221192 | tf_op jit(solution)/shard_map/ppermute | solution.py:776
  11.5 0.5 %other.1 = (f32[15,14,48,128]{3,2,1,0:T(8,128)S(1)}, f32[3,40,128]{2,1,0:T(8,128)S(1)}, f32[3,40,128]{2,1,0:T(8,128)S(1)}, f32[3,40,128]{2,1,0:T(8,128)S(1)}) custom-call(f32[15,14,48,128]{3,2,1,0:T(8,128)S(1)} %get-tuple-element.34.st_in, f32[304,128]{1,0:T(8,128)S(1)} %collective-permute-done.one, ...), custom_call_target="tpu_custom_call", output_to_operand_aliasing={{0}: (0, {})} | custom-call | tf_op jit(solution)/shard_map/other/pallas_call | solution.py:825
  12.0 2.9 %collective-permute-start.3 = (f32[3,40,128]{2,1,0:T(8,128)S(1)}, f32[3,40,128]{2,1,0:T(8,128)S(1)}, u32[]{:S(2)}, u32[]{:S(2)}) collective-permute-start(f32[3,40,128]{2,1,0:T(8,128)S(1)} %get-tuple-element.39), channel_id=1, source_target_pairs={{0,1},{1,0},{2,3},{3,2},{4,5},{5,4},{6,7},{7,6},{8,9},{9,8},{10,11... | collective-permute-start | bytes 184328 | tf_op jit(solution)/shard_map/ppermute | solution.py:776
  15.0 0.1 collective-permute-start.4
  15.0 0.4 %collective-permute-start.5 = (f32[3,40,128]{2,1,0:T(8,128)S(1)}, f32[3,40,128]{2,1,0:T(8,128)S(1)}, u32[]{:S(2)}, u32[]{:S(2)}) collective-permute-start(f32[3,40,128]{2,1,0:T(8,128)S(1)} %get-tuple-element.41), channel_id=1, source_target_pairs={{0,1},{1,0},{2,3},{3,2},{4,5},{5,4},{6,7},{7,6},{8,9},{9,8},{10,11... | collective-permute-start | bytes 184328 | tf_op jit(solution)/shard_map/ppermute | solution.py:776
  15.5 0.0 collective-permute-done.2.early
  15.5 1.6 %inner.1 = (f32[15,14,48,128]{3,2,1,0:T(8,128)S(1)}, f32[4,6,48,128]{3,2,1,0:T(8,128)S(1)}) custom-call(f32[15,14,48,128]{3,2,1,0:T(8,128)S(1)} %get-tuple-element.35.st_in, f32[7,32,128]{2,1,0:T(8,128)S(1)} %collective-permute-done.2.early), custom_call_target="tpu_custom_call", output_to_operand_aliasing={{0}: (0, {})} | custom-call | flops 14745600 | bytes 18874368 | tf_op jit(solution)/shard_map/inner/pallas_call | solution.py:837
  17.1 0.6 %near.1 = (f32[15,14,48,128]{3,2,1,0:T(8,128)S(1)}, f32[4,6,48,128]{3,2,1,0:T(8,128)S(1)}, f32[6,48,128]{2,1,0:T(8,128)S(1)}) custom-call(f32[15,14,48,128]{3,2,1,0:T(8,128)S(1)} %get-tuple-element.37.st_in, f32[4,6,48,128]{3,2,1,0:T(8,128)S(1)} %get-tuple-element.38.coarse_in, ...), custom_call_target="tpu_custom_call", output_to_operand_aliasing={{0}: (0, {}), {1}: (1, {})} | custom-call | tf_op jit(solution)/shard_map/near/pallas_call | solution.py:857
  17.7 0.6 %second.1 = (f32[15,14,48,128]{3,2,1,0:T(8,128)S(1)}, f32[4,6,48,128]{3,2,1,0:T(8,128)S(1)}, f32[6,48,128]{2,1,0:T(8,128)S(1)}, f32[40,128]{1,0:T(8,128)S(1)}, f...) custom-call(f32[15,14,48,128]{3,2,1,0:T(8,128)S(1)} %get-tuple-eleme, ...), custom_call_target="tpu_custom_call", output_to_operand_aliasing={{0}: (0, {}), {1}: (1, {}), {2}: (2, {})} | custom-call | tf_op jit(solution)/shard_map/second/pallas_call | solution.py:867
  18.3 0.1 collective-permute-start.7
  18.5 1.2 %collective-permute-done.7.refs_4_ = f32[176,128]{1,0:T(8,128)S(1)} collective-permute-done((f32[176,128]{1,0:T(8,128)S(1)}, f32[176,128]{1,0:T(8,128)S(1)}, u32[]{:S(2)}, u32[]{:S(2)}) %collective-permute-start.7) | collective-permute-done | bytes 90144 | tf_op jit(solution)/shard_map/ppermute | solution.py:561
  19.7 1.1 %collective-permute-start.8 = (f32[144,128]{1,0:T(8,128)S(1)}, f32[144,128]{1,0:T(8,128)S(1)}, u32[]{:S(2)}, u32[]{:S(2)}) collective-permute-start(f32[144,128]{1,0:T(8,128)S(1)} %get-tuple-element.54), channel_id=1, source_target_pairs={{7,0},{2,1},{1,2},{4,3},{3,4},{6,5},{5,6},{0,7},{15,8},{10,9},{9,1... | collective-permute-start | bytes 221192 | tf_op jit(solution)/shard_map/ppermute | solution.py:561
  20.8 1.7 %collective-permute-start.9 = (f32[40,128]{1,0:T(8,128)S(1)}, f32[40,128]{1,0:T(8,128)S(1)}, u32[]{:S(2)}, u32[]{:S(2)}) collective-permute-start(f32[40,128]{1,0:T(8,128)S(1)} %get-tuple-element.55), channel_id=1, source_target_pairs={{3,0},{5,1},{6,2},{0,3},{7,4},{1,5},{2,6},{4,7},{11,8},{13,9},{14,... | collective-permute-start | bytes 61448 | tf_op jit(solution)/shard_map/ppermute | solution.py:561
  22.5 0.5 %collective-permute-start.10 = (f32[40,128]{1,0:T(8,128)S(1)}, f32[40,128]{1,0:T(8,128)S(1)}, u32[]{:S(2)}, u32[]{:S(2)}) collective-permute-start(f32[40,128]{1,0:T(8,128)S(1)} %get-tuple-element.56), channel_id=1, source_target_pairs={{4,0},{6,1},{5,2},{7,3},{0,4},{2,5},{1,6},{3,7},{12,8},{14,9},{13,... | collective-permute-start | bytes 61448 | tf_op jit(solution)/shard_map/ppermute | solution.py:561
  23.0 1.9 %collective-permute-done.9.refs_5_ = f32[40,128]{1,0:T(8,128)S(1)} collective-permute-done((f32[40,128]{1,0:T(8,128)S(1)}, f32[40,128]{1,0:T(8,128)S(1)}, u32[]{:S(2)}, u32[]{:S(2)}) %collective-permute-start.9) | collective-permute-done | bytes 20512 | tf_op jit(solution)/shard_map/ppermute | solution.py:561
  24.9 1.4 %collective-permute-done.10.refs_6_ = f32[40,128]{1,0:T(8,128)S(1)} collective-permute-done((f32[40,128]{1,0:T(8,128)S(1)}, f32[40,128]{1,0:T(8,128)S(1)}, u32[]{:S(2)}, u32[]{:S(2)}) %collective-permute-start.10) | collective-permute-done | bytes 20512 | tf_op jit(solution)/shard_map/ppermute | solution.py:561
  26.3 2.1 %third.1 = f32[2,12,32,128]{3,2,1,0:T(8,128)} custom-call(f32[15,14,48,128]{3,2,1,0:T(8,128)S(1)} %get-tuple-element.46.refs_0_, f32[6,48,128]{2,1,0:T(8,128)S(1)} %get-tuple-element.47.refs_1_, f32[4,6,48,128]{3,2,1,0:T(8,128)S(1)} %get-tuple-element.48.refs_2_, f32[280,128]{1,0:T(8,128)S(1)} %get-tuple-element.53.refs_3_, ...), custom_call_target="tpu_custom_call" | custom-call | tf_op jit(solution)/shard_map/third/pallas_call | solution.py:901
  (7 shorter events, 0.1 us)
Async XLA Ops:
  1.6 5.8 %collective-permute-start = (f32[304,128]{1,0:T(8,128)S(1)}, f32[304,128]{1,0:T(8,128)S(1)}, u32[]{:S(2)}, u32[]{:S(2)}) collective-permute-start(f32[304,128]{1,0:T(8,128)S(1)} %get-tuple-element.32), channel_id=1, source_target_pairs={{0,8},{8,0},{16,24},{24,16},{1,9},{9,1},{17,25},{25,17},{2,10},{10... | collective-permute-start | bytes 466952 | tf_op jit(solution)/shard_map/ppermute | solution.py:776
  3.3 7.4 %collective-permute-start.1 = (f32[304,128]{1,0:T(8,128)S(1)}, f32[304,128]{1,0:T(8,128)S(1)}, u32[]{:S(2)}, u32[]{:S(2)}) collective-permute-start(f32[304,128]{1,0:T(8,128)S(1)} %get-tuple-element.33), channel_id=1, source_target_pairs={{8,16},{16,8},{9,17},{17,9},{10,18},{18,10},{11,19},{19,11},{12,20... | collective-permute-start | bytes 466952 | tf_op jit(solution)/shard_map/ppermute | solution.py:776
  5.2 10.3 %collective-permute-start.2 = (f32[7,32,128]{2,1,0:T(8,128)S(1)}, f32[7,32,128]{2,1,0:T(8,128)S(1)}, u32[]{:S(2)}, u32[]{:S(2)}) collective-permute-start(f32[7,32,128]{2,1,0:T(8,128)S(1)} %get-tuple-element.36), channel_id=1, source_target_pairs={{1,2},{2,1},{3,4},{4,3},{5,6},{6,5},{9,10},{10,9},{11,12},{12,11},... | collective-permute-start | bytes 344072 | tf_op jit(solution)/shard_map/ppermute | solution.py:776
  10.8 6.8 %collective-permute-start.6 = (f32[144,128]{1,0:T(8,128)S(1)}, f32[144,128]{1,0:T(8,128)S(1)}, u32[]{:S(2)}, u32[]{:S(2)}) collective-permute-start(f32[144,128]{1,0:T(8,128)S(1)} %get-tuple-element.45), channel_id=1, source_target_pairs={{1,2},{2,1},{3,4},{4,3},{5,6},{6,5},{9,10},{10,9},{11,12},{12,11},... | collective-permute-start | bytes 221192 | tf_op jit(solution)/shard_map/ppermute | solution.py:776
  12.0 5.0 %collective-permute-start.3 = (f32[3,40,128]{2,1,0:T(8,128)S(1)}, f32[3,40,128]{2,1,0:T(8,128)S(1)}, u32[]{:S(2)}, u32[]{:S(2)}) collective-permute-start(f32[3,40,128]{2,1,0:T(8,128)S(1)} %get-tuple-element.39), channel_id=1, source_target_pairs={{0,1},{1,0},{2,3},{3,2},{4,5},{5,4},{6,7},{7,6},{8,9},{9,8},{10,11... | collective-permute-start | bytes 184328 | tf_op jit(solution)/shard_map/ppermute | solution.py:776
  15.0 2.1 %collective-permute-start.4 = (f32[3,40,128]{2,1,0:T(8,128)S(1)}, f32[3,40,128]{2,1,0:T(8,128)S(1)}, u32[]{:S(2)}, u32[]{:S(2)}) collective-permute-start(f32[3,40,128]{2,1,0:T(8,128)S(1)} %get-tuple-element.40), channel_id=1, source_target_pairs={{0,1},{1,0},{2,3},{3,2},{4,5},{5,4},{6,7},{7,6},{8,9},{9,8},{10,11... | collective-permute-start | bytes 184328 | tf_op jit(solution)/shard_map/ppermute | solution.py:776
  15.0 2.1 %collective-permute-start.5 = (f32[3,40,128]{2,1,0:T(8,128)S(1)}, f32[3,40,128]{2,1,0:T(8,128)S(1)}, u32[]{:S(2)}, u32[]{:S(2)}) collective-permute-start(f32[3,40,128]{2,1,0:T(8,128)S(1)} %get-tuple-element.41), channel_id=1, source_target_pairs={{0,1},{1,0},{2,3},{3,2},{4,5},{5,4},{6,7},{7,6},{8,9},{9,8},{10,11... | collective-permute-start | bytes 184328 | tf_op jit(solution)/shard_map/ppermute | solution.py:776
  18.3 1.4 %collective-permute-start.7 = (f32[176,128]{1,0:T(8,128)S(1)}, f32[176,128]{1,0:T(8,128)S(1)}, u32[]{:S(2)}, u32[]{:S(2)}) collective-permute-start(f32[176,128]{1,0:T(8,128)S(1)} %get-tuple-element.52), channel_id=1, source_target_pairs={{1,0},{0,1},{3,2},{2,3},{5,4},{4,5},{7,6},{6,7},{9,8},{8,9},{11,10... | collective-permute-start | bytes 270344 | tf_op jit(solution)/shard_map/ppermute | solution.py:561
  19.7 6.6 %collective-permute-start.8 = (f32[144,128]{1,0:T(8,128)S(1)}, f32[144,128]{1,0:T(8,128)S(1)}, u32[]{:S(2)}, u32[]{:S(2)}) collective-permute-start(f32[144,128]{1,0:T(8,128)S(1)} %get-tuple-element.54), channel_id=1, source_target_pairs={{7,0},{2,1},{1,2},{4,3},{3,4},{6,5},{5,6},{0,7},{15,8},{10,9},{9,1... | collective-permute-start | bytes 221192 | tf_op jit(solution)/shard_map/ppermute | solution.py:561
  20.8 4.1 %collective-permute-start.9 = (f32[40,128]{1,0:T(8,128)S(1)}, f32[40,128]{1,0:T(8,128)S(1)}, u32[]{:S(2)}, u32[]{:S(2)}) collective-permute-start(f32[40,128]{1,0:T(8,128)S(1)} %get-tuple-element.55), channel_id=1, source_target_pairs={{3,0},{5,1},{6,2},{0,3},{7,4},{1,5},{2,6},{4,7},{11,8},{13,9},{14,... | collective-permute-start | bytes 61448 | tf_op jit(solution)/shard_map/ppermute | solution.py:561
  22.5 3.8 %collective-permute-start.10 = (f32[40,128]{1,0:T(8,128)S(1)}, f32[40,128]{1,0:T(8,128)S(1)}, u32[]{:S(2)}, u32[]{:S(2)}) collective-permute-start(f32[40,128]{1,0:T(8,128)S(1)} %get-tuple-element.56), channel_id=1, source_target_pairs={{4,0},{6,1},{5,2},{7,3},{0,4},{2,5},{1,6},{3,7},{12,8},{14,9},{13,... | collective-permute-start | bytes 61448 | tf_op jit(solution)/shard_map/ppermute | solution.py:561

commit v16 on v15

--- a/solution.py
+++ b/solution.py
@@ -225,10 +225,10 @@
     return s + ss * res_s + sg * res_g, g + sg * res_s + gg * res_g
 
 
-def grouped(rows, work):
-    for start in range(0, len(rows), GROUP):
+def grouped(rows, work, size=8):
+    for start in range(0, len(rows), size):
         stores = []
-        for i in rows[start : start + GROUP]:
+        for i in rows[start : start + size]:
             stores += work(i)
         for ref, at, value in stores:
             ref[at] = value
@@ -385,9 +385,7 @@
     edge = edge_weights(shape)
     grouped(list(range(3, ny - 1)), lambda i: row_sweep(st, i, SA, SB, edge))
     grouped(list(range(3, ny - 1)), lambda i: row_sweep(st, i, SB, SA, edge))
-    for j in range(2, ny // 2 - 2):
-        for ref, at, value in coarse_row(st, coarse, j, mask, edge):
-            ref[at] = value
+    grouped(list(range(2, ny // 2 - 2)), lambda j: coarse_row(st, coarse, j, mask, edge))
 
 
 def end_work(st, coarse, extra, read, outer, is_after):
@@ -668,7 +666,7 @@
 
 def third_kernel(radix, stride, *refs):
     st, extra, coarse, near_in = refs[:4]
-    others, (out, sc, wide, near, done, sems) = refs[4 : 3 + radix], refs[3 + radix :]
+    others, (out, sc, sc_b, wide, near, done, sems) = refs[4 : 3 + radix], refs[3 + radix :]
     planes, rows, ext, nz = st.shape
     ny, nx = rows - 2, ext - 2 * PAD
     edge = edge_weights((ext, nz))
@@ -715,7 +713,7 @@
     sc[0, last] = st[SA, last] + solid_high
     sc[1, last] = st[GA, last] + gas_high
 
-    view = Fields(st, sc)
+    view = Fields(st, sc, sc_b)
     for i, is_after, solid, gas in ((0, False, solid_low, gas_in), (last, True, solid_high, gas_high)):
         side = 3 if is_after else 0
         fy = extra[side + 2]
@@ -723,46 +721,36 @@
         rs = extra[side] + wide[to] + fy * solid
         rg = extra[side + 1] + wide[to + 1] + (CONDUCT if is_after else CONDUCT + FLOW) * gas
         res = outer_residual(view, i, SA, rs, rg, fy, edge, is_after)
-        sc[2, i], sc[3, i] = relaxed(view, i, SA, *res)
-
-    def sweep(k, carry):
-        stores = []
-        for r in range(GROUP):
-            i = GROUP * k + 1 + r
-            new_s, new_g = relaxed(view, i, SA, *row_residual(view, i, SA, edge))
-            stores += [((2, i), new_s), ((3, i), new_g)]
-        for at, value in stores:
-            sc[at] = value
-        return carry
-
-    lax.fori_loop(0, ny // GROUP, sweep, 0)
+        sc_b[0, i], sc_b[1, i] = relaxed(view, i, SA, *res)
+
+    def sweep(i):
+        new_s, new_g = relaxed(view, i, SA, *row_residual(view, i, SA, edge))
+        return [(sc_b, (0, i), new_s), (sc_b, (1, i), new_g)]
+
+    def final(i):
+        new_s, new_g = last_relaxed(view, i, SB, edge, slice(PAD, PAD + nx))
+        return [(done, (0, i - 1), new_s), (done, (1, i - 1), new_g)]
 
     def leaving(k):
         part = pl.ds(GROUP * k, GROUP)
         return pltpu.make_async_copy(done.at[:, part], out.at[:, part], sems.at[k])
 
-    def final(k, carry):
-        stores = []
-        for r in range(GROUP):
-            i = GROUP * k + 1 + r
-            new_s, new_g = last_relaxed(view, i, SB, edge, slice(PAD, PAD + nx))
-            stores += [((0, i - 1), new_s), ((1, i - 1), new_g)]
-        for at, value in stores:
-            done[at] = value
+    grouped(list(range(1, ny + 1)), sweep, GROUP)
+    for k in range(ny // GROUP):
+        grouped(list(range(GROUP * k + 1, GROUP * k + GROUP + 1)), final, GROUP)
         leaving(k).start()
-        return carry
-
-    lax.fori_loop(0, ny // GROUP, final, 0)
     for k in range(ny // GROUP):
         leaving(k).wait()
 
 
 class Fields:
-    def __init__(self, st, sc):
-        self.st, self.sc = st, sc
+    def __init__(self, st, first, second):
+        self.st, self.first, self.second = st, first, second
 
     def __getitem__(self, at):
-        return (self.sc if at[0] <= GB else self.st)[at]
+        if at[0] > GB:
+            return self.st[at]
+        return self.first[at] if at[0] <= GA else self.second[(at[0] - SB,) + at[1:]]
 
 
 def cost(rows, cells):
@@ -904,7 +892,8 @@
         in_specs=[VMEM] * (4 + len(got)),
         out_specs=HBM,
         scratch_shapes=[
-            pltpu.VMEM((4, ny + 2, ext, nz), jnp.float32),
+            pltpu.VMEM((2, ny + 2, ext, nz), jnp.float32),
+            pltpu.VMEM((2, ny + 2, ext, nz), jnp.float32),
             pltpu.VMEM((11, ext, nz), jnp.float32),
             pltpu.VMEM(tall(lay.near).shape, jnp.float32),
             pltpu.VMEM((2, ny, nx, nz), jnp.float32),

time: 28.7 us -> 29.2 us (1.017)
  Pallas kernels: 7.35 us -> 7.94 us
    pallas_call x1, Pallas kernels: 2.14 us -> 2.73 us  [shards(): pl.pallas_call(functools.partial(third_kernel, radices[-1], stride), out_...]
where the time goes in v16:
time: 29.2 us; the launch traced here: 29 us
  starting transfers between devices  11.7 us (40%)
  waiting for transfers between devices  9.23 us (32%)
  Pallas kernels  7.94 us (27%)
    ppermute x7, starting transfers between devices, swap(): return lax.ppermute(x, axis, pairs)  8.31 us
    ppermute x7, waiting for transfers between devices, swap(): return lax.ppermute(x, axis, pairs)  4.74 us
    ppermute x4, waiting for transfers between devices, exchange_stage(): lax.ppermute(message, 'gy', [(sender, me) for me, sender in enumerate(sen...  4.49 us
    ppermute x4, starting transfers between devices, exchange_stage(): lax.ppermute(message, 'gy', [(sender, me) for me, sender in enumerate(sen...  3.41 us
    pallas_call x1, Pallas kernels, shards(): pl.pallas_call(functools.partial(third_kernel, radices[-1], stride), out_...  2.73 us
    pallas_call x1, Pallas kernels, shards(): pl.pallas_call(pack_kernel, out_shape=(strip, strip, f32((EARLY, nx, nz))...  1.63 us
    pallas_call x1, Pallas kernels, shards(): pl.pallas_call(inner_kernel, out_shape=(state, rows), in_specs=[VMEM] * 2...  1.59 us
    pallas_call x1, Pallas kernels, shards(): pl.pallas_call(second_kernel, out_shape=(state, rows, more, tall(lay.map)...  0.62 us
  transfers between devices with their start and end apart: 11, of which 5 were waited for; matrix products, arithmetic and copies ran while one was open for 0% of the time, Pallas kernels for 10%

profile of v16, /device:TPU:16, one launch (start us, length us, event | category | flops | bytes accessed | tf_op | source)
XLA Modules:
  0.0 29.0 jit_solution(6674893591916162486)
XLA Ops:
  0.0 1.6 %pack_x.1 = (f32[304,128]{1,0:T(8,128)S(1)}, f32[304,128]{1,0:T(8,128)S(1)}, f32[7,32,128]{2,1,0:T(8,128)S(1)}, f32[15,14,48,128]{3,2,1,0:T(8,128)S(1)}) custom-call(f32[2,12,32,128]{3,2,1,0:T(8,128)} %bitcast.5, f32[2,12,32,128]{3,2,1,0:T(8,128)} %bitcast.6, f32[12,32,128]{2,1,0:T(8,128)} %bitcast.7, f32[12,32,128]{2,1,0:T(8,128)} %bitcast.8), custom_call_target="tpu_custom_call" | custom-call | tf_op jit(solution)/shard_map/pack_x/pallas_call | solution.py:779
  1.6 1.6 %collective-permute-start = (f32[304,128]{1,0:T(8,128)S(1)}, f32[304,128]{1,0:T(8,128)S(1)}, u32[]{:S(2)}, u32[]{:S(2)}) collective-permute-start(f32[304,128]{1,0:T(8,128)S(1)} %get-tuple-element.32), channel_id=1, source_target_pairs={{0,8},{8,0},{16,24},{24,16},{1,9},{9,1},{17,25},{25,17},{2,10},{10... | collective-permute-start | bytes 466952 | tf_op jit(solution)/shard_map/ppermute | solution.py:764
  3.3 1.9 %collective-permute-start.1 = (f32[304,128]{1,0:T(8,128)S(1)}, f32[304,128]{1,0:T(8,128)S(1)}, u32[]{:S(2)}, u32[]{:S(2)}) collective-permute-start(f32[304,128]{1,0:T(8,128)S(1)} %get-tuple-element.33), channel_id=1, source_target_pairs={{8,16},{16,8},{9,17},{17,9},{10,18},{18,10},{11,19},{19,11},{12,20... | collective-permute-start | bytes 466952 | tf_op jit(solution)/shard_map/ppermute | solution.py:764
  5.2 0.7 %collective-permute-start.2 = (f32[7,32,128]{2,1,0:T(8,128)S(1)}, f32[7,32,128]{2,1,0:T(8,128)S(1)}, u32[]{:S(2)}, u32[]{:S(2)}) collective-permute-start(f32[7,32,128]{2,1,0:T(8,128)S(1)} %get-tuple-element.36), channel_id=1, source_target_pairs={{1,2},{2,1},{3,4},{4,3},{5,6},{6,5},{9,10},{10,9},{11,12},{12,11},... | collective-permute-start | bytes 344072 | tf_op jit(solution)/shard_map/ppermute | solution.py:764
  5.9 1.5 %collective-permute-done.one = f32[304,128]{1,0:T(8,128)S(1)} collective-permute-done((f32[304,128]{1,0:T(8,128)S(1)}, f32[304,128]{1,0:T(8,128)S(1)}, u32[]{:S(2)}, u32[]{:S(2)}) %collective-permute-start) | collective-permute-done | bytes 155680 | tf_op jit(solution)/shard_map/ppermute | solution.py:764
  7.5 3.2 %collective-permute-done.1.two = f32[304,128]{1,0:T(8,128)S(1)} collective-permute-done((f32[304,128]{1,0:T(8,128)S(1)}, f32[304,128]{1,0:T(8,128)S(1)}, u32[]{:S(2)}, u32[]{:S(2)}) %collective-permute-start.1) | collective-permute-done | bytes 155680 | tf_op jit(solution)/shard_map/ppermute | solution.py:764
  10.6 0.2 first.1
  10.8 0.7 %collective-permute-start.6 = (f32[144,128]{1,0:T(8,128)S(1)}, f32[144,128]{1,0:T(8,128)S(1)}, u32[]{:S(2)}, u32[]{:S(2)}) collective-permute-start(f32[144,128]{1,0:T(8,128)S(1)} %get-tuple-element.45), channel_id=1, source_target_pairs={{1,2},{2,1},{3,4},{4,3},{5,6},{6,5},{9,10},{10,9},{11,12},{12,11},... | collective-permute-start | bytes 221192 | tf_op jit(solution)/shard_map/ppermute | solution.py:764
  11.5 0.5 %other.1 = (f32[15,14,48,128]{3,2,1,0:T(8,128)S(1)}, f32[3,40,128]{2,1,0:T(8,128)S(1)}, f32[3,40,128]{2,1,0:T(8,128)S(1)}, f32[3,40,128]{2,1,0:T(8,128)S(1)}) custom-call(f32[15,14,48,128]{3,2,1,0:T(8,128)S(1)} %get-tuple-element.34.st_in, f32[304,128]{1,0:T(8,128)S(1)} %collective-permute-done.one, ...), custom_call_target="tpu_custom_call", output_to_operand_aliasing={{0}: (0, {})} | custom-call | tf_op jit(solution)/shard_map/other/pallas_call | solution.py:813
  12.0 2.9 %collective-permute-start.3 = (f32[3,40,128]{2,1,0:T(8,128)S(1)}, f32[3,40,128]{2,1,0:T(8,128)S(1)}, u32[]{:S(2)}, u32[]{:S(2)}) collective-permute-start(f32[3,40,128]{2,1,0:T(8,128)S(1)} %get-tuple-element.39), channel_id=1, source_target_pairs={{0,1},{1,0},{2,3},{3,2},{4,5},{5,4},{6,7},{7,6},{8,9},{9,8},{10,11... | collective-permute-start | bytes 184328 | tf_op jit(solution)/shard_map/ppermute | solution.py:764
  15.0 0.1 collective-permute-start.4
  15.0 0.4 %collective-permute-start.5 = (f32[3,40,128]{2,1,0:T(8,128)S(1)}, f32[3,40,128]{2,1,0:T(8,128)S(1)}, u32[]{:S(2)}, u32[]{:S(2)}) collective-permute-start(f32[3,40,128]{2,1,0:T(8,128)S(1)} %get-tuple-element.41), channel_id=1, source_target_pairs={{0,1},{1,0},{2,3},{3,2},{4,5},{5,4},{6,7},{7,6},{8,9},{9,8},{10,11... | collective-permute-start | bytes 184328 | tf_op jit(solution)/shard_map/ppermute | solution.py:764
  15.5 1.6 %inner.1 = (f32[15,14,48,128]{3,2,1,0:T(8,128)S(1)}, f32[4,6,48,128]{3,2,1,0:T(8,128)S(1)}) custom-call(f32[15,14,48,128]{3,2,1,0:T(8,128)S(1)} %get-tuple-element.35.st_in, f32[7,32,128]{2,1,0:T(8,128)S(1)} %collective-permute-done.2.early), custom_call_target="tpu_custom_call", output_to_operand_aliasing={{0}: (0, {})} | custom-call | flops 14745600 | bytes 18874368 | tf_op jit(solution)/shard_map/inner/pallas_call | solution.py:825
  17.1 0.0 collective-permute-done.3.refs_0_
  17.1 0.6 %near.1 = (f32[15,14,48,128]{3,2,1,0:T(8,128)S(1)}, f32[4,6,48,128]{3,2,1,0:T(8,128)S(1)}, f32[6,48,128]{2,1,0:T(8,128)S(1)}) custom-call(f32[15,14,48,128]{3,2,1,0:T(8,128)S(1)} %get-tuple-element.37.st_in, f32[4,6,48,128]{3,2,1,0:T(8,128)S(1)} %get-tuple-element.38.coarse_in, ...), custom_call_target="tpu_custom_call", output_to_operand_aliasing={{0}: (0, {}), {1}: (1, {})} | custom-call | tf_op jit(solution)/shard_map/near/pallas_call | solution.py:845
  17.7 0.6 %second.1 = (f32[15,14,48,128]{3,2,1,0:T(8,128)S(1)}, f32[4,6,48,128]{3,2,1,0:T(8,128)S(1)}, f32[6,48,128]{2,1,0:T(8,128)S(1)}, f32[40,128]{1,0:T(8,128)S(1)}, f...) custom-call(f32[15,14,48,128]{3,2,1,0:T(8,128)S(1)} %get-tuple-eleme, ...), custom_call_target="tpu_custom_call", output_to_operand_aliasing={{0}: (0, {}), {1}: (1, {}), {2}: (2, {})} | custom-call | tf_op jit(solution)/shard_map/second/pallas_call | solution.py:855
  18.3 0.1 collective-permute-start.7
  18.5 1.2 %collective-permute-done.7.refs_4_ = f32[176,128]{1,0:T(8,128)S(1)} collective-permute-done((f32[176,128]{1,0:T(8,128)S(1)}, f32[176,128]{1,0:T(8,128)S(1)}, u32[]{:S(2)}, u32[]{:S(2)}) %collective-permute-start.7) | collective-permute-done | bytes 90144 | tf_op jit(solution)/shard_map/ppermute | solution.py:559
  19.7 1.1 %collective-permute-start.8 = (f32[144,128]{1,0:T(8,128)S(1)}, f32[144,128]{1,0:T(8,128)S(1)}, u32[]{:S(2)}, u32[]{:S(2)}) collective-permute-start(f32[144,128]{1,0:T(8,128)S(1)} %get-tuple-element.54), channel_id=1, source_target_pairs={{7,0},{2,1},{1,2},{4,3},{3,4},{6,5},{5,6},{0,7},{15,8},{10,9},{9,1... | collective-permute-start | bytes 221192 | tf_op jit(solution)/shard_map/ppermute | solution.py:559
  20.8 1.7 %collective-permute-start.9 = (f32[40,128]{1,0:T(8,128)S(1)}, f32[40,128]{1,0:T(8,128)S(1)}, u32[]{:S(2)}, u32[]{:S(2)}) collective-permute-start(f32[40,128]{1,0:T(8,128)S(1)} %get-tuple-element.55), channel_id=1, source_target_pairs={{3,0},{5,1},{6,2},{0,3},{7,4},{1,5},{2,6},{4,7},{11,8},{13,9},{14,... | collective-permute-start | bytes 61448 | tf_op jit(solution)/shard_map/ppermute | solution.py:559
  22.5 0.5 %collective-permute-start.10 = (f32[40,128]{1,0:T(8,128)S(1)}, f32[40,128]{1,0:T(8,128)S(1)}, u32[]{:S(2)}, u32[]{:S(2)}) collective-permute-start(f32[40,128]{1,0:T(8,128)S(1)} %get-tuple-element.56), channel_id=1, source_target_pairs={{4,0},{6,1},{5,2},{7,3},{0,4},{2,5},{1,6},{3,7},{12,8},{14,9},{13,... | collective-permute-start | bytes 61448 | tf_op jit(solution)/shard_map/ppermute | solution.py:559
  23.0 1.9 %collective-permute-done.9.refs_5_ = f32[40,128]{1,0:T(8,128)S(1)} collective-permute-done((f32[40,128]{1,0:T(8,128)S(1)}, f32[40,128]{1,0:T(8,128)S(1)}, u32[]{:S(2)}, u32[]{:S(2)}) %collective-permute-start.9) | collective-permute-done | bytes 20512 | tf_op jit(solution)/shard_map/ppermute | solution.py:559
  24.9 1.4 %collective-permute-done.10.refs_6_ = f32[40,128]{1,0:T(8,128)S(1)} collective-permute-done((f32[40,128]{1,0:T(8,128)S(1)}, f32[40,128]{1,0:T(8,128)S(1)}, u32[]{:S(2)}, u32[]{:S(2)}) %collective-permute-start.10) | collective-permute-done | bytes 20512 | tf_op jit(solution)/shard_map/ppermute | solution.py:559
  26.3 2.7 %third.1 = f32[2,12,32,128]{3,2,1,0:T(8,128)} custom-call(f32[15,14,48,128]{3,2,1,0:T(8,128)S(1)} %get-tuple-element.46.refs_0_, f32[6,48,128]{2,1,0:T(8,128)S(1)} %get-tuple-element.47.refs_1_, f32[4,6,48,128]{3,2,1,0:T(8,128)S(1)} %get-tuple-element.48.refs_2_, f32[280,128]{1,0:T(8,128)S(1)} %get-tuple-element.53.refs_3_, ...), custom_call_target="tpu_custom_call" | custom-call | tf_op jit(solution)/shard_map/third/pallas_call | solution.py:889
  (7 shorter events, 0.1 us)
Async XLA Ops:
  1.6 5.8 %collective-permute-start = (f32[304,128]{1,0:T(8,128)S(1)}, f32[304,128]{1,0:T(8,128)S(1)}, u32[]{:S(2)}, u32[]{:S(2)}) collective-permute-start(f32[304,128]{1,0:T(8,128)S(1)} %get-tuple-element.32), channel_id=1, source_target_pairs={{0,8},{8,0},{16,24},{24,16},{1,9},{9,1},{17,25},{25,17},{2,10},{10... | collective-permute-start | bytes 466952 | tf_op jit(solution)/shard_map/ppermute | solution.py:764
  3.3 7.4 %collective-permute-start.1 = (f32[304,128]{1,0:T(8,128)S(1)}, f32[304,128]{1,0:T(8,128)S(1)}, u32[]{:S(2)}, u32[]{:S(2)}) collective-permute-start(f32[304,128]{1,0:T(8,128)S(1)} %get-tuple-element.33), channel_id=1, source_target_pairs={{8,16},{16,8},{9,17},{17,9},{10,18},{18,10},{11,19},{19,11},{12,20... | collective-permute-start | bytes 466952 | tf_op jit(solution)/shard_map/ppermute | solution.py:764
  5.2 10.3 %collective-permute-start.2 = (f32[7,32,128]{2,1,0:T(8,128)S(1)}, f32[7,32,128]{2,1,0:T(8,128)S(1)}, u32[]{:S(2)}, u32[]{:S(2)}) collective-permute-start(f32[7,32,128]{2,1,0:T(8,128)S(1)} %get-tuple-element.36), channel_id=1, source_target_pairs={{1,2},{2,1},{3,4},{4,3},{5,6},{6,5},{9,10},{10,9},{11,12},{12,11},... | collective-permute-start | bytes 344072 | tf_op jit(solution)/shard_map/ppermute | solution.py:764
  10.8 6.8 %collective-permute-start.6 = (f32[144,128]{1,0:T(8,128)S(1)}, f32[144,128]{1,0:T(8,128)S(1)}, u32[]{:S(2)}, u32[]{:S(2)}) collective-permute-start(f32[144,128]{1,0:T(8,128)S(1)} %get-tuple-element.45), channel_id=1, source_target_pairs={{1,2},{2,1},{3,4},{4,3},{5,6},{6,5},{9,10},{10,9},{11,12},{12,11},... | collective-permute-start | bytes 221192 | tf_op jit(solution)/shard_map/ppermute | solution.py:764
  12.0 5.0 %collective-permute-start.3 = (f32[3,40,128]{2,1,0:T(8,128)S(1)}, f32[3,40,128]{2,1,0:T(8,128)S(1)}, u32[]{:S(2)}, u32[]{:S(2)}) collective-permute-start(f32[3,40,128]{2,1,0:T(8,128)S(1)} %get-tuple-element.39), channel_id=1, source_target_pairs={{0,1},{1,0},{2,3},{3,2},{4,5},{5,4},{6,7},{7,6},{8,9},{9,8},{10,11... | collective-permute-start | bytes 184328 | tf_op jit(solution)/shard_map/ppermute | solution.py:764
  15.0 2.1 %collective-permute-start.4 = (f32[3,40,128]{2,1,0:T(8,128)S(1)}, f32[3,40,128]{2,1,0:T(8,128)S(1)}, u32[]{:S(2)}, u32[]{:S(2)}) collective-permute-start(f32[3,40,128]{2,1,0:T(8,128)S(1)} %get-tuple-element.40), channel_id=1, source_target_pairs={{0,1},{1,0},{2,3},{3,2},{4,5},{5,4},{6,7},{7,6},{8,9},{9,8},{10,11... | collective-permute-start | bytes 184328 | tf_op jit(solution)/shard_map/ppermute | solution.py:764
  15.0 2.1 %collective-permute-start.5 = (f32[3,40,128]{2,1,0:T(8,128)S(1)}, f32[3,40,128]{2,1,0:T(8,128)S(1)}, u32[]{:S(2)}, u32[]{:S(2)}) collective-permute-start(f32[3,40,128]{2,1,0:T(8,128)S(1)} %get-tuple-element.41), channel_id=1, source_target_pairs={{0,1},{1,0},{2,3},{3,2},{4,5},{5,4},{6,7},{7,6},{8,9},{9,8},{10,11... | collective-permute-start | bytes 184328 | tf_op jit(solution)/shard_map/ppermute | solution.py:764
  18.3 1.4 %collective-permute-start.7 = (f32[176,128]{1,0:T(8,128)S(1)}, f32[176,128]{1,0:T(8,128)S(1)}, u32[]{:S(2)}, u32[]{:S(2)}) collective-permute-start(f32[176,128]{1,0:T(8,128)S(1)} %get-tuple-element.52), channel_id=1, source_target_pairs={{1,0},{0,1},{3,2},{2,3},{5,4},{4,5},{7,6},{6,7},{9,8},{8,9},{11,10... | collective-permute-start | bytes 270344 | tf_op jit(solution)/shard_map/ppermute | solution.py:559
  19.7 6.6 %collective-permute-start.8 = (f32[144,128]{1,0:T(8,128)S(1)}, f32[144,128]{1,0:T(8,128)S(1)}, u32[]{:S(2)}, u32[]{:S(2)}) collective-permute-start(f32[144,128]{1,0:T(8,128)S(1)} %get-tuple-element.54), channel_id=1, source_target_pairs={{7,0},{2,1},{1,2},{4,3},{3,4},{6,5},{5,6},{0,7},{15,8},{10,9},{9,1... | collective-permute-start | bytes 221192 | tf_op jit(solution)/shard_map/ppermute | solution.py:559
  20.8 4.1 %collective-permute-start.9 = (f32[40,128]{1,0:T(8,128)S(1)}, f32[40,128]{1,0:T(8,128)S(1)}, u32[]{:S(2)}, u32[]{:S(2)}) collective-permute-start(f32[40,128]{1,0:T(8,128)S(1)} %get-tuple-element.55), channel_id=1, source_target_pairs={{3,0},{5,1},{6,2},{0,3},{7,4},{1,5},{2,6},{4,7},{11,8},{13,9},{14,... | collective-permute-start | bytes 61448 | tf_op jit(solution)/shard_map/ppermute | solution.py:559
  22.5 3.8 %collective-permute-start.10 = (f32[40,128]{1,0:T(8,128)S(1)}, f32[40,128]{1,0:T(8,128)S(1)}, u32[]{:S(2)}, u32[]{:S(2)}) collective-permute-start(f32[40,128]{1,0:T(8,128)S(1)} %get-tuple-element.56), channel_id=1, source_target_pairs={{4,0},{6,1},{5,2},{7,3},{0,4},{2,5},{1,6},{3,7},{12,8},{14,9},{13,... | collective-permute-start | bytes 61448 | tf_op jit(solution)/shard_map/ppermute | solution.py:559

commit v17 on v15

--- a/solution.py
+++ b/solution.py
@@ -59,6 +59,10 @@
 
 def strip_height(ny):
     return ny * STRIP_ROWS + (ny + 7) // 8 * 8
+
+
+def strip_tile(y, p):
+    return pl.ds(pl.multiple_of(y * STRIP_ROWS + 8 * p, 8), 8)
 
 
 def sublanes(nz):
@@ -98,19 +102,23 @@
         copy.start()
     for copy in copies:
         copy.wait()
-    for i in range(1, ny + 1):
+
+    def row(y, carry):
         sides = []
         for start in (PAD, PAD + nx - 8):
-            s, g, e, rs, rg, c = (st[plane, i, start : start + 8] for plane in (SA, GA, K, RS, RG, C))
+            s, g, e, rs, rg, c = (st[plane, y + 1, start : start + 8] for plane in (SA, GA, K, RS, RG, C))
             sides.append(strip_side(s, g, conductivity_of(s, e), rs, rg, c, start == PAD))
         (low, low_k), (high, high_k) = sides
         for p in range(len(PAIRS)):
-            part = slice((i - 1) * STRIP_ROWS + 8 * p, (i - 1) * STRIP_ROWS + 8 * p + 8)
+            part = strip_tile(y, p)
             one[part] = jnp.where(even, high[p], low[p])
             two[part] = jnp.where(even, low[p], high[p])
-        part = slice(ny * STRIP_ROWS + i - 1, ny * STRIP_ROWS + i)
+        part = pl.ds(ny * STRIP_ROWS + y, 1)
         one[part] = jnp.where(even, high_k, low_k)
         two[part] = jnp.where(even, low_k, high_k)
+        return carry
+
+    lax.fori_loop(0, ny, row, 0, unroll=2)
     own = slice(PAD, PAD + nx)
     for is_odd, e, d in ((True, ny, ny - 1), (False, 1, 2)):
 
@@ -144,13 +152,13 @@
         return jnp.where(even, b, a), jnp.where(even, a, b)
 
     for p, (plane_a, plane_b) in enumerate(PAIRS):
-        before, after = received(slice(y * STRIP_ROWS + 8 * p, y * STRIP_ROWS + 8 * p + 8))
+        before, after = received(strip_tile(y, p))
         before = {plane_a: pltpu.roll(before, 4, 0), plane_b: before}
         after = {plane_a: after, plane_b: pltpu.roll(after, 4, 0)}
         for plane in (plane_a, plane_b):
             low, high = jnp.where(row >= 4, before[plane], 0.0), jnp.where(row < 4, after[plane], 0.0)
             if plane == K:
-                k_low, k_high = received(slice(ny * STRIP_ROWS + y, ny * STRIP_ROWS + y + 1))
+                k_low, k_high = received(pl.ds(ny * STRIP_ROWS + y, 1))
                 low, high = jnp.where(row == 3, k_low, low), jnp.where(row == 4, k_high, high)
             st[plane, i, :PAD] = low
             st[plane, i, PAD + nx :] = high
@@ -232,6 +240,15 @@
             stores += work(i)
         for ref, at, value in stores:
             ref[at] = value
+
+
+def looped(first, last, size, work):
+    def group(k, carry):
+        grouped([first + size * k + r for r in range(size)], work)
+        return carry
+
+    lax.fori_loop(0, (last - first) // size, group, 0)
+    grouped(list(range(last - (last - first) % size, last)), work)
 
 
 def row_coefficients(st, i, mask):
@@ -336,9 +353,13 @@
     planes, rows, ext, nz = st.shape
     ny, nx = rows - 2, ext - 2 * PAD
     mask = x_mask((ext, nz), nx)
-    for y in range(3, ny - 3):
+
+    def halo(y, carry):
         place_halo(st, one, two, y, nx)
-    grouped(list(range(3, ny - 1)), lambda i: row_coefficients(st, i, mask))
+        return carry
+
+    lax.fori_loop(3, ny - 3, halo, 0, unroll=2)
+    looped(3, ny - 1, 4, lambda i: row_coefficients(st, i, mask))
 
 
 def outer_residual(st, i, s_at, rs, rg, fy_out, edge, after):
@@ -383,11 +404,9 @@
     shape = (ext, nz)
     mask = x_mask(shape, nx)
     edge = edge_weights(shape)
-    grouped(list(range(3, ny - 1)), lambda i: row_sweep(st, i, SA, SB, edge))
-    grouped(list(range(3, ny - 1)), lambda i: row_sweep(st, i, SB, SA, edge))
-    for j in range(2, ny // 2 - 2):
-        for ref, at, value in coarse_row(st, coarse, j, mask, edge):
-            ref[at] = value
+    looped(3, ny - 1, 4, lambda i: row_sweep(st, i, SA, SB, edge))
+    looped(3, ny - 1, 4, lambda i: row_sweep(st, i, SB, SA, edge))
+    looped(2, ny // 2 - 2, 1, lambda j: coarse_row(st, coarse, j, mask, edge))
 
 
 def end_work(st, coarse, extra, read, outer, is_after):
@@ -432,11 +451,8 @@
     for k, plane in enumerate((M_2S, M_2G, M_FY)):
         extra[(3 if is_after else 0) + k] = outer[plane]
     blocks = ny // 2
-    stores = []
-    for j in (blocks - 2, blocks - 1) if is_after else (0, 1):
-        stores += coarse_row(st, coarse, j, mask, edge)
-    for ref, at, value in stores:
-        ref[at] = value
+    at = blocks - 2 if is_after else 0
+    looped(at, at + 2, 1, lambda j: coarse_row(st, coarse, j, mask, edge))
 
 
 def either_end(after, st, coarse, extra, read, outer):

time: 28.7 us -> 28.9 us (level)
    pallas_call x1, Pallas kernels: 1.59 us -> 1.27 us  [shards(): pl.pallas_call(inner_kernel, out_shape=(state, rows), in_specs=[VMEM] * 2...]
where the time goes in v17:
time: 28.9 us; the launch traced here: 28.7 us
  starting transfers between devices  11.7 us (40%)
  waiting for transfers between devices  9.23 us (32%)
  Pallas kernels  7.6 us (26%)
    ppermute x7, starting transfers between devices, swap(): return lax.ppermute(x, axis, pairs)  8.31 us
    ppermute x7, waiting for transfers between devices, swap(): return lax.ppermute(x, axis, pairs)  4.74 us
    ppermute x4, waiting for transfers between devices, exchange_stage(): lax.ppermute(message, 'gy', [(sender, me) for me, sender in enumerate(sen...  4.49 us
    ppermute x4, starting transfers between devices, exchange_stage(): lax.ppermute(message, 'gy', [(sender, me) for me, sender in enumerate(sen...  3.41 us
    pallas_call x1, Pallas kernels, shards(): pl.pallas_call(functools.partial(third_kernel, radices[-1], stride), out_...  2.14 us
    pallas_call x1, Pallas kernels, shards(): pl.pallas_call(pack_kernel, out_shape=(strip, strip, f32((EARLY, nx, nz))...  1.66 us
    pallas_call x1, Pallas kernels, shards(): pl.pallas_call(inner_kernel, out_shape=(state, rows), in_specs=[VMEM] * 2...  1.27 us
    pallas_call x1, Pallas kernels, shards(): pl.pallas_call(second_kernel, out_shape=(state, rows, more, tall(lay.map)...  0.82 us
  transfers between devices with their start and end apart: 11, of which 5 were waited for; matrix products, arithmetic and copies ran while one was open for 0% of the time, Pallas kernels for 10%

profile of v17, /device:TPU:16, one launch (start us, length us, event | category | flops | bytes accessed | tf_op | source)
XLA Modules:
  0.0 28.7 jit_solution(14494369525662396817)
XLA Ops:
  0.0 1.7 %pack_x.1 = (f32[304,128]{1,0:T(8,128)S(1)}, f32[304,128]{1,0:T(8,128)S(1)}, f32[7,32,128]{2,1,0:T(8,128)S(1)}, f32[15,14,48,128]{3,2,1,0:T(8,128)S(1)}) custom-call(f32[2,12,32,128]{3,2,1,0:T(8,128)} %bitcast.5, f32[2,12,32,128]{3,2,1,0:T(8,128)} %bitcast.6, f32[12,32,128]{2,1,0:T(8,128)} %bitcast.7, f32[12,32,128]{2,1,0:T(8,128)} %bitcast.8), custom_call_target="tpu_custom_call" | custom-call | tf_op jit(solution)/shard_map/pack_x/pallas_call | solution.py:807
  1.7 1.6 %collective-permute-start = (f32[304,128]{1,0:T(8,128)S(1)}, f32[304,128]{1,0:T(8,128)S(1)}, u32[]{:S(2)}, u32[]{:S(2)}) collective-permute-start(f32[304,128]{1,0:T(8,128)S(1)} %get-tuple-element.32), channel_id=1, source_target_pairs={{0,8},{8,0},{16,24},{24,16},{1,9},{9,1},{17,25},{25,17},{2,10},{10... | collective-permute-start | bytes 466952 | tf_op jit(solution)/shard_map/ppermute | solution.py:792
  3.3 1.9 %collective-permute-start.1 = (f32[304,128]{1,0:T(8,128)S(1)}, f32[304,128]{1,0:T(8,128)S(1)}, u32[]{:S(2)}, u32[]{:S(2)}) collective-permute-start(f32[304,128]{1,0:T(8,128)S(1)} %get-tuple-element.33), channel_id=1, source_target_pairs={{8,16},{16,8},{9,17},{17,9},{10,18},{18,10},{11,19},{19,11},{12,20... | collective-permute-start | bytes 466952 | tf_op jit(solution)/shard_map/ppermute | solution.py:792
  5.2 0.7 %collective-permute-start.2 = (f32[7,32,128]{2,1,0:T(8,128)S(1)}, f32[7,32,128]{2,1,0:T(8,128)S(1)}, u32[]{:S(2)}, u32[]{:S(2)}) collective-permute-start(f32[7,32,128]{2,1,0:T(8,128)S(1)} %get-tuple-element.36), channel_id=1, source_target_pairs={{1,2},{2,1},{3,4},{4,3},{5,6},{6,5},{9,10},{10,9},{11,12},{12,11},... | collective-permute-start | bytes 344072 | tf_op jit(solution)/shard_map/ppermute | solution.py:792
  5.9 1.5 %collective-permute-done.one = f32[304,128]{1,0:T(8,128)S(1)} collective-permute-done((f32[304,128]{1,0:T(8,128)S(1)}, f32[304,128]{1,0:T(8,128)S(1)}, u32[]{:S(2)}, u32[]{:S(2)}) %collective-permute-start) | collective-permute-done | bytes 155680 | tf_op jit(solution)/shard_map/ppermute | solution.py:792
  7.5 3.2 %collective-permute-done.1.two = f32[304,128]{1,0:T(8,128)S(1)} collective-permute-done((f32[304,128]{1,0:T(8,128)S(1)}, f32[304,128]{1,0:T(8,128)S(1)}, u32[]{:S(2)}, u32[]{:S(2)}) %collective-permute-start.1) | collective-permute-done | bytes 155680 | tf_op jit(solution)/shard_map/ppermute | solution.py:792
  10.7 0.2 first.1
  10.9 0.7 %collective-permute-start.6 = (f32[144,128]{1,0:T(8,128)S(1)}, f32[144,128]{1,0:T(8,128)S(1)}, u32[]{:S(2)}, u32[]{:S(2)}) collective-permute-start(f32[144,128]{1,0:T(8,128)S(1)} %get-tuple-element.45), channel_id=1, source_target_pairs={{1,2},{2,1},{3,4},{4,3},{5,6},{6,5},{9,10},{10,9},{11,12},{12,11},... | collective-permute-start | bytes 221192 | tf_op jit(solution)/shard_map/ppermute | solution.py:792
  11.6 0.7 %other.1 = (f32[15,14,48,128]{3,2,1,0:T(8,128)S(1)}, f32[3,40,128]{2,1,0:T(8,128)S(1)}, f32[3,40,128]{2,1,0:T(8,128)S(1)}, f32[3,40,128]{2,1,0:T(8,128)S(1)}) custom-call(f32[15,14,48,128]{3,2,1,0:T(8,128)S(1)} %get-tuple-element.34.st_in, f32[304,128]{1,0:T(8,128)S(1)} %collective-permute-done.one, ...), custom_call_target="tpu_custom_call", output_to_operand_aliasing={{0}: (0, {})} | custom-call | tf_op jit(solution)/shard_map/other/pallas_call | solution.py:841
  12.2 2.9 %collective-permute-start.3 = (f32[3,40,128]{2,1,0:T(8,128)S(1)}, f32[3,40,128]{2,1,0:T(8,128)S(1)}, u32[]{:S(2)}, u32[]{:S(2)}) collective-permute-start(f32[3,40,128]{2,1,0:T(8,128)S(1)} %get-tuple-element.39), channel_id=1, source_target_pairs={{0,1},{1,0},{2,3},{3,2},{4,5},{5,4},{6,7},{7,6},{8,9},{9,8},{10,11... | collective-permute-start | bytes 184328 | tf_op jit(solution)/shard_map/ppermute | solution.py:792
  15.2 0.1 collective-permute-start.4
  15.2 0.4 %collective-permute-start.5 = (f32[3,40,128]{2,1,0:T(8,128)S(1)}, f32[3,40,128]{2,1,0:T(8,128)S(1)}, u32[]{:S(2)}, u32[]{:S(2)}) collective-permute-start(f32[3,40,128]{2,1,0:T(8,128)S(1)} %get-tuple-element.41), channel_id=1, source_target_pairs={{0,1},{1,0},{2,3},{3,2},{4,5},{5,4},{6,7},{7,6},{8,9},{9,8},{10,11... | collective-permute-start | bytes 184328 | tf_op jit(solution)/shard_map/ppermute | solution.py:792
  15.7 0.0 collective-permute-done.2.early
  15.7 1.3 %inner.1 = (f32[15,14,48,128]{3,2,1,0:T(8,128)S(1)}, f32[4,6,48,128]{3,2,1,0:T(8,128)S(1)}) custom-call(f32[15,14,48,128]{3,2,1,0:T(8,128)S(1)} %get-tuple-element.35.st_in, f32[7,32,128]{2,1,0:T(8,128)S(1)} %collective-permute-done.2.early), custom_call_target="tpu_custom_call", output_to_operand_aliasing={{0}: (0, {})} | custom-call | flops 14745600 | bytes 18874368 | tf_op jit(solution)/shard_map/inner/pallas_call | solution.py:853
  17.0 0.8 %near.1 = (f32[15,14,48,128]{3,2,1,0:T(8,128)S(1)}, f32[4,6,48,128]{3,2,1,0:T(8,128)S(1)}, f32[6,48,128]{2,1,0:T(8,128)S(1)}) custom-call(f32[15,14,48,128]{3,2,1,0:T(8,128)S(1)} %get-tuple-element.37.st_in, f32[4,6,48,128]{3,2,1,0:T(8,128)S(1)} %get-tuple-element.38.coarse_in, ...), custom_call_target="tpu_custom_call", output_to_operand_aliasing={{0}: (0, {}), {1}: (1, {})} | custom-call | tf_op jit(solution)/shard_map/near/pallas_call | solution.py:873
  17.8 0.8 %second.1 = (f32[15,14,48,128]{3,2,1,0:T(8,128)S(1)}, f32[4,6,48,128]{3,2,1,0:T(8,128)S(1)}, f32[6,48,128]{2,1,0:T(8,128)S(1)}, f32[40,128]{1,0:T(8,128)S(1)}, f...) custom-call(f32[15,14,48,128]{3,2,1,0:T(8,128)S(1)} %get-tuple-eleme, ...), custom_call_target="tpu_custom_call", output_to_operand_aliasing={{0}: (0, {}), {1}: (1, {}), {2}: (2, {})} | custom-call | tf_op jit(solution)/shard_map/second/pallas_call | solution.py:883
  18.6 0.1 collective-permute-start.7
  18.7 1.2 %collective-permute-done.7.refs_4_ = f32[176,128]{1,0:T(8,128)S(1)} collective-permute-done((f32[176,128]{1,0:T(8,128)S(1)}, f32[176,128]{1,0:T(8,128)S(1)}, u32[]{:S(2)}, u32[]{:S(2)}) %collective-permute-start.7) | collective-permute-done | bytes 90144 | tf_op jit(solution)/shard_map/ppermute | solution.py:577
  20.0 1.0 %collective-permute-start.8 = (f32[144,128]{1,0:T(8,128)S(1)}, f32[144,128]{1,0:T(8,128)S(1)}, u32[]{:S(2)}, u32[]{:S(2)}) collective-permute-start(f32[144,128]{1,0:T(8,128)S(1)} %get-tuple-element.54), channel_id=1, source_target_pairs={{7,0},{2,1},{1,2},{4,3},{3,4},{6,5},{5,6},{0,7},{15,8},{10,9},{9,1... | collective-permute-start | bytes 221192 | tf_op jit(solution)/shard_map/ppermute | solution.py:577
  21.0 1.7 %collective-permute-start.9 = (f32[40,128]{1,0:T(8,128)S(1)}, f32[40,128]{1,0:T(8,128)S(1)}, u32[]{:S(2)}, u32[]{:S(2)}) collective-permute-start(f32[40,128]{1,0:T(8,128)S(1)} %get-tuple-element.55), channel_id=1, source_target_pairs={{3,0},{5,1},{6,2},{0,3},{7,4},{1,5},{2,6},{4,7},{11,8},{13,9},{14,... | collective-permute-start | bytes 61448 | tf_op jit(solution)/shard_map/ppermute | solution.py:577
  22.8 0.5 %collective-permute-start.10 = (f32[40,128]{1,0:T(8,128)S(1)}, f32[40,128]{1,0:T(8,128)S(1)}, u32[]{:S(2)}, u32[]{:S(2)}) collective-permute-start(f32[40,128]{1,0:T(8,128)S(1)} %get-tuple-element.56), channel_id=1, source_target_pairs={{4,0},{6,1},{5,2},{7,3},{0,4},{2,5},{1,6},{3,7},{12,8},{14,9},{13,... | collective-permute-start | bytes 61448 | tf_op jit(solution)/shard_map/ppermute | solution.py:577
  23.3 1.9 %collective-permute-done.9.refs_5_ = f32[40,128]{1,0:T(8,128)S(1)} collective-permute-done((f32[40,128]{1,0:T(8,128)S(1)}, f32[40,128]{1,0:T(8,128)S(1)}, u32[]{:S(2)}, u32[]{:S(2)}) %collective-permute-start.9) | collective-permute-done | bytes 20512 | tf_op jit(solution)/shard_map/ppermute | solution.py:577
  25.2 1.4 %collective-permute-done.10.refs_6_ = f32[40,128]{1,0:T(8,128)S(1)} collective-permute-done((f32[40,128]{1,0:T(8,128)S(1)}, f32[40,128]{1,0:T(8,128)S(1)}, u32[]{:S(2)}, u32[]{:S(2)}) %collective-permute-start.10) | collective-permute-done | bytes 20512 | tf_op jit(solution)/shard_map/ppermute | solution.py:577
  26.5 2.1 %third.1 = f32[2,12,32,128]{3,2,1,0:T(8,128)} custom-call(f32[15,14,48,128]{3,2,1,0:T(8,128)S(1)} %get-tuple-element.46.refs_0_, f32[6,48,128]{2,1,0:T(8,128)S(1)} %get-tuple-element.47.refs_1_, f32[4,6,48,128]{3,2,1,0:T(8,128)S(1)} %get-tuple-element.48.refs_2_, f32[280,128]{1,0:T(8,128)S(1)} %get-tuple-element.53.refs_3_, ...), custom_call_target="tpu_custom_call" | custom-call | tf_op jit(solution)/shard_map/third/pallas_call | solution.py:917
  (7 shorter events, 0.1 us)
Async XLA Ops:
  1.7 5.8 %collective-permute-start = (f32[304,128]{1,0:T(8,128)S(1)}, f32[304,128]{1,0:T(8,128)S(1)}, u32[]{:S(2)}, u32[]{:S(2)}) collective-permute-start(f32[304,128]{1,0:T(8,128)S(1)} %get-tuple-element.32), channel_id=1, source_target_pairs={{0,8},{8,0},{16,24},{24,16},{1,9},{9,1},{17,25},{25,17},{2,10},{10... | collective-permute-start | bytes 466952 | tf_op jit(solution)/shard_map/ppermute | solution.py:792
  3.3 7.4 %collective-permute-start.1 = (f32[304,128]{1,0:T(8,128)S(1)}, f32[304,128]{1,0:T(8,128)S(1)}, u32[]{:S(2)}, u32[]{:S(2)}) collective-permute-start(f32[304,128]{1,0:T(8,128)S(1)} %get-tuple-element.33), channel_id=1, source_target_pairs={{8,16},{16,8},{9,17},{17,9},{10,18},{18,10},{11,19},{19,11},{12,20... | collective-permute-start | bytes 466952 | tf_op jit(solution)/shard_map/ppermute | solution.py:792
  5.2 10.4 %collective-permute-start.2 = (f32[7,32,128]{2,1,0:T(8,128)S(1)}, f32[7,32,128]{2,1,0:T(8,128)S(1)}, u32[]{:S(2)}, u32[]{:S(2)}) collective-permute-start(f32[7,32,128]{2,1,0:T(8,128)S(1)} %get-tuple-element.36), channel_id=1, source_target_pairs={{1,2},{2,1},{3,4},{4,3},{5,6},{6,5},{9,10},{10,9},{11,12},{12,11},... | collective-permute-start | bytes 344072 | tf_op jit(solution)/shard_map/ppermute | solution.py:792
  10.9 6.9 %collective-permute-start.6 = (f32[144,128]{1,0:T(8,128)S(1)}, f32[144,128]{1,0:T(8,128)S(1)}, u32[]{:S(2)}, u32[]{:S(2)}) collective-permute-start(f32[144,128]{1,0:T(8,128)S(1)} %get-tuple-element.45), channel_id=1, source_target_pairs={{1,2},{2,1},{3,4},{4,3},{5,6},{6,5},{9,10},{10,9},{11,12},{12,11},... | collective-permute-start | bytes 221192 | tf_op jit(solution)/shard_map/ppermute | solution.py:792
  12.2 4.7 %collective-permute-start.3 = (f32[3,40,128]{2,1,0:T(8,128)S(1)}, f32[3,40,128]{2,1,0:T(8,128)S(1)}, u32[]{:S(2)}, u32[]{:S(2)}) collective-permute-start(f32[3,40,128]{2,1,0:T(8,128)S(1)} %get-tuple-element.39), channel_id=1, source_target_pairs={{0,1},{1,0},{2,3},{3,2},{4,5},{5,4},{6,7},{7,6},{8,9},{9,8},{10,11... | collective-permute-start | bytes 184328 | tf_op jit(solution)/shard_map/ppermute | solution.py:792
  15.2 1.8 %collective-permute-start.4 = (f32[3,40,128]{2,1,0:T(8,128)S(1)}, f32[3,40,128]{2,1,0:T(8,128)S(1)}, u32[]{:S(2)}, u32[]{:S(2)}) collective-permute-start(f32[3,40,128]{2,1,0:T(8,128)S(1)} %get-tuple-element.40), channel_id=1, source_target_pairs={{0,1},{1,0},{2,3},{3,2},{4,5},{5,4},{6,7},{7,6},{8,9},{9,8},{10,11... | collective-permute-start | bytes 184328 | tf_op jit(solution)/shard_map/ppermute | solution.py:792
  15.2 1.7 %collective-permute-start.5 = (f32[3,40,128]{2,1,0:T(8,128)S(1)}, f32[3,40,128]{2,1,0:T(8,128)S(1)}, u32[]{:S(2)}, u32[]{:S(2)}) collective-permute-start(f32[3,40,128]{2,1,0:T(8,128)S(1)} %get-tuple-element.41), channel_id=1, source_target_pairs={{0,1},{1,0},{2,3},{3,2},{4,5},{5,4},{6,7},{7,6},{8,9},{9,8},{10,11... | collective-permute-start | bytes 184328 | tf_op jit(solution)/shard_map/ppermute | solution.py:792
  18.6 1.4 %collective-permute-start.7 = (f32[176,128]{1,0:T(8,128)S(1)}, f32[176,128]{1,0:T(8,128)S(1)}, u32[]{:S(2)}, u32[]{:S(2)}) collective-permute-start(f32[176,128]{1,0:T(8,128)S(1)} %get-tuple-element.52), channel_id=1, source_target_pairs={{1,0},{0,1},{3,2},{2,3},{5,4},{4,5},{7,6},{6,7},{9,8},{8,9},{11,10... | collective-permute-start | bytes 270344 | tf_op jit(solution)/shard_map/ppermute | solution.py:577
  20.0 6.6 %collective-permute-start.8 = (f32[144,128]{1,0:T(8,128)S(1)}, f32[144,128]{1,0:T(8,128)S(1)}, u32[]{:S(2)}, u32[]{:S(2)}) collective-permute-start(f32[144,128]{1,0:T(8,128)S(1)} %get-tuple-element.54), channel_id=1, source_target_pairs={{7,0},{2,1},{1,2},{4,3},{3,4},{6,5},{5,6},{0,7},{15,8},{10,9},{9,1... | collective-permute-start | bytes 221192 | tf_op jit(solution)/shard_map/ppermute | solution.py:577
  21.0 4.1 %collective-permute-start.9 = (f32[40,128]{1,0:T(8,128)S(1)}, f32[40,128]{1,0:T(8,128)S(1)}, u32[]{:S(2)}, u32[]{:S(2)}) collective-permute-start(f32[40,128]{1,0:T(8,128)S(1)} %get-tuple-element.55), channel_id=1, source_target_pairs={{3,0},{5,1},{6,2},{0,3},{7,4},{1,5},{2,6},{4,7},{11,8},{13,9},{14,... | collective-permute-start | bytes 61448 | tf_op jit(solution)/shard_map/ppermute | solution.py:577
  22.8 3.8 %collective-permute-start.10 = (f32[40,128]{1,0:T(8,128)S(1)}, f32[40,128]{1,0:T(8,128)S(1)}, u32[]{:S(2)}, u32[]{:S(2)}) collective-permute-start(f32[40,128]{1,0:T(8,128)S(1)} %get-tuple-element.56), channel_id=1, source_target_pairs={{4,0},{6,1},{5,2},{7,3},{0,4},{2,5},{1,6},{3,7},{12,8},{14,9},{13,... | collective-permute-start | bytes 61448 | tf_op jit(solution)/shard_map/ppermute | solution.py:577

commit v18 on v15

--- a/solution.py
+++ b/solution.py
@@ -234,6 +234,15 @@
             ref[at] = value
 
 
+def looped(first, last, size, work):
+    def group(k, carry):
+        grouped([first + size * k + r for r in range(size)], work)
+        return carry
+
+    lax.fori_loop(0, (last - first) // size, group, 0)
+    grouped(list(range(last - (last - first) % size, last)), work)
+
+
 def row_coefficients(st, i, mask):
     fx, fz, h, diag = faces(st[K, i])
     fy = 0.5 * (st[K, i] + st[K, i + 1])
@@ -383,11 +392,9 @@
     shape = (ext, nz)
     mask = x_mask(shape, nx)
     edge = edge_weights(shape)
-    grouped(list(range(3, ny - 1)), lambda i: row_sweep(st, i, SA, SB, edge))
-    grouped(list(range(3, ny - 1)), lambda i: row_sweep(st, i, SB, SA, edge))
-    for j in range(2, ny // 2 - 2):
-        for ref, at, value in coarse_row(st, coarse, j, mask, edge):
-            ref[at] = value
+    looped(3, ny - 1, 4, lambda i: row_sweep(st, i, SA, SB, edge))
+    looped(3, ny - 1, 4, lambda i: row_sweep(st, i, SB, SA, edge))
+    grouped(list(range(2, ny // 2 - 2)), lambda j: coarse_row(st, coarse, j, mask, edge))
 
 
 def end_work(st, coarse, extra, read, outer, is_after):

time: 28.7 us -> 28.7 us (level); the launches traced: 28.4 us -> 28.1 us
  Pallas kernels: 7.35 us -> 6.95 us
    pallas_call x1, Pallas kernels: 1.59 us -> 1.18 us  [shards(): pl.pallas_call(inner_kernel, out_shape=(state, rows), in_specs=[VMEM] * 2...]
  transfers between devices with their start and end apart: 11 -> 11, of which waited for: 5 -> 5; matrix products, arithmetic and copies ran while one was open for 0% -> 0% of each run, Pallas kernels for 10% -> 9%
where the time goes in v18:
time: 28.7 us; the launch traced here: 28.1 us
  starting transfers between devices  11.7 us (41%)
  waiting for transfers between devices  9.33 us (33%)
  Pallas kernels  6.95 us (24%)
    ppermute x7, starting transfers between devices, swap(): return lax.ppermute(x, axis, pairs)  8.31 us
    ppermute x7, waiting for transfers between devices, swap(): return lax.ppermute(x, axis, pairs)  4.74 us
    ppermute x4, waiting for transfers between devices, exchange_stage(): lax.ppermute(message, 'gy', [(sender, me) for me, sender in enumerate(sen...  4.6 us
    ppermute x4, starting transfers between devices, exchange_stage(): lax.ppermute(message, 'gy', [(sender, me) for me, sender in enumerate(sen...  3.41 us
    pallas_call x1, Pallas kernels, shards(): pl.pallas_call(functools.partial(third_kernel, radices[-1], stride), out_...  2.14 us
    pallas_call x1, Pallas kernels, shards(): pl.pallas_call(pack_kernel, out_shape=(strip, strip, f32((EARLY, nx, nz))...  1.63 us
    pallas_call x1, Pallas kernels, shards(): pl.pallas_call(inner_kernel, out_shape=(state, rows), in_specs=[VMEM] * 2...  1.18 us
    pallas_call x1, Pallas kernels, shards(): pl.pallas_call(second_kernel, out_shape=(state, rows, more, tall(lay.map)...  0.62 us
  transfers between devices with their start and end apart: 11, of which 5 were waited for; matrix products, arithmetic and copies ran while one was open for 0% of the time, Pallas kernels for 9%

profile of v18, /device:TPU:16, one launch (start us, length us, event | category | flops | bytes accessed | tf_op | source)
XLA Modules:
  0.0 28.1 jit_solution(16168000218952644277)
XLA Ops:
  0.0 1.6 %pack_x.1 = (f32[304,128]{1,0:T(8,128)S(1)}, f32[304,128]{1,0:T(8,128)S(1)}, f32[7,32,128]{2,1,0:T(8,128)S(1)}, f32[15,14,48,128]{3,2,1,0:T(8,128)S(1)}) custom-call(f32[2,12,32,128]{3,2,1,0:T(8,128)} %bitcast.5, f32[2,12,32,128]{3,2,1,0:T(8,128)} %bitcast.6, f32[12,32,128]{2,1,0:T(8,128)} %bitcast.7, f32[12,32,128]{2,1,0:T(8,128)} %bitcast.8), custom_call_target="tpu_custom_call" | custom-call | tf_op jit(solution)/shard_map/pack_x/pallas_call | solution.py:798
  1.6 1.6 %collective-permute-start = (f32[304,128]{1,0:T(8,128)S(1)}, f32[304,128]{1,0:T(8,128)S(1)}, u32[]{:S(2)}, u32[]{:S(2)}) collective-permute-start(f32[304,128]{1,0:T(8,128)S(1)} %get-tuple-element.32), channel_id=1, source_target_pairs={{0,8},{8,0},{16,24},{24,16},{1,9},{9,1},{17,25},{25,17},{2,10},{10... | collective-permute-start | bytes 466952 | tf_op jit(solution)/shard_map/ppermute | solution.py:783
  3.3 1.9 %collective-permute-start.1 = (f32[304,128]{1,0:T(8,128)S(1)}, f32[304,128]{1,0:T(8,128)S(1)}, u32[]{:S(2)}, u32[]{:S(2)}) collective-permute-start(f32[304,128]{1,0:T(8,128)S(1)} %get-tuple-element.33), channel_id=1, source_target_pairs={{8,16},{16,8},{9,17},{17,9},{10,18},{18,10},{11,19},{19,11},{12,20... | collective-permute-start | bytes 466952 | tf_op jit(solution)/shard_map/ppermute | solution.py:783
  5.2 0.7 %collective-permute-start.2 = (f32[7,32,128]{2,1,0:T(8,128)S(1)}, f32[7,32,128]{2,1,0:T(8,128)S(1)}, u32[]{:S(2)}, u32[]{:S(2)}) collective-permute-start(f32[7,32,128]{2,1,0:T(8,128)S(1)} %get-tuple-element.36), channel_id=1, source_target_pairs={{1,2},{2,1},{3,4},{4,3},{5,6},{6,5},{9,10},{10,9},{11,12},{12,11},... | collective-permute-start | bytes 344072 | tf_op jit(solution)/shard_map/ppermute | solution.py:783
  5.9 1.5 %collective-permute-done.one = f32[304,128]{1,0:T(8,128)S(1)} collective-permute-done((f32[304,128]{1,0:T(8,128)S(1)}, f32[304,128]{1,0:T(8,128)S(1)}, u32[]{:S(2)}, u32[]{:S(2)}) %collective-permute-start) | collective-permute-done | bytes 155680 | tf_op jit(solution)/shard_map/ppermute | solution.py:783
  7.5 3.2 %collective-permute-done.1.two = f32[304,128]{1,0:T(8,128)S(1)} collective-permute-done((f32[304,128]{1,0:T(8,128)S(1)}, f32[304,128]{1,0:T(8,128)S(1)}, u32[]{:S(2)}, u32[]{:S(2)}) %collective-permute-start.1) | collective-permute-done | bytes 155680 | tf_op jit(solution)/shard_map/ppermute | solution.py:783
  10.6 0.2 first.1
  10.8 0.7 %collective-permute-start.6 = (f32[144,128]{1,0:T(8,128)S(1)}, f32[144,128]{1,0:T(8,128)S(1)}, u32[]{:S(2)}, u32[]{:S(2)}) collective-permute-start(f32[144,128]{1,0:T(8,128)S(1)} %get-tuple-element.45), channel_id=1, source_target_pairs={{1,2},{2,1},{3,4},{4,3},{5,6},{6,5},{9,10},{10,9},{11,12},{12,11},... | collective-permute-start | bytes 221192 | tf_op jit(solution)/shard_map/ppermute | solution.py:783
  11.5 0.5 %other.1 = (f32[15,14,48,128]{3,2,1,0:T(8,128)S(1)}, f32[3,40,128]{2,1,0:T(8,128)S(1)}, f32[3,40,128]{2,1,0:T(8,128)S(1)}, f32[3,40,128]{2,1,0:T(8,128)S(1)}) custom-call(f32[15,14,48,128]{3,2,1,0:T(8,128)S(1)} %get-tuple-element.34.st_in, f32[304,128]{1,0:T(8,128)S(1)} %collective-permute-done.one, ...), custom_call_target="tpu_custom_call", output_to_operand_aliasing={{0}: (0, {})} | custom-call | tf_op jit(solution)/shard_map/other/pallas_call | solution.py:832
  12.0 2.9 %collective-permute-start.3 = (f32[3,40,128]{2,1,0:T(8,128)S(1)}, f32[3,40,128]{2,1,0:T(8,128)S(1)}, u32[]{:S(2)}, u32[]{:S(2)}) collective-permute-start(f32[3,40,128]{2,1,0:T(8,128)S(1)} %get-tuple-element.39), channel_id=1, source_target_pairs={{0,1},{1,0},{2,3},{3,2},{4,5},{5,4},{6,7},{7,6},{8,9},{9,8},{10,11... | collective-permute-start | bytes 184328 | tf_op jit(solution)/shard_map/ppermute | solution.py:783
  15.0 0.1 collective-permute-start.4
  15.0 0.4 %collective-permute-start.5 = (f32[3,40,128]{2,1,0:T(8,128)S(1)}, f32[3,40,128]{2,1,0:T(8,128)S(1)}, u32[]{:S(2)}, u32[]{:S(2)}) collective-permute-start(f32[3,40,128]{2,1,0:T(8,128)S(1)} %get-tuple-element.41), channel_id=1, source_target_pairs={{0,1},{1,0},{2,3},{3,2},{4,5},{5,4},{6,7},{7,6},{8,9},{9,8},{10,11... | collective-permute-start | bytes 184328 | tf_op jit(solution)/shard_map/ppermute | solution.py:783
  15.5 0.0 collective-permute-done.2.early
  15.5 1.2 %inner.1 = (f32[15,14,48,128]{3,2,1,0:T(8,128)S(1)}, f32[4,6,48,128]{3,2,1,0:T(8,128)S(1)}) custom-call(f32[15,14,48,128]{3,2,1,0:T(8,128)S(1)} %get-tuple-element.35.st_in, f32[7,32,128]{2,1,0:T(8,128)S(1)} %collective-permute-done.2.early), custom_call_target="tpu_custom_call", output_to_operand_aliasing={{0}: (0, {})} | custom-call | flops 14745600 | bytes 18874368 | tf_op jit(solution)/shard_map/inner/pallas_call | solution.py:844
  16.7 0.6 %near.1 = (f32[15,14,48,128]{3,2,1,0:T(8,128)S(1)}, f32[4,6,48,128]{3,2,1,0:T(8,128)S(1)}, f32[6,48,128]{2,1,0:T(8,128)S(1)}) custom-call(f32[15,14,48,128]{3,2,1,0:T(8,128)S(1)} %get-tuple-element.37.st_in, f32[4,6,48,128]{3,2,1,0:T(8,128)S(1)} %get-tuple-element.38.coarse_in, ...), custom_call_target="tpu_custom_call", output_to_operand_aliasing={{0}: (0, {}), {1}: (1, {})} | custom-call | tf_op jit(solution)/shard_map/near/pallas_call | solution.py:864
  17.3 0.6 %second.1 = (f32[15,14,48,128]{3,2,1,0:T(8,128)S(1)}, f32[4,6,48,128]{3,2,1,0:T(8,128)S(1)}, f32[6,48,128]{2,1,0:T(8,128)S(1)}, f32[40,128]{1,0:T(8,128)S(1)}, f...) custom-call(f32[15,14,48,128]{3,2,1,0:T(8,128)S(1)} %get-tuple-eleme, ...), custom_call_target="tpu_custom_call", output_to_operand_aliasing={{0}: (0, {}), {1}: (1, {}), {2}: (2, {})} | custom-call | tf_op jit(solution)/shard_map/second/pallas_call | solution.py:874
  17.9 0.1 collective-permute-start.7
  18.1 1.2 %collective-permute-done.7.refs_4_ = f32[176,128]{1,0:T(8,128)S(1)} collective-permute-done((f32[176,128]{1,0:T(8,128)S(1)}, f32[176,128]{1,0:T(8,128)S(1)}, u32[]{:S(2)}, u32[]{:S(2)}) %collective-permute-start.7) | collective-permute-done | bytes 90144 | tf_op jit(solution)/shard_map/ppermute | solution.py:568
  19.3 1.5 %collective-permute-start.8 = (f32[144,128]{1,0:T(8,128)S(1)}, f32[144,128]{1,0:T(8,128)S(1)}, u32[]{:S(2)}, u32[]{:S(2)}) collective-permute-start(f32[144,128]{1,0:T(8,128)S(1)} %get-tuple-element.54), channel_id=1, source_target_pairs={{7,0},{2,1},{1,2},{4,3},{3,4},{6,5},{5,6},{0,7},{15,8},{10,9},{9,1... | collective-permute-start | bytes 221192 | tf_op jit(solution)/shard_map/ppermute | solution.py:568
  20.8 1.4 %collective-permute-start.9 = (f32[40,128]{1,0:T(8,128)S(1)}, f32[40,128]{1,0:T(8,128)S(1)}, u32[]{:S(2)}, u32[]{:S(2)}) collective-permute-start(f32[40,128]{1,0:T(8,128)S(1)} %get-tuple-element.55), channel_id=1, source_target_pairs={{3,0},{5,1},{6,2},{0,3},{7,4},{1,5},{2,6},{4,7},{11,8},{13,9},{14,... | collective-permute-start | bytes 61448 | tf_op jit(solution)/shard_map/ppermute | solution.py:568
  22.2 0.4 %collective-permute-start.10 = (f32[40,128]{1,0:T(8,128)S(1)}, f32[40,128]{1,0:T(8,128)S(1)}, u32[]{:S(2)}, u32[]{:S(2)}) collective-permute-start(f32[40,128]{1,0:T(8,128)S(1)} %get-tuple-element.56), channel_id=1, source_target_pairs={{4,0},{6,1},{5,2},{7,3},{0,4},{2,5},{1,6},{3,7},{12,8},{14,9},{13,... | collective-permute-start | bytes 61448 | tf_op jit(solution)/shard_map/ppermute | solution.py:568
  22.6 1.9 %collective-permute-done.9.refs_5_ = f32[40,128]{1,0:T(8,128)S(1)} collective-permute-done((f32[40,128]{1,0:T(8,128)S(1)}, f32[40,128]{1,0:T(8,128)S(1)}, u32[]{:S(2)}, u32[]{:S(2)}) %collective-permute-start.9) | collective-permute-done | bytes 20512 | tf_op jit(solution)/shard_map/ppermute | solution.py:568
  24.5 1.5 %collective-permute-done.10.refs_6_ = f32[40,128]{1,0:T(8,128)S(1)} collective-permute-done((f32[40,128]{1,0:T(8,128)S(1)}, f32[40,128]{1,0:T(8,128)S(1)}, u32[]{:S(2)}, u32[]{:S(2)}) %collective-permute-start.10) | collective-permute-done | bytes 20512 | tf_op jit(solution)/shard_map/ppermute | solution.py:568
  26.0 2.1 %third.1 = f32[2,12,32,128]{3,2,1,0:T(8,128)} custom-call(f32[15,14,48,128]{3,2,1,0:T(8,128)S(1)} %get-tuple-element.46.refs_0_, f32[6,48,128]{2,1,0:T(8,128)S(1)} %get-tuple-element.47.refs_1_, f32[4,6,48,128]{3,2,1,0:T(8,128)S(1)} %get-tuple-element.48.refs_2_, f32[280,128]{1,0:T(8,128)S(1)} %get-tuple-element.53.refs_3_, ...), custom_call_target="tpu_custom_call" | custom-call | tf_op jit(solution)/shard_map/third/pallas_call | solution.py:908
  (7 shorter events, 0.1 us)
Async XLA Ops:
  1.6 5.8 %collective-permute-start = (f32[304,128]{1,0:T(8,128)S(1)}, f32[304,128]{1,0:T(8,128)S(1)}, u32[]{:S(2)}, u32[]{:S(2)}) collective-permute-start(f32[304,128]{1,0:T(8,128)S(1)} %get-tuple-element.32), channel_id=1, source_target_pairs={{0,8},{8,0},{16,24},{24,16},{1,9},{9,1},{17,25},{25,17},{2,10},{10... | collective-permute-start | bytes 466952 | tf_op jit(solution)/shard_map/ppermute | solution.py:783
  3.3 7.4 %collective-permute-start.1 = (f32[304,128]{1,0:T(8,128)S(1)}, f32[304,128]{1,0:T(8,128)S(1)}, u32[]{:S(2)}, u32[]{:S(2)}) collective-permute-start(f32[304,128]{1,0:T(8,128)S(1)} %get-tuple-element.33), channel_id=1, source_target_pairs={{8,16},{16,8},{9,17},{17,9},{10,18},{18,10},{11,19},{19,11},{12,20... | collective-permute-start | bytes 466952 | tf_op jit(solution)/shard_map/ppermute | solution.py:783
  5.2 10.3 %collective-permute-start.2 = (f32[7,32,128]{2,1,0:T(8,128)S(1)}, f32[7,32,128]{2,1,0:T(8,128)S(1)}, u32[]{:S(2)}, u32[]{:S(2)}) collective-permute-start(f32[7,32,128]{2,1,0:T(8,128)S(1)} %get-tuple-element.36), channel_id=1, source_target_pairs={{1,2},{2,1},{3,4},{4,3},{5,6},{6,5},{9,10},{10,9},{11,12},{12,11},... | collective-permute-start | bytes 344072 | tf_op jit(solution)/shard_map/ppermute | solution.py:783
  10.8 6.4 %collective-permute-start.6 = (f32[144,128]{1,0:T(8,128)S(1)}, f32[144,128]{1,0:T(8,128)S(1)}, u32[]{:S(2)}, u32[]{:S(2)}) collective-permute-start(f32[144,128]{1,0:T(8,128)S(1)} %get-tuple-element.45), channel_id=1, source_target_pairs={{1,2},{2,1},{3,4},{4,3},{5,6},{6,5},{9,10},{10,9},{11,12},{12,11},... | collective-permute-start | bytes 221192 | tf_op jit(solution)/shard_map/ppermute | solution.py:783
  12.0 4.6 %collective-permute-start.3 = (f32[3,40,128]{2,1,0:T(8,128)S(1)}, f32[3,40,128]{2,1,0:T(8,128)S(1)}, u32[]{:S(2)}, u32[]{:S(2)}) collective-permute-start(f32[3,40,128]{2,1,0:T(8,128)S(1)} %get-tuple-element.39), channel_id=1, source_target_pairs={{0,1},{1,0},{2,3},{3,2},{4,5},{5,4},{6,7},{7,6},{8,9},{9,8},{10,11... | collective-permute-start | bytes 184328 | tf_op jit(solution)/shard_map/ppermute | solution.py:783
  15.0 1.7 %collective-permute-start.4 = (f32[3,40,128]{2,1,0:T(8,128)S(1)}, f32[3,40,128]{2,1,0:T(8,128)S(1)}, u32[]{:S(2)}, u32[]{:S(2)}) collective-permute-start(f32[3,40,128]{2,1,0:T(8,128)S(1)} %get-tuple-element.40), channel_id=1, source_target_pairs={{0,1},{1,0},{2,3},{3,2},{4,5},{5,4},{6,7},{7,6},{8,9},{9,8},{10,11... | collective-permute-start | bytes 184328 | tf_op jit(solution)/shard_map/ppermute | solution.py:783
  15.0 1.6 %collective-permute-start.5 = (f32[3,40,128]{2,1,0:T(8,128)S(1)}, f32[3,40,128]{2,1,0:T(8,128)S(1)}, u32[]{:S(2)}, u32[]{:S(2)}) collective-permute-start(f32[3,40,128]{2,1,0:T(8,128)S(1)} %get-tuple-element.41), channel_id=1, source_target_pairs={{0,1},{1,0},{2,3},{3,2},{4,5},{5,4},{6,7},{7,6},{8,9},{9,8},{10,11... | collective-permute-start | bytes 184328 | tf_op jit(solution)/shard_map/ppermute | solution.py:783
  17.9 1.4 %collective-permute-start.7 = (f32[176,128]{1,0:T(8,128)S(1)}, f32[176,128]{1,0:T(8,128)S(1)}, u32[]{:S(2)}, u32[]{:S(2)}) collective-permute-start(f32[176,128]{1,0:T(8,128)S(1)} %get-tuple-element.52), channel_id=1, source_target_pairs={{1,0},{0,1},{3,2},{2,3},{5,4},{4,5},{7,6},{6,7},{9,8},{8,9},{11,10... | collective-permute-start | bytes 270344 | tf_op jit(solution)/shard_map/ppermute | solution.py:568
  19.3 6.7 %collective-permute-start.8 = (f32[144,128]{1,0:T(8,128)S(1)}, f32[144,128]{1,0:T(8,128)S(1)}, u32[]{:S(2)}, u32[]{:S(2)}) collective-permute-start(f32[144,128]{1,0:T(8,128)S(1)} %get-tuple-element.54), channel_id=1, source_target_pairs={{7,0},{2,1},{1,2},{4,3},{3,4},{6,5},{5,6},{0,7},{15,8},{10,9},{9,1... | collective-permute-start | bytes 221192 | tf_op jit(solution)/shard_map/ppermute | solution.py:568
  20.8 3.7 %collective-permute-start.9 = (f32[40,128]{1,0:T(8,128)S(1)}, f32[40,128]{1,0:T(8,128)S(1)}, u32[]{:S(2)}, u32[]{:S(2)}) collective-permute-start(f32[40,128]{1,0:T(8,128)S(1)} %get-tuple-element.55), channel_id=1, source_target_pairs={{3,0},{5,1},{6,2},{0,3},{7,4},{1,5},{2,6},{4,7},{11,8},{13,9},{14,... | collective-permute-start | bytes 61448 | tf_op jit(solution)/shard_map/ppermute | solution.py:568
  22.2 3.8 %collective-permute-start.10 = (f32[40,128]{1,0:T(8,128)S(1)}, f32[40,128]{1,0:T(8,128)S(1)}, u32[]{:S(2)}, u32[]{:S(2)}) collective-permute-start(f32[40,128]{1,0:T(8,128)S(1)} %get-tuple-element.56), channel_id=1, source_target_pairs={{4,0},{6,1},{5,2},{7,3},{0,4},{2,5},{1,6},{3,7},{12,8},{14,9},{13,... | collective-permute-start | bytes 61448 | tf_op jit(solution)/shard_map/ppermute | solution.py:568

commit v19 on v18

--- a/solution.py
+++ b/solution.py
@@ -527,22 +527,29 @@
 
 def matchings(count, radix, stride):
     if (count, radix, stride) == (8, 4, 2):
-        swaps = ((1, 2), (3, 4), (5, 6), (0, 7)), ((0, 3), (1, 5), (2, 6), (4, 7)), ((0, 4), (1, 6), (2, 5), (3, 7))
-        out = []
-        for pairs in swaps:
-            senders = [0] * count
-            for a, b in pairs:
-                senders[a], senders[b] = b, a
-            out.append((senders, len(out) == 0))
-        return out
+        return [
+            (((1, 2), (2, 1), (3, 4), (4, 3), (5, 6), (6, 5), (0, 7)), True),
+            (((0, 3), (1, 5), (2, 6), (4, 7)), False),
+            (((0, 4), (1, 6), (2, 5), (3, 7)), False),
+        ]
     out = []
     for k in range(1, radix):
-        senders = []
+        pairs = []
         for me in range(count):
             at, low = me // stride % radix, me % stride
-            senders.append(me - low + (source(at, k, radix) - at) * stride + (stride - 1 - low))
-        out.append((senders, any(abs(source(at, k, radix) - at) == 1 for at in range(radix))))
+            pairs.append((me - low + (source(at, k, radix) - at) * stride + (stride - 1 - low), me))
+        out.append((tuple(pairs), any(abs(source(at, k, radix) - at) == 1 for at in range(radix))))
     return sorted(out, key=lambda item: not item[1])
+
+
+def senders_of(pairs, count):
+    found = {receiver: sender for sender, receiver in pairs}
+    return [found.get(me, -1) for me in range(count)]
+
+
+def receivers_of(pairs, count):
+    found = dict(pairs)
+    return [found.get(me, -1) for me in range(count)]
 
 
 def look_up(table):
@@ -565,8 +572,7 @@
 
 def exchange_stage(messages, swaps):
     return [
-        lax.ppermute(message, "gy", [(sender, me) for me, sender in enumerate(senders)])
-        for (senders, near), message in zip(swaps, messages)
+        lax.ppermute(message, "gy", list(pairs)) for (pairs, near), message in zip(swaps, messages)
     ]
 
 
@@ -574,10 +580,11 @@
     def __init__(self, radix, stride, others, nx):
         self.radix, self.others, self.nx = radix, others, nx
         me = lax.axis_index("gy")
-        self.swaps = [
-            (look_up([sender // stride % radix for sender in senders]), near)
-            for senders, near in matchings(lax.axis_size("gy"), radix, stride)
-        ]
+        count = lax.axis_size("gy")
+        self.swaps = []
+        for pairs, near in matchings(count, radix, stride):
+            places = [radix + 1 if sender < 0 else sender // stride % radix for sender in senders_of(pairs, count)]
+            self.swaps.append((look_up(places), near))
         self.at = lax.rem(lax.div(me, stride), radix)
         low = lax.rem(me, stride)
         self.lowest, self.highest = low == 0, low == stride - 1
@@ -648,8 +655,8 @@
         write_rows(outs[0], whole)
         return
     me, count = lax.axis_index("gy"), lax.axis_size("gy")
-    for (senders, adjacent), out in zip(matchings(count, final, stride * radix), outs):
-        up = look_up(senders) > me
+    for (pairs, adjacent), out in zip(matchings(count, final, stride * radix), outs):
+        up = look_up(receivers_of(pairs, count)) > me
         if not adjacent:
             write_rows(out, whole)
             continue
@@ -665,11 +672,11 @@
             out[rows.map : rows.final] = first_info[: rows.info]
 
 
-def full_message(nx, total, last_info, first_info, senders):
+def full_message(nx, total, last_info, first_info, receivers):
     rows = Rows(nx)
     onward = jnp.concatenate([total[: rows.map], last_info[: rows.info], first_info[rows.info : rows.info + rows.rest]])
     back = jnp.concatenate([total[: rows.map], first_info[: rows.info + rows.rest]])
-    message = jnp.where(look_up(senders) > lax.axis_index("gy"), onward, back)
+    message = jnp.where(look_up(receivers) > lax.axis_index("gy"), onward, back)
     return jnp.pad(message, ((0, -rows.full % 8), (0, 0)))
 
 
@@ -888,7 +895,7 @@
     for place, radix in enumerate(radices[:-1]):
         swaps = matchings(count, radix, stride)
         if place:
-            messages = [full_message(nx, total, last_info, first_info, senders) for senders, _ in swaps]
+            messages = [full_message(nx, total, last_info, first_info, receivers_of(pairs, count)) for pairs, _ in swaps]
         others = exchange_stage(messages, swaps)
         final = radices[-1] if place == len(radices) - 2 else 0
         following = matchings(count, final, stride * radix) if final else []

time: 28.7 us -> 32.5 us (1.13)
  the two profiles are of different devices: /device:TPU:16 before, /device:TPU:13 now
where the time goes in v19:
time: 32.5 us; the launch traced here: 32.3 us
  starting transfers between devices  19.5 us (60%)
  Pallas kernels  6.96 us (21%)
  waiting for transfers between devices  5.65 us (17%)
    ppermute x7, starting transfers between devices, swap(): return lax.ppermute(x, axis, pairs)  13.1 us
    ppermute x4, starting transfers between devices, exchange_stage(): lax.ppermute(message, 'gy', list(pairs))  6.43 us
    ppermute x4, waiting for transfers between devices, exchange_stage(): lax.ppermute(message, 'gy', list(pairs))  5.64 us
    pallas_call x1, Pallas kernels, shards(): pl.pallas_call(functools.partial(third_kernel, radices[-1], stride), out_...  2.14 us
    pallas_call x1, Pallas kernels, shards(): pl.pallas_call(pack_kernel, out_shape=(strip, strip, f32((EARLY, nx, nz))...  1.63 us
    pallas_call x1, Pallas kernels, shards(): pl.pallas_call(inner_kernel, out_shape=(state, rows), in_specs=[VMEM] * 2...  1.18 us
  transfers between devices with their start and end apart: 11, of which 3 were waited for; matrix products, arithmetic and copies ran while one was open for 0% of the time, Pallas kernels for 8%

profile of v19, /device:TPU:13, one launch (start us, length us, event | category | flops | bytes accessed | tf_op | source)
XLA Modules:
  0.0 32.3 jit_solution(14698265325871438171)
XLA Ops:
  0.0 1.6 %pack_x.1 = (f32[304,128]{1,0:T(8,128)S(1)}, f32[304,128]{1,0:T(8,128)S(1)}, f32[7,32,128]{2,1,0:T(8,128)S(1)}, f32[15,14,48,128]{3,2,1,0:T(8,128)S(1)}) custom-call(f32[2,12,32,128]{3,2,1,0:T(8,128)} %bitcast.5, f32[2,12,32,128]{3,2,1,0:T(8,128)} %bitcast.6, f32[12,32,128]{2,1,0:T(8,128)} %bitcast.7, f32[12,32,128]{2,1,0:T(8,128)} %bitcast.8), custom_call_target="tpu_custom_call" | custom-call | tf_op jit(solution)/shard_map/pack_x/pallas_call | solution.py:805
  1.6 0.2 collective-permute-start
  1.9 4.3 %collective-permute-start.1 = (f32[304,128]{1,0:T(8,128)S(1)}, f32[304,128]{1,0:T(8,128)S(1)}, u32[]{:S(2)}, u32[]{:S(2)}) collective-permute-start(f32[304,128]{1,0:T(8,128)S(1)} %get-tuple-element.33), channel_id=1, source_target_pairs={{8,16},{16,8},{9,17},{17,9},{10,18},{18,10},{11,19},{19,11},{12,20... | collective-permute-start | bytes 466952 | tf_op jit(solution)/shard_map/ppermute | solution.py:790
  6.2 4.2 %collective-permute-start.2 = (f32[7,32,128]{2,1,0:T(8,128)S(1)}, f32[7,32,128]{2,1,0:T(8,128)S(1)}, u32[]{:S(2)}, u32[]{:S(2)}) collective-permute-start(f32[7,32,128]{2,1,0:T(8,128)S(1)} %get-tuple-element.36), channel_id=1, source_target_pairs={{1,2},{2,1},{3,4},{4,3},{5,6},{6,5},{9,10},{10,9},{11,12},{12,11},... | collective-permute-start | bytes 344072 | tf_op jit(solution)/shard_map/ppermute | solution.py:790
  10.5 0.0 collective-permute-done.1.two
  10.5 0.2 first.1
  10.7 3.6 %collective-permute-start.6 = (f32[144,128]{1,0:T(8,128)S(1)}, f32[144,128]{1,0:T(8,128)S(1)}, u32[]{:S(2)}, u32[]{:S(2)}) collective-permute-start(f32[144,128]{1,0:T(8,128)S(1)} %get-tuple-element.45), channel_id=1, source_target_pairs={{1,2},{2,1},{3,4},{4,3},{5,6},{6,5},{9,10},{10,9},{11,12},{12,11},... | collective-permute-start | bytes 221192 | tf_op jit(solution)/shard_map/ppermute | solution.py:790
  14.4 0.5 %other.1 = (f32[15,14,48,128]{3,2,1,0:T(8,128)S(1)}, f32[3,40,128]{2,1,0:T(8,128)S(1)}, f32[3,40,128]{2,1,0:T(8,128)S(1)}, f32[3,40,128]{2,1,0:T(8,128)S(1)}) custom-call(f32[15,14,48,128]{3,2,1,0:T(8,128)S(1)} %get-tuple-element.34.st_in, f32[304,128]{1,0:T(8,128)S(1)} %collective-permute-done.one, ...), custom_call_target="tpu_custom_call", output_to_operand_aliasing={{0}: (0, {})} | custom-call | tf_op jit(solution)/shard_map/other/pallas_call | solution.py:839
  14.9 0.1 collective-permute-start.3
  15.0 0.5 %collective-permute-start.4 = (f32[3,40,128]{2,1,0:T(8,128)S(1)}, f32[3,40,128]{2,1,0:T(8,128)S(1)}, u32[]{:S(2)}, u32[]{:S(2)}) collective-permute-start(f32[3,40,128]{2,1,0:T(8,128)S(1)} %get-tuple-element.40), channel_id=1, source_target_pairs={{0,1},{1,0},{2,3},{3,2},{4,5},{5,4},{6,7},{7,6},{8,9},{9,8},{10,11... | collective-permute-start | bytes 184328 | tf_op jit(solution)/shard_map/ppermute | solution.py:790
  15.5 0.1 collective-permute-start.5
  15.6 0.0 collective-permute-done.2.early
  15.6 1.2 %inner.1 = (f32[15,14,48,128]{3,2,1,0:T(8,128)S(1)}, f32[4,6,48,128]{3,2,1,0:T(8,128)S(1)}) custom-call(f32[15,14,48,128]{3,2,1,0:T(8,128)S(1)} %get-tuple-element.35.st_in, f32[7,32,128]{2,1,0:T(8,128)S(1)} %collective-permute-done.2.early), custom_call_target="tpu_custom_call", output_to_operand_aliasing={{0}: (0, {})} | custom-call | flops 14745600 | bytes 18874368 | tf_op jit(solution)/shard_map/inner/pallas_call | solution.py:851
  16.8 0.0 collective-permute-done.4.refs_1_
  16.8 0.6 %near.1 = (f32[15,14,48,128]{3,2,1,0:T(8,128)S(1)}, f32[4,6,48,128]{3,2,1,0:T(8,128)S(1)}, f32[6,48,128]{2,1,0:T(8,128)S(1)}) custom-call(f32[15,14,48,128]{3,2,1,0:T(8,128)S(1)} %get-tuple-element.37.st_in, f32[4,6,48,128]{3,2,1,0:T(8,128)S(1)} %get-tuple-element.38.coarse_in, ...), custom_call_target="tpu_custom_call", output_to_operand_aliasing={{0}: (0, {}), {1}: (1, {})} | custom-call | tf_op jit(solution)/shard_map/near/pallas_call | solution.py:871
  17.4 0.6 %second.1 = (f32[15,14,48,128]{3,2,1,0:T(8,128)S(1)}, f32[4,6,48,128]{3,2,1,0:T(8,128)S(1)}, f32[6,48,128]{2,1,0:T(8,128)S(1)}, f32[40,128]{1,0:T(8,128)S(1)}, f...) custom-call(f32[15,14,48,128]{3,2,1,0:T(8,128)S(1)} %get-tuple-eleme, ...), custom_call_target="tpu_custom_call", output_to_operand_aliasing={{0}: (0, {}), {1}: (1, {}), {2}: (2, {})} | custom-call | tf_op jit(solution)/shard_map/second/pallas_call | solution.py:881
  18.0 0.6 %collective-permute-start.7 = (f32[176,128]{1,0:T(8,128)S(1)}, f32[176,128]{1,0:T(8,128)S(1)}, u32[]{:S(2)}, u32[]{:S(2)}) collective-permute-start(f32[176,128]{1,0:T(8,128)S(1)} %get-tuple-element.52), channel_id=1, source_target_pairs={{1,0},{0,1},{3,2},{2,3},{5,4},{4,5},{7,6},{6,7},{9,8},{8,9},{11,10... | collective-permute-start | bytes 270344 | tf_op jit(solution)/shard_map/ppermute | solution.py:575
  18.6 0.9 %collective-permute-done.7.refs_4_ = f32[176,128]{1,0:T(8,128)S(1)} collective-permute-done((f32[176,128]{1,0:T(8,128)S(1)}, f32[176,128]{1,0:T(8,128)S(1)}, u32[]{:S(2)}, u32[]{:S(2)}) %collective-permute-start.7) | collective-permute-done | bytes 90144 | tf_op jit(solution)/shard_map/ppermute | solution.py:575
  19.6 3.2 %collective-permute-start.8 = (f32[144,128]{1,0:T(8,128)S(1)}, f32[144,128]{1,0:T(8,128)S(1)}, u32[]{:S(2)}, u32[]{:S(2)}) collective-permute-start(f32[144,128]{1,0:T(8,128)S(1)} %get-tuple-element.54), channel_id=1, source_target_pairs={{1,2},{2,1},{3,4},{4,3},{5,6},{6,5},{0,7},{9,10},{10,9},{11,12},{1... | collective-permute-start | bytes 221192 | tf_op jit(solution)/shard_map/ppermute | solution.py:575
  22.8 1.3 %collective-permute-start.9 = (f32[40,128]{1,0:T(8,128)S(1)}, f32[40,128]{1,0:T(8,128)S(1)}, u32[]{:S(2)}, u32[]{:S(2)}) collective-permute-start(f32[40,128]{1,0:T(8,128)S(1)} %get-tuple-element.55), channel_id=1, source_target_pairs={{0,3},{1,5},{2,6},{4,7},{8,11},{9,13},{10,14},{12,15},{16,19},{17,... | collective-permute-start | bytes 61448 | tf_op jit(solution)/shard_map/ppermute | solution.py:575
  24.1 1.3 %collective-permute-start.10 = (f32[40,128]{1,0:T(8,128)S(1)}, f32[40,128]{1,0:T(8,128)S(1)}, u32[]{:S(2)}, u32[]{:S(2)}) collective-permute-start(f32[40,128]{1,0:T(8,128)S(1)} %get-tuple-element.56), channel_id=1, source_target_pairs={{0,4},{1,6},{2,5},{3,7},{8,12},{9,14},{10,13},{11,15},{16,20},{17,... | collective-permute-start | bytes 61448 | tf_op jit(solution)/shard_map/ppermute | solution.py:575
  25.4 1.9 %collective-permute-done.9.refs_5_ = f32[40,128]{1,0:T(8,128)S(1)} collective-permute-done((f32[40,128]{1,0:T(8,128)S(1)}, f32[40,128]{1,0:T(8,128)S(1)}, u32[]{:S(2)}, u32[]{:S(2)}) %collective-permute-start.9) | collective-permute-done | bytes 20512 | tf_op jit(solution)/shard_map/ppermute | solution.py:575
  27.4 2.8 %collective-permute-done.10.refs_6_ = f32[40,128]{1,0:T(8,128)S(1)} collective-permute-done((f32[40,128]{1,0:T(8,128)S(1)}, f32[40,128]{1,0:T(8,128)S(1)}, u32[]{:S(2)}, u32[]{:S(2)}) %collective-permute-start.10) | collective-permute-done | bytes 20512 | tf_op jit(solution)/shard_map/ppermute | solution.py:575
  30.1 2.1 %third.1 = f32[2,12,32,128]{3,2,1,0:T(8,128)} custom-call(f32[15,14,48,128]{3,2,1,0:T(8,128)S(1)} %get-tuple-element.46.refs_0_, f32[6,48,128]{2,1,0:T(8,128)S(1)} %get-tuple-element.47.refs_1_, f32[4,6,48,128]{3,2,1,0:T(8,128)S(1)} %get-tuple-element.48.refs_2_, f32[280,128]{1,0:T(8,128)S(1)} %get-tuple-element.53.refs_3_, ...), custom_call_target="tpu_custom_call" | custom-call | tf_op jit(solution)/shard_map/third/pallas_call | solution.py:915
  (7 shorter events, 0.1 us)
Async XLA Ops:
  1.6 8.9 %collective-permute-start = (f32[304,128]{1,0:T(8,128)S(1)}, f32[304,128]{1,0:T(8,128)S(1)}, u32[]{:S(2)}, u32[]{:S(2)}) collective-permute-start(f32[304,128]{1,0:T(8,128)S(1)} %get-tuple-element.32), channel_id=1, source_target_pairs={{0,8},{8,0},{16,24},{24,16},{1,9},{9,1},{17,25},{25,17},{2,10},{10... | collective-permute-start | bytes 466952 | tf_op jit(solution)/shard_map/ppermute | solution.py:790
  1.9 8.6 %collective-permute-start.1 = (f32[304,128]{1,0:T(8,128)S(1)}, f32[304,128]{1,0:T(8,128)S(1)}, u32[]{:S(2)}, u32[]{:S(2)}) collective-permute-start(f32[304,128]{1,0:T(8,128)S(1)} %get-tuple-element.33), channel_id=1, source_target_pairs={{8,16},{16,8},{9,17},{17,9},{10,18},{18,10},{11,19},{19,11},{12,20... | collective-permute-start | bytes 466952 | tf_op jit(solution)/shard_map/ppermute | solution.py:790
  6.2 9.4 %collective-permute-start.2 = (f32[7,32,128]{2,1,0:T(8,128)S(1)}, f32[7,32,128]{2,1,0:T(8,128)S(1)}, u32[]{:S(2)}, u32[]{:S(2)}) collective-permute-start(f32[7,32,128]{2,1,0:T(8,128)S(1)} %get-tuple-element.36), channel_id=1, source_target_pairs={{1,2},{2,1},{3,4},{4,3},{5,6},{6,5},{9,10},{10,9},{11,12},{12,11},... | collective-permute-start | bytes 344072 | tf_op jit(solution)/shard_map/ppermute | solution.py:790
  10.7 6.6 %collective-permute-start.6 = (f32[144,128]{1,0:T(8,128)S(1)}, f32[144,128]{1,0:T(8,128)S(1)}, u32[]{:S(2)}, u32[]{:S(2)}) collective-permute-start(f32[144,128]{1,0:T(8,128)S(1)} %get-tuple-element.45), channel_id=1, source_target_pairs={{1,2},{2,1},{3,4},{4,3},{5,6},{6,5},{9,10},{10,9},{11,12},{12,11},... | collective-permute-start | bytes 221192 | tf_op jit(solution)/shard_map/ppermute | solution.py:790
  14.9 1.9 %collective-permute-start.3 = (f32[3,40,128]{2,1,0:T(8,128)S(1)}, f32[3,40,128]{2,1,0:T(8,128)S(1)}, u32[]{:S(2)}, u32[]{:S(2)}) collective-permute-start(f32[3,40,128]{2,1,0:T(8,128)S(1)} %get-tuple-element.39), channel_id=1, source_target_pairs={{0,1},{1,0},{2,3},{3,2},{4,5},{5,4},{6,7},{7,6},{8,9},{9,8},{10,11... | collective-permute-start | bytes 184328 | tf_op jit(solution)/shard_map/ppermute | solution.py:790
  15.0 1.8 %collective-permute-start.4 = (f32[3,40,128]{2,1,0:T(8,128)S(1)}, f32[3,40,128]{2,1,0:T(8,128)S(1)}, u32[]{:S(2)}, u32[]{:S(2)}) collective-permute-start(f32[3,40,128]{2,1,0:T(8,128)S(1)} %get-tuple-element.40), channel_id=1, source_target_pairs={{0,1},{1,0},{2,3},{3,2},{4,5},{5,4},{6,7},{7,6},{8,9},{9,8},{10,11... | collective-permute-start | bytes 184328 | tf_op jit(solution)/shard_map/ppermute | solution.py:790
  15.5 1.3 %collective-permute-start.5 = (f32[3,40,128]{2,1,0:T(8,128)S(1)}, f32[3,40,128]{2,1,0:T(8,128)S(1)}, u32[]{:S(2)}, u32[]{:S(2)}) collective-permute-start(f32[3,40,128]{2,1,0:T(8,128)S(1)} %get-tuple-element.41), channel_id=1, source_target_pairs={{0,1},{1,0},{2,3},{3,2},{4,5},{5,4},{6,7},{7,6},{8,9},{9,8},{10,11... | collective-permute-start | bytes 184328 | tf_op jit(solution)/shard_map/ppermute | solution.py:790
  18.0 1.5 %collective-permute-start.7 = (f32[176,128]{1,0:T(8,128)S(1)}, f32[176,128]{1,0:T(8,128)S(1)}, u32[]{:S(2)}, u32[]{:S(2)}) collective-permute-start(f32[176,128]{1,0:T(8,128)S(1)} %get-tuple-element.52), channel_id=1, source_target_pairs={{1,0},{0,1},{3,2},{2,3},{5,4},{4,5},{7,6},{6,7},{9,8},{8,9},{11,10... | collective-permute-start | bytes 270344 | tf_op jit(solution)/shard_map/ppermute | solution.py:575
  19.6 10.6 %collective-permute-start.8 = (f32[144,128]{1,0:T(8,128)S(1)}, f32[144,128]{1,0:T(8,128)S(1)}, u32[]{:S(2)}, u32[]{:S(2)}) collective-permute-start(f32[144,128]{1,0:T(8,128)S(1)} %get-tuple-element.54), channel_id=1, source_target_pairs={{1,2},{2,1},{3,4},{4,3},{5,6},{6,5},{0,7},{9,10},{10,9},{11,12},{1... | collective-permute-start | bytes 221192 | tf_op jit(solution)/shard_map/ppermute | solution.py:575
  22.8 4.5 %collective-permute-start.9 = (f32[40,128]{1,0:T(8,128)S(1)}, f32[40,128]{1,0:T(8,128)S(1)}, u32[]{:S(2)}, u32[]{:S(2)}) collective-permute-start(f32[40,128]{1,0:T(8,128)S(1)} %get-tuple-element.55), channel_id=1, source_target_pairs={{0,3},{1,5},{2,6},{4,7},{8,11},{9,13},{10,14},{12,15},{16,19},{17,... | collective-permute-start | bytes 61448 | tf_op jit(solution)/shard_map/ppermute | solution.py:575
  24.1 6.0 %collective-permute-start.10 = (f32[40,128]{1,0:T(8,128)S(1)}, f32[40,128]{1,0:T(8,128)S(1)}, u32[]{:S(2)}, u32[]{:S(2)}) collective-permute-start(f32[40,128]{1,0:T(8,128)S(1)} %get-tuple-element.56), channel_id=1, source_target_pairs={{0,4},{1,6},{2,5},{3,7},{8,12},{9,14},{10,13},{11,15},{16,20},{17,... | collective-permute-start | bytes 61448 | tf_op jit(solution)/shard_map/ppermute | solution.py:575

commit v20 on v18

--- a/solution.py
+++ b/solution.py
@@ -673,35 +673,51 @@
     return jnp.pad(message, ((0, -rows.full % 8), (0, 0)))
 
 
-def third_kernel(radix, stride, *refs):
-    st, extra, coarse, near_in = refs[:4]
-    others, (out, sc, wide, near, done, sems) = refs[4 : 3 + radix], refs[3 + radix :]
-    planes, rows, ext, nz = st.shape
-    ny, nx = rows - 2, ext - 2 * PAD
-    edge = edge_weights((ext, nz))
-    blocks = ny // 2
-
+def spread_x(ref, k, values, span):
+    ext, nz = ref.shape[1:]
+    ref[k, : PAD - 2] = jnp.zeros((PAD - 2, nz), jnp.float32)
+    ref[k, ext - PAD + 2 :] = jnp.zeros((PAD - 2, nz), jnp.float32)
+    ref[k, pl.ds(PAD - 2, span, 2), :] = values
+    ref[k, pl.ds(PAD - 1, span, 2), :] = values
+
+
+def widen_kernel(radix, stride, *refs):
+    near_in, others, (wide, near) = refs[0], refs[1:-2], refs[-2:]
+    ext, nz = wide.shape[1:]
+    nx = ext - 2 * PAD
     lay = Rows(nx)
     span = lay.span
     near[...] = near_in[...]
-    group = Group(radix, stride, others, nx)
-    if radix > 1:
+    if others:
+        following = iter(others)
+        group = Group(radix, stride, None, nx)
+        group.others = [next(following) if adjacent else None for _, adjacent in group.swaps]
         group.collect(near, True)
-    gas_in = group.ahead(near[:span], near[span : lay.map])[1]
     at_high = lay.high + lay.info
-    starts = [lay.low, lay.low + span, lay.high, lay.high + span, at_high, at_high + span]
-    for k, v in enumerate([gas_in] + [near[start : start + span] for start in starts]):
-        wide[k, : PAD - 2] = jnp.zeros((PAD - 2, nz), jnp.float32)
-        wide[k, ext - PAD + 2 :] = jnp.zeros((PAD - 2, nz), jnp.float32)
-        wide[k, pl.ds(PAD - 2, span, 2), :] = v
-        wide[k, pl.ds(PAD - 1, span, 2), :] = v
+    starts = (lay.low, lay.low + span, lay.high, lay.high + span, at_high, at_high + span)
+    for k, start in enumerate(starts, 1):
+        spread_x(wide, k, near[start : start + span], span)
     for k, start in enumerate((lay.low, lay.low + nx + 2, lay.high, lay.high + nx + 2)):
         start += lay.map
         wide[7 + k, :PAD] = jnp.zeros((PAD, nz), jnp.float32)
         wide[7 + k, ext - PAD :] = jnp.zeros((PAD, nz), jnp.float32)
         wide[7 + k, PAD - 1 : PAD + nx + 1] = near[start : start + nx + 2]
-
-    gas_in = wide[0]
+    wide[0] = jnp.zeros((ext, nz), jnp.float32)
+
+
+def third_kernel(radix, stride, *refs):
+    st, extra, coarse, near, wide = refs[:5]
+    others, (out, sc, entering, done, sems) = refs[5 : 4 + radix], refs[4 + radix :]
+    planes, rows, ext, nz = st.shape
+    ny, nx = rows - 2, ext - 2 * PAD
+    edge = edge_weights((ext, nz))
+    blocks = ny // 2
+
+    lay = Rows(nx)
+    span = lay.span
+    group = Group(radix, stride, others, nx)
+    spread_x(entering, 0, group.ahead(near[:span], near[span : lay.map])[1], span)
+    gas_in = entering[0]
     last = ny + 1
     solid_low = wide[1] + wide[2] * gas_in
     sc[0, 0] = st[SA, 0] + solid_low
@@ -905,21 +921,31 @@
         stride *= radix
     got = exchange_stage(messages, matchings(count, radices[-1], stride))
 
+    last = matchings(count, radices[-1], stride)
+    beside = [message for (_, adjacent), message in zip(last, got) if adjacent]
+    wide = pl.pallas_call(
+        functools.partial(widen_kernel, radices[-1], stride),
+        out_shape=f32((11, ext, nz)),
+        in_specs=[VMEM] * (1 + len(beside)),
+        out_specs=VMEM,
+        scratch_shapes=[pltpu.VMEM(near.shape, jnp.float32)],
+        compiler_params=PARAMS,
+        name="widen",
+    )(near, *beside)
     out = pl.pallas_call(
         functools.partial(third_kernel, radices[-1], stride),
         out_shape=f32((2, ny, nx, nz)),
-        in_specs=[VMEM] * (4 + len(got)),
+        in_specs=[VMEM] * (5 + len(got)),
         out_specs=HBM,
         scratch_shapes=[
             pltpu.VMEM((4, ny + 2, ext, nz), jnp.float32),
-            pltpu.VMEM((11, ext, nz), jnp.float32),
-            pltpu.VMEM(tall(lay.near).shape, jnp.float32),
+            pltpu.VMEM((1, ext, nz), jnp.float32),
             pltpu.VMEM((2, ny, nx, nz), jnp.float32),
             pltpu.SemaphoreType.DMA((ny // GROUP,)),
         ],
         compiler_params=PARAMS,
         name="third",
-    )(st, extra, coarse, near, *got)
+    )(st, extra, coarse, near, wide, *got)
     return jnp.transpose(out, (0, 2, 1, 3))
 
 

time: 28.7 us -> 28.8 us (level)
  Pallas kernels: 6.95 us -> 7.33 us
  transfers between devices with their start and end apart: 11 -> 11, of which waited for: 5 -> 5; matrix products, arithmetic and copies ran while one was open for 0% -> 0% of each run, Pallas kernels for 9% -> 10%
where the time goes in v20:
time: 28.8 us; the launch traced here: 28.4 us
  starting transfers between devices  11.7 us (41%)
  waiting for transfers between devices  9.16 us (32%)
  Pallas kernels  7.33 us (25%)
    ppermute x7, starting transfers between devices, swap(): return lax.ppermute(x, axis, pairs)  8.31 us
    ppermute x7, waiting for transfers between devices, swap(): return lax.ppermute(x, axis, pairs)  4.74 us
    ppermute x4, waiting for transfers between devices, exchange_stage(): lax.ppermute(message, 'gy', [(sender, me) for me, sender in enumerate(sen...  4.43 us
    ppermute x4, starting transfers between devices, exchange_stage(): lax.ppermute(message, 'gy', [(sender, me) for me, sender in enumerate(sen...  3.41 us
    pallas_call x1, Pallas kernels, shards(): pl.pallas_call(functools.partial(third_kernel, radices[-1], stride), out_...  2.23 us
    pallas_call x1, Pallas kernels, shards(): pl.pallas_call(pack_kernel, out_shape=(strip, strip, f32((EARLY, nx, nz))...  1.63 us
    pallas_call x1, Pallas kernels, shards(): pl.pallas_call(inner_kernel, out_shape=(state, rows), in_specs=[VMEM] * 2...  1.3 us
    pallas_call x1, Pallas kernels, shards(): pl.pallas_call(second_kernel, out_shape=(state, rows, more, tall(lay.map)...  0.67 us
  transfers between devices with their start and end apart: 11, of which 5 were waited for; matrix products, arithmetic and copies ran while one was open for 0% of the time, Pallas kernels for 10%

profile of v20, /device:TPU:16, one launch (start us, length us, event | category | flops | bytes accessed | tf_op | source)
XLA Modules:
  0.0 28.4 jit_solution(11363456613388308540)
XLA Ops:
  0.0 1.6 %pack_x.1 = (f32[304,128]{1,0:T(8,128)S(1)}, f32[304,128]{1,0:T(8,128)S(1)}, f32[7,32,128]{2,1,0:T(8,128)S(1)}, f32[15,14,48,128]{3,2,1,0:T(8,128)S(1)}) custom-call(f32[2,12,32,128]{3,2,1,0:T(8,128)} %bitcast.5, f32[2,12,32,128]{3,2,1,0:T(8,128)} %bitcast.6, f32[12,32,128]{2,1,0:T(8,128)} %bitcast.7, f32[12,32,128]{2,1,0:T(8,128)} %bitcast.8), custom_call_target="tpu_custom_call" | custom-call | tf_op jit(solution)/shard_map/pack_x/pallas_call | solution.py:814
  1.6 1.6 %collective-permute-start = (f32[304,128]{1,0:T(8,128)S(1)}, f32[304,128]{1,0:T(8,128)S(1)}, u32[]{:S(2)}, u32[]{:S(2)}) collective-permute-start(f32[304,128]{1,0:T(8,128)S(1)} %get-tuple-element.32), channel_id=1, source_target_pairs={{0,8},{8,0},{16,24},{24,16},{1,9},{9,1},{17,25},{25,17},{2,10},{10... | collective-permute-start | bytes 466952 | tf_op jit(solution)/shard_map/ppermute | solution.py:799
  3.3 1.9 %collective-permute-start.1 = (f32[304,128]{1,0:T(8,128)S(1)}, f32[304,128]{1,0:T(8,128)S(1)}, u32[]{:S(2)}, u32[]{:S(2)}) collective-permute-start(f32[304,128]{1,0:T(8,128)S(1)} %get-tuple-element.33), channel_id=1, source_target_pairs={{8,16},{16,8},{9,17},{17,9},{10,18},{18,10},{11,19},{19,11},{12,20... | collective-permute-start | bytes 466952 | tf_op jit(solution)/shard_map/ppermute | solution.py:799
  5.2 0.7 %collective-permute-start.2 = (f32[7,32,128]{2,1,0:T(8,128)S(1)}, f32[7,32,128]{2,1,0:T(8,128)S(1)}, u32[]{:S(2)}, u32[]{:S(2)}) collective-permute-start(f32[7,32,128]{2,1,0:T(8,128)S(1)} %get-tuple-element.36), channel_id=1, source_target_pairs={{1,2},{2,1},{3,4},{4,3},{5,6},{6,5},{9,10},{10,9},{11,12},{12,11},... | collective-permute-start | bytes 344072 | tf_op jit(solution)/shard_map/ppermute | solution.py:799
  5.9 1.5 %collective-permute-done.one = f32[304,128]{1,0:T(8,128)S(1)} collective-permute-done((f32[304,128]{1,0:T(8,128)S(1)}, f32[304,128]{1,0:T(8,128)S(1)}, u32[]{:S(2)}, u32[]{:S(2)}) %collective-permute-start) | collective-permute-done | bytes 155680 | tf_op jit(solution)/shard_map/ppermute | solution.py:799
  7.5 3.2 %collective-permute-done.1.two = f32[304,128]{1,0:T(8,128)S(1)} collective-permute-done((f32[304,128]{1,0:T(8,128)S(1)}, f32[304,128]{1,0:T(8,128)S(1)}, u32[]{:S(2)}, u32[]{:S(2)}) %collective-permute-start.1) | collective-permute-done | bytes 155680 | tf_op jit(solution)/shard_map/ppermute | solution.py:799
  10.6 0.2 first.1
  10.9 0.7 %collective-permute-start.6 = (f32[144,128]{1,0:T(8,128)S(1)}, f32[144,128]{1,0:T(8,128)S(1)}, u32[]{:S(2)}, u32[]{:S(2)}) collective-permute-start(f32[144,128]{1,0:T(8,128)S(1)} %get-tuple-element.45), channel_id=1, source_target_pairs={{1,2},{2,1},{3,4},{4,3},{5,6},{6,5},{9,10},{10,9},{11,12},{12,11},... | collective-permute-start | bytes 221192 | tf_op jit(solution)/shard_map/ppermute | solution.py:799
  11.5 0.5 %other.1 = (f32[15,14,48,128]{3,2,1,0:T(8,128)S(1)}, f32[3,40,128]{2,1,0:T(8,128)S(1)}, f32[3,40,128]{2,1,0:T(8,128)S(1)}, f32[3,40,128]{2,1,0:T(8,128)S(1)}) custom-call(f32[15,14,48,128]{3,2,1,0:T(8,128)S(1)} %get-tuple-element.34.st_in, f32[304,128]{1,0:T(8,128)S(1)} %collective-permute-done.one, ...), custom_call_target="tpu_custom_call", output_to_operand_aliasing={{0}: (0, {})} | custom-call | tf_op jit(solution)/shard_map/other/pallas_call | solution.py:848
  12.1 2.9 %collective-permute-start.3 = (f32[3,40,128]{2,1,0:T(8,128)S(1)}, f32[3,40,128]{2,1,0:T(8,128)S(1)}, u32[]{:S(2)}, u32[]{:S(2)}) collective-permute-start(f32[3,40,128]{2,1,0:T(8,128)S(1)} %get-tuple-element.39), channel_id=1, source_target_pairs={{0,1},{1,0},{2,3},{3,2},{4,5},{5,4},{6,7},{7,6},{8,9},{9,8},{10,11... | collective-permute-start | bytes 184328 | tf_op jit(solution)/shard_map/ppermute | solution.py:799
  15.0 0.1 collective-permute-start.4
  15.1 0.4 %collective-permute-start.5 = (f32[3,40,128]{2,1,0:T(8,128)S(1)}, f32[3,40,128]{2,1,0:T(8,128)S(1)}, u32[]{:S(2)}, u32[]{:S(2)}) collective-permute-start(f32[3,40,128]{2,1,0:T(8,128)S(1)} %get-tuple-element.41), channel_id=1, source_target_pairs={{0,1},{1,0},{2,3},{3,2},{4,5},{5,4},{6,7},{7,6},{8,9},{9,8},{10,11... | collective-permute-start | bytes 184328 | tf_op jit(solution)/shard_map/ppermute | solution.py:799
  15.5 1.3 %inner.1 = (f32[15,14,48,128]{3,2,1,0:T(8,128)S(1)}, f32[4,6,48,128]{3,2,1,0:T(8,128)S(1)}) custom-call(f32[15,14,48,128]{3,2,1,0:T(8,128)S(1)} %get-tuple-element.35.st_in, f32[7,32,128]{2,1,0:T(8,128)S(1)} %collective-permute-done.2.early), custom_call_target="tpu_custom_call", output_to_operand_aliasing={{0}: (0, {})} | custom-call | flops 14745600 | bytes 18874368 | tf_op jit(solution)/shard_map/inner/pallas_call | solution.py:860
  16.8 0.0 collective-permute-done.3.refs_0_
  16.8 0.6 %near.1 = (f32[15,14,48,128]{3,2,1,0:T(8,128)S(1)}, f32[4,6,48,128]{3,2,1,0:T(8,128)S(1)}, f32[6,48,128]{2,1,0:T(8,128)S(1)}) custom-call(f32[15,14,48,128]{3,2,1,0:T(8,128)S(1)} %get-tuple-element.37.st_in, f32[4,6,48,128]{3,2,1,0:T(8,128)S(1)} %get-tuple-element.38.coarse_in, ...), custom_call_target="tpu_custom_call", output_to_operand_aliasing={{0}: (0, {}), {1}: (1, {})} | custom-call | tf_op jit(solution)/shard_map/near/pallas_call | solution.py:880
  17.5 0.7 %second.1 = (f32[15,14,48,128]{3,2,1,0:T(8,128)S(1)}, f32[4,6,48,128]{3,2,1,0:T(8,128)S(1)}, f32[6,48,128]{2,1,0:T(8,128)S(1)}, f32[40,128]{1,0:T(8,128)S(1)}, f...) custom-call(f32[15,14,48,128]{3,2,1,0:T(8,128)S(1)} %get-tuple-eleme, ...), custom_call_target="tpu_custom_call", output_to_operand_aliasing={{0}: (0, {}), {1}: (1, {}), {2}: (2, {})} | custom-call | tf_op jit(solution)/shard_map/second/pallas_call | solution.py:890
  18.2 0.1 collective-permute-start.7
  18.3 1.2 %collective-permute-done.7.refs_4_ = f32[176,128]{1,0:T(8,128)S(1)} collective-permute-done((f32[176,128]{1,0:T(8,128)S(1)}, f32[176,128]{1,0:T(8,128)S(1)}, u32[]{:S(2)}, u32[]{:S(2)}) %collective-permute-start.7) | collective-permute-done | bytes 90144 | tf_op jit(solution)/shard_map/ppermute | solution.py:568
  19.6 1.3 %collective-permute-start.8 = (f32[144,128]{1,0:T(8,128)S(1)}, f32[144,128]{1,0:T(8,128)S(1)}, u32[]{:S(2)}, u32[]{:S(2)}) collective-permute-start(f32[144,128]{1,0:T(8,128)S(1)} %get-tuple-element.54), channel_id=1, source_target_pairs={{7,0},{2,1},{1,2},{4,3},{3,4},{6,5},{5,6},{0,7},{15,8},{10,9},{9,1... | collective-permute-start | bytes 221192 | tf_op jit(solution)/shard_map/ppermute | solution.py:568
  20.9 1.5 %collective-permute-start.9 = (f32[40,128]{1,0:T(8,128)S(1)}, f32[40,128]{1,0:T(8,128)S(1)}, u32[]{:S(2)}, u32[]{:S(2)}) collective-permute-start(f32[40,128]{1,0:T(8,128)S(1)} %get-tuple-element.55), channel_id=1, source_target_pairs={{3,0},{5,1},{6,2},{0,3},{7,4},{1,5},{2,6},{4,7},{11,8},{13,9},{14,... | collective-permute-start | bytes 61448 | tf_op jit(solution)/shard_map/ppermute | solution.py:568
  22.3 0.5 %collective-permute-start.10 = (f32[40,128]{1,0:T(8,128)S(1)}, f32[40,128]{1,0:T(8,128)S(1)}, u32[]{:S(2)}, u32[]{:S(2)}) collective-permute-start(f32[40,128]{1,0:T(8,128)S(1)} %get-tuple-element.56), channel_id=1, source_target_pairs={{4,0},{6,1},{5,2},{7,3},{0,4},{2,5},{1,6},{3,7},{12,8},{14,9},{13,... | collective-permute-start | bytes 61448 | tf_op jit(solution)/shard_map/ppermute | solution.py:568
  22.8 2.0 %collective-permute-done.8.refs_1_.refs_5_ = f32[144,128]{1,0:T(8,128)S(1)} collective-permute-done((f32[144,128]{1,0:T(8,128)S(1)}, f32[144,128]{1,0:T(8,128)S(1)}, u32[]{:S(2)}, u32[]{:S(2)}) %collective-permute-start.8) | collective-permute-done | bytes 73760 | tf_op jit(solution)/shard_map/ppermute | solution.py:568
  24.9 1.3 %collective-permute-done.10.refs_7_ = f32[40,128]{1,0:T(8,128)S(1)} collective-permute-done((f32[40,128]{1,0:T(8,128)S(1)}, f32[40,128]{1,0:T(8,128)S(1)}, u32[]{:S(2)}, u32[]{:S(2)}) %collective-permute-start.10) | collective-permute-done | bytes 20512 | tf_op jit(solution)/shard_map/ppermute | solution.py:568
  26.1 2.2 %third.1 = f32[2,12,32,128]{3,2,1,0:T(8,128)} custom-call(f32[15,14,48,128]{3,2,1,0:T(8,128)S(1)} %get-tuple-element.46.refs_0_, f32[6,48,128]{2,1,0:T(8,128)S(1)} %get-tuple-element.47.refs_1_, f32[4,6,48,128]{3,2,1,0:T(8,128)S(1)} %get-tuple-element.48.refs_2_, f32[280,128]{1,0:T(8,128)S(1)} %get-tuple-element.53.refs_0_.refs_3_, ...), custom_call_target="tpu_custom_call" | custom-call | tf_op jit(solution)/shard_map/third/pallas_call | solution.py:935
  (8 shorter events, 0.1 us)
Async XLA Ops:
  1.6 5.8 %collective-permute-start = (f32[304,128]{1,0:T(8,128)S(1)}, f32[304,128]{1,0:T(8,128)S(1)}, u32[]{:S(2)}, u32[]{:S(2)}) collective-permute-start(f32[304,128]{1,0:T(8,128)S(1)} %get-tuple-element.32), channel_id=1, source_target_pairs={{0,8},{8,0},{16,24},{24,16},{1,9},{9,1},{17,25},{25,17},{2,10},{10... | collective-permute-start | bytes 466952 | tf_op jit(solution)/shard_map/ppermute | solution.py:799
  3.3 7.4 %collective-permute-start.1 = (f32[304,128]{1,0:T(8,128)S(1)}, f32[304,128]{1,0:T(8,128)S(1)}, u32[]{:S(2)}, u32[]{:S(2)}) collective-permute-start(f32[304,128]{1,0:T(8,128)S(1)} %get-tuple-element.33), channel_id=1, source_target_pairs={{8,16},{16,8},{9,17},{17,9},{10,18},{18,10},{11,19},{19,11},{12,20... | collective-permute-start | bytes 466952 | tf_op jit(solution)/shard_map/ppermute | solution.py:799
  5.2 10.3 %collective-permute-start.2 = (f32[7,32,128]{2,1,0:T(8,128)S(1)}, f32[7,32,128]{2,1,0:T(8,128)S(1)}, u32[]{:S(2)}, u32[]{:S(2)}) collective-permute-start(f32[7,32,128]{2,1,0:T(8,128)S(1)} %get-tuple-element.36), channel_id=1, source_target_pairs={{1,2},{2,1},{3,4},{4,3},{5,6},{6,5},{9,10},{10,9},{11,12},{12,11},... | collective-permute-start | bytes 344072 | tf_op jit(solution)/shard_map/ppermute | solution.py:799
  10.9 6.6 %collective-permute-start.6 = (f32[144,128]{1,0:T(8,128)S(1)}, f32[144,128]{1,0:T(8,128)S(1)}, u32[]{:S(2)}, u32[]{:S(2)}) collective-permute-start(f32[144,128]{1,0:T(8,128)S(1)} %get-tuple-element.45), channel_id=1, source_target_pairs={{1,2},{2,1},{3,4},{4,3},{5,6},{6,5},{9,10},{10,9},{11,12},{12,11},... | collective-permute-start | bytes 221192 | tf_op jit(solution)/shard_map/ppermute | solution.py:799
  12.1 4.7 %collective-permute-start.3 = (f32[3,40,128]{2,1,0:T(8,128)S(1)}, f32[3,40,128]{2,1,0:T(8,128)S(1)}, u32[]{:S(2)}, u32[]{:S(2)}) collective-permute-start(f32[3,40,128]{2,1,0:T(8,128)S(1)} %get-tuple-element.39), channel_id=1, source_target_pairs={{0,1},{1,0},{2,3},{3,2},{4,5},{5,4},{6,7},{7,6},{8,9},{9,8},{10,11... | collective-permute-start | bytes 184328 | tf_op jit(solution)/shard_map/ppermute | solution.py:799
  15.0 1.8 %collective-permute-start.4 = (f32[3,40,128]{2,1,0:T(8,128)S(1)}, f32[3,40,128]{2,1,0:T(8,128)S(1)}, u32[]{:S(2)}, u32[]{:S(2)}) collective-permute-start(f32[3,40,128]{2,1,0:T(8,128)S(1)} %get-tuple-element.40), channel_id=1, source_target_pairs={{0,1},{1,0},{2,3},{3,2},{4,5},{5,4},{6,7},{7,6},{8,9},{9,8},{10,11... | collective-permute-start | bytes 184328 | tf_op jit(solution)/shard_map/ppermute | solution.py:799
  15.1 1.8 %collective-permute-start.5 = (f32[3,40,128]{2,1,0:T(8,128)S(1)}, f32[3,40,128]{2,1,0:T(8,128)S(1)}, u32[]{:S(2)}, u32[]{:S(2)}) collective-permute-start(f32[3,40,128]{2,1,0:T(8,128)S(1)} %get-tuple-element.41), channel_id=1, source_target_pairs={{0,1},{1,0},{2,3},{3,2},{4,5},{5,4},{6,7},{7,6},{8,9},{9,8},{10,11... | collective-permute-start | bytes 184328 | tf_op jit(solution)/shard_map/ppermute | solution.py:799
  18.2 1.4 %collective-permute-start.7 = (f32[176,128]{1,0:T(8,128)S(1)}, f32[176,128]{1,0:T(8,128)S(1)}, u32[]{:S(2)}, u32[]{:S(2)}) collective-permute-start(f32[176,128]{1,0:T(8,128)S(1)} %get-tuple-element.52), channel_id=1, source_target_pairs={{1,0},{0,1},{3,2},{2,3},{5,4},{4,5},{7,6},{6,7},{9,8},{8,9},{11,10... | collective-permute-start | bytes 270344 | tf_op jit(solution)/shard_map/ppermute | solution.py:568
  19.6 5.2 %collective-permute-start.8 = (f32[144,128]{1,0:T(8,128)S(1)}, f32[144,128]{1,0:T(8,128)S(1)}, u32[]{:S(2)}, u32[]{:S(2)}) collective-permute-start(f32[144,128]{1,0:T(8,128)S(1)} %get-tuple-element.54), channel_id=1, source_target_pairs={{7,0},{2,1},{1,2},{4,3},{3,4},{6,5},{5,6},{0,7},{15,8},{10,9},{9,1... | collective-permute-start | bytes 221192 | tf_op jit(solution)/shard_map/ppermute | solution.py:568
  20.9 4.0 %collective-permute-start.9 = (f32[40,128]{1,0:T(8,128)S(1)}, f32[40,128]{1,0:T(8,128)S(1)}, u32[]{:S(2)}, u32[]{:S(2)}) collective-permute-start(f32[40,128]{1,0:T(8,128)S(1)} %get-tuple-element.55), channel_id=1, source_target_pairs={{3,0},{5,1},{6,2},{0,3},{7,4},{1,5},{2,6},{4,7},{11,8},{13,9},{14,... | collective-permute-start | bytes 61448 | tf_op jit(solution)/shard_map/ppermute | solution.py:568
  22.3 3.8 %collective-permute-start.10 = (f32[40,128]{1,0:T(8,128)S(1)}, f32[40,128]{1,0:T(8,128)S(1)}, u32[]{:S(2)}, u32[]{:S(2)}) collective-permute-start(f32[40,128]{1,0:T(8,128)S(1)} %get-tuple-element.56), channel_id=1, source_target_pairs={{4,0},{6,1},{5,2},{7,3},{0,4},{2,5},{1,6},{3,7},{12,8},{14,9},{13,... | collective-permute-start | bytes 61448 | tf_op jit(solution)/shard_map/ppermute | solution.py:568

commit v21 on v18

--- a/solution.py
+++ b/solution.py
@@ -84,9 +84,8 @@
     return tiles, (k[4:5] if low else k[3:4])
 
 
-def pack_kernel(temps, right, exchange, coupling, one, two, early, st, sems):
+def pack_kernel(temps, right, exchange, coupling, one, two, st, sems):
     even = lax.axis_index("gx") % 2 == 0
-    odd = lax.axis_index("gy") % 2 == 1
     ny, nx, nz = exchange.shape
     copies = []
     for k, (plane, ref) in enumerate(
@@ -111,27 +110,28 @@
         part = slice(ny * STRIP_ROWS + i - 1, ny * STRIP_ROWS + i)
         one[part] = jnp.where(even, high_k, low_k)
         two[part] = jnp.where(even, low_k, high_k)
+
+
+def conduct_kernel(st_in, st, early):
+    del st_in
+    planes, rows, ext, nz = st.shape
+    ny, nx = rows - 2, ext - 2 * PAD
+    odd = lax.axis_index("gy") % 2 == 1
     own = slice(PAD, PAD + nx)
+    for i in range(1, ny + 1):
+        st[K, i, own] = conductivity_of(st[SA, i, own], st[K, i, own])
     for is_odd, e, d in ((True, ny, ny - 1), (False, 1, 2)):
 
         @pl.when(odd == is_odd)
         def _():
             s, s_d, g, g_d = st[SA, e, own], st[SA, d, own], st[GA, e, own], st[GA, d, own]
-            c, k, k_d = st[C, e, own], conductivity_of(s, st[K, e, own]), conductivity_of(s_d, st[K, d, own])
+            c, k, k_d = st[C, e, own], st[K, e, own], st[K, d, own]
             fx, fz, h, _ = faces(k)
             fy = 0.5 * (k + k_d)
             part_s, part_g = inner(s, g, c, h, fx, fz, edge_weights((nx, nz)))
             m_1s, m_1g = first_partial(st[RS, e, own] + part_s, st[RG, e, own] + part_g, s, s_d, g, g_d, fy, is_odd)
             for plane, value in enumerate((s, g, k, c, fy, m_1s, m_1g)):
                 early[plane] = value
-
-
-def conduct_kernel(st_in, st):
-    del st_in
-    planes, rows, ext, nz = st.shape
-    own = slice(PAD, ext - PAD)
-    for i in range(1, rows - 1):
-        st[K, i, own] = conductivity_of(st[SA, i, own], st[K, i, own])
 
 
 def place_halo(st, one, two, y, nx):
@@ -527,7 +527,7 @@
 
 def matchings(count, radix, stride):
     if (count, radix, stride) == (8, 4, 2):
-        swaps = ((1, 2), (3, 4), (5, 6), (0, 7)), ((0, 3), (1, 5), (2, 6), (4, 7)), ((0, 4), (1, 6), (2, 5), (3, 7))
+        swaps = ((1, 2), (3, 4), (5, 6), (0, 7)), ((0, 4), (1, 6), (2, 5), (3, 7)), ((0, 3), (1, 5), (2, 6), (4, 7))
         out = []
         for pairs in swaps:
             senders = [0] * count
@@ -795,31 +795,31 @@
 
     strip = f32((strip_height(ny), nz))
     state = f32((PLANES, ny + 2, ext, nz))
-    one, two, early, st = pl.pallas_call(
+    one, two, st = pl.pallas_call(
         pack_kernel,
-        out_shape=(strip, strip, f32((EARLY, nx, nz)), state),
+        out_shape=(strip, strip, state),
         in_specs=[HBM] * 4,
-        out_specs=(VMEM,) * 4,
+        out_specs=(VMEM,) * 3,
         scratch_shapes=[pltpu.SemaphoreType.DMA((6,))],
         compiler_params=PARAMS,
         name="pack_x",
     )(temps, right_side, exchange, coupling)
     one, two = swap(one, "gx", 0), swap(two, "gx", 1)
-    early = swap(early, "gy", 1)
 
     def letter(planes):
         return f32((planes, ext - 2 * CROP, nz))
 
-    st = pl.pallas_call(
+    st, early = pl.pallas_call(
         conduct_kernel,
-        out_shape=state,
+        out_shape=(state, f32((EARLY, nx, nz))),
         in_specs=[VMEM],
-        out_specs=VMEM,
+        out_specs=(VMEM,) * 2,
         input_output_aliases={0: 0},
         compiler_params=PARAMS,
         cost_estimate=cost(2 * ny, ext * nz),
         name="conduct",
     )(st)
+    early = swap(early, "gy", 1)
     st, across = pl.pallas_call(
         first_kernel,
         out_shape=(state, f32((across_parts(ext)[1], nz))),

time: 28.7 us -> 28 us (0.976)
  the two profiles are of different devices: /device:TPU:16 before, /device:TPU:8 now
where the time goes in v21:
time: 28 us; the launch traced here: 27.8 us
  starting transfers between devices  13.4 us (48%)
  waiting for transfers between devices  7.28 us (26%)
  Pallas kernels  6.94 us (25%)
    ppermute x7, starting transfers between devices, swap(): return lax.ppermute(x, axis, pairs)  9.87 us
    ppermute x4, waiting for transfers between devices, exchange_stage(): lax.ppermute(message, 'gy', [(sender, me) for me, sender in enumerate(sen...  4.42 us
    ppermute x4, starting transfers between devices, exchange_stage(): lax.ppermute(message, 'gy', [(sender, me) for me, sender in enumerate(sen...  3.56 us
    ppermute x7, waiting for transfers between devices, swap(): return lax.ppermute(x, axis, pairs)  2.86 us
    pallas_call x1, Pallas kernels, shards(): pl.pallas_call(functools.partial(third_kernel, radices[-1], stride), out_...  2.14 us
    pallas_call x1, Pallas kernels, shards(): pl.pallas_call(pack_kernel, out_shape=(strip, strip, state), in_specs=[HB...  1.47 us
    pallas_call x1, Pallas kernels, shards(): pl.pallas_call(inner_kernel, out_shape=(state, rows), in_specs=[VMEM] * 2...  1.18 us
    pallas_call x1, Pallas kernels, shards(): pl.pallas_call(second_kernel, out_shape=(state, rows, more, tall(lay.map)...  0.62 us
  transfers between devices with their start and end apart: 11, of which 4 were waited for; matrix products, arithmetic and copies ran while one was open for 0% of the time, Pallas kernels for 10%

profile of v21, /device:TPU:8, one launch (start us, length us, event | category | flops | bytes accessed | tf_op | source)
XLA Modules:
  0.0 27.8 jit_solution(15327331041005618043)
XLA Ops:
  0.0 1.5 %pack_x.1 = (f32[304,128]{1,0:T(8,128)S(1)}, f32[304,128]{1,0:T(8,128)S(1)}, f32[15,14,48,128]{3,2,1,0:T(8,128)S(1)}) custom-call(f32[2,12,32,128]{3,2,1,0:T(8,128)} %bitcast.5, f32[2,12,32,128]{3,2,1,0:T(8,128)} %bitcast.6, f32[12,32,128]{2,1,0:T(8,128)} %bitcast.7, f32[12,32,128]{2,1,0:T(8,128)} %bitcast.8), custom_call_target="tpu_custom_call" | custom-call | tf_op jit(solution)/shard_map/pack_x/pallas_call | solution.py:798
  1.5 0.1 collective-permute-start
  1.6 5.0 %collective-permute-start.1 = (f32[304,128]{1,0:T(8,128)S(1)}, f32[304,128]{1,0:T(8,128)S(1)}, u32[]{:S(2)}, u32[]{:S(2)}) collective-permute-start(f32[304,128]{1,0:T(8,128)S(1)} %get-tuple-element.35), channel_id=1, source_target_pairs={{8,16},{16,8},{9,17},{17,9},{10,18},{18,10},{11,19},{19,11},{12,20... | collective-permute-start | bytes 466952 | tf_op jit(solution)/shard_map/ppermute | solution.py:783
  6.6 0.2 conduct.1
  6.8 0.7 %collective-permute-start.2 = (f32[7,32,128]{2,1,0:T(8,128)S(1)}, f32[7,32,128]{2,1,0:T(8,128)S(1)}, u32[]{:S(2)}, u32[]{:S(2)}) collective-permute-start(f32[7,32,128]{2,1,0:T(8,128)S(1)} %get-tuple-element.38), channel_id=1, source_target_pairs={{1,2},{2,1},{3,4},{4,3},{5,6},{6,5},{9,10},{10,9},{11,12},{12,11},... | collective-permute-start | bytes 344072 | tf_op jit(solution)/shard_map/ppermute | solution.py:783
  7.5 0.0 collective-permute-done.one
  7.5 2.8 %collective-permute-done.1.two = f32[304,128]{1,0:T(8,128)S(1)} collective-permute-done((f32[304,128]{1,0:T(8,128)S(1)}, f32[304,128]{1,0:T(8,128)S(1)}, u32[]{:S(2)}, u32[]{:S(2)}) %collective-permute-start.1) | collective-permute-done | bytes 155680 | tf_op jit(solution)/shard_map/ppermute | solution.py:783
  10.3 0.2 first.1
  10.5 0.7 %collective-permute-start.6 = (f32[144,128]{1,0:T(8,128)S(1)}, f32[144,128]{1,0:T(8,128)S(1)}, u32[]{:S(2)}, u32[]{:S(2)}) collective-permute-start(f32[144,128]{1,0:T(8,128)S(1)} %get-tuple-element.47), channel_id=1, source_target_pairs={{1,2},{2,1},{3,4},{4,3},{5,6},{6,5},{9,10},{10,9},{11,12},{12,11},... | collective-permute-start | bytes 221192 | tf_op jit(solution)/shard_map/ppermute | solution.py:783
  11.2 0.5 %other.1 = (f32[15,14,48,128]{3,2,1,0:T(8,128)S(1)}, f32[3,40,128]{2,1,0:T(8,128)S(1)}, f32[3,40,128]{2,1,0:T(8,128)S(1)}, f32[3,40,128]{2,1,0:T(8,128)S(1)}) custom-call(f32[15,14,48,128]{3,2,1,0:T(8,128)S(1)} %get-tuple-element.36.st_in, f32[304,128]{1,0:T(8,128)S(1)} %collective-permute-done.one, ...), custom_call_target="tpu_custom_call", output_to_operand_aliasing={{0}: (0, {})} | custom-call | tf_op jit(solution)/shard_map/other/pallas_call | solution.py:832
  11.7 2.9 %collective-permute-start.3 = (f32[3,40,128]{2,1,0:T(8,128)S(1)}, f32[3,40,128]{2,1,0:T(8,128)S(1)}, u32[]{:S(2)}, u32[]{:S(2)}) collective-permute-start(f32[3,40,128]{2,1,0:T(8,128)S(1)} %get-tuple-element.41), channel_id=1, source_target_pairs={{0,1},{1,0},{2,3},{3,2},{4,5},{5,4},{6,7},{7,6},{8,9},{9,8},{10,11... | collective-permute-start | bytes 184328 | tf_op jit(solution)/shard_map/ppermute | solution.py:783
  14.7 0.1 collective-permute-start.4
  14.7 0.4 %collective-permute-start.5 = (f32[3,40,128]{2,1,0:T(8,128)S(1)}, f32[3,40,128]{2,1,0:T(8,128)S(1)}, u32[]{:S(2)}, u32[]{:S(2)}) collective-permute-start(f32[3,40,128]{2,1,0:T(8,128)S(1)} %get-tuple-element.43), channel_id=1, source_target_pairs={{0,1},{1,0},{2,3},{3,2},{4,5},{5,4},{6,7},{7,6},{8,9},{9,8},{10,11... | collective-permute-start | bytes 184328 | tf_op jit(solution)/shard_map/ppermute | solution.py:783
  15.2 1.2 %inner.1 = (f32[15,14,48,128]{3,2,1,0:T(8,128)S(1)}, f32[4,6,48,128]{3,2,1,0:T(8,128)S(1)}) custom-call(f32[15,14,48,128]{3,2,1,0:T(8,128)S(1)} %get-tuple-element.37.st_in, f32[7,32,128]{2,1,0:T(8,128)S(1)} %collective-permute-done.2.early), custom_call_target="tpu_custom_call", output_to_operand_aliasing={{0}: (0, {})} | custom-call | flops 14745600 | bytes 18874368 | tf_op jit(solution)/shard_map/inner/pallas_call | solution.py:844
  16.4 0.0 collective-permute-done.3.refs_0_
  16.4 0.6 %near.1 = (f32[15,14,48,128]{3,2,1,0:T(8,128)S(1)}, f32[4,6,48,128]{3,2,1,0:T(8,128)S(1)}, f32[6,48,128]{2,1,0:T(8,128)S(1)}) custom-call(f32[15,14,48,128]{3,2,1,0:T(8,128)S(1)} %get-tuple-element.39.st_in, f32[4,6,48,128]{3,2,1,0:T(8,128)S(1)} %get-tuple-element.40.coarse_in, ...), custom_call_target="tpu_custom_call", output_to_operand_aliasing={{0}: (0, {}), {1}: (1, {})} | custom-call | tf_op jit(solution)/shard_map/near/pallas_call | solution.py:864
  17.0 0.6 %second.1 = (f32[15,14,48,128]{3,2,1,0:T(8,128)S(1)}, f32[4,6,48,128]{3,2,1,0:T(8,128)S(1)}, f32[6,48,128]{2,1,0:T(8,128)S(1)}, f32[40,128]{1,0:T(8,128)S(1)}, f...) custom-call(f32[15,14,48,128]{3,2,1,0:T(8,128)S(1)} %get-tuple-eleme, ...), custom_call_target="tpu_custom_call", output_to_operand_aliasing={{0}: (0, {}), {1}: (1, {}), {2}: (2, {})} | custom-call | tf_op jit(solution)/shard_map/second/pallas_call | solution.py:874
  17.6 0.1 collective-permute-start.7
  17.8 1.2 %collective-permute-done.7.refs_4_ = f32[176,128]{1,0:T(8,128)S(1)} collective-permute-done((f32[176,128]{1,0:T(8,128)S(1)}, f32[176,128]{1,0:T(8,128)S(1)}, u32[]{:S(2)}, u32[]{:S(2)}) %collective-permute-start.7) | collective-permute-done | bytes 90144 | tf_op jit(solution)/shard_map/ppermute | solution.py:568
  19.0 2.1 %collective-permute-start.8 = (f32[144,128]{1,0:T(8,128)S(1)}, f32[144,128]{1,0:T(8,128)S(1)}, u32[]{:S(2)}, u32[]{:S(2)}) collective-permute-start(f32[144,128]{1,0:T(8,128)S(1)} %get-tuple-element.56), channel_id=1, source_target_pairs={{7,0},{2,1},{1,2},{4,3},{3,4},{6,5},{5,6},{0,7},{15,8},{10,9},{9,1... | collective-permute-start | bytes 221192 | tf_op jit(solution)/shard_map/ppermute | solution.py:568
  21.1 1.3 %collective-permute-start.9 = (f32[40,128]{1,0:T(8,128)S(1)}, f32[40,128]{1,0:T(8,128)S(1)}, u32[]{:S(2)}, u32[]{:S(2)}) collective-permute-start(f32[40,128]{1,0:T(8,128)S(1)} %get-tuple-element.57), channel_id=1, source_target_pairs={{4,0},{6,1},{5,2},{7,3},{0,4},{2,5},{1,6},{3,7},{12,8},{14,9},{13,... | collective-permute-start | bytes 61448 | tf_op jit(solution)/shard_map/ppermute | solution.py:568
  22.4 2.7 %collective-permute-done.9.refs_5_ = f32[40,128]{1,0:T(8,128)S(1)} collective-permute-done((f32[40,128]{1,0:T(8,128)S(1)}, f32[40,128]{1,0:T(8,128)S(1)}, u32[]{:S(2)}, u32[]{:S(2)}) %collective-permute-start.9) | collective-permute-done | bytes 20512 | tf_op jit(solution)/shard_map/ppermute | solution.py:568
  25.1 0.5 %collective-permute-done.10.refs_6_ = f32[40,128]{1,0:T(8,128)S(1)} collective-permute-done((f32[40,128]{1,0:T(8,128)S(1)}, f32[40,128]{1,0:T(8,128)S(1)}, u32[]{:S(2)}, u32[]{:S(2)}) %collective-permute-start.10) | collective-permute-done | bytes 20512 | tf_op jit(solution)/shard_map/ppermute | solution.py:568
  25.6 2.1 %third.1 = f32[2,12,32,128]{3,2,1,0:T(8,128)} custom-call(f32[15,14,48,128]{3,2,1,0:T(8,128)S(1)} %get-tuple-element.48.refs_0_, f32[6,48,128]{2,1,0:T(8,128)S(1)} %get-tuple-element.49.refs_1_, f32[4,6,48,128]{3,2,1,0:T(8,128)S(1)} %get-tuple-element.50.refs_2_, f32[280,128]{1,0:T(8,128)S(1)} %get-tuple-element.55.refs_3_, ...), custom_call_target="tpu_custom_call" | custom-call | tf_op jit(solution)/shard_map/third/pallas_call | solution.py:908
  (7 shorter events, 0.1 us)
Async XLA Ops:
  1.5 6.0 %collective-permute-start = (f32[304,128]{1,0:T(8,128)S(1)}, f32[304,128]{1,0:T(8,128)S(1)}, u32[]{:S(2)}, u32[]{:S(2)}) collective-permute-start(f32[304,128]{1,0:T(8,128)S(1)} %get-tuple-element.34), channel_id=1, source_target_pairs={{0,8},{8,0},{16,24},{24,16},{1,9},{9,1},{17,25},{25,17},{2,10},{10... | collective-permute-start | bytes 466952 | tf_op jit(solution)/shard_map/ppermute | solution.py:783
  1.6 8.8 %collective-permute-start.1 = (f32[304,128]{1,0:T(8,128)S(1)}, f32[304,128]{1,0:T(8,128)S(1)}, u32[]{:S(2)}, u32[]{:S(2)}) collective-permute-start(f32[304,128]{1,0:T(8,128)S(1)} %get-tuple-element.35), channel_id=1, source_target_pairs={{8,16},{16,8},{9,17},{17,9},{10,18},{18,10},{11,19},{19,11},{12,20... | collective-permute-start | bytes 466952 | tf_op jit(solution)/shard_map/ppermute | solution.py:783
  6.8 8.4 %collective-permute-start.2 = (f32[7,32,128]{2,1,0:T(8,128)S(1)}, f32[7,32,128]{2,1,0:T(8,128)S(1)}, u32[]{:S(2)}, u32[]{:S(2)}) collective-permute-start(f32[7,32,128]{2,1,0:T(8,128)S(1)} %get-tuple-element.38), channel_id=1, source_target_pairs={{1,2},{2,1},{3,4},{4,3},{5,6},{6,5},{9,10},{10,9},{11,12},{12,11},... | collective-permute-start | bytes 344072 | tf_op jit(solution)/shard_map/ppermute | solution.py:783
  10.5 6.4 %collective-permute-start.6 = (f32[144,128]{1,0:T(8,128)S(1)}, f32[144,128]{1,0:T(8,128)S(1)}, u32[]{:S(2)}, u32[]{:S(2)}) collective-permute-start(f32[144,128]{1,0:T(8,128)S(1)} %get-tuple-element.47), channel_id=1, source_target_pairs={{1,2},{2,1},{3,4},{4,3},{5,6},{6,5},{9,10},{10,9},{11,12},{12,11},... | collective-permute-start | bytes 221192 | tf_op jit(solution)/shard_map/ppermute | solution.py:783
  11.7 4.6 %collective-permute-start.3 = (f32[3,40,128]{2,1,0:T(8,128)S(1)}, f32[3,40,128]{2,1,0:T(8,128)S(1)}, u32[]{:S(2)}, u32[]{:S(2)}) collective-permute-start(f32[3,40,128]{2,1,0:T(8,128)S(1)} %get-tuple-element.41), channel_id=1, source_target_pairs={{0,1},{1,0},{2,3},{3,2},{4,5},{5,4},{6,7},{7,6},{8,9},{9,8},{10,11... | collective-permute-start | bytes 184328 | tf_op jit(solution)/shard_map/ppermute | solution.py:783
  14.7 1.7 %collective-permute-start.4 = (f32[3,40,128]{2,1,0:T(8,128)S(1)}, f32[3,40,128]{2,1,0:T(8,128)S(1)}, u32[]{:S(2)}, u32[]{:S(2)}) collective-permute-start(f32[3,40,128]{2,1,0:T(8,128)S(1)} %get-tuple-element.42), channel_id=1, source_target_pairs={{0,1},{1,0},{2,3},{3,2},{4,5},{5,4},{6,7},{7,6},{8,9},{9,8},{10,11... | collective-permute-start | bytes 184328 | tf_op jit(solution)/shard_map/ppermute | solution.py:783
  14.7 1.6 %collective-permute-start.5 = (f32[3,40,128]{2,1,0:T(8,128)S(1)}, f32[3,40,128]{2,1,0:T(8,128)S(1)}, u32[]{:S(2)}, u32[]{:S(2)}) collective-permute-start(f32[3,40,128]{2,1,0:T(8,128)S(1)} %get-tuple-element.43), channel_id=1, source_target_pairs={{0,1},{1,0},{2,3},{3,2},{4,5},{5,4},{6,7},{7,6},{8,9},{9,8},{10,11... | collective-permute-start | bytes 184328 | tf_op jit(solution)/shard_map/ppermute | solution.py:783
  17.6 1.4 %collective-permute-start.7 = (f32[176,128]{1,0:T(8,128)S(1)}, f32[176,128]{1,0:T(8,128)S(1)}, u32[]{:S(2)}, u32[]{:S(2)}) collective-permute-start(f32[176,128]{1,0:T(8,128)S(1)} %get-tuple-element.54), channel_id=1, source_target_pairs={{1,0},{0,1},{3,2},{2,3},{5,4},{4,5},{7,6},{6,7},{9,8},{8,9},{11,10... | collective-permute-start | bytes 270344 | tf_op jit(solution)/shard_map/ppermute | solution.py:568
  19.0 6.6 %collective-permute-start.8 = (f32[144,128]{1,0:T(8,128)S(1)}, f32[144,128]{1,0:T(8,128)S(1)}, u32[]{:S(2)}, u32[]{:S(2)}) collective-permute-start(f32[144,128]{1,0:T(8,128)S(1)} %get-tuple-element.56), channel_id=1, source_target_pairs={{7,0},{2,1},{1,2},{4,3},{3,4},{6,5},{5,6},{0,7},{15,8},{10,9},{9,1... | collective-permute-start | bytes 221192 | tf_op jit(solution)/shard_map/ppermute | solution.py:568
  21.1 4.0 %collective-permute-start.9 = (f32[40,128]{1,0:T(8,128)S(1)}, f32[40,128]{1,0:T(8,128)S(1)}, u32[]{:S(2)}, u32[]{:S(2)}) collective-permute-start(f32[40,128]{1,0:T(8,128)S(1)} %get-tuple-element.57), channel_id=1, source_target_pairs={{4,0},{6,1},{5,2},{7,3},{0,4},{2,5},{1,6},{3,7},{12,8},{14,9},{13,... | collective-permute-start | bytes 61448 | tf_op jit(solution)/shard_map/ppermute | solution.py:568
  22.4 3.2 %collective-permute-start.10 = (f32[40,128]{1,0:T(8,128)S(1)}, f32[40,128]{1,0:T(8,128)S(1)}, u32[]{:S(2)}, u32[]{:S(2)}) collective-permute-start(f32[40,128]{1,0:T(8,128)S(1)} %get-tuple-element.58), channel_id=1, source_target_pairs={{3,0},{5,1},{6,2},{0,3},{7,4},{1,5},{2,6},{4,7},{11,8},{13,9},{14,... | collective-permute-start | bytes 61448 | tf_op jit(solution)/shard_map/ppermute | solution.py:568

commit v22 on v21

--- a/solution.py
+++ b/solution.py
@@ -58,7 +58,7 @@
 
 
 def strip_height(ny):
-    return ny * STRIP_ROWS + (ny + 7) // 8 * 8
+    return ny * STRIP_ROWS + ny
 
 
 def sublanes(nz):
@@ -84,7 +84,7 @@
     return tiles, (k[4:5] if low else k[3:4])
 
 
-def pack_kernel(temps, right, exchange, coupling, one, two, st, sems):
+def pack_kernel(temps, right, exchange, coupling, one, two, late, st, sems):
     even = lax.axis_index("gx") % 2 == 0
     ny, nx, nz = exchange.shape
     copies = []
@@ -106,9 +106,11 @@
         for p in range(len(PAIRS)):
             part = slice((i - 1) * STRIP_ROWS + 8 * p, (i - 1) * STRIP_ROWS + 8 * p + 8)
             one[part] = jnp.where(even, high[p], low[p])
+            late[part] = jnp.where(even, high[p], low[p])
             two[part] = jnp.where(even, low[p], high[p])
         part = slice(ny * STRIP_ROWS + i - 1, ny * STRIP_ROWS + i)
         one[part] = jnp.where(even, high_k, low_k)
+        late[part] = jnp.where(even, high_k, low_k)
         two[part] = jnp.where(even, low_k, high_k)
 
 
@@ -134,13 +136,15 @@
                 early[plane] = value
 
 
-def place_halo(st, one, two, y, nx):
-    even = lax.axis_index("gx") % 2 == 0
+def place_halo(st, strips, y, nx):
+    one, two, late = strips
+    place = lax.axis_index("gx")
+    even, soon = place % 2 == 0, place % 4 < 2
     ny, row = st.shape[1] - 2, sublanes(st.shape[3])
     i = y + 1
 
     def received(part):
-        a, b = one[part], two[part]
+        a, b = jnp.where(soon, one[part], late[part]), two[part]
         return jnp.where(even, b, a), jnp.where(even, a, b)
 
     for p, (plane_a, plane_b) in enumerate(PAIRS):
@@ -308,14 +312,14 @@
     outer[k, CROP : outer.shape[1] - CROP] = refs[k // THIRD][k % THIRD]
 
 
-def first_end(st, one, two, after, write):
+def first_end(st, strips, after, write):
     planes, rows, ext, nz = st.shape
     ny, nx = rows - 2, ext - 2 * PAD
     mask = x_mask((ext, nz), nx)
     edge = edge_weights((ext, nz))
     e, d, f = (ny, ny - 1, ny - 2) if after else (1, 2, 3)
     for i in (e, d, f):
-        place_halo(st, one, two, i - 1, nx)
+        place_halo(st, strips, i - 1, nx)
     fx, fz, h, diag = faces(st[K, e])
     st[FX, e], st[FZ, e], st[H, e] = fx, fz, h
     st[FY, min(e, d)] = 0.5 * (st[K, e] + st[K, d])
@@ -326,27 +330,27 @@
         write(k, value)
 
 
-def either_first(st, one, two, after, write):
+def either_first(st, strips, after, write):
     for is_after in (True, False):
 
         @pl.when(after == is_after)
         def _():
-            first_end(st, one, two, is_after, write)
-
-
-def first_kernel(st_in, one, two, st, across):
+            first_end(st, strips, is_after, write)
+
+
+def first_kernel(st_in, one, two, late, st, across):
     del st_in
-    either_first(st, one, two, lax.axis_index("gy") % 2 == 1, functools.partial(write_across, across))
-
-
-def other_kernel(st_in, one, two, st, *beside):
+    either_first(st, (one, two, late), lax.axis_index("gy") % 2 == 1, functools.partial(write_across, across))
+
+
+def other_kernel(st_in, one, two, late, st, *beside):
     del st_in
-    either_first(st, one, two, lax.axis_index("gy") % 2 == 0, functools.partial(write_beside, beside))
+    either_first(st, (one, two, late), lax.axis_index("gy") % 2 == 0, functools.partial(write_beside, beside))
     planes, rows, ext, nz = st.shape
     ny, nx = rows - 2, ext - 2 * PAD
     mask = x_mask((ext, nz), nx)
     for y in range(3, ny - 3):
-        place_halo(st, one, two, y, nx)
+        place_halo(st, (one, two, late), y, nx)
     grouped(list(range(3, ny - 1)), lambda i: row_coefficients(st, i, mask))
 
 
@@ -715,7 +719,7 @@
             sc[1, i] = st[GA, i] + gas
         return carry
 
-    lax.fori_loop(0, blocks, correct, 0)
+    lax.fori_loop(0, blocks, correct, 0, unroll=3)
     gas = coarse[2, blocks - 1] * gas_in + coarse[3, blocks - 1]
     gas_high = wide[5] * gas + wide[4]
     solid_high = wide[3] + wide[6] * gas_high
@@ -776,9 +780,9 @@
     return pl.CostEstimate(flops=50 * rows * cells, bytes_accessed=16 * 4 * rows * cells, transcendentals=0)
 
 
-def swap(x, axis, first):
+def swap(x, axis, first, step=2):
     pairs = []
-    for i in range(first, lax.axis_size(axis) - 1, 2):
+    for i in range(first, lax.axis_size(axis) - 1, step):
         pairs += [(i, i + 1), (i + 1, i)]
     return lax.ppermute(x, axis, pairs)
 
@@ -793,18 +797,18 @@
     ext = nx + 2 * PAD
     f32 = functools.partial(jax.ShapeDtypeStruct, dtype=jnp.float32)
 
-    strip = f32((strip_height(ny), nz))
+    strips = tuple(f32((strip_height(ny) + more, nz)) for more in (2, 1, 0))
     state = f32((PLANES, ny + 2, ext, nz))
-    one, two, st = pl.pallas_call(
+    one, two, late, st = pl.pallas_call(
         pack_kernel,
-        out_shape=(strip, strip, state),
+        out_shape=strips + (state,),
         in_specs=[HBM] * 4,
-        out_specs=(VMEM,) * 3,
+        out_specs=(VMEM,) * 4,
         scratch_shapes=[pltpu.SemaphoreType.DMA((6,))],
         compiler_params=PARAMS,
         name="pack_x",
     )(temps, right_side, exchange, coupling)
-    one, two = swap(one, "gx", 0), swap(two, "gx", 1)
+    one, two, late = swap(one, "gx", 0, 4), swap(two, "gx", 1), swap(late, "gx", 2, 4)
 
     def letter(planes):
         return f32((planes, ext - 2 * CROP, nz))
@@ -823,21 +827,21 @@
     st, across = pl.pallas_call(
         first_kernel,
         out_shape=(state, f32((across_parts(ext)[1], nz))),
-        in_specs=[VMEM] * 3,
+        in_specs=[VMEM] * 4,
         out_specs=(VMEM,) * 2,
         input_output_aliases={0: 0},
         compiler_params=PARAMS,
         name="first",
-    )(st, one, two)
+    )(st, one, two, late)
     st, *beside = pl.pallas_call(
         other_kernel,
         out_shape=(state,) + (letter(THIRD),) * (MESSAGE // THIRD),
-        in_specs=[VMEM] * 3,
+        in_specs=[VMEM] * 4,
         out_specs=(VMEM,) * (1 + MESSAGE // THIRD),
         input_output_aliases={0: 0},
         compiler_params=PARAMS,
         name="other",
-    )(st, one, two)
+    )(st, one, two, late)
     across = swap(across, "gy", 1)
 
     rows = f32((4, ny // 2, ext, nz))

time: 28 us -> 30.5 us (1.089)
  the two profiles are of different devices: /device:TPU:8 before, /device:TPU:16 now
where the time goes in v22:
time: 30.5 us; the launch traced here: 30.2 us
  starting transfers between devices  14.3 us (47%)
  waiting for transfers between devices  8.8 us (29%)
  Pallas kernels  6.95 us (23%)
    ppermute x8, starting transfers between devices, swap(): return lax.ppermute(x, axis, pairs)  11.1 us
    ppermute x8, waiting for transfers between devices, swap(): return lax.ppermute(x, axis, pairs)  4.6 us
    ppermute x4, waiting for transfers between devices, exchange_stage(): lax.ppermute(message, 'gy', [(sender, me) for me, sender in enumerate(sen...  4.2 us
    ppermute x4, starting transfers between devices, exchange_stage(): lax.ppermute(message, 'gy', [(sender, me) for me, sender in enumerate(sen...  3.14 us
    pallas_call x1, Pallas kernels, shards(): pl.pallas_call(functools.partial(third_kernel, radices[-1], stride), out_...  2.13 us
    pallas_call x1, Pallas kernels, shards(): pl.pallas_call(pack_kernel, out_shape=strips + (state,), in_specs=[HBM] *...  1.47 us
    pallas_call x1, Pallas kernels, shards(): pl.pallas_call(inner_kernel, out_shape=(state, rows), in_specs=[VMEM] * 2...  1.18 us
    pallas_call x1, Pallas kernels, shards(): pl.pallas_call(second_kernel, out_shape=(state, rows, more, tall(lay.map)...  0.62 us
  transfers between devices with their start and end apart: 12, of which 4 were waited for; matrix products, arithmetic and copies ran while one was open for 0% of the time, Pallas kernels for 9%

profile of v22, /device:TPU:16, one launch (start us, length us, event | category | flops | bytes accessed | tf_op | source)
XLA Modules:
  0.0 30.2 jit_solution(4224977842055271401)
XLA Ops:
  0.0 1.5 %pack_x.1 = (f32[302,128]{1,0:T(8,128)S(1)}, f32[301,128]{1,0:T(8,128)S(1)}, f32[300,128]{1,0:T(8,128)S(1)}, f32[15,14,48,128]{3,2,1,0:T(8,128)S(1)}) custom-call(f32[2,12,32,128]{3,2,1,0:T(8,128)} %bitcast.5, f32[2,12,32,128]{3,2,1,0:T(8,128)} %bitcast.6, f32[12,32,128]{2,1,0:T(8,128)} %bitcast.7, f32[12,32,128]{2,1,0:T(8,128)} %bitcast.8), custom_call_target="tpu_custom_call" | custom-call | tf_op jit(solution)/shard_map/pack_x/pallas_call | solution.py:802
  1.5 0.7 %collective-permute-start = (f32[302,128]{1,0:T(8,128)S(1)}, f32[302,128]{1,0:T(8,128)S(1)}, u32[]{:S(2)}, u32[]{:S(2)}) collective-permute-start(f32[302,128]{1,0:T(8,128)S(1)} %get-tuple-element.35), channel_id=1, source_target_pairs={{0,8},{8,0},{1,9},{9,1},{2,10},{10,2},{3,11},{11,3},{4,12},{12,4},... | collective-permute-start | bytes 463880 | tf_op jit(solution)/shard_map/ppermute | solution.py:787
  2.2 3.6 %collective-permute-start.1 = (f32[301,128]{1,0:T(8,128)S(1)}, f32[301,128]{1,0:T(8,128)S(1)}, u32[]{:S(2)}, u32[]{:S(2)}) collective-permute-start(f32[301,128]{1,0:T(8,128)S(1)} %get-tuple-element.36), channel_id=1, source_target_pairs={{8,16},{16,8},{9,17},{17,9},{10,18},{18,10},{11,19},{19,11},{12,20... | collective-permute-start | bytes 462344 | tf_op jit(solution)/shard_map/ppermute | solution.py:787
  5.8 1.9 %collective-permute-start.2 = (f32[300,128]{1,0:T(8,128)S(1)}, f32[300,128]{1,0:T(8,128)S(1)}, u32[]{:S(2)}, u32[]{:S(2)}) collective-permute-start(f32[300,128]{1,0:T(8,128)S(1)} %get-tuple-element.37), channel_id=1, source_target_pairs={{16,24},{24,16},{17,25},{25,17},{18,26},{26,18},{19,27},{27,19},{2... | collective-permute-start | bytes 460808 | tf_op jit(solution)/shard_map/ppermute | solution.py:787
  7.7 0.2 conduct.1
  7.9 0.7 %collective-permute-start.3 = (f32[7,32,128]{2,1,0:T(8,128)S(1)}, f32[7,32,128]{2,1,0:T(8,128)S(1)}, u32[]{:S(2)}, u32[]{:S(2)}) collective-permute-start(f32[7,32,128]{2,1,0:T(8,128)S(1)} %get-tuple-element.40), channel_id=1, source_target_pairs={{1,2},{2,1},{3,4},{4,3},{5,6},{6,5},{9,10},{10,9},{11,12},{12,11},... | collective-permute-start | bytes 344072 | tf_op jit(solution)/shard_map/ppermute | solution.py:787
  8.6 4.6 %collective-permute-done.2.late = f32[300,128]{1,0:T(8,128)S(1)} collective-permute-done((f32[300,128]{1,0:T(8,128)S(1)}, f32[300,128]{1,0:T(8,128)S(1)}, u32[]{:S(2)}, u32[]{:S(2)}) %collective-permute-start.2) | collective-permute-done | bytes 153632 | tf_op jit(solution)/shard_map/ppermute | solution.py:787
  13.2 0.2 first.1
  13.4 0.7 %collective-permute-start.7 = (f32[144,128]{1,0:T(8,128)S(1)}, f32[144,128]{1,0:T(8,128)S(1)}, u32[]{:S(2)}, u32[]{:S(2)}) collective-permute-start(f32[144,128]{1,0:T(8,128)S(1)} %get-tuple-element.49), channel_id=1, source_target_pairs={{1,2},{2,1},{3,4},{4,3},{5,6},{6,5},{9,10},{10,9},{11,12},{12,11},... | collective-permute-start | bytes 221192 | tf_op jit(solution)/shard_map/ppermute | solution.py:787
  14.0 0.5 %other.1 = (f32[15,14,48,128]{3,2,1,0:T(8,128)S(1)}, f32[3,40,128]{2,1,0:T(8,128)S(1)}, f32[3,40,128]{2,1,0:T(8,128)S(1)}, f32[3,40,128]{2,1,0:T(8,128)S(1)}) custom-call(f32[15,14,48,128]{3,2,1,0:T(8,128)S(1)} %get-tuple-element.38.st_in, f32[302,128]{1,0:T(8,128)S(1)} %collective-permute-done.one, ...), custom_call_target="tpu_custom_call", output_to_operand_aliasing={{0}: (0, {})} | custom-call | tf_op jit(solution)/shard_map/other/pallas_call | solution.py:836
  14.6 3.1 %collective-permute-start.4 = (f32[3,40,128]{2,1,0:T(8,128)S(1)}, f32[3,40,128]{2,1,0:T(8,128)S(1)}, u32[]{:S(2)}, u32[]{:S(2)}) collective-permute-start(f32[3,40,128]{2,1,0:T(8,128)S(1)} %get-tuple-element.43), channel_id=1, source_target_pairs={{0,1},{1,0},{2,3},{3,2},{4,5},{5,4},{6,7},{7,6},{8,9},{9,8},{10,11... | collective-permute-start | bytes 184328 | tf_op jit(solution)/shard_map/ppermute | solution.py:787
  17.7 0.1 collective-permute-start.5
  17.8 0.4 %collective-permute-start.6 = (f32[3,40,128]{2,1,0:T(8,128)S(1)}, f32[3,40,128]{2,1,0:T(8,128)S(1)}, u32[]{:S(2)}, u32[]{:S(2)}) collective-permute-start(f32[3,40,128]{2,1,0:T(8,128)S(1)} %get-tuple-element.45), channel_id=1, source_target_pairs={{0,1},{1,0},{2,3},{3,2},{4,5},{5,4},{6,7},{7,6},{8,9},{9,8},{10,11... | collective-permute-start | bytes 184328 | tf_op jit(solution)/shard_map/ppermute | solution.py:787
  18.2 1.2 %inner.1 = (f32[15,14,48,128]{3,2,1,0:T(8,128)S(1)}, f32[4,6,48,128]{3,2,1,0:T(8,128)S(1)}) custom-call(f32[15,14,48,128]{3,2,1,0:T(8,128)S(1)} %get-tuple-element.39.st_in, f32[7,32,128]{2,1,0:T(8,128)S(1)} %collective-permute-done.3.early), custom_call_target="tpu_custom_call", output_to_operand_aliasing={{0}: (0, {})} | custom-call | flops 14745600 | bytes 18874368 | tf_op jit(solution)/shard_map/inner/pallas_call | solution.py:848
  19.4 0.6 %near.1 = (f32[15,14,48,128]{3,2,1,0:T(8,128)S(1)}, f32[4,6,48,128]{3,2,1,0:T(8,128)S(1)}, f32[6,48,128]{2,1,0:T(8,128)S(1)}) custom-call(f32[15,14,48,128]{3,2,1,0:T(8,128)S(1)} %get-tuple-element.41.st_in, f32[4,6,48,128]{3,2,1,0:T(8,128)S(1)} %get-tuple-element.42.coarse_in, ...), custom_call_target="tpu_custom_call", output_to_operand_aliasing={{0}: (0, {}), {1}: (1, {})} | custom-call | tf_op jit(solution)/shard_map/near/pallas_call | solution.py:868
  20.0 0.6 %second.1 = (f32[15,14,48,128]{3,2,1,0:T(8,128)S(1)}, f32[4,6,48,128]{3,2,1,0:T(8,128)S(1)}, f32[6,48,128]{2,1,0:T(8,128)S(1)}, f32[40,128]{1,0:T(8,128)S(1)}, f...) custom-call(f32[15,14,48,128]{3,2,1,0:T(8,128)S(1)} %get-tuple-eleme, ...), custom_call_target="tpu_custom_call", output_to_operand_aliasing={{0}: (0, {}), {1}: (1, {}), {2}: (2, {})} | custom-call | tf_op jit(solution)/shard_map/second/pallas_call | solution.py:878
  20.6 0.1 collective-permute-start.8
  20.8 1.2 %collective-permute-done.8.refs_4_ = f32[176,128]{1,0:T(8,128)S(1)} collective-permute-done((f32[176,128]{1,0:T(8,128)S(1)}, f32[176,128]{1,0:T(8,128)S(1)}, u32[]{:S(2)}, u32[]{:S(2)}) %collective-permute-start.8) | collective-permute-done | bytes 90144 | tf_op jit(solution)/shard_map/ppermute | solution.py:572
  22.0 1.5 %collective-permute-start.9 = (f32[144,128]{1,0:T(8,128)S(1)}, f32[144,128]{1,0:T(8,128)S(1)}, u32[]{:S(2)}, u32[]{:S(2)}) collective-permute-start(f32[144,128]{1,0:T(8,128)S(1)} %get-tuple-element.58), channel_id=1, source_target_pairs={{7,0},{2,1},{1,2},{4,3},{3,4},{6,5},{5,6},{0,7},{15,8},{10,9},{9,1... | collective-permute-start | bytes 221192 | tf_op jit(solution)/shard_map/ppermute | solution.py:572
  23.5 1.3 %collective-permute-start.10 = (f32[40,128]{1,0:T(8,128)S(1)}, f32[40,128]{1,0:T(8,128)S(1)}, u32[]{:S(2)}, u32[]{:S(2)}) collective-permute-start(f32[40,128]{1,0:T(8,128)S(1)} %get-tuple-element.59), channel_id=1, source_target_pairs={{4,0},{6,1},{5,2},{7,3},{0,4},{2,5},{1,6},{3,7},{12,8},{14,9},{13,... | collective-permute-start | bytes 61448 | tf_op jit(solution)/shard_map/ppermute | solution.py:572
  24.8 0.2 collective-permute-start.11
  25.0 2.3 %collective-permute-done.10.refs_5_ = f32[40,128]{1,0:T(8,128)S(1)} collective-permute-done((f32[40,128]{1,0:T(8,128)S(1)}, f32[40,128]{1,0:T(8,128)S(1)}, u32[]{:S(2)}, u32[]{:S(2)}) %collective-permute-start.10) | collective-permute-done | bytes 20512 | tf_op jit(solution)/shard_map/ppermute | solution.py:572
  27.3 0.7 %collective-permute-done.11.refs_6_ = f32[40,128]{1,0:T(8,128)S(1)} collective-permute-done((f32[40,128]{1,0:T(8,128)S(1)}, f32[40,128]{1,0:T(8,128)S(1)}, u32[]{:S(2)}, u32[]{:S(2)}) %collective-permute-start.11) | collective-permute-done | bytes 20512 | tf_op jit(solution)/shard_map/ppermute | solution.py:572
  28.0 2.1 %third.1 = f32[2,12,32,128]{3,2,1,0:T(8,128)} custom-call(f32[15,14,48,128]{3,2,1,0:T(8,128)S(1)} %get-tuple-element.50.refs_0_, f32[6,48,128]{2,1,0:T(8,128)S(1)} %get-tuple-element.51.refs_1_, f32[4,6,48,128]{3,2,1,0:T(8,128)S(1)} %get-tuple-element.52.refs_2_, f32[280,128]{1,0:T(8,128)S(1)} %get-tuple-element.57.refs_3_, ...), custom_call_target="tpu_custom_call" | custom-call | tf_op jit(solution)/shard_map/third/pallas_call | solution.py:912
  (9 shorter events, 0.1 us)
Async XLA Ops:
  1.5 11.7 %collective-permute-start = (f32[302,128]{1,0:T(8,128)S(1)}, f32[302,128]{1,0:T(8,128)S(1)}, u32[]{:S(2)}, u32[]{:S(2)}) collective-permute-start(f32[302,128]{1,0:T(8,128)S(1)} %get-tuple-element.35), channel_id=1, source_target_pairs={{0,8},{8,0},{1,9},{9,1},{2,10},{10,2},{3,11},{11,3},{4,12},{12,4},... | collective-permute-start | bytes 463880 | tf_op jit(solution)/shard_map/ppermute | solution.py:787
  2.2 11.0 %collective-permute-start.1 = (f32[301,128]{1,0:T(8,128)S(1)}, f32[301,128]{1,0:T(8,128)S(1)}, u32[]{:S(2)}, u32[]{:S(2)}) collective-permute-start(f32[301,128]{1,0:T(8,128)S(1)} %get-tuple-element.36), channel_id=1, source_target_pairs={{8,16},{16,8},{9,17},{17,9},{10,18},{18,10},{11,19},{19,11},{12,20... | collective-permute-start | bytes 462344 | tf_op jit(solution)/shard_map/ppermute | solution.py:787
  5.8 7.4 %collective-permute-start.2 = (f32[300,128]{1,0:T(8,128)S(1)}, f32[300,128]{1,0:T(8,128)S(1)}, u32[]{:S(2)}, u32[]{:S(2)}) collective-permute-start(f32[300,128]{1,0:T(8,128)S(1)} %get-tuple-element.37), channel_id=1, source_target_pairs={{16,24},{24,16},{17,25},{25,17},{18,26},{26,18},{19,27},{27,19},{2... | collective-permute-start | bytes 460808 | tf_op jit(solution)/shard_map/ppermute | solution.py:787
  7.9 10.3 %collective-permute-start.3 = (f32[7,32,128]{2,1,0:T(8,128)S(1)}, f32[7,32,128]{2,1,0:T(8,128)S(1)}, u32[]{:S(2)}, u32[]{:S(2)}) collective-permute-start(f32[7,32,128]{2,1,0:T(8,128)S(1)} %get-tuple-element.40), channel_id=1, source_target_pairs={{1,2},{2,1},{3,4},{4,3},{5,6},{6,5},{9,10},{10,9},{11,12},{12,11},... | collective-permute-start | bytes 344072 | tf_op jit(solution)/shard_map/ppermute | solution.py:787
  13.4 6.6 %collective-permute-start.7 = (f32[144,128]{1,0:T(8,128)S(1)}, f32[144,128]{1,0:T(8,128)S(1)}, u32[]{:S(2)}, u32[]{:S(2)}) collective-permute-start(f32[144,128]{1,0:T(8,128)S(1)} %get-tuple-element.49), channel_id=1, source_target_pairs={{1,2},{2,1},{3,4},{4,3},{5,6},{6,5},{9,10},{10,9},{11,12},{12,11},... | collective-permute-start | bytes 221192 | tf_op jit(solution)/shard_map/ppermute | solution.py:787
  14.6 4.8 %collective-permute-start.4 = (f32[3,40,128]{2,1,0:T(8,128)S(1)}, f32[3,40,128]{2,1,0:T(8,128)S(1)}, u32[]{:S(2)}, u32[]{:S(2)}) collective-permute-start(f32[3,40,128]{2,1,0:T(8,128)S(1)} %get-tuple-element.43), channel_id=1, source_target_pairs={{0,1},{1,0},{2,3},{3,2},{4,5},{5,4},{6,7},{7,6},{8,9},{9,8},{10,11... | collective-permute-start | bytes 184328 | tf_op jit(solution)/shard_map/ppermute | solution.py:787
  17.7 1.7 %collective-permute-start.5 = (f32[3,40,128]{2,1,0:T(8,128)S(1)}, f32[3,40,128]{2,1,0:T(8,128)S(1)}, u32[]{:S(2)}, u32[]{:S(2)}) collective-permute-start(f32[3,40,128]{2,1,0:T(8,128)S(1)} %get-tuple-element.44), channel_id=1, source_target_pairs={{0,1},{1,0},{2,3},{3,2},{4,5},{5,4},{6,7},{7,6},{8,9},{9,8},{10,11... | collective-permute-start | bytes 184328 | tf_op jit(solution)/shard_map/ppermute | solution.py:787
  17.8 1.6 %collective-permute-start.6 = (f32[3,40,128]{2,1,0:T(8,128)S(1)}, f32[3,40,128]{2,1,0:T(8,128)S(1)}, u32[]{:S(2)}, u32[]{:S(2)}) collective-permute-start(f32[3,40,128]{2,1,0:T(8,128)S(1)} %get-tuple-element.45), channel_id=1, source_target_pairs={{0,1},{1,0},{2,3},{3,2},{4,5},{5,4},{6,7},{7,6},{8,9},{9,8},{10,11... | collective-permute-start | bytes 184328 | tf_op jit(solution)/shard_map/ppermute | solution.py:787
  20.6 1.4 %collective-permute-start.8 = (f32[176,128]{1,0:T(8,128)S(1)}, f32[176,128]{1,0:T(8,128)S(1)}, u32[]{:S(2)}, u32[]{:S(2)}) collective-permute-start(f32[176,128]{1,0:T(8,128)S(1)} %get-tuple-element.56), channel_id=1, source_target_pairs={{1,0},{0,1},{3,2},{2,3},{5,4},{4,5},{7,6},{6,7},{9,8},{8,9},{11,10... | collective-permute-start | bytes 270344 | tf_op jit(solution)/shard_map/ppermute | solution.py:572
  22.0 6.0 %collective-permute-start.9 = (f32[144,128]{1,0:T(8,128)S(1)}, f32[144,128]{1,0:T(8,128)S(1)}, u32[]{:S(2)}, u32[]{:S(2)}) collective-permute-start(f32[144,128]{1,0:T(8,128)S(1)} %get-tuple-element.58), channel_id=1, source_target_pairs={{7,0},{2,1},{1,2},{4,3},{3,4},{6,5},{5,6},{0,7},{15,8},{10,9},{9,1... | collective-permute-start | bytes 221192 | tf_op jit(solution)/shard_map/ppermute | solution.py:572
  23.5 3.8 %collective-permute-start.10 = (f32[40,128]{1,0:T(8,128)S(1)}, f32[40,128]{1,0:T(8,128)S(1)}, u32[]{:S(2)}, u32[]{:S(2)}) collective-permute-start(f32[40,128]{1,0:T(8,128)S(1)} %get-tuple-element.59), channel_id=1, source_target_pairs={{4,0},{6,1},{5,2},{7,3},{0,4},{2,5},{1,6},{3,7},{12,8},{14,9},{13,... | collective-permute-start | bytes 61448 | tf_op jit(solution)/shard_map/ppermute | solution.py:572
  24.8 3.2 %collective-permute-start.11 = (f32[40,128]{1,0:T(8,128)S(1)}, f32[40,128]{1,0:T(8,128)S(1)}, u32[]{:S(2)}, u32[]{:S(2)}) collective-permute-start(f32[40,128]{1,0:T(8,128)S(1)} %get-tuple-element.60), channel_id=1, source_target_pairs={{3,0},{5,1},{6,2},{0,3},{7,4},{1,5},{2,6},{4,7},{11,8},{13,9},{14,... | collective-permute-start | bytes 61448 | tf_op jit(solution)/shard_map/ppermute | solution.py:572

commit v23 on v21

--- a/solution.py
+++ b/solution.py
@@ -87,17 +87,21 @@
 def pack_kernel(temps, right, exchange, coupling, one, two, st, sems):
     even = lax.axis_index("gx") % 2 == 0
     ny, nx, nz = exchange.shape
-    copies = []
+    halves = [(0, ny // 2), (ny // 2, ny - ny // 2)]
+    copies = [[], []]
     for k, (plane, ref) in enumerate(
         ((SA, temps.at[0]), (K, exchange), (GA, temps.at[1]), (C, coupling), (RS, right.at[0]), (RG, right.at[1]))
     ):
-        to = st.at[plane, pl.ds(1, ny), pl.ds(PAD, nx)]
-        copies.append(pltpu.make_async_copy(ref, to, sems.at[k]))
-    for copy in copies:
+        for h, (start, count) in enumerate(halves):
+            to = st.at[plane, pl.ds(1 + start, count), pl.ds(PAD, nx)]
+            copies[h].append(pltpu.make_async_copy(ref.at[pl.ds(start, count)], to, sems.at[6 * h + k]))
+    for copy in copies[0] + copies[1]:
         copy.start()
-    for copy in copies:
-        copy.wait()
     for i in range(1, ny + 1):
+        for h, (start, count) in enumerate(halves):
+            if i == start + 1:
+                for copy in copies[h]:
+                    copy.wait()
         sides = []
         for start in (PAD, PAD + nx - 8):
             s, g, e, rs, rg, c = (st[plane, i, start : start + 8] for plane in (SA, GA, K, RS, RG, C))
@@ -800,7 +804,7 @@
         out_shape=(strip, strip, state),
         in_specs=[HBM] * 4,
         out_specs=(VMEM,) * 3,
-        scratch_shapes=[pltpu.SemaphoreType.DMA((6,))],
+        scratch_shapes=[pltpu.SemaphoreType.DMA((12,))],
         compiler_params=PARAMS,
         name="pack_x",
     )(temps, right_side, exchange, coupling)

time: 28 us -> 28 us (level)
  no operation moved by 1% of the time
where the time goes in v23:
time: 28 us; the launch traced here: 27.8 us
  starting transfers between devices  13.4 us (48%)
  waiting for transfers between devices  7.28 us (26%)
  Pallas kernels  6.94 us (25%)
    ppermute x7, starting transfers between devices, swap(): return lax.ppermute(x, axis, pairs)  9.87 us
    ppermute x4, waiting for transfers between devices, exchange_stage(): lax.ppermute(message, 'gy', [(sender, me) for me, sender in enumerate(sen...  4.42 us
    ppermute x4, starting transfers between devices, exchange_stage(): lax.ppermute(message, 'gy', [(sender, me) for me, sender in enumerate(sen...  3.56 us
    ppermute x7, waiting for transfers between devices, swap(): return lax.ppermute(x, axis, pairs)  2.86 us
    pallas_call x1, Pallas kernels, shards(): pl.pallas_call(functools.partial(third_kernel, radices[-1], stride), out_...  2.14 us
    pallas_call x1, Pallas kernels, shards(): pl.pallas_call(pack_kernel, out_shape=(strip, strip, state), in_specs=[HB...  1.48 us
    pallas_call x1, Pallas kernels, shards(): pl.pallas_call(inner_kernel, out_shape=(state, rows), in_specs=[VMEM] * 2...  1.18 us
    pallas_call x1, Pallas kernels, shards(): pl.pallas_call(second_kernel, out_shape=(state, rows, more, tall(lay.map)...  0.62 us
  transfers between devices with their start and end apart: 11, of which 4 were waited for; matrix products, arithmetic and copies ran while one was open for 0% of the time, Pallas kernels for 10%

profile of v23, /device:TPU:8, one launch (start us, length us, event | category | flops | bytes accessed | tf_op | source)
XLA Modules:
  0.0 27.8 jit_solution(18004855479083593663)
XLA Ops:
  0.0 1.5 %pack_x.1 = (f32[304,128]{1,0:T(8,128)S(1)}, f32[304,128]{1,0:T(8,128)S(1)}, f32[15,14,48,128]{3,2,1,0:T(8,128)S(1)}) custom-call(f32[2,12,32,128]{3,2,1,0:T(8,128)} %bitcast.5, f32[2,12,32,128]{3,2,1,0:T(8,128)} %bitcast.6, f32[12,32,128]{2,1,0:T(8,128)} %bitcast.7, f32[12,32,128]{2,1,0:T(8,128)} %bitcast.8), custom_call_target="tpu_custom_call" | custom-call | tf_op jit(solution)/shard_map/pack_x/pallas_call | solution.py:802
  1.5 0.1 collective-permute-start
  1.6 5.0 %collective-permute-start.1 = (f32[304,128]{1,0:T(8,128)S(1)}, f32[304,128]{1,0:T(8,128)S(1)}, u32[]{:S(2)}, u32[]{:S(2)}) collective-permute-start(f32[304,128]{1,0:T(8,128)S(1)} %get-tuple-element.35), channel_id=1, source_target_pairs={{8,16},{16,8},{9,17},{17,9},{10,18},{18,10},{11,19},{19,11},{12,20... | collective-permute-start | bytes 466952 | tf_op jit(solution)/shard_map/ppermute | solution.py:787
  6.6 0.2 conduct.1
  6.8 0.7 %collective-permute-start.2 = (f32[7,32,128]{2,1,0:T(8,128)S(1)}, f32[7,32,128]{2,1,0:T(8,128)S(1)}, u32[]{:S(2)}, u32[]{:S(2)}) collective-permute-start(f32[7,32,128]{2,1,0:T(8,128)S(1)} %get-tuple-element.38), channel_id=1, source_target_pairs={{1,2},{2,1},{3,4},{4,3},{5,6},{6,5},{9,10},{10,9},{11,12},{12,11},... | collective-permute-start | bytes 344072 | tf_op jit(solution)/shard_map/ppermute | solution.py:787
  7.5 2.8 %collective-permute-done.1.two = f32[304,128]{1,0:T(8,128)S(1)} collective-permute-done((f32[304,128]{1,0:T(8,128)S(1)}, f32[304,128]{1,0:T(8,128)S(1)}, u32[]{:S(2)}, u32[]{:S(2)}) %collective-permute-start.1) | collective-permute-done | bytes 155680 | tf_op jit(solution)/shard_map/ppermute | solution.py:787
  10.3 0.2 first.1
  10.5 0.7 %collective-permute-start.6 = (f32[144,128]{1,0:T(8,128)S(1)}, f32[144,128]{1,0:T(8,128)S(1)}, u32[]{:S(2)}, u32[]{:S(2)}) collective-permute-start(f32[144,128]{1,0:T(8,128)S(1)} %get-tuple-element.47), channel_id=1, source_target_pairs={{1,2},{2,1},{3,4},{4,3},{5,6},{6,5},{9,10},{10,9},{11,12},{12,11},... | collective-permute-start | bytes 221192 | tf_op jit(solution)/shard_map/ppermute | solution.py:787
  11.2 0.5 %other.1 = (f32[15,14,48,128]{3,2,1,0:T(8,128)S(1)}, f32[3,40,128]{2,1,0:T(8,128)S(1)}, f32[3,40,128]{2,1,0:T(8,128)S(1)}, f32[3,40,128]{2,1,0:T(8,128)S(1)}) custom-call(f32[15,14,48,128]{3,2,1,0:T(8,128)S(1)} %get-tuple-element.36.st_in, f32[304,128]{1,0:T(8,128)S(1)} %collective-permute-done.one, ...), custom_call_target="tpu_custom_call", output_to_operand_aliasing={{0}: (0, {})} | custom-call | tf_op jit(solution)/shard_map/other/pallas_call | solution.py:836
  11.7 2.9 %collective-permute-start.3 = (f32[3,40,128]{2,1,0:T(8,128)S(1)}, f32[3,40,128]{2,1,0:T(8,128)S(1)}, u32[]{:S(2)}, u32[]{:S(2)}) collective-permute-start(f32[3,40,128]{2,1,0:T(8,128)S(1)} %get-tuple-element.41), channel_id=1, source_target_pairs={{0,1},{1,0},{2,3},{3,2},{4,5},{5,4},{6,7},{7,6},{8,9},{9,8},{10,11... | collective-permute-start | bytes 184328 | tf_op jit(solution)/shard_map/ppermute | solution.py:787
  14.7 0.1 collective-permute-start.4
  14.7 0.4 %collective-permute-start.5 = (f32[3,40,128]{2,1,0:T(8,128)S(1)}, f32[3,40,128]{2,1,0:T(8,128)S(1)}, u32[]{:S(2)}, u32[]{:S(2)}) collective-permute-start(f32[3,40,128]{2,1,0:T(8,128)S(1)} %get-tuple-element.43), channel_id=1, source_target_pairs={{0,1},{1,0},{2,3},{3,2},{4,5},{5,4},{6,7},{7,6},{8,9},{9,8},{10,11... | collective-permute-start | bytes 184328 | tf_op jit(solution)/shard_map/ppermute | solution.py:787
  15.2 0.0 collective-permute-done.2.early
  15.2 1.2 %inner.1 = (f32[15,14,48,128]{3,2,1,0:T(8,128)S(1)}, f32[4,6,48,128]{3,2,1,0:T(8,128)S(1)}) custom-call(f32[15,14,48,128]{3,2,1,0:T(8,128)S(1)} %get-tuple-element.37.st_in, f32[7,32,128]{2,1,0:T(8,128)S(1)} %collective-permute-done.2.early), custom_call_target="tpu_custom_call", output_to_operand_aliasing={{0}: (0, {})} | custom-call | flops 14745600 | bytes 18874368 | tf_op jit(solution)/shard_map/inner/pallas_call | solution.py:848
  16.4 0.0 collective-permute-done.5.refs_2_
  16.4 0.6 %near.1 = (f32[15,14,48,128]{3,2,1,0:T(8,128)S(1)}, f32[4,6,48,128]{3,2,1,0:T(8,128)S(1)}, f32[6,48,128]{2,1,0:T(8,128)S(1)}) custom-call(f32[15,14,48,128]{3,2,1,0:T(8,128)S(1)} %get-tuple-element.39.st_in, f32[4,6,48,128]{3,2,1,0:T(8,128)S(1)} %get-tuple-element.40.coarse_in, ...), custom_call_target="tpu_custom_call", output_to_operand_aliasing={{0}: (0, {}), {1}: (1, {})} | custom-call | tf_op jit(solution)/shard_map/near/pallas_call | solution.py:868
  17.0 0.6 %second.1 = (f32[15,14,48,128]{3,2,1,0:T(8,128)S(1)}, f32[4,6,48,128]{3,2,1,0:T(8,128)S(1)}, f32[6,48,128]{2,1,0:T(8,128)S(1)}, f32[40,128]{1,0:T(8,128)S(1)}, f...) custom-call(f32[15,14,48,128]{3,2,1,0:T(8,128)S(1)} %get-tuple-eleme, ...), custom_call_target="tpu_custom_call", output_to_operand_aliasing={{0}: (0, {}), {1}: (1, {}), {2}: (2, {})} | custom-call | tf_op jit(solution)/shard_map/second/pallas_call | solution.py:878
  17.6 0.1 collective-permute-start.7
  17.8 1.2 %collective-permute-done.7.refs_4_ = f32[176,128]{1,0:T(8,128)S(1)} collective-permute-done((f32[176,128]{1,0:T(8,128)S(1)}, f32[176,128]{1,0:T(8,128)S(1)}, u32[]{:S(2)}, u32[]{:S(2)}) %collective-permute-start.7) | collective-permute-done | bytes 90144 | tf_op jit(solution)/shard_map/ppermute | solution.py:572
  19.0 2.1 %collective-permute-start.8 = (f32[144,128]{1,0:T(8,128)S(1)}, f32[144,128]{1,0:T(8,128)S(1)}, u32[]{:S(2)}, u32[]{:S(2)}) collective-permute-start(f32[144,128]{1,0:T(8,128)S(1)} %get-tuple-element.56), channel_id=1, source_target_pairs={{7,0},{2,1},{1,2},{4,3},{3,4},{6,5},{5,6},{0,7},{15,8},{10,9},{9,1... | collective-permute-start | bytes 221192 | tf_op jit(solution)/shard_map/ppermute | solution.py:572
  21.1 1.3 %collective-permute-start.9 = (f32[40,128]{1,0:T(8,128)S(1)}, f32[40,128]{1,0:T(8,128)S(1)}, u32[]{:S(2)}, u32[]{:S(2)}) collective-permute-start(f32[40,128]{1,0:T(8,128)S(1)} %get-tuple-element.57), channel_id=1, source_target_pairs={{4,0},{6,1},{5,2},{7,3},{0,4},{2,5},{1,6},{3,7},{12,8},{14,9},{13,... | collective-permute-start | bytes 61448 | tf_op jit(solution)/shard_map/ppermute | solution.py:572
  22.4 2.7 %collective-permute-done.9.refs_5_ = f32[40,128]{1,0:T(8,128)S(1)} collective-permute-done((f32[40,128]{1,0:T(8,128)S(1)}, f32[40,128]{1,0:T(8,128)S(1)}, u32[]{:S(2)}, u32[]{:S(2)}) %collective-permute-start.9) | collective-permute-done | bytes 20512 | tf_op jit(solution)/shard_map/ppermute | solution.py:572
  25.1 0.5 %collective-permute-done.10.refs_6_ = f32[40,128]{1,0:T(8,128)S(1)} collective-permute-done((f32[40,128]{1,0:T(8,128)S(1)}, f32[40,128]{1,0:T(8,128)S(1)}, u32[]{:S(2)}, u32[]{:S(2)}) %collective-permute-start.10) | collective-permute-done | bytes 20512 | tf_op jit(solution)/shard_map/ppermute | solution.py:572
  25.6 2.1 %third.1 = f32[2,12,32,128]{3,2,1,0:T(8,128)} custom-call(f32[15,14,48,128]{3,2,1,0:T(8,128)S(1)} %get-tuple-element.48.refs_0_, f32[6,48,128]{2,1,0:T(8,128)S(1)} %get-tuple-element.49.refs_1_, f32[4,6,48,128]{3,2,1,0:T(8,128)S(1)} %get-tuple-element.50.refs_2_, f32[280,128]{1,0:T(8,128)S(1)} %get-tuple-element.55.refs_3_, ...), custom_call_target="tpu_custom_call" | custom-call | tf_op jit(solution)/shard_map/third/pallas_call | solution.py:912
  (7 shorter events, 0.1 us)
Async XLA Ops:
  1.5 6.0 %collective-permute-start = (f32[304,128]{1,0:T(8,128)S(1)}, f32[304,128]{1,0:T(8,128)S(1)}, u32[]{:S(2)}, u32[]{:S(2)}) collective-permute-start(f32[304,128]{1,0:T(8,128)S(1)} %get-tuple-element.34), channel_id=1, source_target_pairs={{0,8},{8,0},{16,24},{24,16},{1,9},{9,1},{17,25},{25,17},{2,10},{10... | collective-permute-start | bytes 466952 | tf_op jit(solution)/shard_map/ppermute | solution.py:787
  1.6 8.8 %collective-permute-start.1 = (f32[304,128]{1,0:T(8,128)S(1)}, f32[304,128]{1,0:T(8,128)S(1)}, u32[]{:S(2)}, u32[]{:S(2)}) collective-permute-start(f32[304,128]{1,0:T(8,128)S(1)} %get-tuple-element.35), channel_id=1, source_target_pairs={{8,16},{16,8},{9,17},{17,9},{10,18},{18,10},{11,19},{19,11},{12,20... | collective-permute-start | bytes 466952 | tf_op jit(solution)/shard_map/ppermute | solution.py:787
  6.8 8.4 %collective-permute-start.2 = (f32[7,32,128]{2,1,0:T(8,128)S(1)}, f32[7,32,128]{2,1,0:T(8,128)S(1)}, u32[]{:S(2)}, u32[]{:S(2)}) collective-permute-start(f32[7,32,128]{2,1,0:T(8,128)S(1)} %get-tuple-element.38), channel_id=1, source_target_pairs={{1,2},{2,1},{3,4},{4,3},{5,6},{6,5},{9,10},{10,9},{11,12},{12,11},... | collective-permute-start | bytes 344072 | tf_op jit(solution)/shard_map/ppermute | solution.py:787
  10.5 6.4 %collective-permute-start.6 = (f32[144,128]{1,0:T(8,128)S(1)}, f32[144,128]{1,0:T(8,128)S(1)}, u32[]{:S(2)}, u32[]{:S(2)}) collective-permute-start(f32[144,128]{1,0:T(8,128)S(1)} %get-tuple-element.47), channel_id=1, source_target_pairs={{1,2},{2,1},{3,4},{4,3},{5,6},{6,5},{9,10},{10,9},{11,12},{12,11},... | collective-permute-start | bytes 221192 | tf_op jit(solution)/shard_map/ppermute | solution.py:787
  11.7 4.6 %collective-permute-start.3 = (f32[3,40,128]{2,1,0:T(8,128)S(1)}, f32[3,40,128]{2,1,0:T(8,128)S(1)}, u32[]{:S(2)}, u32[]{:S(2)}) collective-permute-start(f32[3,40,128]{2,1,0:T(8,128)S(1)} %get-tuple-element.41), channel_id=1, source_target_pairs={{0,1},{1,0},{2,3},{3,2},{4,5},{5,4},{6,7},{7,6},{8,9},{9,8},{10,11... | collective-permute-start | bytes 184328 | tf_op jit(solution)/shard_map/ppermute | solution.py:787
  14.7 1.7 %collective-permute-start.4 = (f32[3,40,128]{2,1,0:T(8,128)S(1)}, f32[3,40,128]{2,1,0:T(8,128)S(1)}, u32[]{:S(2)}, u32[]{:S(2)}) collective-permute-start(f32[3,40,128]{2,1,0:T(8,128)S(1)} %get-tuple-element.42), channel_id=1, source_target_pairs={{0,1},{1,0},{2,3},{3,2},{4,5},{5,4},{6,7},{7,6},{8,9},{9,8},{10,11... | collective-permute-start | bytes 184328 | tf_op jit(solution)/shard_map/ppermute | solution.py:787
  14.7 1.6 %collective-permute-start.5 = (f32[3,40,128]{2,1,0:T(8,128)S(1)}, f32[3,40,128]{2,1,0:T(8,128)S(1)}, u32[]{:S(2)}, u32[]{:S(2)}) collective-permute-start(f32[3,40,128]{2,1,0:T(8,128)S(1)} %get-tuple-element.43), channel_id=1, source_target_pairs={{0,1},{1,0},{2,3},{3,2},{4,5},{5,4},{6,7},{7,6},{8,9},{9,8},{10,11... | collective-permute-start | bytes 184328 | tf_op jit(solution)/shard_map/ppermute | solution.py:787
  17.6 1.4 %collective-permute-start.7 = (f32[176,128]{1,0:T(8,128)S(1)}, f32[176,128]{1,0:T(8,128)S(1)}, u32[]{:S(2)}, u32[]{:S(2)}) collective-permute-start(f32[176,128]{1,0:T(8,128)S(1)} %get-tuple-element.54), channel_id=1, source_target_pairs={{1,0},{0,1},{3,2},{2,3},{5,4},{4,5},{7,6},{6,7},{9,8},{8,9},{11,10... | collective-permute-start | bytes 270344 | tf_op jit(solution)/shard_map/ppermute | solution.py:572
  19.0 6.6 %collective-permute-start.8 = (f32[144,128]{1,0:T(8,128)S(1)}, f32[144,128]{1,0:T(8,128)S(1)}, u32[]{:S(2)}, u32[]{:S(2)}) collective-permute-start(f32[144,128]{1,0:T(8,128)S(1)} %get-tuple-element.56), channel_id=1, source_target_pairs={{7,0},{2,1},{1,2},{4,3},{3,4},{6,5},{5,6},{0,7},{15,8},{10,9},{9,1... | collective-permute-start | bytes 221192 | tf_op jit(solution)/shard_map/ppermute | solution.py:572
  21.1 4.0 %collective-permute-start.9 = (f32[40,128]{1,0:T(8,128)S(1)}, f32[40,128]{1,0:T(8,128)S(1)}, u32[]{:S(2)}, u32[]{:S(2)}) collective-permute-start(f32[40,128]{1,0:T(8,128)S(1)} %get-tuple-element.57), channel_id=1, source_target_pairs={{4,0},{6,1},{5,2},{7,3},{0,4},{2,5},{1,6},{3,7},{12,8},{14,9},{13,... | collective-permute-start | bytes 61448 | tf_op jit(solution)/shard_map/ppermute | solution.py:572
  22.4 3.2 %collective-permute-start.10 = (f32[40,128]{1,0:T(8,128)S(1)}, f32[40,128]{1,0:T(8,128)S(1)}, u32[]{:S(2)}, u32[]{:S(2)}) collective-permute-start(f32[40,128]{1,0:T(8,128)S(1)} %get-tuple-element.58), channel_id=1, source_target_pairs={{3,0},{5,1},{6,2},{0,3},{7,4},{1,5},{2,6},{4,7},{11,8},{13,9},{14,... | collective-permute-start | bytes 61448 | tf_op jit(solution)/shard_map/ppermute | solution.py:572

commit v24 on v23

--- a/solution.py
+++ b/solution.py
@@ -486,7 +486,7 @@
     lead, ratio, slope, offset, slopes, offsets, lead_last, ratio_last = (
         squeeze[k, pl.ds(PAD - 2, span, 2), :] for k in range(8)
     )
-    part = slice(PAD - 1, PAD + nx + 1)
+    part = slice(PAD, PAD + nx)
 
     def increments(d, face, gas):
         return [(st[FY, face] * (st[SA, d] - st[SB, d]))[part], (gas * (st[GA, d] - st[GB, d]))[part]]
@@ -514,7 +514,7 @@
     def __init__(self, nx):
         self.span = nx // 2 + 2
         self.map = 2 * self.span
-        self.info = self.map + 2 * (nx + 2)
+        self.info = self.map + 2 * nx
         self.rest = self.map
         self.final = self.map + self.info
         self.full = self.final + self.rest
@@ -699,11 +699,11 @@
         wide[k, ext - PAD + 2 :] = jnp.zeros((PAD - 2, nz), jnp.float32)
         wide[k, pl.ds(PAD - 2, span, 2), :] = v
         wide[k, pl.ds(PAD - 1, span, 2), :] = v
-    for k, start in enumerate((lay.low, lay.low + nx + 2, lay.high, lay.high + nx + 2)):
+    for k, start in enumerate((lay.low, lay.low + nx, lay.high, lay.high + nx)):
         start += lay.map
         wide[7 + k, :PAD] = jnp.zeros((PAD, nz), jnp.float32)
         wide[7 + k, ext - PAD :] = jnp.zeros((PAD, nz), jnp.float32)
-        wide[7 + k, PAD - 1 : PAD + nx + 1] = near[start : start + nx + 2]
+        wide[7 + k, PAD : PAD + nx] = near[start : start + nx]
 
     gas_in = wide[0]
     last = ny + 1
@@ -719,7 +719,7 @@
             sc[1, i] = st[GA, i] + gas
         return carry
 
-    lax.fori_loop(0, blocks, correct, 0)
+    lax.fori_loop(0, blocks, correct, 0, unroll=3)
     gas = coarse[2, blocks - 1] * gas_in + coarse[3, blocks - 1]
     gas_high = wide[5] * gas + wide[4]
     solid_high = wide[3] + wide[6] * gas_high

time: 28 us -> 28.2 us (level)
  the two profiles are of different devices: /device:TPU:8 before, /device:TPU:16 now
where the time goes in v24:
time: 28.2 us; the launch traced here: 27.7 us
  starting transfers between devices  11.4 us (40%)
  waiting for transfers between devices  8.8 us (31%)
  Pallas kernels  7.33 us (26%)
    ppermute x7, starting transfers between devices, swap(): return lax.ppermute(x, axis, pairs)  8.31 us
    ppermute x7, waiting for transfers between devices, swap(): return lax.ppermute(x, axis, pairs)  4.59 us
    ppermute x4, waiting for transfers between devices, exchange_stage(): lax.ppermute(message, 'gy', [(sender, me) for me, sender in enumerate(sen...  4.21 us
    ppermute x4, starting transfers between devices, exchange_stage(): lax.ppermute(message, 'gy', [(sender, me) for me, sender in enumerate(sen...  3.13 us
    pallas_call x1, Pallas kernels, shards(): pl.pallas_call(functools.partial(third_kernel, radices[-1], stride), out_...  2.29 us
    pallas_call x1, Pallas kernels, shards(): pl.pallas_call(pack_kernel, out_shape=(strip, strip, state), in_specs=[HB...  1.48 us
    pallas_call x1, Pallas kernels, shards(): pl.pallas_call(inner_kernel, out_shape=(state, rows), in_specs=[VMEM] * 2...  1.3 us
    pallas_call x1, Pallas kernels, shards(): pl.pallas_call(second_kernel, out_shape=(state, rows, more, tall(lay.map)...  0.66 us
  transfers between devices with their start and end apart: 11, of which 5 were waited for; matrix products, arithmetic and copies ran while one was open for 0% of the time, Pallas kernels for 10%

profile of v24, /device:TPU:16, one launch (start us, length us, event | category | flops | bytes accessed | tf_op | source)
XLA Modules:
  0.0 27.7 jit_solution(1290610907173487517)
XLA Ops:
  0.0 1.5 %pack_x.1 = (f32[304,128]{1,0:T(8,128)S(1)}, f32[304,128]{1,0:T(8,128)S(1)}, f32[15,14,48,128]{3,2,1,0:T(8,128)S(1)}) custom-call(f32[2,12,32,128]{3,2,1,0:T(8,128)} %bitcast.5, f32[2,12,32,128]{3,2,1,0:T(8,128)} %bitcast.6, f32[12,32,128]{2,1,0:T(8,128)} %bitcast.7, f32[12,32,128]{2,1,0:T(8,128)} %bitcast.8), custom_call_target="tpu_custom_call" | custom-call | tf_op jit(solution)/shard_map/pack_x/pallas_call | solution.py:802
  1.5 1.6 %collective-permute-start = (f32[304,128]{1,0:T(8,128)S(1)}, f32[304,128]{1,0:T(8,128)S(1)}, u32[]{:S(2)}, u32[]{:S(2)}) collective-permute-start(f32[304,128]{1,0:T(8,128)S(1)} %get-tuple-element.34), channel_id=1, source_target_pairs={{0,8},{8,0},{16,24},{24,16},{1,9},{9,1},{17,25},{25,17},{2,10},{10... | collective-permute-start | bytes 466952 | tf_op jit(solution)/shard_map/ppermute | solution.py:787
  3.1 1.9 %collective-permute-start.1 = (f32[304,128]{1,0:T(8,128)S(1)}, f32[304,128]{1,0:T(8,128)S(1)}, u32[]{:S(2)}, u32[]{:S(2)}) collective-permute-start(f32[304,128]{1,0:T(8,128)S(1)} %get-tuple-element.35), channel_id=1, source_target_pairs={{8,16},{16,8},{9,17},{17,9},{10,18},{18,10},{11,19},{19,11},{12,20... | collective-permute-start | bytes 466952 | tf_op jit(solution)/shard_map/ppermute | solution.py:787
  5.0 0.2 conduct.1
  5.2 0.7 %collective-permute-start.2 = (f32[7,32,128]{2,1,0:T(8,128)S(1)}, f32[7,32,128]{2,1,0:T(8,128)S(1)}, u32[]{:S(2)}, u32[]{:S(2)}) collective-permute-start(f32[7,32,128]{2,1,0:T(8,128)S(1)} %get-tuple-element.38), channel_id=1, source_target_pairs={{1,2},{2,1},{3,4},{4,3},{5,6},{6,5},{9,10},{10,9},{11,12},{12,11},... | collective-permute-start | bytes 344072 | tf_op jit(solution)/shard_map/ppermute | solution.py:787
  5.9 1.4 %collective-permute-done.one = f32[304,128]{1,0:T(8,128)S(1)} collective-permute-done((f32[304,128]{1,0:T(8,128)S(1)}, f32[304,128]{1,0:T(8,128)S(1)}, u32[]{:S(2)}, u32[]{:S(2)}) %collective-permute-start) | collective-permute-done | bytes 155680 | tf_op jit(solution)/shard_map/ppermute | solution.py:787
  7.3 3.2 %collective-permute-done.1.two = f32[304,128]{1,0:T(8,128)S(1)} collective-permute-done((f32[304,128]{1,0:T(8,128)S(1)}, f32[304,128]{1,0:T(8,128)S(1)}, u32[]{:S(2)}, u32[]{:S(2)}) %collective-permute-start.1) | collective-permute-done | bytes 155680 | tf_op jit(solution)/shard_map/ppermute | solution.py:787
  10.5 0.2 first.1
  10.7 0.7 %collective-permute-start.6 = (f32[144,128]{1,0:T(8,128)S(1)}, f32[144,128]{1,0:T(8,128)S(1)}, u32[]{:S(2)}, u32[]{:S(2)}) collective-permute-start(f32[144,128]{1,0:T(8,128)S(1)} %get-tuple-element.47), channel_id=1, source_target_pairs={{1,2},{2,1},{3,4},{4,3},{5,6},{6,5},{9,10},{10,9},{11,12},{12,11},... | collective-permute-start | bytes 221192 | tf_op jit(solution)/shard_map/ppermute | solution.py:787
  11.4 0.5 %other.1 = (f32[15,14,48,128]{3,2,1,0:T(8,128)S(1)}, f32[3,40,128]{2,1,0:T(8,128)S(1)}, f32[3,40,128]{2,1,0:T(8,128)S(1)}, f32[3,40,128]{2,1,0:T(8,128)S(1)}) custom-call(f32[15,14,48,128]{3,2,1,0:T(8,128)S(1)} %get-tuple-element.36.st_in, f32[304,128]{1,0:T(8,128)S(1)} %collective-permute-done.one, ...), custom_call_target="tpu_custom_call", output_to_operand_aliasing={{0}: (0, {})} | custom-call | tf_op jit(solution)/shard_map/other/pallas_call | solution.py:836
  11.9 2.9 %collective-permute-start.3 = (f32[3,40,128]{2,1,0:T(8,128)S(1)}, f32[3,40,128]{2,1,0:T(8,128)S(1)}, u32[]{:S(2)}, u32[]{:S(2)}) collective-permute-start(f32[3,40,128]{2,1,0:T(8,128)S(1)} %get-tuple-element.41), channel_id=1, source_target_pairs={{0,1},{1,0},{2,3},{3,2},{4,5},{5,4},{6,7},{7,6},{8,9},{9,8},{10,11... | collective-permute-start | bytes 184328 | tf_op jit(solution)/shard_map/ppermute | solution.py:787
  14.8 0.1 collective-permute-start.4
  14.9 0.4 %collective-permute-start.5 = (f32[3,40,128]{2,1,0:T(8,128)S(1)}, f32[3,40,128]{2,1,0:T(8,128)S(1)}, u32[]{:S(2)}, u32[]{:S(2)}) collective-permute-start(f32[3,40,128]{2,1,0:T(8,128)S(1)} %get-tuple-element.43), channel_id=1, source_target_pairs={{0,1},{1,0},{2,3},{3,2},{4,5},{5,4},{6,7},{7,6},{8,9},{9,8},{10,11... | collective-permute-start | bytes 184328 | tf_op jit(solution)/shard_map/ppermute | solution.py:787
  15.3 1.3 %inner.1 = (f32[15,14,48,128]{3,2,1,0:T(8,128)S(1)}, f32[4,6,48,128]{3,2,1,0:T(8,128)S(1)}) custom-call(f32[15,14,48,128]{3,2,1,0:T(8,128)S(1)} %get-tuple-element.37.st_in, f32[7,32,128]{2,1,0:T(8,128)S(1)} %collective-permute-done.2.early), custom_call_target="tpu_custom_call", output_to_operand_aliasing={{0}: (0, {})} | custom-call | flops 14745600 | bytes 18874368 | tf_op jit(solution)/shard_map/inner/pallas_call | solution.py:848
  16.7 0.6 %near.1 = (f32[15,14,48,128]{3,2,1,0:T(8,128)S(1)}, f32[4,6,48,128]{3,2,1,0:T(8,128)S(1)}, f32[6,48,128]{2,1,0:T(8,128)S(1)}) custom-call(f32[15,14,48,128]{3,2,1,0:T(8,128)S(1)} %get-tuple-element.39.st_in, f32[4,6,48,128]{3,2,1,0:T(8,128)S(1)} %get-tuple-element.40.coarse_in, ...), custom_call_target="tpu_custom_call", output_to_operand_aliasing={{0}: (0, {}), {1}: (1, {})} | custom-call | tf_op jit(solution)/shard_map/near/pallas_call | solution.py:868
  17.3 0.7 %second.1 = (f32[15,14,48,128]{3,2,1,0:T(8,128)S(1)}, f32[4,6,48,128]{3,2,1,0:T(8,128)S(1)}, f32[6,48,128]{2,1,0:T(8,128)S(1)}, f32[40,128]{1,0:T(8,128)S(1)}, f...) custom-call(f32[15,14,48,128]{3,2,1,0:T(8,128)S(1)} %get-tuple-eleme, ...), custom_call_target="tpu_custom_call", output_to_operand_aliasing={{0}: (0, {}), {1}: (1, {}), {2}: (2, {})} | custom-call | tf_op jit(solution)/shard_map/second/pallas_call | solution.py:878
  18.0 0.1 collective-permute-start.7
  18.1 1.2 %collective-permute-done.7.refs_4_ = f32[176,128]{1,0:T(8,128)S(1)} collective-permute-done((f32[176,128]{1,0:T(8,128)S(1)}, f32[176,128]{1,0:T(8,128)S(1)}, u32[]{:S(2)}, u32[]{:S(2)}) %collective-permute-start.7) | collective-permute-done | bytes 90144 | tf_op jit(solution)/shard_map/ppermute | solution.py:572
  19.4 1.3 %collective-permute-start.8 = (f32[136,128]{1,0:T(8,128)S(1)}, f32[136,128]{1,0:T(8,128)S(1)}, u32[]{:S(2)}, u32[]{:S(2)}) collective-permute-start(f32[136,128]{1,0:T(8,128)S(1)} %get-tuple-element.56), channel_id=1, source_target_pairs={{7,0},{2,1},{1,2},{4,3},{3,4},{6,5},{5,6},{0,7},{15,8},{10,9},{9,1... | collective-permute-start | bytes 208904 | tf_op jit(solution)/shard_map/ppermute | solution.py:572
  20.7 1.5 %collective-permute-start.9 = (f32[40,128]{1,0:T(8,128)S(1)}, f32[40,128]{1,0:T(8,128)S(1)}, u32[]{:S(2)}, u32[]{:S(2)}) collective-permute-start(f32[40,128]{1,0:T(8,128)S(1)} %get-tuple-element.57), channel_id=1, source_target_pairs={{4,0},{6,1},{5,2},{7,3},{0,4},{2,5},{1,6},{3,7},{12,8},{14,9},{13,... | collective-permute-start | bytes 61448 | tf_op jit(solution)/shard_map/ppermute | solution.py:572
  22.2 0.2 collective-permute-start.10
  22.4 2.2 %collective-permute-done.9.refs_5_ = f32[40,128]{1,0:T(8,128)S(1)} collective-permute-done((f32[40,128]{1,0:T(8,128)S(1)}, f32[40,128]{1,0:T(8,128)S(1)}, u32[]{:S(2)}, u32[]{:S(2)}) %collective-permute-start.9) | collective-permute-done | bytes 20512 | tf_op jit(solution)/shard_map/ppermute | solution.py:572
  24.6 0.8 %collective-permute-done.10.refs_6_ = f32[40,128]{1,0:T(8,128)S(1)} collective-permute-done((f32[40,128]{1,0:T(8,128)S(1)}, f32[40,128]{1,0:T(8,128)S(1)}, u32[]{:S(2)}, u32[]{:S(2)}) %collective-permute-start.10) | collective-permute-done | bytes 20512 | tf_op jit(solution)/shard_map/ppermute | solution.py:572
  25.4 2.3 %third.1 = f32[2,12,32,128]{3,2,1,0:T(8,128)} custom-call(f32[15,14,48,128]{3,2,1,0:T(8,128)S(1)} %get-tuple-element.48.refs_0_, f32[6,48,128]{2,1,0:T(8,128)S(1)} %get-tuple-element.49.refs_1_, f32[4,6,48,128]{3,2,1,0:T(8,128)S(1)} %get-tuple-element.50.refs_2_, f32[272,128]{1,0:T(8,128)S(1)} %get-tuple-element.55.refs_3_, ...), custom_call_target="tpu_custom_call" | custom-call | tf_op jit(solution)/shard_map/third/pallas_call | solution.py:912
  (7 shorter events, 0.1 us)
Async XLA Ops:
  1.5 5.8 %collective-permute-start = (f32[304,128]{1,0:T(8,128)S(1)}, f32[304,128]{1,0:T(8,128)S(1)}, u32[]{:S(2)}, u32[]{:S(2)}) collective-permute-start(f32[304,128]{1,0:T(8,128)S(1)} %get-tuple-element.34), channel_id=1, source_target_pairs={{0,8},{8,0},{16,24},{24,16},{1,9},{9,1},{17,25},{25,17},{2,10},{10... | collective-permute-start | bytes 466952 | tf_op jit(solution)/shard_map/ppermute | solution.py:787
  3.1 7.4 %collective-permute-start.1 = (f32[304,128]{1,0:T(8,128)S(1)}, f32[304,128]{1,0:T(8,128)S(1)}, u32[]{:S(2)}, u32[]{:S(2)}) collective-permute-start(f32[304,128]{1,0:T(8,128)S(1)} %get-tuple-element.35), channel_id=1, source_target_pairs={{8,16},{16,8},{9,17},{17,9},{10,18},{18,10},{11,19},{19,11},{12,20... | collective-permute-start | bytes 466952 | tf_op jit(solution)/shard_map/ppermute | solution.py:787
  5.2 10.1 %collective-permute-start.2 = (f32[7,32,128]{2,1,0:T(8,128)S(1)}, f32[7,32,128]{2,1,0:T(8,128)S(1)}, u32[]{:S(2)}, u32[]{:S(2)}) collective-permute-start(f32[7,32,128]{2,1,0:T(8,128)S(1)} %get-tuple-element.38), channel_id=1, source_target_pairs={{1,2},{2,1},{3,4},{4,3},{5,6},{6,5},{9,10},{10,9},{11,12},{12,11},... | collective-permute-start | bytes 344072 | tf_op jit(solution)/shard_map/ppermute | solution.py:787
  10.7 6.6 %collective-permute-start.6 = (f32[144,128]{1,0:T(8,128)S(1)}, f32[144,128]{1,0:T(8,128)S(1)}, u32[]{:S(2)}, u32[]{:S(2)}) collective-permute-start(f32[144,128]{1,0:T(8,128)S(1)} %get-tuple-element.47), channel_id=1, source_target_pairs={{1,2},{2,1},{3,4},{4,3},{5,6},{6,5},{9,10},{10,9},{11,12},{12,11},... | collective-permute-start | bytes 221192 | tf_op jit(solution)/shard_map/ppermute | solution.py:787
  11.9 4.7 %collective-permute-start.3 = (f32[3,40,128]{2,1,0:T(8,128)S(1)}, f32[3,40,128]{2,1,0:T(8,128)S(1)}, u32[]{:S(2)}, u32[]{:S(2)}) collective-permute-start(f32[3,40,128]{2,1,0:T(8,128)S(1)} %get-tuple-element.41), channel_id=1, source_target_pairs={{0,1},{1,0},{2,3},{3,2},{4,5},{5,4},{6,7},{7,6},{8,9},{9,8},{10,11... | collective-permute-start | bytes 184328 | tf_op jit(solution)/shard_map/ppermute | solution.py:787
  14.8 1.8 %collective-permute-start.4 = (f32[3,40,128]{2,1,0:T(8,128)S(1)}, f32[3,40,128]{2,1,0:T(8,128)S(1)}, u32[]{:S(2)}, u32[]{:S(2)}) collective-permute-start(f32[3,40,128]{2,1,0:T(8,128)S(1)} %get-tuple-element.42), channel_id=1, source_target_pairs={{0,1},{1,0},{2,3},{3,2},{4,5},{5,4},{6,7},{7,6},{8,9},{9,8},{10,11... | collective-permute-start | bytes 184328 | tf_op jit(solution)/shard_map/ppermute | solution.py:787
  14.9 1.8 %collective-permute-start.5 = (f32[3,40,128]{2,1,0:T(8,128)S(1)}, f32[3,40,128]{2,1,0:T(8,128)S(1)}, u32[]{:S(2)}, u32[]{:S(2)}) collective-permute-start(f32[3,40,128]{2,1,0:T(8,128)S(1)} %get-tuple-element.43), channel_id=1, source_target_pairs={{0,1},{1,0},{2,3},{3,2},{4,5},{5,4},{6,7},{7,6},{8,9},{9,8},{10,11... | collective-permute-start | bytes 184328 | tf_op jit(solution)/shard_map/ppermute | solution.py:787
  18.0 1.4 %collective-permute-start.7 = (f32[176,128]{1,0:T(8,128)S(1)}, f32[176,128]{1,0:T(8,128)S(1)}, u32[]{:S(2)}, u32[]{:S(2)}) collective-permute-start(f32[176,128]{1,0:T(8,128)S(1)} %get-tuple-element.54), channel_id=1, source_target_pairs={{1,0},{0,1},{3,2},{2,3},{5,4},{4,5},{7,6},{6,7},{9,8},{8,9},{11,10... | collective-permute-start | bytes 270344 | tf_op jit(solution)/shard_map/ppermute | solution.py:572
  19.4 6.0 %collective-permute-start.8 = (f32[136,128]{1,0:T(8,128)S(1)}, f32[136,128]{1,0:T(8,128)S(1)}, u32[]{:S(2)}, u32[]{:S(2)}) collective-permute-start(f32[136,128]{1,0:T(8,128)S(1)} %get-tuple-element.56), channel_id=1, source_target_pairs={{7,0},{2,1},{1,2},{4,3},{3,4},{6,5},{5,6},{0,7},{15,8},{10,9},{9,1... | collective-permute-start | bytes 208904 | tf_op jit(solution)/shard_map/ppermute | solution.py:572
  20.7 3.9 %collective-permute-start.9 = (f32[40,128]{1,0:T(8,128)S(1)}, f32[40,128]{1,0:T(8,128)S(1)}, u32[]{:S(2)}, u32[]{:S(2)}) collective-permute-start(f32[40,128]{1,0:T(8,128)S(1)} %get-tuple-element.57), channel_id=1, source_target_pairs={{4,0},{6,1},{5,2},{7,3},{0,4},{2,5},{1,6},{3,7},{12,8},{14,9},{13,... | collective-permute-start | bytes 61448 | tf_op jit(solution)/shard_map/ppermute | solution.py:572
  22.2 3.2 %collective-permute-start.10 = (f32[40,128]{1,0:T(8,128)S(1)}, f32[40,128]{1,0:T(8,128)S(1)}, u32[]{:S(2)}, u32[]{:S(2)}) collective-permute-start(f32[40,128]{1,0:T(8,128)S(1)} %get-tuple-element.58), channel_id=1, source_target_pairs={{3,0},{5,1},{6,2},{0,3},{7,4},{1,5},{2,6},{4,7},{11,8},{13,9},{14,... | collective-permute-start | bytes 61448 | tf_op jit(solution)/shard_map/ppermute | solution.py:572

commit v25 on v24

--- a/solution.py
+++ b/solution.py
@@ -719,7 +719,7 @@
             sc[1, i] = st[GA, i] + gas
         return carry
 
-    lax.fori_loop(0, blocks, correct, 0, unroll=3)
+    lax.fori_loop(0, blocks, correct, 0)
     gas = coarse[2, blocks - 1] * gas_in + coarse[3, blocks - 1]
     gas_high = wide[5] * gas + wide[4]
     solid_high = wide[3] + wide[6] * gas_high

time: 28.2 us -> 28.2 us (level)
  no operation moved by 1% of the time
where the time goes in v25:
time: 28.2 us; the launch traced here: 27.7 us
  starting transfers between devices  11.4 us (40%)
  waiting for transfers between devices  8.8 us (31%)
  Pallas kernels  7.34 us (26%)
    ppermute x7, starting transfers between devices, swap(): return lax.ppermute(x, axis, pairs)  8.31 us
    ppermute x7, waiting for transfers between devices, swap(): return lax.ppermute(x, axis, pairs)  4.59 us
    ppermute x4, waiting for transfers between devices, exchange_stage(): lax.ppermute(message, 'gy', [(sender, me) for me, sender in enumerate(sen...  4.21 us
    ppermute x4, starting transfers between devices, exchange_stage(): lax.ppermute(message, 'gy', [(sender, me) for me, sender in enumerate(sen...  3.13 us
    pallas_call x1, Pallas kernels, shards(): pl.pallas_call(functools.partial(third_kernel, radices[-1], stride), out_...  2.3 us
    pallas_call x1, Pallas kernels, shards(): pl.pallas_call(pack_kernel, out_shape=(strip, strip, state), in_specs=[HB...  1.48 us
    pallas_call x1, Pallas kernels, shards(): pl.pallas_call(inner_kernel, out_shape=(state, rows), in_specs=[VMEM] * 2...  1.3 us
    pallas_call x1, Pallas kernels, shards(): pl.pallas_call(second_kernel, out_shape=(state, rows, more, tall(lay.map)...  0.66 us
  transfers between devices with their start and end apart: 11, of which 5 were waited for; matrix products, arithmetic and copies ran while one was open for 0% of the time, Pallas kernels for 10%

profile of v25, /device:TPU:16, one launch (start us, length us, event | category | flops | bytes accessed | tf_op | source)
XLA Modules:
  0.0 27.7 jit_solution(11249632317123866813)
XLA Ops:
  0.0 1.5 %pack_x.1 = (f32[304,128]{1,0:T(8,128)S(1)}, f32[304,128]{1,0:T(8,128)S(1)}, f32[15,14,48,128]{3,2,1,0:T(8,128)S(1)}) custom-call(f32[2,12,32,128]{3,2,1,0:T(8,128)} %bitcast.5, f32[2,12,32,128]{3,2,1,0:T(8,128)} %bitcast.6, f32[12,32,128]{2,1,0:T(8,128)} %bitcast.7, f32[12,32,128]{2,1,0:T(8,128)} %bitcast.8), custom_call_target="tpu_custom_call" | custom-call | tf_op jit(solution)/shard_map/pack_x/pallas_call | solution.py:802
  1.5 1.6 %collective-permute-start = (f32[304,128]{1,0:T(8,128)S(1)}, f32[304,128]{1,0:T(8,128)S(1)}, u32[]{:S(2)}, u32[]{:S(2)}) collective-permute-start(f32[304,128]{1,0:T(8,128)S(1)} %get-tuple-element.34), channel_id=1, source_target_pairs={{0,8},{8,0},{16,24},{24,16},{1,9},{9,1},{17,25},{25,17},{2,10},{10... | collective-permute-start | bytes 466952 | tf_op jit(solution)/shard_map/ppermute | solution.py:787
  3.1 1.9 %collective-permute-start.1 = (f32[304,128]{1,0:T(8,128)S(1)}, f32[304,128]{1,0:T(8,128)S(1)}, u32[]{:S(2)}, u32[]{:S(2)}) collective-permute-start(f32[304,128]{1,0:T(8,128)S(1)} %get-tuple-element.35), channel_id=1, source_target_pairs={{8,16},{16,8},{9,17},{17,9},{10,18},{18,10},{11,19},{19,11},{12,20... | collective-permute-start | bytes 466952 | tf_op jit(solution)/shard_map/ppermute | solution.py:787
  5.0 0.2 conduct.1
  5.2 0.7 %collective-permute-start.2 = (f32[7,32,128]{2,1,0:T(8,128)S(1)}, f32[7,32,128]{2,1,0:T(8,128)S(1)}, u32[]{:S(2)}, u32[]{:S(2)}) collective-permute-start(f32[7,32,128]{2,1,0:T(8,128)S(1)} %get-tuple-element.38), channel_id=1, source_target_pairs={{1,2},{2,1},{3,4},{4,3},{5,6},{6,5},{9,10},{10,9},{11,12},{12,11},... | collective-permute-start | bytes 344072 | tf_op jit(solution)/shard_map/ppermute | solution.py:787
  5.9 1.4 %collective-permute-done.one = f32[304,128]{1,0:T(8,128)S(1)} collective-permute-done((f32[304,128]{1,0:T(8,128)S(1)}, f32[304,128]{1,0:T(8,128)S(1)}, u32[]{:S(2)}, u32[]{:S(2)}) %collective-permute-start) | collective-permute-done | bytes 155680 | tf_op jit(solution)/shard_map/ppermute | solution.py:787
  7.3 3.2 %collective-permute-done.1.two = f32[304,128]{1,0:T(8,128)S(1)} collective-permute-done((f32[304,128]{1,0:T(8,128)S(1)}, f32[304,128]{1,0:T(8,128)S(1)}, u32[]{:S(2)}, u32[]{:S(2)}) %collective-permute-start.1) | collective-permute-done | bytes 155680 | tf_op jit(solution)/shard_map/ppermute | solution.py:787
  10.5 0.2 first.1
  10.7 0.7 %collective-permute-start.6 = (f32[144,128]{1,0:T(8,128)S(1)}, f32[144,128]{1,0:T(8,128)S(1)}, u32[]{:S(2)}, u32[]{:S(2)}) collective-permute-start(f32[144,128]{1,0:T(8,128)S(1)} %get-tuple-element.47), channel_id=1, source_target_pairs={{1,2},{2,1},{3,4},{4,3},{5,6},{6,5},{9,10},{10,9},{11,12},{12,11},... | collective-permute-start | bytes 221192 | tf_op jit(solution)/shard_map/ppermute | solution.py:787
  11.4 0.5 %other.1 = (f32[15,14,48,128]{3,2,1,0:T(8,128)S(1)}, f32[3,40,128]{2,1,0:T(8,128)S(1)}, f32[3,40,128]{2,1,0:T(8,128)S(1)}, f32[3,40,128]{2,1,0:T(8,128)S(1)}) custom-call(f32[15,14,48,128]{3,2,1,0:T(8,128)S(1)} %get-tuple-element.36.st_in, f32[304,128]{1,0:T(8,128)S(1)} %collective-permute-done.one, ...), custom_call_target="tpu_custom_call", output_to_operand_aliasing={{0}: (0, {})} | custom-call | tf_op jit(solution)/shard_map/other/pallas_call | solution.py:836
  11.9 2.9 %collective-permute-start.3 = (f32[3,40,128]{2,1,0:T(8,128)S(1)}, f32[3,40,128]{2,1,0:T(8,128)S(1)}, u32[]{:S(2)}, u32[]{:S(2)}) collective-permute-start(f32[3,40,128]{2,1,0:T(8,128)S(1)} %get-tuple-element.41), channel_id=1, source_target_pairs={{0,1},{1,0},{2,3},{3,2},{4,5},{5,4},{6,7},{7,6},{8,9},{9,8},{10,11... | collective-permute-start | bytes 184328 | tf_op jit(solution)/shard_map/ppermute | solution.py:787
  14.8 0.1 collective-permute-start.4
  14.9 0.4 %collective-permute-start.5 = (f32[3,40,128]{2,1,0:T(8,128)S(1)}, f32[3,40,128]{2,1,0:T(8,128)S(1)}, u32[]{:S(2)}, u32[]{:S(2)}) collective-permute-start(f32[3,40,128]{2,1,0:T(8,128)S(1)} %get-tuple-element.43), channel_id=1, source_target_pairs={{0,1},{1,0},{2,3},{3,2},{4,5},{5,4},{6,7},{7,6},{8,9},{9,8},{10,11... | collective-permute-start | bytes 184328 | tf_op jit(solution)/shard_map/ppermute | solution.py:787
  15.3 1.3 %inner.1 = (f32[15,14,48,128]{3,2,1,0:T(8,128)S(1)}, f32[4,6,48,128]{3,2,1,0:T(8,128)S(1)}) custom-call(f32[15,14,48,128]{3,2,1,0:T(8,128)S(1)} %get-tuple-element.37.st_in, f32[7,32,128]{2,1,0:T(8,128)S(1)} %collective-permute-done.2.early), custom_call_target="tpu_custom_call", output_to_operand_aliasing={{0}: (0, {})} | custom-call | flops 14745600 | bytes 18874368 | tf_op jit(solution)/shard_map/inner/pallas_call | solution.py:848
  16.7 0.6 %near.1 = (f32[15,14,48,128]{3,2,1,0:T(8,128)S(1)}, f32[4,6,48,128]{3,2,1,0:T(8,128)S(1)}, f32[6,48,128]{2,1,0:T(8,128)S(1)}) custom-call(f32[15,14,48,128]{3,2,1,0:T(8,128)S(1)} %get-tuple-element.39.st_in, f32[4,6,48,128]{3,2,1,0:T(8,128)S(1)} %get-tuple-element.40.coarse_in, ...), custom_call_target="tpu_custom_call", output_to_operand_aliasing={{0}: (0, {}), {1}: (1, {})} | custom-call | tf_op jit(solution)/shard_map/near/pallas_call | solution.py:868
  17.3 0.7 %second.1 = (f32[15,14,48,128]{3,2,1,0:T(8,128)S(1)}, f32[4,6,48,128]{3,2,1,0:T(8,128)S(1)}, f32[6,48,128]{2,1,0:T(8,128)S(1)}, f32[40,128]{1,0:T(8,128)S(1)}, f...) custom-call(f32[15,14,48,128]{3,2,1,0:T(8,128)S(1)} %get-tuple-eleme, ...), custom_call_target="tpu_custom_call", output_to_operand_aliasing={{0}: (0, {}), {1}: (1, {}), {2}: (2, {})} | custom-call | tf_op jit(solution)/shard_map/second/pallas_call | solution.py:878
  18.0 0.1 collective-permute-start.7
  18.1 1.2 %collective-permute-done.7.refs_4_ = f32[176,128]{1,0:T(8,128)S(1)} collective-permute-done((f32[176,128]{1,0:T(8,128)S(1)}, f32[176,128]{1,0:T(8,128)S(1)}, u32[]{:S(2)}, u32[]{:S(2)}) %collective-permute-start.7) | collective-permute-done | bytes 90144 | tf_op jit(solution)/shard_map/ppermute | solution.py:572
  19.4 1.3 %collective-permute-start.8 = (f32[136,128]{1,0:T(8,128)S(1)}, f32[136,128]{1,0:T(8,128)S(1)}, u32[]{:S(2)}, u32[]{:S(2)}) collective-permute-start(f32[136,128]{1,0:T(8,128)S(1)} %get-tuple-element.56), channel_id=1, source_target_pairs={{7,0},{2,1},{1,2},{4,3},{3,4},{6,5},{5,6},{0,7},{15,8},{10,9},{9,1... | collective-permute-start | bytes 208904 | tf_op jit(solution)/shard_map/ppermute | solution.py:572
  20.7 1.5 %collective-permute-start.9 = (f32[40,128]{1,0:T(8,128)S(1)}, f32[40,128]{1,0:T(8,128)S(1)}, u32[]{:S(2)}, u32[]{:S(2)}) collective-permute-start(f32[40,128]{1,0:T(8,128)S(1)} %get-tuple-element.57), channel_id=1, source_target_pairs={{4,0},{6,1},{5,2},{7,3},{0,4},{2,5},{1,6},{3,7},{12,8},{14,9},{13,... | collective-permute-start | bytes 61448 | tf_op jit(solution)/shard_map/ppermute | solution.py:572
  22.2 0.2 collective-permute-start.10
  22.4 2.2 %collective-permute-done.9.refs_5_ = f32[40,128]{1,0:T(8,128)S(1)} collective-permute-done((f32[40,128]{1,0:T(8,128)S(1)}, f32[40,128]{1,0:T(8,128)S(1)}, u32[]{:S(2)}, u32[]{:S(2)}) %collective-permute-start.9) | collective-permute-done | bytes 20512 | tf_op jit(solution)/shard_map/ppermute | solution.py:572
  24.6 0.8 %collective-permute-done.10.refs_6_ = f32[40,128]{1,0:T(8,128)S(1)} collective-permute-done((f32[40,128]{1,0:T(8,128)S(1)}, f32[40,128]{1,0:T(8,128)S(1)}, u32[]{:S(2)}, u32[]{:S(2)}) %collective-permute-start.10) | collective-permute-done | bytes 20512 | tf_op jit(solution)/shard_map/ppermute | solution.py:572
  25.4 2.3 %third.1 = f32[2,12,32,128]{3,2,1,0:T(8,128)} custom-call(f32[15,14,48,128]{3,2,1,0:T(8,128)S(1)} %get-tuple-element.48.refs_0_, f32[6,48,128]{2,1,0:T(8,128)S(1)} %get-tuple-element.49.refs_1_, f32[4,6,48,128]{3,2,1,0:T(8,128)S(1)} %get-tuple-element.50.refs_2_, f32[272,128]{1,0:T(8,128)S(1)} %get-tuple-element.55.refs_3_, ...), custom_call_target="tpu_custom_call" | custom-call | tf_op jit(solution)/shard_map/third/pallas_call | solution.py:912
  (7 shorter events, 0.1 us)
Async XLA Ops:
  1.5 5.8 %collective-permute-start = (f32[304,128]{1,0:T(8,128)S(1)}, f32[304,128]{1,0:T(8,128)S(1)}, u32[]{:S(2)}, u32[]{:S(2)}) collective-permute-start(f32[304,128]{1,0:T(8,128)S(1)} %get-tuple-element.34), channel_id=1, source_target_pairs={{0,8},{8,0},{16,24},{24,16},{1,9},{9,1},{17,25},{25,17},{2,10},{10... | collective-permute-start | bytes 466952 | tf_op jit(solution)/shard_map/ppermute | solution.py:787
  3.1 7.4 %collective-permute-start.1 = (f32[304,128]{1,0:T(8,128)S(1)}, f32[304,128]{1,0:T(8,128)S(1)}, u32[]{:S(2)}, u32[]{:S(2)}) collective-permute-start(f32[304,128]{1,0:T(8,128)S(1)} %get-tuple-element.35), channel_id=1, source_target_pairs={{8,16},{16,8},{9,17},{17,9},{10,18},{18,10},{11,19},{19,11},{12,20... | collective-permute-start | bytes 466952 | tf_op jit(solution)/shard_map/ppermute | solution.py:787
  5.2 10.1 %collective-permute-start.2 = (f32[7,32,128]{2,1,0:T(8,128)S(1)}, f32[7,32,128]{2,1,0:T(8,128)S(1)}, u32[]{:S(2)}, u32[]{:S(2)}) collective-permute-start(f32[7,32,128]{2,1,0:T(8,128)S(1)} %get-tuple-element.38), channel_id=1, source_target_pairs={{1,2},{2,1},{3,4},{4,3},{5,6},{6,5},{9,10},{10,9},{11,12},{12,11},... | collective-permute-start | bytes 344072 | tf_op jit(solution)/shard_map/ppermute | solution.py:787
  10.7 6.6 %collective-permute-start.6 = (f32[144,128]{1,0:T(8,128)S(1)}, f32[144,128]{1,0:T(8,128)S(1)}, u32[]{:S(2)}, u32[]{:S(2)}) collective-permute-start(f32[144,128]{1,0:T(8,128)S(1)} %get-tuple-element.47), channel_id=1, source_target_pairs={{1,2},{2,1},{3,4},{4,3},{5,6},{6,5},{9,10},{10,9},{11,12},{12,11},... | collective-permute-start | bytes 221192 | tf_op jit(solution)/shard_map/ppermute | solution.py:787
  11.9 4.7 %collective-permute-start.3 = (f32[3,40,128]{2,1,0:T(8,128)S(1)}, f32[3,40,128]{2,1,0:T(8,128)S(1)}, u32[]{:S(2)}, u32[]{:S(2)}) collective-permute-start(f32[3,40,128]{2,1,0:T(8,128)S(1)} %get-tuple-element.41), channel_id=1, source_target_pairs={{0,1},{1,0},{2,3},{3,2},{4,5},{5,4},{6,7},{7,6},{8,9},{9,8},{10,11... | collective-permute-start | bytes 184328 | tf_op jit(solution)/shard_map/ppermute | solution.py:787
  14.8 1.8 %collective-permute-start.4 = (f32[3,40,128]{2,1,0:T(8,128)S(1)}, f32[3,40,128]{2,1,0:T(8,128)S(1)}, u32[]{:S(2)}, u32[]{:S(2)}) collective-permute-start(f32[3,40,128]{2,1,0:T(8,128)S(1)} %get-tuple-element.42), channel_id=1, source_target_pairs={{0,1},{1,0},{2,3},{3,2},{4,5},{5,4},{6,7},{7,6},{8,9},{9,8},{10,11... | collective-permute-start | bytes 184328 | tf_op jit(solution)/shard_map/ppermute | solution.py:787
  14.9 1.8 %collective-permute-start.5 = (f32[3,40,128]{2,1,0:T(8,128)S(1)}, f32[3,40,128]{2,1,0:T(8,128)S(1)}, u32[]{:S(2)}, u32[]{:S(2)}) collective-permute-start(f32[3,40,128]{2,1,0:T(8,128)S(1)} %get-tuple-element.43), channel_id=1, source_target_pairs={{0,1},{1,0},{2,3},{3,2},{4,5},{5,4},{6,7},{7,6},{8,9},{9,8},{10,11... | collective-permute-start | bytes 184328 | tf_op jit(solution)/shard_map/ppermute | solution.py:787
  18.0 1.4 %collective-permute-start.7 = (f32[176,128]{1,0:T(8,128)S(1)}, f32[176,128]{1,0:T(8,128)S(1)}, u32[]{:S(2)}, u32[]{:S(2)}) collective-permute-start(f32[176,128]{1,0:T(8,128)S(1)} %get-tuple-element.54), channel_id=1, source_target_pairs={{1,0},{0,1},{3,2},{2,3},{5,4},{4,5},{7,6},{6,7},{9,8},{8,9},{11,10... | collective-permute-start | bytes 270344 | tf_op jit(solution)/shard_map/ppermute | solution.py:572
  19.4 6.0 %collective-permute-start.8 = (f32[136,128]{1,0:T(8,128)S(1)}, f32[136,128]{1,0:T(8,128)S(1)}, u32[]{:S(2)}, u32[]{:S(2)}) collective-permute-start(f32[136,128]{1,0:T(8,128)S(1)} %get-tuple-element.56), channel_id=1, source_target_pairs={{7,0},{2,1},{1,2},{4,3},{3,4},{6,5},{5,6},{0,7},{15,8},{10,9},{9,1... | collective-permute-start | bytes 208904 | tf_op jit(solution)/shard_map/ppermute | solution.py:572
  20.7 3.9 %collective-permute-start.9 = (f32[40,128]{1,0:T(8,128)S(1)}, f32[40,128]{1,0:T(8,128)S(1)}, u32[]{:S(2)}, u32[]{:S(2)}) collective-permute-start(f32[40,128]{1,0:T(8,128)S(1)} %get-tuple-element.57), channel_id=1, source_target_pairs={{4,0},{6,1},{5,2},{7,3},{0,4},{2,5},{1,6},{3,7},{12,8},{14,9},{13,... | collective-permute-start | bytes 61448 | tf_op jit(solution)/shard_map/ppermute | solution.py:572
  22.2 3.2 %collective-permute-start.10 = (f32[40,128]{1,0:T(8,128)S(1)}, f32[40,128]{1,0:T(8,128)S(1)}, u32[]{:S(2)}, u32[]{:S(2)}) collective-permute-start(f32[40,128]{1,0:T(8,128)S(1)} %get-tuple-element.58), channel_id=1, source_target_pairs={{3,0},{5,1},{6,2},{0,3},{7,4},{1,5},{2,6},{4,7},{11,8},{13,9},{14,... | collective-permute-start | bytes 61448 | tf_op jit(solution)/shard_map/ppermute | solution.py:572
